TPU v7x, 32 devices: a whole 2x2x4 slice. The times are simulated.
32 devices in a mesh: dp: 4 (over z), cout: 4 (over y, x), cin: 2 (over core).
Axes of the slice: x: 2, y: 2, z: 4, core: 2. Of those that a mesh axis runs over, the one named last changes fastest.
Arguments:
- images: bfloat16 [16, 512, 512], P(None, ('dp', 'cin')), may hold values from -6 to 6
- masks: int32 [16, 512], P(None, ('dp', 'cin')), may hold values from 0 to 1, as said below
- labels: int32 [512], P(('dp', 'cin')), may hold values from 0 to 9
- w_first: float32 [9, 512, 512], P(None, None, 'cout'), may hold values from -0.09375 to 0.09375
- w_second: float32 [9, 512, 512], P(None, 'cout'), may hold values from -0.09375 to 0.09375
- norm_params: float32 [4, 512], P(None, 'cout'), may hold values from 0.1 to 1.9
- head_w: float32 [512, 10], P('cout'), may hold values from -1 to 1
- head_b: float32 [10], replicated, may hold values from -1.75 to 1.75
- bases: bfloat16 [2, 2, 512, 512], replicated, may hold values from -1 to 1
- scales_first: float32 [9, 512, 512], P(None, None, 'cout'), may hold values from 0.0090112 to 0.073728
- scales_second: float32 [9, 512, 512], P(None, 'cout'), may hold values from 0.0090112 to 0.073728
- w_first_mean: float32 [9, 512, 512], P(None, None, 'cout'), may hold values from -0.00030517578 to 0.00030517578
- w_first_square: float32 [9, 512, 512], P(None, None, 'cout'), may hold values from 2.1192763e-10 to 8.477105e-10
- w_second_mean: float32 [9, 512, 512], P(None, 'cout'), may hold values from -0.00030517578 to 0.00030517578
- w_second_square: float32 [9, 512, 512], P(None, 'cout'), may hold values from 2.1192763e-10 to 8.477105e-10
- norm_mean: float32 [4, 512], P(None, 'cout'), may hold values from -9.3789174e-05 to 9.3789174e-05
- norm_square: float32 [4, 512], P(None, 'cout'), may hold values from 1.28e-14 to 1.573376e-10
- head_w_mean: float32 [512, 10], P('cout'), may hold values from -0.00012207031 to 0.00012207031
- head_w_square: float32 [512, 10], P('cout'), may hold values from 4.194304e-11 to 1.6777216e-10
- head_b_mean: float32 [10], replicated, may hold values from -0.00024414062 to 0.00024414062
- head_b_square: float32 [10], replicated, may hold values from 1.6777216e-10 to 6.815744e-10
Outputs:
- loss_total: float32 [], replicated
- grad_norm: float32 [], replicated
- w_first_new: float32 [9, 512, 512], P(None, None, 'cout')
- w_first_mean_new: float32 [9, 512, 512], P(None, None, 'cout')
- w_first_square_new: float32 [9, 512, 512], P(None, None, 'cout')
- w_second_new: float32 [9, 512, 512], P(None, 'cout')
- w_second_mean_new: float32 [9, 512, 512], P(None, 'cout')
- w_second_square_new: float32 [9, 512, 512], P(None, 'cout')
- norm_first_mean_new: float32 [2, 512], P(None, 'cout')
- norm_first_square_new: float32 [2, 512], P(None, 'cout')
- norm_second_mean_new: float32 [2, 512], P(None, 'cout')
- norm_second_square_new: float32 [2, 512], P(None, 'cout')
- head_w_mean_new: float32 [512, 10], P('cout')
- head_w_square_new: float32 [512, 10], P('cout')
- head_b_mean_new: float32 [10], replicated
- head_b_square_new: float32 [10], replicated
- scales_first_new: float32 [9, 512, 512], P(None, None, 'cout')
- scales_second_new: float32 [9, 512, 512], P(None, 'cout')
Inputs may be any that keep to these rules, and one draw needn't show every extreme that they name: `masks`: each image keeps one rectangle of 2 to 4 by 2 to 4 pixels.
All inputs are finite; a program needn't handle non-finite values.
Results may differ from a plain program's by a relative error of at most 0.025.
Values may be sent and summed in bfloat16 or wider, within the bound.
No kernel may reach another device: no remote copies, remote signals or barrier semaphores. Data moves between devices by JAX's collectives and lax.ppermute only.
A program may use at most 128 MiB of HBM per device.

v0:
```python
import jax
import jax.numpy as jnp
from jax import lax
from jax.sharding import PartitionSpec as P

CLASSES = 10
SIDE = 4
PIX = 16
TAPS = 9
STEP = 10


PRECISE = lax.Precision.HIGHEST
EPS_NORM = 1e-05
SCALE_DECAY = 0.95
DAMPING = 0.001
CLIP_NORM = 1.0
LEARN_RATE = 0.01
BETA_ONE = 0.9
BETA_TWO = 0.999
ADAM_EPS = 1e-08
WEIGHT_DECAY = 0.01
SMOOTH = 0.1
OFFSETS = [(row_step, col_step) for row_step in (-1, 0, 1) for col_step in (-1, 0, 1)]


def shifted(values, row_step, col_step):
    cell_grid = values.reshape((SIDE, SIDE) + values.shape[1:])
    padding = [(1, 1), (1, 1)] + [(0, 0)] * (values.ndim - 1)
    padded = jnp.pad(cell_grid, padding)
    window = padded[1 + row_step : 1 + row_step + SIDE, 1 + col_step : 1 + col_step + SIDE]
    return window.reshape(values.shape)


def convolve(values, weight):
    summed = None
    for tap_index, (row_step, col_step) in enumerate(OFFSETS):
        product = jnp.einsum(
            "pbi,io->pbo",
            shifted(values, row_step, col_step),
            weight[tap_index],
            preferred_element_type=jnp.float32,
        )
        summed = product if summed is None else summed + product
    return summed


def convolve_back(cotangent, weight):
    summed = None
    for tap_index, (row_step, col_step) in enumerate(OFFSETS):
        product = jnp.einsum(
            "pbo,io->pbi", cotangent, weight[tap_index], preferred_element_type=jnp.float32
        )
        moved = shifted(product, -row_step, -col_step)
        summed = moved if summed is None else summed + moved
    return summed


def moments_of(values, mask_cube):
    return (
        jnp.sum(values * mask_cube, axis=(0, 1)),
        jnp.sum(values * values * mask_cube, axis=(0, 1)),
    )


def normalized(values, first_sum, square_sum, kept_count):
    mean_value = first_sum / kept_count
    inverse_std = lax.rsqrt(square_sum / kept_count - mean_value * mean_value + EPS_NORM)
    return ((values - mean_value) * inverse_std, inverse_std)


def gelu_back(pre_values, upstream):
    return jax.vjp(jax.nn.gelu, pre_values)[1](upstream)[0]


def norm_back(dz_values, scaled, inverse_std, gain, gain_grad, shift_grad, mask_cube, kept_count):
    return inverse_std * (
        gain * dz_values - mask_cube * gain * (shift_grad + scaled * gain_grad) / kept_count
    )


def project(values, basis):
    return jnp.einsum("pbi,ij->pbj", values, basis, preferred_element_type=jnp.float32).astype(
        jnp.bfloat16
    )


def tap_products(left_side, right_side):
    return jnp.stack(
        [
            jnp.einsum(
                "pbj,pbk->jk",
                shifted(left_side, row_step, col_step),
                right_side,
                preferred_element_type=jnp.float32,
            )
            for row_step, col_step in OFFSETS
        ]
    )


def over_batch(values):
    return lax.psum(values, ("dp", "cin"))


def rows_from(block_fn, block_rows, first_row, row_total):
    first_block = first_row // block_rows
    pieces = [block_fn(first_block + offset) for offset in range(row_total // block_rows)]
    return jnp.concatenate(pieces, axis=0)


def moments(gradient, mean_old, square_old):
    mean_new = BETA_ONE * mean_old + (1.0 - BETA_ONE) * gradient
    square_new = BETA_TWO * square_old + (1.0 - BETA_TWO) * gradient * gradient
    return (mean_new, square_new)


def adamw(weight, gradient, mean_old, square_old):
    mean_new, square_new = moments(gradient, mean_old, square_old)
    mean_hat = mean_new / (1.0 - BETA_ONE**STEP)
    square_hat = square_new / (1.0 - BETA_TWO**STEP)
    updated = weight - LEARN_RATE * (
        mean_hat / (jnp.sqrt(square_hat) + ADAM_EPS) + WEIGHT_DECAY * weight
    )
    return (updated, mean_new, square_new)


def local(
    images,
    masks,
    labels,
    w_first,
    w_second,
    norm_params,
    head_w,
    head_b,
    bases,
    scales_first,
    scales_second,
    w_first_mean,
    w_first_square,
    w_second_mean,
    w_second_square,
    norm_mean,
    norm_square,
    head_w_mean,
    head_w_square,
    head_b_mean,
    head_b_square,
):
    cout_index = lax.axis_index("cout")
    channels = w_first.shape[1]
    block_width = w_first.shape[2]
    mask_plane = masks.astype(jnp.float32)
    mask_cube = mask_plane[:, :, None]
    inputs = images * masks.astype(jnp.bfloat16)[:, :, None]
    first_out = convolve(inputs, w_first.astype(jnp.bfloat16))
    first_sum, first_square, kept_count = lax.psum(
        moments_of(first_out, mask_cube) + (jnp.sum(mask_plane),), ("dp", "cin")
    )
    scaled_first, rstd_first = normalized(first_out, first_sum, first_square, kept_count)
    pre_first = norm_params[0] * scaled_first + norm_params[1]
    hidden = (jax.nn.gelu(pre_first) * mask_cube).astype(jnp.bfloat16)
    second_low = w_second.astype(jnp.bfloat16)
    second_out = lax.psum_scatter(
        convolve(hidden, second_low).astype(jnp.bfloat16), "cout", scatter_dimension=2, tiled=True
    ).astype(jnp.float32)
    second_sum, second_square = lax.psum(moments_of(second_out, mask_cube), ("dp", "cin"))
    scaled_second, rstd_second = normalized(second_out, second_sum, second_square, kept_count)
    pre_second = norm_params[2] * scaled_second + norm_params[3]
    pooled_low = (jnp.sum(jax.nn.gelu(pre_second) * mask_cube, axis=0) / PIX).astype(jnp.bfloat16)
    head_low = head_w.astype(jnp.bfloat16)
    logit_part = jnp.dot(pooled_low, head_low, preferred_element_type=jnp.float32)
    logits = lax.psum(logit_part, "cout") + head_b
    log_probs = jax.nn.log_softmax(logits, axis=-1)
    smoothed = (1.0 - SMOOTH) * jax.nn.one_hot(
        labels, CLASSES, dtype=jnp.float32
    ) + SMOOTH / CLASSES
    loss_local = -jnp.sum(smoothed * log_probs)
    logit_grad = jnp.exp(log_probs) - smoothed
    pooled_wide = pooled_low.astype(jnp.float32)
    head_w_part = jnp.dot(pooled_wide.T, logit_grad, precision=PRECISE)
    head_b_part = jnp.sum(logit_grad, axis=0)
    pooled_grad = jnp.dot(logit_grad, head_low.astype(jnp.float32).T, precision=PRECISE)
    dz_second = gelu_back(pre_second, mask_cube * pooled_grad[None, :, :] / PIX)
    gain_two, shift_two, head_w_grad, head_b_grad, loss_total = lax.psum(
        (
            jnp.sum(dz_second * scaled_second, axis=(0, 1)),
            jnp.sum(dz_second, axis=(0, 1)),
            head_w_part,
            head_b_part,
            loss_local,
        ),
        ("dp", "cin"),
    )
    grad_second = norm_back(
        dz_second,
        scaled_second,
        rstd_second,
        norm_params[2],
        gain_two,
        shift_two,
        mask_cube,
        kept_count,
    ).astype(jnp.bfloat16)
    grad_second_full = lax.all_gather(grad_second, "cout", axis=2, tiled=True)
    hidden_grad = convolve_back(grad_second_full, second_low)
    dz_first = gelu_back(pre_first, hidden_grad * mask_cube)
    gain_one, shift_one = lax.psum(
        (jnp.sum(dz_first * scaled_first, axis=(0, 1)), jnp.sum(dz_first, axis=(0, 1))),
        ("dp", "cin"),
    )
    grad_first = norm_back(
        dz_first,
        scaled_first,
        rstd_first,
        norm_params[0],
        gain_one,
        shift_one,
        mask_cube,
        kept_count,
    ).astype(jnp.bfloat16)
    first_rows = TAPS * channels
    block_rows = 2 * first_rows
    hidden_full, grad_first_full = (
        lax.all_gather(hidden, "cout", axis=2, tiled=True),
        lax.all_gather(grad_first, "cout", axis=2, tiled=True),
    )
    out_basis_first = lax.dynamic_slice_in_dim(
        bases[0, 1], cout_index * block_width, block_width, 1
    )
    in_basis_second = lax.dynamic_slice_in_dim(
        bases[1, 0], cout_index * block_width, block_width, 1
    )
    left_first = project(inputs, bases[0, 0])
    right_cols = project(grad_first_full, out_basis_first)
    left_cols = project(hidden_full, in_basis_second)
    right_second = project(grad_second_full, bases[1, 1])
    first_block = tap_products(left_first, right_cols)
    second_block = tap_products(left_cols, right_second)
    own_block = over_batch(
        jnp.concatenate(
            [first_block.reshape(-1, block_width), second_block.reshape(-1, block_width)], axis=0
        )
    )
    coeff_first = own_block[:first_rows].reshape(TAPS, channels, block_width)
    coeff_second = own_block[first_rows:].reshape(TAPS, block_width, channels)
    scales_first_new = SCALE_DECAY * scales_first + (1.0 - SCALE_DECAY) * coeff_first * coeff_first
    scales_second_new = (
        SCALE_DECAY * scales_second + (1.0 - SCALE_DECAY) * coeff_second * coeff_second
    )
    ratio_first = coeff_first / (scales_first_new + DAMPING)
    ratio_second = coeff_second / (scales_second_new + DAMPING)
    basis_in_first = bases[0, 0].astype(jnp.float32)
    basis_out_first = bases[0, 1].astype(jnp.float32)
    basis_in_second = bases[1, 0].astype(jnp.float32)
    basis_out_second = bases[1, 1].astype(jnp.float32)
    first_middle = jnp.einsum("ij,tjk->tik", basis_in_first, ratio_first, precision=PRECISE)
    second_middle = jnp.einsum("tjk,lk->tjl", ratio_second, basis_out_second, precision=PRECISE)
    out_mine = lax.dynamic_slice_in_dim(basis_out_first, cout_index * block_width, block_width, 1)
    in_mine = lax.dynamic_slice_in_dim(basis_in_second, cout_index * block_width, block_width, 1)

    def restore_block(block_index):
        out_rows = lax.dynamic_slice_in_dim(out_mine, block_index * block_width, block_width, 0)
        in_rows = lax.dynamic_slice_in_dim(in_mine, block_index * block_width, block_width, 0)
        first_part = jnp.einsum("tik,lk->til", first_middle, out_rows, precision=PRECISE)
        second_part = jnp.einsum("ij,tjl->til", in_rows, second_middle, precision=PRECISE)
        return jnp.concatenate(
            [first_part.reshape(-1, block_width), second_part.reshape(-1, block_width)], axis=0
        )

    restored = lax.psum_scatter(
        rows_from(
            restore_block, block_rows, jnp.int32(0), lax.axis_size("cout") * block_rows
        ).astype(jnp.bfloat16),
        "cout",
        scatter_dimension=0,
        tiled=True,
    ).astype(jnp.float32)
    precond_first = restored[:first_rows].reshape(TAPS, channels, block_width)
    precond_second = restored[first_rows:].reshape(TAPS, block_width, channels)
    norm_grad = jnp.stack([gain_one, shift_one, gain_two, shift_two])
    bias_square = jnp.where(cout_index == 0, jnp.sum(head_b_grad * head_b_grad), 0.0)
    local_square = jnp.sum(precond_first * precond_first) + jnp.sum(precond_second * precond_second)
    local_square = (
        local_square
        + jnp.sum(norm_grad * norm_grad)
        + jnp.sum(head_w_grad * head_w_grad)
        + bias_square
    )
    grad_norm = jnp.sqrt(lax.psum(local_square, "cout"))
    factor = CLIP_NORM / jnp.maximum(grad_norm, CLIP_NORM)
    first_new, first_mean_new, first_square_new = adamw(
        w_first, factor * precond_first, w_first_mean, w_first_square
    )
    second_new, second_mean_new, second_square_new = adamw(
        w_second, factor * precond_second, w_second_mean, w_second_square
    )
    norm_mean_new, norm_square_new = moments(factor * norm_grad, norm_mean, norm_square)
    head_mean_new, head_square_new = moments(factor * head_w_grad, head_w_mean, head_w_square)
    bias_mean_new, bias_square_new = moments(factor * head_b_grad, head_b_mean, head_b_square)
    return (
        loss_total,
        grad_norm,
        first_new,
        first_mean_new,
        first_square_new,
        second_new,
        second_mean_new,
        second_square_new,
        norm_mean_new[:2],
        norm_square_new[:2],
        norm_mean_new[2:],
        norm_square_new[2:],
        head_mean_new,
        head_square_new,
        bias_mean_new,
        bias_square_new,
        scales_first_new,
        scales_second_new,
    )


def solution(mesh):
    return jax.shard_map(
        local,
        mesh=mesh,
        in_specs=(
            P(None, ("dp", "cin"), None),
            P(None, ("dp", "cin")),
            P(("dp", "cin")),
            P(None, None, "cout"),
            P(None, "cout", None),
            P(None, "cout"),
            P("cout", None),
            P(),
            P(),
            P(None, None, "cout"),
            P(None, "cout", None),
            P(None, None, "cout"),
            P(None, None, "cout"),
            P(None, "cout", None),
            P(None, "cout", None),
            P(None, "cout"),
            P(None, "cout"),
            P("cout", None),
            P("cout", None),
            P(),
            P(),
        ),
        out_specs=(
            P(),
            P(),
            P(None, None, "cout"),
            P(None, None, "cout"),
            P(None, None, "cout"),
            P(None, "cout", None),
            P(None, "cout", None),
            P(None, "cout", None),
            P(None, "cout"),
            P(None, "cout"),
            P(None, "cout"),
            P(None, "cout"),
            P("cout", None),
            P("cout", None),
            P(),
            P(),
            P(None, None, "cout"),
            P(None, "cout", None),
        ),
        check_vma=False,
    )
```

profile of v0, /device:TPU:0, one launch (start us, length us, event | category | flops | bytes accessed | tf_op | source)
XLA Modules:
  0.0 544.3 jit_solution(1581233909830193471)
XLA Ops:
  16.6 18.7 %all-reduce.15 = (f32[128]{0:T(128)S(1)}, f32[]{:T(128)}, f32[128]{0:T(128)S(1)}) all-reduce(f32[128]{0:T(128)S(1)} %get-tuple-element.21, f32[]{:T(128)} %convert_reduce_fusion, f32[128]{0:T(128)S(1)} %get-tuple-element.20), channel_id=1, replica_groups=mesh['dp'=4,'cout'=4,'cin'=2] {'dp','cin'}, use_global_device_ids=true, to_apply=%region_1.2 | all-reduce | flops 257 | bytes 2056 | tf_op jit(solution)/shard_map/psum | solution.py:158
  36.8 1.8 convert_element_type.109
  42.0 1.9 add_convert_fusion
  43.8 3.8 copy.78
  47.6 4.1 reshape.396
  52.6 25.3 %reduce-scatter.7.cloned.1.call-done = bf16[128,1024]{1,0:T(8,128)(2,1)} async-done(((bf16[512,1024]{1,0:T(8,128)(2,1)}), bf16[128,1024]{1,0:T(8,128)(2,1)}) %reduce-scatter.7.cloned.1.call-update) | async-done | bytes 262160
  79.9 16.4 %all-reduce.14 = (f32[128]{0:T(128)S(1)}, f32[128]{0:T(128)S(1)}) all-reduce(f32[128]{0:T(128)S(1)} %get-tuple-element.27, f32[128]{0:T(128)S(1)} %get-tuple-element.26), channel_id=1, replica_groups=mesh['dp'=4,'cout'=4,'cin'=2] {'dp','cin'}, use_global_device_ids=true, to_apply=%region_8.9 | all-reduce | flops 256 | bytes 2048 | tf_op jit(solution)/shard_map/psum | solution.py:168
  98.5 9.7 %psum.110 = f32[64,10]{0,1:T(8,128)S(1)} all-reduce(f32[64,10]{0,1:T(8,128)S(1)} %fusion.155), channel_id=1, replica_groups=mesh['dp'=4,'cout'=4,'cin'=2] {'cout'}, use_global_device_ids=true, to_apply=%region_12.13 | all-reduce | flops 640 | bytes 5120 | tf_op jit(solution)/shard_map/psum | solution.py:174
  113.1 14.3 %all-reduce.13 = (f32[128]{0:T(128)}, f32[128]{0:T(128)}) all-reduce(f32[128]{0:T(128)} %get-tuple-element.25, f32[128]{0:T(128)} %get-tuple-element.24), channel_id=1, replica_groups=mesh['dp'=4,'cout'=4,'cin'=2] {'dp','cin'}, use_global_device_ids=true, to_apply=%region_20.21 | all-reduce | flops 256 | bytes 2048 | tf_op jit(solution)/shard_map/psum | solution.py:186
  127.3 2.3 fusion.82
  129.7 2.1 fusion.188
  131.8 1.9 convolution_convert_fusion.9
  134.7 3.8 pad_slice_fusion
  144.1 9.4 %all-gather.4.cloned.1.call-done = bf16[16,64,512]{2,1,0:T(8,128)(2,1)} async-done(((bf16[16,64,128]{2,1,0:T(8,128)(2,1)}), bf16[16,64,512]{2,1,0:T(8,128)(2,1)}) %all-gather.4.cloned.1.call-update) | async-done | bytes 1048592 | tf_op jit(solution)/shard_map/all_gather | solution.py:206
  159.3 2.0 fusion.182
  161.3 28.7 %all-reduce.12 = (f32[]{:T(128)}, f32[128]{0:T(128)S(1)}, f32[128]{0:T(128)S(1)}, f32[128,10]{0,1:T(8,128)S(1)}, f32[10]{0:T(128)}) all-reduce(f32[]{:T(128)S(6)} %neg.3, f32[128]{0:T(128)} %get-tuple-element.23, f32[128]{0:T(128)} %get-tuple-element.22, ...), channel_id=1, replica_groups=mesh['dp'=4,'cout'=4,'cin'=2] {'dp','cin'}, use_global_device_ids=true, to_apply=%region_16.17 | all-reduce | flops 1547 | bytes 12376 | tf_op jit(solution)/shard_map/psum | solution.py:186
  190.0 2.7 multiply_convert_fusion
  204.4 2.3 reshape.337
  206.8 9.8 %all-gather.6.cloned.1.call-done = bf16[16,64,512]{2,1,0:T(8,128)(2,1)} async-done(((bf16[16,64,128]{2,1,0:T(8,128)(2,1)}), bf16[16,64,512]{2,1,0:T(8,128)(2,1)}) %all-gather.6.cloned.1.call-update) | async-done | bytes 1048592 | tf_op jit(solution)/shard_map/all_gather | solution.py:227
  216.6 1.8 convolution_convert_fusion.11
  218.5 1.8 fusion.45
  224.3 4.3 pad_maximum_fusion
  228.8 106.3 %all-reduce.18.cloned.1.call-done = f32[9216,128]{1,0:T(8,128)} async-done(((f32[9216,128]{1,0:T(8,128)}), f32[9216,128]{1,0:T(8,128)}) %all-reduce.18.cloned.1.call-update) | async-done | bytes 4718608 | tf_op jit(solution)/shard_map/psum | solution.py:103
  335.1 4.9 fusion.187
  340.0 2.4 reshape.339
  342.5 2.3 fusion.5
  344.7 3.9 fusion.8
  348.7 2.1 fusion.17
  350.8 3.1 fusion.18
  353.9 3.1 fusion.19
  357.0 3.1 fusion.20
  361.6 2.6 reshape.340
  364.2 2.0 fusion.4
  367.6 6.3 %fusion.14 = f32[9,512,128]{1,2,0:T(8,128)} fusion(f32[9,512,128]{2,1,0:T(8,128)S(1)} %bitcast.430, f32[9,512,128]{2,1,0:T(8,128)S(1)} %fusion.4, bf16[2,2,512,512]{3,2,1,0:T(8,128)(2,1)} %param.29), kind=kOutput, calls=%fused_computation.48 | convolution fusion | flops 3625058304 | bytes 7602176 | tf_op jit(solution)/shard_map/ij,tjk->tik/dot_general | solution.py:258
  374.0 2.0 copy.59
  376.0 3.2 fusion.3
  380.2 3.2 fusion.2
  384.9 2.4 reshape.341
  388.3 3.2 fusion.1
  393.0 2.4 reshape.342
  396.5 3.3 fusion
  405.7 91.5 %reduce-scatter.5.cloned.1.call-done = bf16[9216,128]{1,0:T(8,128)(2,1)} async-done(((bf16[36864,128]{1,0:T(8,128)(2,1)}), bf16[9216,128]{1,0:T(8,128)(2,1)}) %reduce-scatter.5.cloned.1.call-update) | async-done | bytes 2359312 | tf_op jit(solution)/shard_map/reduce_scatter | solution.py:272
  497.2 1.8 convert_element_type.120
  503.8 9.4 %psum.119 = f32[]{:T(128)} all-reduce(f32[]{:T(128)S(6)} %add.384), channel_id=1, replica_groups=mesh['dp'=4,'cout'=4,'cin'=2] {'cout'}, use_global_device_ids=true, to_apply=%region_35.36 | all-reduce | flops 1 | bytes 8 | tf_op jit(solution)/shard_map/psum | solution.py:291
  513.9 4.9 slice_multiply_fusion
  518.8 3.5 mul.602
  524.1 7.6 %multiply_subtract_fusion = (f32[9,128,512]{2,1,0:T(8,128)}, f32[9,128,512]{2,1,0:T(8,128)}, f32[9,128,512]{2,1,0:T(8,128)}) fusion(f32[9,128,512]{2,1,0:T(8,128)S(1)} %copy-done.3, f32[9,128,512]{2,1,0:T(8,128)} %mul.602, f32[9,128,512]{2,1,0:T(8,128)} %param.34, f32[9,128,512]{2,1,0:T(8,128)} %param.35), kind=kLoop, calls=%fused_computation.33 | loop fusion | flops 8847360 | bytes 16515072 | tf_op jit(solution)/shard_map/sub | solution.py:122
  531.7 4.2 multiply_subtract_fusion.1
  (231 shorter events, 69.5 us)
Async XLA Ops:
  7.2 70.7 %reduce-scatter.7.cloned.1.call-start = ((), (), s32[]{:S(2)}) async-start(), calls=%async_computation.7 | async-start | bytes 1310720
  14.8 21.2 %copy-start.46 = (f32[128]{0:T(128)}, f32[128]{0:T(128)S(1)}, u32[]{:S(2)}) copy-start(f32[128]{0:T(128)S(1)} %get-tuple-element.102) | copy-start | bytes 1540
  14.8 21.2 %copy-start.56 = (f32[128]{0:T(128)}, f32[128]{0:T(128)S(1)}, u32[]{:S(2)}) copy-start(f32[128]{0:T(128)S(1)} %get-tuple-element.104) | copy-start | bytes 1540
  14.8 82.1 %copy-start.37 = (f32[128]{0:T(128)}, f32[128]{0:T(128)S(1)}, u32[]{:S(2)}) copy-start(f32[128]{0:T(128)S(1)} %get-tuple-element.101) | copy-start | bytes 1540
  14.9 82.1 %copy-start.48 = (f32[128]{0:T(128)}, f32[128]{0:T(128)S(1)}, u32[]{:S(2)}) copy-start(f32[128]{0:T(128)S(1)} %get-tuple-element.103) | copy-start | bytes 1540
  36.0 2.7 copy-start.42
  51.8 86.8 %all-gather.8.cloned.1.call-start = ((), (), s32[]{:S(2)}) async-start(), calls=%async_computation.4 | async-start | bytes 1310720 | tf_op jit(solution)/shard_map/all_gather | solution.py:226
  52.5 101.0 %all-gather.4.cloned.1.call-start = ((), (), s32[]{:S(2)}) async-start(), calls=%async_computation.2 | async-start | bytes 1310720 | tf_op jit(solution)/shard_map/all_gather | solution.py:206
  97.7 12.0 %copy-start.33 = (f32[64,128]{1,0:T(8,128)}, f32[64,128]{1,0:T(8,128)S(1)}, u32[]{:S(2)}) copy-start(f32[64,128]{1,0:T(8,128)S(1)} %fusion.69) | copy-start | bytes 98308
  129.6 87.0 %all-gather.6.cloned.1.call-start = ((), (), s32[]{:S(2)}) async-start(), calls=%async_computation.3 | async-start | bytes 1310720 | tf_op jit(solution)/shard_map/all_gather | solution.py:227
  131.8 84.9 %copy-start.15 = (bf16[1,1,512,512]{3,2,1,0:T(8,128)(2,1)}, bf16[1,1,512,512]{3,2,1,0:T(8,128)(2,1)S(1)}, u32[]{:S(2)}) copy-start(bf16[1,1,512,512]{3,2,1,0:T(8,128)(2,1)S(1)} %get-tuple-element.57) | copy-start | bytes 1572868
  138.5 3.4 copy-start.53
  138.5 3.4 copy-start.55
  138.5 3.4 copy-start.61
  138.5 3.4 copy-start.63
  138.5 4.7 copy-start.34
  153.5 3.2 copy-start
  161.3 33.7 %copy-start.32 = (bf16[4,4,64,128]{3,2,1,0:T(8,128)(2,1)S(1)}, bf16[4,4,64,128]{3,2,1,0:T(8,128)(2,1)}, u32[]{:S(2)}) copy-start(bf16[4,4,64,128]{3,2,1,0:T(8,128)(2,1)} %get-tuple-element.82) | copy-start | bytes 786436
  190.0 6.1 %copy-start.49 = (f32[128]{0:T(128)}, f32[128]{0:T(128)S(1)}, u32[]{:S(2)}) copy-start(f32[128]{0:T(128)S(1)} %get-tuple-element.31) | copy-start | bytes 1540
  190.0 6.1 %copy-start.51 = (f32[128]{0:T(128)}, f32[128]{0:T(128)S(1)}, u32[]{:S(2)}) copy-start(f32[128]{0:T(128)S(1)} %get-tuple-element.32) | copy-start | bytes 1540
  192.7 3.4 copy-start.31
  192.7 4.4 copy-start.30
  192.7 142.5 %all-reduce.18.cloned.1.call-start = ((), (), s32[]{:S(2)}) async-start(), calls=%async_computation.5 | async-start | bytes 9437184 | tf_op jit(solution)/shard_map/psum | solution.py:103
  195.0 3.1 copy-start.29
  197.1 3.1 copy-start.28
  198.2 3.2 copy-start.27
  199.2 3.1 copy-start.26
  200.3 3.1 copy-start.25
  216.6 3.6 copy-start.24
  216.6 4.1 copy-start.23
  218.4 2.8 copy-start.22
  228.6 268.6 %reduce-scatter.5.cloned.1.call-start = ((), (), s32[]{:S(2)}) async-start(), calls=%async_computation.6 | async-start | bytes 11796480 | tf_op jit(solution)/shard_map/reduce_scatter | solution.py:272
  344.7 4.0 copy-start.11
  360.1 4.0 copy-start.2
  380.2 3.2 copy-start.9
  388.3 3.3 copy-start.8
  396.5 3.3 copy-start.7
  518.8 3.6 copy-start.64
  518.8 3.6 copy-start.65
  518.8 4.1 copy-start.38
  518.8 4.1 copy-start.39
  518.8 4.7 copy-start.59
  518.8 4.7 copy-start.60
  518.8 5.3 copy-start.3
  524.1 7.6 %copy-start.5 = (f32[9,512,128]{2,1,0:T(8,128)S(1)}, f32[9,512,128]{2,1,0:T(8,128)}, u32[]{:S(2)}) copy-start(f32[9,512,128]{2,1,0:T(8,128)} %param.24) | copy-start | bytes 7077892
  524.1 7.6 %copy-start.6 = (f32[4608,128]{1,0:T(8,128)S(1)}, f32[4608,128]{1,0:T(8,128)}, u32[]{:S(2)}) copy-start(f32[4608,128]{1,0:T(8,128)} %get-tuple-element.54) | copy-start | bytes 7077892
  524.1 7.6 %copy-start.13 = (f32[9,512,128]{2,1,0:T(8,128)S(1)}, f32[9,512,128]{2,1,0:T(8,128)}, u32[]{:S(2)}) copy-start(f32[9,512,128]{2,1,0:T(8,128)} %param.32) | copy-start | bytes 7077892
  524.1 7.6 %copy-start.14 = (f32[9,512,128]{2,1,0:T(8,128)S(1)}, f32[9,512,128]{2,1,0:T(8,128)}, u32[]{:S(2)}) copy-start(f32[9,512,128]{2,1,0:T(8,128)} %param.33) | copy-start | bytes 7077892
  (25 other events, 34.0 us)
Sparse Core Ops, SparseCore 0:
  51.9 25.9 reduce-scatter.6
  79.8 26.8 all-gather.7
  129.8 23.6 all-gather.3
  192.8 23.7 all-gather.5
  228.7 106.3 all-reduce.17
  402.7 94.4 reduce-scatter.4
where the time goes:
time: 554 us; the launch traced here: 544 us
  waiting for transfers between devices  243 us (44%)
  blocking collectives  97.1 us (18%)
  matrix products  76.3 us (14%)
  local copies, waits for them, and re-layouts  57.5 us (10%)
  other arithmetic  48.1 us (9%)
  between operations  21.3 us (4%)
    psum x1, waiting for transfers between devices, over_batch(): return lax.psum(values, ('dp', 'cin'))  106 us
    reduce_scatter x1, waiting for transfers between devices, local(): lax.psum_scatter(rows_from(restore_block, block_rows, jnp.int32(0), lax.a...  91.5 us
    psum x2, blocking collectives, local(): lax.psum((jnp.sum(dz_second * scaled_second, axis=(0, 1)), jnp.sum(dz_sec...  42.9 us
    unnamed x7, waiting for transfers between devices  26.1 us
    psum x1, blocking collectives, local(): lax.psum(moments_of(first_out, mask_cube) + (jnp.sum(mask_plane),), ('dp'...  18.7 us
    unnamed x141, local copies, waits for them, and re-layouts  18.3 us
    psum x1, blocking collectives, local(): lax.psum(moments_of(second_out, mask_cube), ('dp', 'cin'))  16.4 us
    dot_general x18, matrix products, tap_products(): jnp.einsum('pbj,pbk->jk', shifted(left_side, row_step, col_step), right_s...  15 us
  transfers between devices with their start and end apart: 6, of which 5 were waited for; matrix products, arithmetic and copies ran while one was open for 7% of the time, Pallas kernels for 0%

commit v1 on v0

v1 whole, which is shorter than its diff:
```python
import jax
import jax.numpy as jnp
from jax import lax
from jax.sharding import PartitionSpec as P

CLASSES = 10
SIDE = 4
PIX = 16
TAPS = 9
STEP = 10

EPS_NORM = 1e-05
SCALE_DECAY = 0.95
DAMPING = 0.001
CLIP_NORM = 1.0
LEARN_RATE = 0.01
BETA_ONE = 0.9
BETA_TWO = 0.999
ADAM_EPS = 1e-08
WEIGHT_DECAY = 0.01
SMOOTH = 0.1
OFFSETS = [(row_step, col_step) for row_step in (-1, 0, 1) for col_step in (-1, 0, 1)]
EVERY = ("dp", "cout", "cin")
BF = jnp.bfloat16
F32 = jnp.float32


def shifted(values, row_step, col_step):
    cell_grid = values.reshape((SIDE, SIDE) + values.shape[1:])
    padding = [(1, 1), (1, 1)] + [(0, 0)] * (values.ndim - 1)
    padded = jnp.pad(cell_grid, padding)
    window = padded[1 + row_step : 1 + row_step + SIDE, 1 + col_step : 1 + col_step + SIDE]
    return window.reshape(values.shape)


def convolve(values, weight):
    summed = None
    for tap_index, (row_step, col_step) in enumerate(OFFSETS):
        product = jnp.einsum(
            "pbi,io->pbo",
            shifted(values, row_step, col_step),
            weight[tap_index],
            preferred_element_type=F32,
        )
        summed = product if summed is None else summed + product
    return summed


def convolve_back(cotangent, weight):
    summed = None
    for tap_index, (row_step, col_step) in enumerate(OFFSETS):
        product = jnp.einsum(
            "pbo,io->pbi",
            shifted(cotangent, -row_step, -col_step),
            weight[tap_index],
            preferred_element_type=F32,
        )
        summed = product if summed is None else summed + product
    return summed


def swap(values, axis, step):
    count = lax.axis_size(axis)
    return lax.ppermute(values, axis, [(here, here ^ step) for here in range(count)])


def gathered(values, axis):
    return [values] + [swap(values, axis, step) for step in range(1, lax.axis_size(axis))]


def exchanged(block_of, axis):
    me = lax.axis_index(axis)
    return [block_of(me)] + [
        swap(block_of(me ^ step), axis, step) for step in range(1, lax.axis_size(axis))
    ]


def tree_sum(slots):
    while len(slots) > 1:
        slots = [slots[at] + slots[at + 1] for at in range(0, len(slots), 2)]
    return slots[0]


def in_order(slots, axis):
    me = lax.axis_index(axis)
    stacked = jnp.stack(slots)
    return [
        lax.dynamic_index_in_dim(stacked, me ^ place, 0, keepdims=False)
        for place in range(len(slots))
    ]


def spread_sum(block):
    sizes = tuple(lax.axis_size(name) for name in EVERY)
    total = sizes[0] * sizes[1] * sizes[2]
    sent = jnp.broadcast_to(block[None], (total,) + block.shape)
    got = lax.all_to_all(sent, EVERY, 0, 0, tiled=True)
    return got.reshape(sizes + block.shape)


def moments(gradient, mean_old, square_old):
    mean_new = BETA_ONE * mean_old + (1.0 - BETA_ONE) * gradient
    square_new = BETA_TWO * square_old + (1.0 - BETA_TWO) * gradient * gradient
    return (mean_new, square_new)


def adamw(weight, gradient, mean_old, square_old):
    mean_new, square_new = moments(gradient, mean_old, square_old)
    mean_hat = mean_new / (1.0 - BETA_ONE**STEP)
    square_hat = square_new / (1.0 - BETA_TWO**STEP)
    updated = weight - LEARN_RATE * (
        mean_hat / (jnp.sqrt(square_hat) + ADAM_EPS) + WEIGHT_DECAY * weight
    )
    return (updated, mean_new, square_new)


def gelu_back(pre_values, upstream):
    return jax.vjp(jax.nn.gelu, pre_values)[1](upstream)[0]


def norm_back(dz_values, scaled, inverse_std, gain, gain_grad, shift_grad, mask_cube, kept_count):
    return inverse_std * (
        gain * dz_values - mask_cube * gain * (shift_grad + scaled * gain_grad) / kept_count
    )


def project(values, basis):
    return jnp.einsum("pbi,ij->pbj", values, basis, preferred_element_type=F32).astype(BF)


def tap_products(left_side, right_side, spec):
    return jnp.concatenate(
        [
            jnp.einsum(
                spec,
                shifted(left_side, row_step, col_step),
                right_side,
                preferred_element_type=F32,
            ).astype(BF)
            for row_step, col_step in OFFSETS
        ],
        axis=0,
    )


def batch_scatter(partial):
    count_dp, count_cin = lax.axis_size("dp"), lax.axis_size("cin")
    rows, width = partial.shape
    split = partial.reshape(count_dp, count_cin, rows // (count_dp * count_cin), width)
    slots = exchanged(lambda k: lax.dynamic_index_in_dim(split, k, 1, keepdims=False), "cin")
    near = sum(slot.astype(F32) for slot in slots).astype(BF)
    slots = exchanged(lambda k: lax.dynamic_index_in_dim(near, k, 0, keepdims=False), "dp")
    return sum(slot.astype(F32) for slot in slots)


def batch_gather(block):
    far = jnp.stack(in_order(gathered(block, "dp"), "dp"))
    both = in_order(gathered(far, "cin"), "cin")
    return jnp.stack(both, axis=1).reshape(-1, block.shape[-1])


def batch_rows(values):
    count_cin = lax.axis_size("cin")
    count = lax.axis_size("dp") * count_cin
    place = lax.axis_index("dp") * count_cin + lax.axis_index("cin")
    rows = values.shape[0] // count
    return lax.dynamic_slice_in_dim(values, place * rows, rows, 0)


def local(
    images,
    masks,
    labels,
    w_first,
    w_second,
    norm_params,
    head_w,
    head_b,
    bases,
    scales_first,
    scales_second,
    w_first_mean,
    w_first_square,
    w_second_mean,
    w_second_square,
    norm_mean,
    norm_square,
    head_w_mean,
    head_w_square,
    head_b_mean,
    head_b_square,
):
    me = lax.axis_index("cout")
    groups = lax.axis_size("cout")
    count_cin = lax.axis_size("cin")
    channels = w_first.shape[1]
    width = w_first.shape[2]
    part = images.shape[1] // groups
    mine = lambda values, axis: lax.dynamic_slice_in_dim(values, me * part, part, axis)
    block = lambda values, k, axis: lax.dynamic_slice_in_dim(values, k * width, width, axis)
    in_slots = lambda values, axis: jnp.concatenate(
        [block(values, me ^ step, axis) for step in range(groups)], axis
    )

    second_low = w_second.astype(BF)
    depth = width // count_cin
    piece = lax.dynamic_slice_in_dim(second_low, lax.axis_index("cin") * depth, depth, 1)
    w_blocks = []
    for slot in gathered(piece, "cout"):
        w_blocks.append(jnp.concatenate(in_order(gathered(slot, "cin"), "cin"), axis=1))
    w_full = jnp.concatenate(in_order(w_blocks, "cout"), axis=1)

    small = jnp.concatenate([norm_params, head_w.T, jnp.zeros((2, width), F32)], axis=0)
    small = jnp.concatenate(in_order(gathered(small, "cout"), "cout"), axis=1)
    gain_first, offset_first, gain_second, offset_second = (small[row] for row in range(4))
    head_full = small[4 : 4 + CLASSES].T

    mask_plane = masks.astype(F32)
    inputs = images * masks.astype(BF)[:, :, None]
    first_block = convolve(inputs, w_first.astype(BF))
    masked = first_block * mask_plane[:, :, None]
    stats = jnp.stack(
        [
            jnp.sum(masked, axis=(0, 1)),
            jnp.sum(masked * first_block, axis=(0, 1)),
            jnp.full((width,), jnp.sum(mask_plane)),
        ]
        + [jnp.zeros((width,), F32)] * 5
    )
    first_low = first_block.astype(BF)
    first_out = jnp.concatenate(
        in_order(
            exchanged(
                lambda k: lax.dynamic_slice_in_dim(first_low, k * part, part, 1), "cout"
            ),
            "cout",
        ),
        axis=2,
    ).astype(F32)
    stats = jnp.sum(spread_sum(stats), axis=(0, 2))
    stats = jnp.moveaxis(stats, 0, 1).reshape(8, -1)
    kept_count = stats[2, 0]
    mask_cube = mine(mask_plane, 1)[:, :, None]

    def standardised(values, first_sum, square_sum):
        mean_value = first_sum / kept_count
        inverse_std = lax.rsqrt(square_sum / kept_count - mean_value * mean_value + EPS_NORM)
        return ((values - mean_value) * inverse_std, inverse_std)

    def all_sums(*rows):
        packed = jnp.stack(rows).reshape(-1, 128)
        summed = jnp.sum(spread_sum(packed), axis=(0, 1, 2))
        return summed.reshape(len(rows), -1)

    scaled_first, rstd_first = standardised(first_out, stats[0], stats[1])
    pre_first = gain_first * scaled_first + offset_first
    hidden = (jax.nn.gelu(pre_first) * mask_cube).astype(BF)
    second_out = convolve(hidden, w_full)
    masked = second_out * mask_cube
    sums = all_sums(jnp.sum(masked, axis=(0, 1)), jnp.sum(masked * second_out, axis=(0, 1)))
    scaled_second, rstd_second = standardised(second_out, sums[0], sums[1])
    pre_second = gain_second * scaled_second + offset_second
    pooled_low = (jnp.sum(jax.nn.gelu(pre_second) * mask_cube, axis=0) / PIX).astype(BF)
    head_low = head_full.astype(BF)
    logits = jnp.dot(pooled_low, head_low, preferred_element_type=F32) + head_b
    log_probs = jax.nn.log_softmax(logits, axis=-1)
    smoothed = (1.0 - SMOOTH) * jax.nn.one_hot(
        mine(labels, 0), CLASSES, dtype=F32
    ) + SMOOTH / CLASSES
    loss_local = -jnp.sum(smoothed * log_probs)
    logit_grad = jnp.exp(log_probs) - smoothed
    precise = lax.Precision.HIGHEST
    head_part = jnp.dot(logit_grad.T, pooled_low.astype(F32), precision=precise)
    bias_part = jnp.sum(logit_grad, axis=0)
    pooled_grad = jnp.dot(logit_grad, head_low.astype(F32).T, precision=precise)
    dz_second = gelu_back(pre_second, mask_cube * pooled_grad[None, :, :] / PIX)
    gain_two, shift_two = all_sums(
        jnp.sum(dz_second * scaled_second, axis=(0, 1)), jnp.sum(dz_second, axis=(0, 1))
    )
    grad_second = norm_back(
        dz_second, scaled_second, rstd_second, gain_second, gain_two, shift_two, mask_cube, kept_count
    ).astype(BF)
    hidden_grad = convolve_back(grad_second, w_full)
    dz_first = gelu_back(pre_first, hidden_grad * mask_cube)
    gain_one, shift_one = all_sums(
        jnp.sum(dz_first * scaled_first, axis=(0, 1)), jnp.sum(dz_first, axis=(0, 1))
    )
    grad_first = norm_back(
        dz_first, scaled_first, rstd_first, gain_first, gain_one, shift_one, mask_cube, kept_count
    ).astype(BF)

    tail_row = jnp.concatenate([bias_part, loss_local[None], jnp.zeros((width - CLASSES - 1,), F32)])
    tail_row = jnp.broadcast_to(tail_row[None, None], (groups, 1, width))
    head_blocks = jnp.moveaxis(head_part.reshape(CLASSES, groups, width), 1, 0)
    head_blocks = jnp.concatenate(
        [head_blocks, tail_row, jnp.zeros((groups, 5, width), F32)], axis=1
    )
    sizes = tuple(lax.axis_size(name) for name in EVERY)
    sent = jnp.broadcast_to(head_blocks[None, :, None], sizes + head_blocks.shape[1:])
    got = lax.all_to_all(sent.reshape((-1,) + head_blocks.shape[1:]), EVERY, 0, 0, tiled=True)
    head_sums = jnp.sum(got, axis=0)
    head_w_grad = head_sums[:CLASSES].T
    head_b_grad = head_sums[CLASSES, :CLASSES]
    loss_total = head_sums[CLASSES, CLASSES]

    def by_images(values):
        return jnp.concatenate(exchanged(lambda k: block(values, k, 2), "cout"), axis=1)

    def slot_images(values):
        return jnp.concatenate(
            [
                lax.dynamic_slice_in_dim(values, (me ^ step) * part, part, 1)
                for step in range(groups)
            ],
            axis=1,
        )

    basis_in_first, basis_out_first = bases[0, 0], bases[0, 1]
    basis_in_second, basis_out_second = bases[1, 0], bases[1, 1]

    def layer(left, right, spec, scales, basis_rows):
        own = batch_scatter(tap_products(left, right, spec))
        scales_own = batch_rows(scales)
        scales_own = SCALE_DECAY * scales_own + (1.0 - SCALE_DECAY) * own * own
        ratio = (own / (scales_own + DAMPING)).astype(BF)
        ratio = jnp.concatenate(gathered(ratio, "cout"), axis=1)
        middle = jnp.dot(ratio, basis_rows.T, preferred_element_type=F32).astype(BF)
        return batch_gather(own.astype(BF)).astype(F32), batch_gather(middle)

    left_second = by_images(project(hidden, basis_in_second))
    right_second = jnp.concatenate(gathered(project(grad_second, basis_out_second), "cout"), axis=1)
    coeff_second, middle_second = layer(
        left_second,
        right_second,
        "pbj,pbk->kj",
        jnp.swapaxes(scales_second, 1, 2).reshape(-1, width),
        in_slots(block(basis_in_second, me, 0), 1),
    )
    coeff_second = jnp.swapaxes(coeff_second.reshape(TAPS, channels, width), 1, 2)
    precond_second = jnp.einsum(
        "tki,lk->til",
        middle_second.reshape(TAPS, channels, width),
        basis_out_second,
        preferred_element_type=F32,
    )

    left_first = slot_images(project(inputs, basis_in_first))
    right_first = by_images(project(grad_first, basis_out_first))
    coeff_first, middle_first = layer(
        left_first,
        right_first,
        "pbj,pbk->jk",
        scales_first.reshape(-1, width),
        in_slots(block(basis_out_first, me, 0), 1),
    )
    coeff_first = coeff_first.reshape(TAPS, channels, width)
    precond_first = jnp.einsum(
        "ij,tjl->til",
        basis_in_first,
        middle_first.reshape(TAPS, channels, width),
        preferred_element_type=F32,
    )

    scales_first_new = SCALE_DECAY * scales_first + (1.0 - SCALE_DECAY) * coeff_first * coeff_first
    scales_second_new = (
        SCALE_DECAY * scales_second + (1.0 - SCALE_DECAY) * coeff_second * coeff_second
    )
    norm_grad = block(jnp.stack([gain_one, shift_one, gain_two, shift_two]), me, 1)
    bias_square = jnp.where(me == 0, jnp.sum(head_b_grad * head_b_grad), 0.0)
    local_square = jnp.sum(precond_first * precond_first) + jnp.sum(precond_second * precond_second)
    local_square = (
        local_square
        + jnp.sum(norm_grad * norm_grad)
        + jnp.sum(head_w_grad * head_w_grad)
        + bias_square
    )
    square_sum = tree_sum(gathered(jnp.full((8, 128), local_square), "cout"))[0, 0]
    grad_norm = jnp.sqrt(square_sum)
    factor = CLIP_NORM / jnp.maximum(grad_norm, CLIP_NORM)
    first_new, first_mean_new, first_square_new = adamw(
        w_first, factor * precond_first, w_first_mean, w_first_square
    )
    second_new, second_mean_new, second_square_new = adamw(
        w_second, factor * precond_second, w_second_mean, w_second_square
    )
    norm_mean_new, norm_square_new = moments(factor * norm_grad, norm_mean, norm_square)
    head_mean_new, head_square_new = moments(factor * head_w_grad, head_w_mean, head_w_square)
    bias_mean_new, bias_square_new = moments(factor * head_b_grad, head_b_mean, head_b_square)
    return (
        loss_total,
        grad_norm,
        first_new,
        first_mean_new,
        first_square_new,
        second_new,
        second_mean_new,
        second_square_new,
        norm_mean_new[:2],
        norm_square_new[:2],
        norm_mean_new[2:],
        norm_square_new[2:],
        head_mean_new,
        head_square_new,
        bias_mean_new,
        bias_square_new,
        scales_first_new,
        scales_second_new,
    )
def solution(mesh):
    return jax.shard_map(
        local,
        mesh=mesh,
        in_specs=(
            P(None, ("dp", "cin"), None),
            P(None, ("dp", "cin")),
            P(("dp", "cin")),
            P(None, None, "cout"),
            P(None, "cout", None),
            P(None, "cout"),
            P("cout", None),
            P(),
            P(),
            P(None, None, "cout"),
            P(None, "cout", None),
            P(None, None, "cout"),
            P(None, None, "cout"),
            P(None, "cout", None),
            P(None, "cout", None),
            P(None, "cout"),
            P(None, "cout"),
            P("cout", None),
            P("cout", None),
            P(),
            P(),
        ),
        out_specs=(
            P(),
            P(),
            P(None, None, "cout"),
            P(None, None, "cout"),
            P(None, None, "cout"),
            P(None, "cout", None),
            P(None, "cout", None),
            P(None, "cout", None),
            P(None, "cout"),
            P(None, "cout"),
            P(None, "cout"),
            P(None, "cout"),
            P("cout", None),
            P("cout", None),
            P(),
            P(),
            P(None, None, "cout"),
            P(None, "cout", None),
        ),
        check_vma=False,
    )
```

time: 554 us -> 320 us (0.58)
  waiting for transfers between devices: 243 us -> 62.4 us
  blocking collectives: 97.1 us -> 0 us
  starting transfers between devices: 0.94 us -> 86.9 us
  matrix products: 76.3 us -> 48.2 us
  between operations: 21.3 us -> 8.4 us
  other arithmetic: 48.1 us -> 53.8 us
    psum x1 -> x0, waiting for transfers between devices: 106 us -> none  [over_batch(): return lax.psum(values, ('dp', 'cin'))]
    psum x6 -> x0, blocking collectives: 97.1 us -> none  [the longest x2 42.9 us: local(): lax.psum((jnp.sum(dz_second * scaled_second, axis=(0, 1)), jnp.sum(dz_sec...]
    reduce_scatter x1 -> x0, waiting for transfers between devices: 91.5 us -> none  [local(): lax.psum_scatter(rows_from(restore_block, block_rows, jnp.int32(0), lax.a...]
    ppermute x0 -> x55, starting transfers between devices: none -> 67.8 us  [swap(): lax.ppermute(values, axis, [(here, here ^ step) for here in range(count)])]
    ppermute x0 -> x55, waiting for transfers between devices: none -> 46.6 us  [swap(): lax.ppermute(values, axis, [(here, here ^ step) for here in range(count)])]
    unnamed x7 -> x0, waiting for transfers between devices: 26.1 us -> none
    dot_general x36 -> x38, matrix products: 61.5 us -> 41.4 us  [the longest x18 20 us: tap_products(): jnp.einsum(spec, shifted(left_side, row_step, col_step), right_side, pref...]
    all_gather x3 -> x0, waiting for transfers between devices: 19.3 us -> none  [the longest x1 9.82 us: local(): lax.all_gather(grad_first, 'cout', axis=2, tiled=True)]
  transfers between devices with their start and end apart: 6 -> 60, of which waited for: 5 -> 19; matrix products, arithmetic and copies ran while one was open for 7% -> 36% of each run, Pallas kernels for 0% -> 0%
where the time goes in v1:
time: 320 us; the launch traced here: 314 us
  starting transfers between devices  86.9 us (27%)
  waiting for transfers between devices  62.4 us (20%)
  local copies, waits for them, and re-layouts  54.7 us (17%)
  other arithmetic  53.8 us (17%)
  matrix products  48.2 us (15%)
  between operations  8.4 us (3%)
    ppermute x55, starting transfers between devices, swap(): lax.ppermute(values, axis, [(here, here ^ step) for here in range(count)])  67.8 us
    ppermute x55, waiting for transfers between devices, swap(): lax.ppermute(values, axis, [(here, here ^ step) for here in range(count)])  46.6 us
    unnamed x156, local copies, waits for them, and re-layouts  26.7 us
    dot_general x18, matrix products, tap_products(): jnp.einsum(spec, shifted(left_side, row_step, col_step), right_side, pref...  20 us
    all_to_all x4, starting transfers between devices, spread_sum(): got = lax.all_to_all(sent, EVERY, 0, 0, tiled=True)  16.1 us
    sub x2, other arithmetic, adamw(): weight - LEARN_RATE * (mean_hat / (jnp.sqrt(square_hat) + ADAM_EPS) + WEI...  15.6 us
    all_to_all x4, waiting for transfers between devices, spread_sum(): got = lax.all_to_all(sent, EVERY, 0, 0, tiled=True)  14.6 us
    dot_general x4, matrix products, project(): jnp.einsum('pbi,ij->pbj', values, basis, preferred_element_type=F32)  7.94 us
  transfers between devices with their start and end apart: 60, of which 19 were waited for; matrix products, arithmetic and copies ran while one was open for 36% of the time, Pallas kernels for 0%

profile of v1, /device:TPU:0, one launch (start us, length us, event | category | flops | bytes accessed | tf_op | source)
XLA Modules:
  0.0 314.4 jit_solution(18373589236594248591)
XLA Ops:
  1.5 3.9 %collective-permute-start.2 = (f32[16,128]{1,0:T(8,128)S(1)}, f32[16,128]{1,0:T(8,128)S(1)}, u32[]{:S(2)}, u32[]{:S(2)}) collective-permute-start(f32[16,128]{1,0:T(8,128)S(1)} %maximum_maximum_fusion.1), channel_id=1, source_target_pairs={{0,6},{2,4},{4,2},{6,0},{1,7},{3,5},{5,3},{7,1},{8,14},{10,12},{12... | collective-permute-start | bytes 24584 | tf_op jit(solution)/shard_map/ppermute | solution.py:64
  6.1 2.2 dynamic-slice_convert_fusion
  8.2 2.8 collective-permute-start.11
  22.3 5.2 %all-to-all-start = ((f32[32,8,128]{2,1,0:T(8,128)}), f32[32,8,128]{2,1,0:T(8,128)}, u32[]{:S(2)}, u32[]{:S(2)}) async-start(f32[32,8,128]{2,1,0:T(8,128)} %broadcast_in_dim.35), calls=%async_computation | async-start | bytes 262144 | tf_op jit(solution)/shard_map/all_to_all | solution.py:97
  28.9 1.9 convolution_convert_fusion
  33.6 3.7 %pad_slice_fusion = (bf16[4,4,64,512]{3,2,1,0:T(8,128)(2,1)}, bf16[4,4,64,512]{3,2,1,0:T(8,128)(2,1)}, bf16[4,4,64,512]{3,2,1,0:T(8,128)(2,1)}, bf16[4,4,64,512]...) fusion(bf16[4,4,64,512]{3,2,1,0:T(8,128)(2,1)S(1)} %bitcast.571), kind=kLoop, calls=%fused_computation | loop fusion | bytes 9437184 | tf_op jit(solution)/shard_map/slice | solution.py:32
  40.9 2.0 copy.72
  44.0 2.0 copy.67
  46.1 3.1 copy.69
  49.1 3.0 copy.70
  52.2 2.7 collective-permute-start.5
  86.3 4.1 %all-to-all-start.1 = ((f32[32,8,128]{2,1,0:T(8,128)}), f32[32,8,128]{2,1,0:T(8,128)S(1)}, u32[]{:S(2)}, u32[]{:S(2)}) async-start(f32[32,8,128]{2,1,0:T(8,128)} %broadcast_in_dim.37), calls=%async_computation.1 | async-start | bytes 262144 | tf_op jit(solution)/shard_map/all_to_all | solution.py:97
  93.0 5.7 %all-to-all-done.1 = f32[32,8,128]{2,1,0:T(8,128)S(1)} async-done(((f32[32,8,128]{2,1,0:T(8,128)}), f32[32,8,128]{2,1,0:T(8,128)S(1)}, u32[]{:S(2)}, u32[]{:S(2)}) %all-to-all-start.1) | async-done | bytes 131104 | tf_op jit(solution)/shard_map/all_to_all | solution.py:97
  103.4 2.6 all-to-all-start.3
  106.2 8.0 %all-to-all-done.3 = f32[32,8,128]{2,1,0:T(8,128)S(1)} async-done(((f32[32,8,128]{2,1,0:T(8,128)}), f32[32,8,128]{2,1,0:T(8,128)S(1)}, u32[]{:S(2)}, u32[]{:S(2)}) %all-to-all-start.3) | async-done | bytes 131104 | tf_op jit(solution)/shard_map/all_to_all | solution.py:97
  114.9 3.0 all-to-all-start.2
  128.8 4.2 %all-to-all-start.4 = ((f32[32,8,128]{2,1,0:T(8,128)}), f32[32,8,128]{2,1,0:T(8,128)S(1)}, u32[]{:S(2)}, u32[]{:S(2)}) async-start(f32[32,8,128]{2,1,0:T(8,128)} %broadcast_in_dim.83), calls=%async_computation.4 | async-start | bytes 262144 | tf_op jit(solution)/shard_map/all_to_all | solution.py:97
  133.0 2.0 convolution_convert_fusion.2
  135.0 2.7 collective-permute-start.29
  141.3 2.3 convolution_convert_fusion.3
  143.7 1.9 collective-permute-start.15
  147.2 4.2 %collective-permute-done.28 = bf16[16,16,512]{2,1,0:T(8,128)(2,1)} collective-permute-done((bf16[16,16,512]{2,1,0:T(8,128)(2,1)}, bf16[16,16,512]{2,1,0:T(8,128)(2,1)}, u32[]{:S(2)}, u32[]{:S(2)}) %collective-permute-start.28) | collective-permute-done | bytes 262176 | tf_op jit(solution)/shard_map/ppermute | solution.py:64
  175.5 3.3 %collective-permute-start.36 = (bf16[576,128]{1,0:T(8,128)(2,1)S(1)}, bf16[576,128]{1,0:T(8,128)(2,1)S(1)}, u32[]{:S(2)}, u32[]{:S(2)}) collective-permute-start(bf16[576,128]{1,0:T(8,128)(2,1)S(1)} %get-tuple-element.155), channel_id=1, source_target_pairs={{0,24},{8,16},{16,8},{24,0},{1,25},{9,17},{17,9},{25,1},{2,26},{10... | collective-permute-start | bytes 442376 | tf_op jit(solution)/shard_map/ppermute | solution.py:64
  180.1 3.3 %collective-permute-start.19 = (bf16[576,128]{1,0:T(8,128)(2,1)S(1)}, bf16[576,128]{1,0:T(8,128)(2,1)S(1)}, u32[]{:S(2)}, u32[]{:S(2)}) collective-permute-start(bf16[576,128]{1,0:T(8,128)(2,1)S(1)} %get-tuple-element.164), channel_id=1, source_target_pairs={{0,24},{8,16},{16,8},{24,0},{1,25},{9,17},{17,9},{25,1},{2,26},{10... | collective-permute-start | bytes 442376 | tf_op jit(solution)/shard_map/ppermute | solution.py:64
  184.1 5.9 %collective-permute-start.17 = (bf16[576,128]{1,0:T(8,128)(2,1)S(1)}, bf16[576,128]{1,0:T(8,128)(2,1)S(1)}, u32[]{:S(2)}, u32[]{:S(2)}) collective-permute-start(bf16[576,128]{1,0:T(8,128)(2,1)S(1)} %get-tuple-element.163), channel_id=1, source_target_pairs={{0,8},{8,0},{16,24},{24,16},{1,9},{9,1},{17,25},{25,17},{2,10},{10... | collective-permute-start | bytes 442376 | tf_op jit(solution)/shard_map/ppermute | solution.py:64
  190.0 9.0 %collective-permute-done.35 = bf16[576,128]{1,0:T(8,128)(2,1)S(1)} collective-permute-done((bf16[576,128]{1,0:T(8,128)(2,1)S(1)}, bf16[576,128]{1,0:T(8,128)(2,1)S(1)}, u32[]{:S(2)}, u32[]{:S(2)}) %collective-permute-start.35) | collective-permute-done | bytes 147488 | tf_op jit(solution)/shard_map/ppermute | solution.py:64
  199.1 2.3 collective-permute-start.53
  201.4 2.2 collective-permute-start.51
  203.6 8.0 %collective-permute-done.18 = bf16[576,128]{1,0:T(8,128)(2,1)S(1)} collective-permute-done((bf16[576,128]{1,0:T(8,128)(2,1)S(1)}, bf16[576,128]{1,0:T(8,128)(2,1)S(1)}, u32[]{:S(2)}, u32[]{:S(2)}) %collective-permute-start.18) | collective-permute-done | bytes 147488 | tf_op jit(solution)/shard_map/ppermute | solution.py:64
  211.6 2.0 collective-permute-start.39
  217.4 2.2 collective-permute-start.49
  219.7 2.3 collective-permute-start.22
  224.7 2.3 collective-permute-start.47
  228.9 2.9 collective-permute-start.40
  232.1 5.7 %collective-permute-done.48 = bf16[576,128]{1,0:T(8,128)(2,1)S(1)} collective-permute-done((bf16[576,128]{1,0:T(8,128)(2,1)S(1)}, bf16[576,128]{1,0:T(8,128)(2,1)S(1)}, u32[]{:S(2)}, u32[]{:S(2)}) %collective-permute-start.48) | collective-permute-done | bytes 147488 | tf_op jit(solution)/shard_map/ppermute | solution.py:64
  239.3 3.5 %collective-permute-start.24 = (bf16[576,128]{1,0:T(8,128)(2,1)S(1)}, bf16[576,128]{1,0:T(8,128)(2,1)S(1)}, u32[]{:S(2)}, u32[]{:S(2)}) collective-permute-start(bf16[576,128]{1,0:T(8,128)(2,1)S(1)} %convolution_convert_fusion.5), channel_id=1, source_target_pairs={{0,16},{8,24},{16,0},{24,8},{1,17},{9,25},{17,1},{25,9},{2,18},{10... | collective-permute-start | bytes 442376 | tf_op jit(solution)/shard_map/ppermute | solution.py:64
  242.8 8.5 %collective-permute-done.41 = bf16[576,128]{1,0:T(8,128)(2,1)S(1)} collective-permute-done((bf16[576,128]{1,0:T(8,128)(2,1)S(1)}, bf16[576,128]{1,0:T(8,128)(2,1)S(1)}, u32[]{:S(2)}, u32[]{:S(2)}) %collective-permute-start.41) | collective-permute-done | bytes 147488 | tf_op jit(solution)/shard_map/ppermute | solution.py:64
  253.1 3.5 %collective-permute-done.24 = bf16[576,128]{1,0:T(8,128)(2,1)S(1)} collective-permute-done((bf16[576,128]{1,0:T(8,128)(2,1)S(1)}, bf16[576,128]{1,0:T(8,128)(2,1)S(1)}, u32[]{:S(2)}, u32[]{:S(2)}) %collective-permute-start.24) | collective-permute-done | bytes 147488 | tf_op jit(solution)/shard_map/ppermute | solution.py:64
  262.9 3.1 copy.77
  267.6 3.0 multiply_reduce_fusion
  270.6 2.1 fusion.51
  272.8 3.0 multiply_reduce_fusion.1
  282.1 3.6 %fusion.2 = f32[9,512,128]{2,1,0:T(8,128)} fusion(bf16[9,512,128]{2,1,0:T(8,128)(2,1)S(1)} %bitcast.563, f32[9,512,128]{2,1,0:T(8,128)} %param.30), kind=kLoop, calls=%fused_computation.24 | loop fusion | flops 2949120 | bytes 5898240 | tf_op jit(solution)/shard_map/add | solution.py:364
  287.0 7.5 %multiply_subtract_fusion.1 = (f32[9,512,128]{1,2,0:T(8,128)}, f32[9,512,128]{1,2,0:T(8,128)}, f32[9,512,128]{1,2,0:T(8,128)}) fusion(f32[9,512,128]{1,2,0:T(8,128)S(1)} %copy-done.2, f32[9,128,512]{2,1,0:T(8,128)} %get-tuple-element.251, f32[]{:T(128)S(6)} %div.134, f32[9,512,128]{1,2,0:T(8,128)} %copy.69, f32[9,512,128]{1,2,0:T(8,128)} %copy.70), kind=kLoop, calls=%fused_computation.31 | loop fusion | flops 9437184 | bytes 16515076 | tf_op jit(solution)/shard_map/sub | solution.py:111
  294.4 3.0 copy.74
  297.5 3.2 %copy.75 = f32[9,512,128]{2,1,0:T(8,128)} copy(f32[9,512,128]{1,2,0:T(8,128)} %get-tuple-element.86) | data formatting | bytes 4718592
  300.7 1.9 copy.76
  305.0 8.1 %multiply_subtract_fusion = (f32[9,128,512]{2,1,0:T(8,128)}, f32[9,128,512]{2,1,0:T(8,128)}, f32[9,128,512]{2,1,0:T(8,128)}) fusion(f32[9,128,512]{2,1,0:T(8,128)} %param.25, f32[9,128,512]{2,1,0:T(8,128)} %get-tuple-element.253, f32[]{:T(128)S(6)} %div.134, f32[9,128,512]{2,1,0:T(8,128)} %param.34, f32[9,128,512]{2,1,0:T(8,128)} %param.35), kind=kLoop, calls=%fused_computation.29 | loop fusion | flops 9437184 | bytes 16515076 | tf_op jit(solution)/shard_map/sub | solution.py:111
  (410 shorter events, 127.5 us)
Async XLA Ops:
  1.5 50.7 %collective-permute-start.2 = (f32[16,128]{1,0:T(8,128)S(1)}, f32[16,128]{1,0:T(8,128)S(1)}, u32[]{:S(2)}, u32[]{:S(2)}) collective-permute-start(f32[16,128]{1,0:T(8,128)S(1)} %maximum_maximum_fusion.1), channel_id=1, source_target_pairs={{0,6},{2,4},{4,2},{6,0},{1,7},{3,5},{5,3},{7,1},{8,14},{10,12},{12... | collective-permute-start | bytes 24584 | tf_op jit(solution)/shard_map/ppermute | solution.py:64
  5.4 49.5 %collective-permute-start.1 = (f32[16,128]{1,0:T(8,128)S(1)}, f32[16,128]{1,0:T(8,128)S(1)}, u32[]{:S(2)}, u32[]{:S(2)}) collective-permute-start(f32[16,128]{1,0:T(8,128)S(1)} %maximum_maximum_fusion.1), channel_id=1, source_target_pairs={{0,4},{2,6},{4,0},{6,2},{1,5},{3,7},{5,1},{7,3},{8,12},{10,14},{12... | collective-permute-start | bytes 24584 | tf_op jit(solution)/shard_map/ppermute | solution.py:64
  5.9 49.6 %collective-permute-start = (f32[16,128]{1,0:T(8,128)S(1)}, f32[16,128]{1,0:T(8,128)S(1)}, u32[]{:S(2)}, u32[]{:S(2)}) collective-permute-start(f32[16,128]{1,0:T(8,128)S(1)} %maximum_maximum_fusion.1), channel_id=1, source_target_pairs={{0,2},{2,0},{4,6},{6,4},{1,3},{3,1},{5,7},{7,5},{8,10},{10,8},{12,... | collective-permute-start | bytes 24584 | tf_op jit(solution)/shard_map/ppermute | solution.py:64
  8.2 59.7 %collective-permute-start.11 = (bf16[9,64,512]{2,1,0:T(8,128)(2,1)}, bf16[9,64,512]{2,1,0:T(8,128)(2,1)}, u32[]{:S(2)}, u32[]{:S(2)}) collective-permute-start(bf16[9,64,512]{2,1,0:T(8,128)(2,1)} %dynamic-slice_convert_fusion), channel_id=1, source_target_pairs={{0,6},{2,4},{4,2},{6,0},{1,7},{3,5},{5,3},{7,1},{8,14},{10,12},{12... | collective-permute-start | bytes 1769480 | tf_op jit(solution)/shard_map/ppermute | solution.py:64
  11.1 58.2 %collective-permute-start.9 = (bf16[9,64,512]{2,1,0:T(8,128)(2,1)}, bf16[9,64,512]{2,1,0:T(8,128)(2,1)}, u32[]{:S(2)}, u32[]{:S(2)}) collective-permute-start(bf16[9,64,512]{2,1,0:T(8,128)(2,1)} %dynamic-slice_convert_fusion), channel_id=1, source_target_pairs={{0,4},{2,6},{4,0},{6,2},{1,5},{3,7},{5,1},{7,3},{8,12},{10,14},{12... | collective-permute-start | bytes 1769480 | tf_op jit(solution)/shard_map/ppermute | solution.py:64
  22.3 39.7 %all-to-all-start = ((f32[32,8,128]{2,1,0:T(8,128)}), f32[32,8,128]{2,1,0:T(8,128)}, u32[]{:S(2)}, u32[]{:S(2)}) async-start(f32[32,8,128]{2,1,0:T(8,128)} %broadcast_in_dim.35), calls=%async_computation | async-start | bytes 262144 | tf_op jit(solution)/shard_map/all_to_all | solution.py:97
  57.4 15.2 %collective-permute-start.7 = (bf16[9,64,512]{2,1,0:T(8,128)(2,1)}, bf16[9,64,512]{2,1,0:T(8,128)(2,1)S(1)}, u32[]{:S(2)}, u32[]{:S(2)}) collective-permute-start(bf16[9,64,512]{2,1,0:T(8,128)(2,1)} %dynamic-slice_convert_fusion), channel_id=1, source_target_pairs={{0,2},{2,0},{4,6},{6,4},{1,3},{3,1},{5,7},{7,5},{8,10},{10,8},{12,... | collective-permute-start | bytes 1769480 | tf_op jit(solution)/shard_map/ppermute | solution.py:64
  59.4 14.7 %collective-permute-start.6 = (bf16[9,64,512]{2,1,0:T(8,128)(2,1)}, bf16[9,64,512]{2,1,0:T(8,128)(2,1)}, u32[]{:S(2)}, u32[]{:S(2)}) collective-permute-start(bf16[9,64,512]{2,1,0:T(8,128)(2,1)} %dynamic-slice_convert_fusion), channel_id=1, source_target_pairs={{0,1},{1,0},{2,3},{3,2},{4,5},{5,4},{6,7},{7,6},{8,9},{9,8},{10,11... | collective-permute-start | bytes 1769480 | tf_op jit(solution)/shard_map/ppermute | solution.py:64
  67.9 7.8 %collective-permute-start.12 = (bf16[9,64,512]{2,1,0:T(8,128)(2,1)}, bf16[9,64,512]{2,1,0:T(8,128)(2,1)S(1)}, u32[]{:S(2)}, u32[]{:S(2)}) collective-permute-start(bf16[9,64,512]{2,1,0:T(8,128)(2,1)} %collective-permute-done.11), channel_id=1, source_target_pairs={{0,1},{1,0},{2,3},{3,2},{4,5},{5,4},{6,7},{7,6},{8,9},{9,8},{10,11... | collective-permute-start | bytes 1769480 | tf_op jit(solution)/shard_map/ppermute | solution.py:64
  69.3 9.2 %collective-permute-start.10 = (bf16[9,64,512]{2,1,0:T(8,128)(2,1)}, bf16[9,64,512]{2,1,0:T(8,128)(2,1)S(1)}, u32[]{:S(2)}, u32[]{:S(2)}) collective-permute-start(bf16[9,64,512]{2,1,0:T(8,128)(2,1)} %collective-permute-done.9), channel_id=1, source_target_pairs={{0,1},{1,0},{2,3},{3,2},{4,5},{5,4},{6,7},{7,6},{8,9},{9,8},{10,11... | collective-permute-start | bytes 1769480 | tf_op jit(solution)/shard_map/ppermute | solution.py:64
  70.5 19.9 %collective-permute-start.32 = (bf16[16,16,128]{2,1,0:T(8,128)(2,1)}, bf16[16,16,128]{2,1,0:T(8,128)(2,1)}, u32[]{:S(2)}, u32[]{:S(2)}) collective-permute-start(bf16[16,16,128]{2,1,0:T(8,128)(2,1)} %get-tuple-element.184), channel_id=1, source_target_pairs={{0,6},{2,4},{4,2},{6,0},{1,7},{3,5},{5,3},{7,1},{8,14},{10,12},{12... | collective-permute-start | bytes 196616 | tf_op jit(solution)/shard_map/ppermute | solution.py:64
  72.7 17.8 %collective-permute-start.31 = (bf16[16,16,128]{2,1,0:T(8,128)(2,1)}, bf16[16,16,128]{2,1,0:T(8,128)(2,1)}, u32[]{:S(2)}, u32[]{:S(2)}) collective-permute-start(bf16[16,16,128]{2,1,0:T(8,128)(2,1)} %get-tuple-element.185), channel_id=1, source_target_pairs={{0,4},{2,6},{4,0},{6,2},{1,5},{3,7},{5,1},{7,3},{8,12},{10,14},{12... | collective-permute-start | bytes 196616 | tf_op jit(solution)/shard_map/ppermute | solution.py:64
  75.7 14.8 %collective-permute-start.30 = (bf16[16,16,128]{2,1,0:T(8,128)(2,1)}, bf16[16,16,128]{2,1,0:T(8,128)(2,1)}, u32[]{:S(2)}, u32[]{:S(2)}) collective-permute-start(bf16[16,16,128]{2,1,0:T(8,128)(2,1)} %get-tuple-element.186), channel_id=1, source_target_pairs={{0,2},{2,0},{4,6},{6,4},{1,3},{3,1},{5,7},{7,5},{8,10},{10,8},{12,... | collective-permute-start | bytes 196616 | tf_op jit(solution)/shard_map/ppermute | solution.py:64
  86.3 12.4 %all-to-all-start.1 = ((f32[32,8,128]{2,1,0:T(8,128)}), f32[32,8,128]{2,1,0:T(8,128)S(1)}, u32[]{:S(2)}, u32[]{:S(2)}) async-start(f32[32,8,128]{2,1,0:T(8,128)} %broadcast_in_dim.37), calls=%async_computation.1 | async-start | bytes 262144 | tf_op jit(solution)/shard_map/all_to_all | solution.py:97
  103.4 10.8 %all-to-all-start.3 = ((f32[32,8,128]{2,1,0:T(8,128)}), f32[32,8,128]{2,1,0:T(8,128)S(1)}, u32[]{:S(2)}, u32[]{:S(2)}) async-start(f32[32,8,128]{2,1,0:T(8,128)} %broadcast_in_dim.81), calls=%async_computation.3 | async-start | bytes 262144 | tf_op jit(solution)/shard_map/all_to_all | solution.py:97
  114.9 13.2 %all-to-all-start.2 = ((f32[32,16,128]{2,1,0:T(8,128)}), f32[32,16,128]{2,1,0:T(8,128)S(1)}, u32[]{:S(2)}, u32[]{:S(2)}) async-start(f32[32,16,128]{2,1,0:T(8,128)} %bitcast.117), calls=%async_computation.2 | async-start | bytes 524288 | tf_op jit(solution)/shard_map/all_to_all | solution.py:300
  128.8 12.5 %all-to-all-start.4 = ((f32[32,8,128]{2,1,0:T(8,128)}), f32[32,8,128]{2,1,0:T(8,128)S(1)}, u32[]{:S(2)}, u32[]{:S(2)}) async-start(f32[32,8,128]{2,1,0:T(8,128)} %broadcast_in_dim.83), calls=%async_computation.4 | async-start | bytes 262144 | tf_op jit(solution)/shard_map/all_to_all | solution.py:97
  135.0 11.1 %collective-permute-start.29 = (bf16[16,16,512]{2,1,0:T(8,128)(2,1)}, bf16[16,16,512]{2,1,0:T(8,128)(2,1)S(1)}, u32[]{:S(2)}, u32[]{:S(2)}) collective-permute-start(bf16[16,16,512]{2,1,0:T(8,128)(2,1)} %convolution_convert_fusion.2), channel_id=1, source_target_pairs={{0,6},{2,4},{4,2},{6,0},{1,7},{3,5},{5,3},{7,1},{8,14},{10,12},{12... | collective-permute-start | bytes 786440 | tf_op jit(solution)/shard_map/ppermute | solution.py:64
  137.7 13.8 %collective-permute-start.28 = (bf16[16,16,512]{2,1,0:T(8,128)(2,1)}, bf16[16,16,512]{2,1,0:T(8,128)(2,1)}, u32[]{:S(2)}, u32[]{:S(2)}) collective-permute-start(bf16[16,16,512]{2,1,0:T(8,128)(2,1)} %convolution_convert_fusion.2), channel_id=1, source_target_pairs={{0,4},{2,6},{4,0},{6,2},{1,5},{3,7},{5,1},{7,3},{8,12},{10,14},{12... | collective-permute-start | bytes 786440 | tf_op jit(solution)/shard_map/ppermute | solution.py:64
  138.2 13.2 %collective-permute-start.27 = (bf16[16,16,512]{2,1,0:T(8,128)(2,1)}, bf16[16,16,512]{2,1,0:T(8,128)(2,1)}, u32[]{:S(2)}, u32[]{:S(2)}) collective-permute-start(bf16[16,16,512]{2,1,0:T(8,128)(2,1)} %convolution_convert_fusion.2), channel_id=1, source_target_pairs={{0,2},{2,0},{4,6},{6,4},{1,3},{3,1},{5,7},{7,5},{8,10},{10,8},{12,... | collective-permute-start | bytes 786440 | tf_op jit(solution)/shard_map/ppermute | solution.py:64
  143.7 23.4 %collective-permute-start.15 = (bf16[16,16,128]{2,1,0:T(8,128)(2,1)S(1)}, bf16[16,16,128]{2,1,0:T(8,128)(2,1)S(1)}, u32[]{:S(2)}, u32[]{:S(2)}) collective-permute-start(bf16[16,16,128]{2,1,0:T(8,128)(2,1)S(1)} %get-tuple-element.188), channel_id=1, source_target_pairs={{0,6},{2,4},{4,2},{6,0},{1,7},{3,5},{5,3},{7,1},{8,14},{10,12},{12... | collective-permute-start | bytes 196616 | tf_op jit(solution)/shard_map/ppermute | solution.py:64
  145.6 21.5 %collective-permute-start.14 = (bf16[16,16,128]{2,1,0:T(8,128)(2,1)S(1)}, bf16[16,16,128]{2,1,0:T(8,128)(2,1)S(1)}, u32[]{:S(2)}, u32[]{:S(2)}) collective-permute-start(bf16[16,16,128]{2,1,0:T(8,128)(2,1)S(1)} %get-tuple-element.189), channel_id=1, source_target_pairs={{0,4},{2,6},{4,0},{6,2},{1,5},{3,7},{5,1},{7,3},{8,12},{10,14},{12... | collective-permute-start | bytes 196616 | tf_op jit(solution)/shard_map/ppermute | solution.py:64
  146.1 21.0 %collective-permute-start.13 = (bf16[16,16,128]{2,1,0:T(8,128)(2,1)S(1)}, bf16[16,16,128]{2,1,0:T(8,128)(2,1)S(1)}, u32[]{:S(2)}, u32[]{:S(2)}) collective-permute-start(bf16[16,16,128]{2,1,0:T(8,128)(2,1)S(1)} %get-tuple-element.190), channel_id=1, source_target_pairs={{0,2},{2,0},{4,6},{6,4},{1,3},{3,1},{5,7},{7,5},{8,10},{10,8},{12,... | collective-permute-start | bytes 196616 | tf_op jit(solution)/shard_map/ppermute | solution.py:64
  167.0 8.3 %collective-permute-start.33 = (bf16[4,576,128]{2,1,0:T(8,128)(2,1)S(1)}, bf16[4,576,128]{2,1,0:T(8,128)(2,1)S(1)}, u32[]{:S(2)}, u32[]{:S(2)}) collective-permute-start(bf16[4,576,128]{2,1,0:T(8,128)(2,1)S(1)} %dynamic-slice_bitcast_fusion.4), channel_id=1, source_target_pairs={{0,1},{1,0},{2,3},{3,2},{4,5},{5,4},{6,7},{7,6},{8,9},{9,8},{10,11... | collective-permute-start | bytes 1769480 | tf_op jit(solution)/shard_map/ppermute | solution.py:64
  175.5 8.6 %collective-permute-start.36 = (bf16[576,128]{1,0:T(8,128)(2,1)S(1)}, bf16[576,128]{1,0:T(8,128)(2,1)S(1)}, u32[]{:S(2)}, u32[]{:S(2)}) collective-permute-start(bf16[576,128]{1,0:T(8,128)(2,1)S(1)} %get-tuple-element.155), channel_id=1, source_target_pairs={{0,24},{8,16},{16,8},{24,0},{1,25},{9,17},{17,9},{25,1},{2,26},{10... | collective-permute-start | bytes 442376 | tf_op jit(solution)/shard_map/ppermute | solution.py:64
  178.7 20.2 %collective-permute-start.35 = (bf16[576,128]{1,0:T(8,128)(2,1)S(1)}, bf16[576,128]{1,0:T(8,128)(2,1)S(1)}, u32[]{:S(2)}, u32[]{:S(2)}) collective-permute-start(bf16[576,128]{1,0:T(8,128)(2,1)S(1)} %get-tuple-element.156), channel_id=1, source_target_pairs={{0,16},{8,24},{16,0},{24,8},{1,17},{9,25},{17,1},{25,9},{2,18},{10... | collective-permute-start | bytes 442376 | tf_op jit(solution)/shard_map/ppermute | solution.py:64
  178.7 20.2 %collective-permute-start.34 = (bf16[576,128]{1,0:T(8,128)(2,1)S(1)}, bf16[576,128]{1,0:T(8,128)(2,1)S(1)}, u32[]{:S(2)}, u32[]{:S(2)}) collective-permute-start(bf16[576,128]{1,0:T(8,128)(2,1)S(1)} %get-tuple-element.154), channel_id=1, source_target_pairs={{0,8},{8,0},{16,24},{24,16},{1,9},{9,1},{17,25},{25,17},{2,10},{10... | collective-permute-start | bytes 442376 | tf_op jit(solution)/shard_map/ppermute | solution.py:64
  180.1 21.3 %collective-permute-start.19 = (bf16[576,128]{1,0:T(8,128)(2,1)S(1)}, bf16[576,128]{1,0:T(8,128)(2,1)S(1)}, u32[]{:S(2)}, u32[]{:S(2)}) collective-permute-start(bf16[576,128]{1,0:T(8,128)(2,1)S(1)} %get-tuple-element.164), channel_id=1, source_target_pairs={{0,24},{8,16},{16,8},{24,0},{1,25},{9,17},{17,9},{25,1},{2,26},{10... | collective-permute-start | bytes 442376 | tf_op jit(solution)/shard_map/ppermute | solution.py:64
  183.4 28.2 %collective-permute-start.18 = (bf16[576,128]{1,0:T(8,128)(2,1)S(1)}, bf16[576,128]{1,0:T(8,128)(2,1)S(1)}, u32[]{:S(2)}, u32[]{:S(2)}) collective-permute-start(bf16[576,128]{1,0:T(8,128)(2,1)S(1)} %get-tuple-element.165), channel_id=1, source_target_pairs={{0,16},{8,24},{16,0},{24,8},{1,17},{9,25},{17,1},{25,9},{2,18},{10... | collective-permute-start | bytes 442376 | tf_op jit(solution)/shard_map/ppermute | solution.py:64
  184.1 29.5 %collective-permute-start.17 = (bf16[576,128]{1,0:T(8,128)(2,1)S(1)}, bf16[576,128]{1,0:T(8,128)(2,1)S(1)}, u32[]{:S(2)}, u32[]{:S(2)}) collective-permute-start(bf16[576,128]{1,0:T(8,128)(2,1)S(1)} %get-tuple-element.163), channel_id=1, source_target_pairs={{0,8},{8,0},{16,24},{24,16},{1,9},{9,1},{17,25},{25,17},{2,10},{10... | collective-permute-start | bytes 442376 | tf_op jit(solution)/shard_map/ppermute | solution.py:64
  199.1 16.5 %collective-permute-start.53 = (bf16[576,128]{1,0:T(8,128)(2,1)S(1)}, bf16[576,128]{1,0:T(8,128)(2,1)S(1)}, u32[]{:S(2)}, u32[]{:S(2)}) collective-permute-start(bf16[576,128]{1,0:T(8,128)(2,1)S(1)} %get-tuple-element.132), channel_id=1, source_target_pairs={{0,24},{8,16},{16,8},{24,0},{1,25},{9,17},{17,9},{25,1},{2,26},{10... | collective-permute-start | bytes 442376 | tf_op jit(solution)/shard_map/ppermute | solution.py:64
  201.4 16.0 %collective-permute-start.52 = (bf16[576,128]{1,0:T(8,128)(2,1)S(1)}, bf16[576,128]{1,0:T(8,128)(2,1)S(1)}, u32[]{:S(2)}, u32[]{:S(2)}) collective-permute-start(bf16[576,128]{1,0:T(8,128)(2,1)S(1)} %get-tuple-element.132), channel_id=1, source_target_pairs={{0,16},{8,24},{16,0},{24,8},{1,17},{9,25},{17,1},{25,9},{2,18},{10... | collective-permute-start | bytes 442376 | tf_op jit(solution)/shard_map/ppermute | solution.py:64
  201.4 18.2 %collective-permute-start.51 = (bf16[576,128]{1,0:T(8,128)(2,1)S(1)}, bf16[576,128]{1,0:T(8,128)(2,1)S(1)}, u32[]{:S(2)}, u32[]{:S(2)}) collective-permute-start(bf16[576,128]{1,0:T(8,128)(2,1)S(1)} %get-tuple-element.132), channel_id=1, source_target_pairs={{0,8},{8,0},{16,24},{24,16},{1,9},{9,1},{17,25},{25,17},{2,10},{10... | collective-permute-start | bytes 442376 | tf_op jit(solution)/shard_map/ppermute | solution.py:64
  211.6 10.7 %collective-permute-start.39 = (bf16[576,128]{1,0:T(8,128)(2,1)S(1)}, bf16[576,128]{1,0:T(8,128)(2,1)S(1)}, u32[]{:S(2)}, u32[]{:S(2)}) collective-permute-start(bf16[576,128]{1,0:T(8,128)(2,1)S(1)} %get-tuple-element.133), channel_id=1, source_target_pairs={{0,6},{2,4},{4,2},{6,0},{1,7},{3,5},{5,3},{7,1},{8,14},{10,12},{12... | collective-permute-start | bytes 442376 | tf_op jit(solution)/shard_map/ppermute | solution.py:64
  213.6 9.4 %collective-permute-start.38 = (bf16[576,128]{1,0:T(8,128)(2,1)S(1)}, bf16[576,128]{1,0:T(8,128)(2,1)S(1)}, u32[]{:S(2)}, u32[]{:S(2)}) collective-permute-start(bf16[576,128]{1,0:T(8,128)(2,1)S(1)} %get-tuple-element.133), channel_id=1, source_target_pairs={{0,4},{2,6},{4,0},{6,2},{1,5},{3,7},{5,1},{7,3},{8,12},{10,14},{12... | collective-permute-start | bytes 442376 | tf_op jit(solution)/shard_map/ppermute | solution.py:64
  215.6 8.1 %collective-permute-start.37 = (bf16[576,128]{1,0:T(8,128)(2,1)S(1)}, bf16[576,128]{1,0:T(8,128)(2,1)S(1)}, u32[]{:S(2)}, u32[]{:S(2)}) collective-permute-start(bf16[576,128]{1,0:T(8,128)(2,1)S(1)} %get-tuple-element.133), channel_id=1, source_target_pairs={{0,2},{2,0},{4,6},{6,4},{1,3},{3,1},{5,7},{7,5},{8,10},{10,8},{12,... | collective-permute-start | bytes 442376 | tf_op jit(solution)/shard_map/ppermute | solution.py:64
  219.7 7.7 %collective-permute-start.22 = (bf16[576,128]{1,0:T(8,128)(2,1)S(1)}, bf16[576,128]{1,0:T(8,128)(2,1)S(1)}, u32[]{:S(2)}, u32[]{:S(2)}) collective-permute-start(bf16[576,128]{1,0:T(8,128)(2,1)S(1)} %get-tuple-element.135), channel_id=1, source_target_pairs={{0,6},{2,4},{4,2},{6,0},{1,7},{3,5},{5,3},{7,1},{8,14},{10,12},{12... | collective-permute-start | bytes 442376 | tf_op jit(solution)/shard_map/ppermute | solution.py:64
  223.7 14.1 %collective-permute-start.48 = (bf16[576,128]{1,0:T(8,128)(2,1)S(1)}, bf16[576,128]{1,0:T(8,128)(2,1)S(1)}, u32[]{:S(2)}, u32[]{:S(2)}) collective-permute-start(bf16[576,128]{1,0:T(8,128)(2,1)S(1)} %get-tuple-element.134), channel_id=1, source_target_pairs={{0,16},{8,24},{16,0},{24,8},{1,17},{9,25},{17,1},{25,9},{2,18},{10... | collective-permute-start | bytes 442376 | tf_op jit(solution)/shard_map/ppermute | solution.py:64
  224.7 13.1 %collective-permute-start.47 = (bf16[576,128]{1,0:T(8,128)(2,1)S(1)}, bf16[576,128]{1,0:T(8,128)(2,1)S(1)}, u32[]{:S(2)}, u32[]{:S(2)}) collective-permute-start(bf16[576,128]{1,0:T(8,128)(2,1)S(1)} %get-tuple-element.134), channel_id=1, source_target_pairs={{0,8},{8,0},{16,24},{24,16},{1,9},{9,1},{17,25},{25,17},{2,10},{10... | collective-permute-start | bytes 442376 | tf_op jit(solution)/shard_map/ppermute | solution.py:64
  227.3 12.0 %collective-permute-start.42 = (bf16[576,128]{1,0:T(8,128)(2,1)S(1)}, bf16[576,128]{1,0:T(8,128)(2,1)S(1)}, u32[]{:S(2)}, u32[]{:S(2)}) collective-permute-start(bf16[576,128]{1,0:T(8,128)(2,1)S(1)} %convolution_convert_fusion.4), channel_id=1, source_target_pairs={{0,24},{8,16},{16,8},{24,0},{1,25},{9,17},{17,9},{25,1},{2,26},{10... | collective-permute-start | bytes 442376 | tf_op jit(solution)/shard_map/ppermute | solution.py:64
  228.8 22.4 %collective-permute-start.41 = (bf16[576,128]{1,0:T(8,128)(2,1)S(1)}, bf16[576,128]{1,0:T(8,128)(2,1)S(1)}, u32[]{:S(2)}, u32[]{:S(2)}) collective-permute-start(bf16[576,128]{1,0:T(8,128)(2,1)S(1)} %convolution_convert_fusion.4), channel_id=1, source_target_pairs={{0,16},{8,24},{16,0},{24,8},{1,17},{9,25},{17,1},{25,9},{2,18},{10... | collective-permute-start | bytes 442376 | tf_op jit(solution)/shard_map/ppermute | solution.py:64
  228.9 22.4 %collective-permute-start.40 = (bf16[576,128]{1,0:T(8,128)(2,1)S(1)}, bf16[576,128]{1,0:T(8,128)(2,1)S(1)}, u32[]{:S(2)}, u32[]{:S(2)}) collective-permute-start(bf16[576,128]{1,0:T(8,128)(2,1)S(1)} %convolution_convert_fusion.4), channel_id=1, source_target_pairs={{0,8},{8,0},{16,24},{24,16},{1,9},{9,1},{17,25},{25,17},{2,10},{10... | collective-permute-start | bytes 442376 | tf_op jit(solution)/shard_map/ppermute | solution.py:64
  237.8 21.3 %collective-permute-start.54 = (bf16[4,576,128]{2,1,0:T(8,128)(2,1)S(1)}, bf16[4,576,128]{2,1,0:T(8,128)(2,1)S(1)}, u32[]{:S(2)}, u32[]{:S(2)}) collective-permute-start(bf16[4,576,128]{2,1,0:T(8,128)(2,1)S(1)} %get-tuple-element.136), channel_id=1, source_target_pairs={{0,1},{1,0},{2,3},{3,2},{4,5},{5,4},{6,7},{7,6},{8,9},{9,8},{10,11... | collective-permute-start | bytes 1769480 | tf_op jit(solution)/shard_map/ppermute | solution.py:64
  237.8 14.8 %collective-permute-start.25 = (bf16[576,128]{1,0:T(8,128)(2,1)S(1)}, bf16[576,128]{1,0:T(8,128)(2,1)S(1)}, u32[]{:S(2)}, u32[]{:S(2)}) collective-permute-start(bf16[576,128]{1,0:T(8,128)(2,1)S(1)} %convolution_convert_fusion.5), channel_id=1, source_target_pairs={{0,24},{8,16},{16,8},{24,0},{1,25},{9,17},{17,9},{25,1},{2,26},{10... | collective-permute-start | bytes 442376 | tf_op jit(solution)/shard_map/ppermute | solution.py:64
  239.3 17.2 %collective-permute-start.24 = (bf16[576,128]{1,0:T(8,128)(2,1)S(1)}, bf16[576,128]{1,0:T(8,128)(2,1)S(1)}, u32[]{:S(2)}, u32[]{:S(2)}) collective-permute-start(bf16[576,128]{1,0:T(8,128)(2,1)S(1)} %convolution_convert_fusion.5), channel_id=1, source_target_pairs={{0,16},{8,24},{16,0},{24,8},{1,17},{9,25},{17,1},{25,9},{2,18},{10... | collective-permute-start | bytes 442376 | tf_op jit(solution)/shard_map/ppermute | solution.py:64
  251.5 7.5 %collective-permute-start.43 = (bf16[4,576,128]{2,1,0:T(8,128)(2,1)S(1)}, bf16[4,576,128]{2,1,0:T(8,128)(2,1)S(1)}, u32[]{:S(2)}, u32[]{:S(2)}) collective-permute-start(bf16[4,576,128]{2,1,0:T(8,128)(2,1)S(1)} %get-tuple-element.148), channel_id=1, source_target_pairs={{0,1},{1,0},{2,3},{3,2},{4,5},{5,4},{6,7},{7,6},{8,9},{9,8},{10,11... | collective-permute-start | bytes 1769480 | tf_op jit(solution)/shard_map/ppermute | solution.py:64
  252.6 18.0 %collective-permute-start.50 = (bf16[4,576,128]{2,1,0:T(8,128)(2,1)}, bf16[4,576,128]{2,1,0:T(8,128)(2,1)}, u32[]{:S(2)}, u32[]{:S(2)}) collective-permute-start(bf16[4,576,128]{2,1,0:T(8,128)(2,1)} %get-tuple-element.142), channel_id=1, source_target_pairs={{0,1},{1,0},{2,3},{3,2},{4,5},{5,4},{6,7},{7,6},{8,9},{9,8},{10,11... | collective-permute-start | bytes 1769480 | tf_op jit(solution)/shard_map/ppermute | solution.py:64
  259.1 11.5 %collective-permute-start.26 = (bf16[4,576,128]{2,1,0:T(8,128)(2,1)}, bf16[4,576,128]{2,1,0:T(8,128)(2,1)}, u32[]{:S(2)}, u32[]{:S(2)}) collective-permute-start(bf16[4,576,128]{2,1,0:T(8,128)(2,1)} %get-tuple-element.157), channel_id=1, source_target_pairs={{0,1},{1,0},{2,3},{3,2},{4,5},{5,4},{6,7},{7,6},{8,9},{9,8},{10,11... | collective-permute-start | bytes 1769480 | tf_op jit(solution)/shard_map/ppermute | solution.py:64
  (86 other events, 375.5 us)

commit v2 on v0

v2 whole, which is shorter than its diff:
```python
import functools
import math

import jax
import jax.numpy as jnp
from jax import lax
from jax.experimental import pallas as pl
from jax.experimental.pallas import tpu as pltpu
from jax.sharding import PartitionSpec as P

CLASSES = 10
SIDE = 4
PIX = 16
TAPS = 9
STEP = 10
LANES = 128

EPS_NORM = 1e-05
SCALE_DECAY = 0.95
DAMPING = 0.001
CLIP_NORM = 1.0
LEARN_RATE = 0.01
BETA_ONE = 0.9
BETA_TWO = 0.999
ADAM_EPS = 1e-08
WEIGHT_DECAY = 0.01
SMOOTH = 0.1
OFFSETS = [(row_step, col_step) for row_step in (-1, 0, 1) for col_step in (-1, 0, 1)]
EVERY = ("dp", "cout", "cin")
BF = jnp.bfloat16
F32 = jnp.float32
PRECISE = lax.Precision.HIGHEST
NN = (((1,), (0,)), ((), ()))
NT = (((1,), (1,)), ((), ()))
TN = (((0,), (0,)), ((), ()))
VMEM_BYTES = 40 * 1024 * 1024


def matmul(left, right, dims=NN, precision=None):
    return lax.dot_general(
        left, right, dims, precision=precision, preferred_element_type=F32
    )


def runs(row_step, col_step, count):
    low, high = max(0, -col_step), min(SIDE, SIDE - col_step)
    found = []
    for row in range(max(0, -row_step), min(SIDE, SIDE - row_step)):
        to_row = (row * SIDE + low) * count
        from_row = ((row + row_step) * SIDE + low + col_step) * count
        length = (high - low) * count
        if found and found[-1][0] + found[-1][2] == to_row and found[-1][1] + found[-1][2] == from_row:
            found[-1] = (found[-1][0], found[-1][1], found[-1][2] + length)
        else:
            found.append((to_row, from_row, length))
    return found


def call(kernel, outs, args, scratch=(), flops=0, scalars=1):
    specs = [pl.BlockSpec(memory_space=pltpu.SMEM)] * scalars
    specs += [pl.BlockSpec(memory_space=pltpu.VMEM)] * (len(args) - scalars)
    moved = sum(math.prod(a.shape) * a.dtype.itemsize for a in list(args) + list(outs))
    return pl.pallas_call(
        kernel,
        out_shape=list(outs),
        in_specs=specs,
        out_specs=[pl.BlockSpec(memory_space=pltpu.VMEM)] * len(outs),
        scratch_shapes=list(scratch),
        compiler_params=pltpu.CompilerParams(vmem_limit_bytes=VMEM_BYTES),
        cost_estimate=pl.CostEstimate(flops=flops, bytes_accessed=moved, transcendentals=0),
    )(*args)


def shape(dims, dtype):
    return jax.ShapeDtypeStruct(dims, dtype)


def gelu_parts(values):
    rate = math.sqrt(2.0 / math.pi)
    bend = jnp.tanh(rate * (values + 0.044715 * values * values * values))
    share = 0.5 * (1.0 + bend)
    slope = share + 0.5 * values * (1.0 - bend * bend) * rate * (1.0 + 0.134145 * values * values)
    return values * share, slope


def fill_mask(masks_ref, mask_ref):
    count = masks_ref.shape[1]
    same = lax.broadcasted_iota(jnp.int32, (count, count), 0) == lax.broadcasted_iota(
        jnp.int32, (count, count), 1
    )
    for pixel in range(PIX):
        row = masks_ref[pixel : pixel + 1, :].astype(F32)
        column = jnp.sum(jnp.where(same, row, 0.0), axis=1, keepdims=True)
        mask_ref[pixel * count : (pixel + 1) * count, :] = jnp.broadcast_to(column, (count, LANES))


def fill_inputs(images_ref, mask_ref, inputs_ref):
    low = mask_ref[...].astype(BF)
    for lane in range(0, images_ref.shape[1], LANES):
        inputs_ref[:, lane : lane + LANES] = images_ref[:, lane : lane + LANES] * low


def first_kernel(
    groups, place_ref, images_ref, masks_ref, weight_ref, params_ref,
    out_ref, stats_ref, own_mask_ref, mask_ref, inputs_ref, low_ref, sum_ref,
):
    count = masks_ref.shape[1]
    part = count // groups
    me = place_ref[0]
    fill_mask(masks_ref, mask_ref)
    fill_inputs(images_ref, mask_ref, inputs_ref)
    for tap in range(TAPS):
        low_ref[:, tap * LANES : (tap + 1) * LANES] = weight_ref[tap].astype(BF)
    sum_ref[...] = jnp.zeros_like(sum_ref)
    for tap in range(0, TAPS, 2):
        taps = min(2, TAPS - tap)
        product = matmul(inputs_ref[...], low_ref[:, tap * LANES : (tap + taps) * LANES])
        for nth in range(taps):
            for to_row, from_row, length in runs(*OFFSETS[tap + nth], count):
                sum_ref[to_row : to_row + length, :] += product[
                    from_row : from_row + length, nth * LANES : (nth + 1) * LANES
                ]
    mask = mask_ref[...]
    total = sum_ref[...]
    masked = total * mask
    tile = jnp.concatenate(
        [
            jnp.sum(masked, axis=0, keepdims=True),
            jnp.sum(masked * total, axis=0, keepdims=True),
            jnp.sum(mask, axis=0, keepdims=True),
            params_ref[0:2, :],
            jnp.zeros((3, LANES), F32),
        ],
        axis=0,
    )
    stats_ref[...] = jnp.broadcast_to(tile[None], stats_ref.shape)
    for pixel in range(PIX):
        for group in range(groups):
            base = pixel * count + group * part
            out_ref[group, pixel * part : (pixel + 1) * part, :] = sum_ref[base : base + part, :].astype(BF)
        own = pl.multiple_of(pixel * count + me * part, part)
        own_mask_ref[pixel * part : (pixel + 1) * part, :] = mask_ref[pl.ds(own, part), :]


def first_norm_kernel(sizes, place_ref, slot_refs, got_ref, mask_ref, hidden_ref, first_ref, norm_ref):
    count_dp, groups, count_cin = sizes
    me = place_ref[0]
    tiles = []
    for group in range(groups):
        total = None
        for far in range(count_dp):
            for near in range(count_cin):
                tile = got_ref[(far * groups + group) * count_cin + near]
                total = tile if total is None else total + tile
        tiles.append((total, got_ref[group * count_cin]))
    kept = tiles[0][0][2:3, :]
    for group, (total, single) in enumerate(tiles):
        lanes = slice(group * LANES, (group + 1) * LANES)
        mean = total[0:1, :] / kept
        norm_ref[0:1, lanes] = mean
        norm_ref[1:2, lanes] = lax.rsqrt(total[1:2, :] / kept - mean * mean + EPS_NORM)
        norm_ref[2:4, lanes] = single[3:5, :]
        norm_ref[4:5, lanes] = kept
        norm_ref[5:8, lanes] = jnp.zeros((3, LANES), F32)
    for step, slot_ref in enumerate(slot_refs):
        lanes = pl.ds(pl.multiple_of((me ^ step) * LANES, LANES), LANES)
        low = slot_ref[...]
        scaled = (low.astype(F32) - norm_ref[0:1, lanes]) * norm_ref[1:2, lanes]
        value, _ = gelu_parts(norm_ref[2:3, lanes] * scaled + norm_ref[3:4, lanes])
        hidden_ref[:, lanes] = (value * mask_ref[...]).astype(BF)
        first_ref[:, lanes] = low


def second_kernel(
    place_ref, own_ref, other_ref, own_mask_ref, other_mask_ref, params_ref, slot_refs,
    mine_ref, theirs_ref, stats_ref, inputs_ref, weight_ref, sum_ref,
):
    me = place_ref[0]
    rows = own_ref.shape[0]
    part = rows // PIX
    depth, half = slot_refs[0].shape[1:]
    inputs_ref[0:rows, :] = own_ref[...]
    inputs_ref[rows : 2 * rows, :] = other_ref[...]
    for step, slot_ref in enumerate(slot_refs):
        span = pl.ds(pl.multiple_of((me ^ step) * depth, depth), depth)
        for tap in range(TAPS):
            weight_ref[span, tap * half : (tap + 1) * half] = slot_ref[tap]
    sum_ref[...] = jnp.zeros_like(sum_ref)
    for tap in range(TAPS):
        product = matmul(inputs_ref[...], weight_ref[:, tap * half : (tap + 1) * half])
        for to_row, from_row, length in runs(*OFFSETS[tap], part):
            for base in (0, rows):
                sum_ref[base + to_row : base + to_row + length, :] += product[
                    base + from_row : base + from_row + length, :
                ]
    mine_ref[...] = sum_ref[0:rows, :]
    theirs_ref[...] = sum_ref[rows : 2 * rows, :]
    lines = [[], []]
    for lane in range(0, half, LANES):
        first = square = None
        for base, mask_ref in ((0, own_mask_ref), (rows, other_mask_ref)):
            total = sum_ref[base : base + rows, lane : lane + LANES]
            masked = total * mask_ref[...]
            first_part = jnp.sum(masked, axis=0, keepdims=True)
            square_part = jnp.sum(masked * total, axis=0, keepdims=True)
            first = first_part if first is None else first + first_part
            square = square_part if square is None else square + square_part
        lines[0].append(first)
        lines[1].append(square)
    spare = 8 - 2 * (half // LANES) - 2
    tile = jnp.concatenate(
        lines[0] + lines[1] + [params_ref[2:4, :], jnp.zeros((spare, LANES), F32)], axis=0
    )
    stats_ref[...] = jnp.broadcast_to(tile[None], stats_ref.shape)


def head_kernel(
    sizes, place_ref, mine_ref, got_ref_rows, got_ref, norm_first_ref, mask_ref, head_ref, bias_ref, labels_ref,
    wide_ref, norm_ref, dz_ref, sums_ref, head_out_ref, slope_ref, pooled_ref, weight_ref,
):
    count_dp, groups, count_cin = sizes
    side = place_ref[1]
    rows, half = mine_ref.shape
    part = rows // PIX
    blocks = half // LANES
    wide_ref[:, pl.ds(pl.multiple_of(side * half, half), half)] = mine_ref[...]
    wide_ref[:, pl.ds(pl.multiple_of((1 - side) * half, half), half)] = got_ref_rows[...]
    totals = [None, None]
    for source in range(count_dp * groups * count_cin):
        which = source % count_cin % 2
        tile = got_ref[source]
        totals[which] = tile if totals[which] is None else totals[which] + tile
    kept = norm_first_ref[4:5, 0:LANES]
    mask = mask_ref[...]
    for group in range(groups):
        lanes = slice(group * LANES, (group + 1) * LANES)
        total, line = totals[group // blocks], group % blocks
        mean = total[line : line + 1, :] / kept
        rstd = lax.rsqrt(total[blocks + line : blocks + line + 1, :] / kept - mean * mean + EPS_NORM)
        single = got_ref[group * count_cin]
        gain = single[2 * blocks : 2 * blocks + 1, :]
        shift = single[2 * blocks + 1 : 2 * blocks + 2, :]
        norm_ref[0:1, lanes] = mean
        norm_ref[1:2, lanes] = rstd
        norm_ref[2:3, lanes] = gain
        norm_ref[3:4, lanes] = shift
        norm_ref[4:8, lanes] = jnp.broadcast_to(kept, (4, LANES))
        value, slope = gelu_parts(gain * ((wide_ref[:, lanes] - mean) * rstd) + shift)
        slope_ref[:, lanes] = slope * mask * (1.0 / PIX)
        pooled_ref[:, lanes] = jnp.sum((value * mask).reshape(PIX, part, LANES), axis=0) * (1.0 / PIX)
        weight_ref[0:16, lanes] = head_ref[group]
    weight_ref[16:LANES, :] = jnp.zeros((LANES - 16, weight_ref.shape[1]), F32)
    pooled = pooled_ref[...].astype(BF)
    head = weight_ref[...].astype(BF)
    class_index = lax.broadcasted_iota(jnp.int32, (part, LANES), 1)
    logits = matmul(pooled, head, NT) + bias_ref[...]
    logits = jnp.where(class_index < CLASSES, logits, -1e30)
    logits = logits - jnp.max(logits, axis=1, keepdims=True)
    log_probs = logits - jnp.log(jnp.sum(jnp.exp(logits), axis=1, keepdims=True))
    wanted = jnp.where(class_index == labels_ref[...], 1.0 - SMOOTH, 0.0) + SMOOTH / CLASSES
    wanted = jnp.where(class_index < CLASSES, wanted, 0.0)
    loss = -jnp.sum(jnp.sum(wanted * log_probs, axis=1, keepdims=True), axis=0, keepdims=True)
    logit_grad = jnp.exp(log_probs) - wanted
    head_grad = matmul(logit_grad, pooled.astype(F32), TN, PRECISE)
    pooled_grad = matmul(logit_grad, head.astype(F32), NN, PRECISE)
    extra = jnp.sum(logit_grad, axis=0, keepdims=True)
    extra = jnp.where(class_index[0:1, :] == CLASSES, loss, extra)
    line = lax.broadcasted_iota(jnp.int32, (16, LANES), 0)
    gains, shifts = [], []
    for group in range(groups):
        lanes = slice(group * LANES, (group + 1) * LANES)
        head_out_ref[group] = jnp.where(line == CLASSES, extra, head_grad[0:16, lanes])
        spread = jnp.broadcast_to(pooled_grad[:, lanes][None], (PIX, part, LANES)).reshape(rows, LANES)
        dz = slope_ref[:, lanes] * spread
        dz_ref[:, lanes] = dz
        scaled = (wide_ref[:, lanes] - norm_ref[0:1, lanes]) * norm_ref[1:2, lanes]
        gains.append(jnp.sum(dz * scaled, axis=0, keepdims=True))
        shifts.append(jnp.sum(dz, axis=0, keepdims=True))
    sums_ref[...] = jnp.broadcast_to(jnp.concatenate(gains + shifts, axis=0)[None], sums_ref.shape)


def total_of(got_ref):
    total = got_ref[0]
    for source in range(1, got_ref.shape[0]):
        total = total + got_ref[source]
    return total


def norm_back(values, dz, norm, mask, gain_grad, shift_grad):
    scaled = (values - norm[0:1, :]) * norm[1:2, :]
    gain = norm[2:3, :]
    return norm[1:2, :] * (
        gain * dz - mask * (gain / norm[4:5, :]) * (shift_grad + scaled * gain_grad)
    )


def second_back_kernel(
    dz_ref, wide_ref, norm_ref, got_ref, mask_ref, basis_ref, grad_ref, right_ref, sums_ref
):
    total = total_of(got_ref)
    sums_ref[...] = total
    groups = total.shape[0] // 2
    for group in range(groups):
        lanes = slice(group * LANES, (group + 1) * LANES)
        grad_ref[:, lanes] = norm_back(
            wide_ref[:, lanes], dz_ref[:, lanes], norm_ref[:, lanes], mask_ref[...],
            total[group : group + 1, :], total[groups + group : groups + group + 1, :],
        ).astype(BF)
    right_ref[...] = jnp.transpose(matmul(grad_ref[...], basis_ref[...])).astype(BF)


def conv_back_kernel(grad_ref, weight_ref, first_ref, norm_ref, mask_ref, dz_ref, sums_ref, sum_ref):
    rows, channels = grad_ref.shape
    part = rows // PIX
    sum_ref[...] = jnp.zeros_like(sum_ref)
    for tap in range(TAPS):
        product = matmul(grad_ref[...], weight_ref[tap], NT)
        row_step, col_step = OFFSETS[tap]
        for to_row, from_row, length in runs(-row_step, -col_step, part):
            sum_ref[to_row : to_row + length, :] += product[from_row : from_row + length, :]
    mask = mask_ref[...]
    gains, shifts = [], []
    for lane in range(0, channels, LANES):
        lanes = slice(lane, lane + LANES)
        norm = norm_ref[:, lanes]
        scaled = (first_ref[:, lanes].astype(F32) - norm[0:1, :]) * norm[1:2, :]
        _, slope = gelu_parts(norm[2:3, :] * scaled + norm[3:4, :])
        dz = slope * mask * sum_ref[:, lanes]
        dz_ref[:, lanes] = dz
        gains.append(jnp.sum(dz * scaled, axis=0, keepdims=True))
        shifts.append(jnp.sum(dz, axis=0, keepdims=True))
    sums_ref[...] = jnp.broadcast_to(jnp.concatenate(gains + shifts, axis=0)[None], sums_ref.shape)


def first_back_kernel(
    dz_ref, first_ref, norm_ref, got_ref, mask_ref, basis_ref, right_ref, sums_ref, grad_ref
):
    total = total_of(got_ref)
    sums_ref[...] = total
    groups = total.shape[0] // 2
    for group in range(groups):
        lanes = slice(group * LANES, (group + 1) * LANES)
        grad_ref[:, lanes] = norm_back(
            first_ref[:, lanes].astype(F32), dz_ref[:, lanes], norm_ref[:, lanes], mask_ref[...],
            total[group : group + 1, :], total[groups + group : groups + group + 1, :],
        ).astype(BF)
    product = matmul(grad_ref[...], basis_ref[...])
    for group in range(groups):
        right_ref[group] = product[:, group * LANES : (group + 1) * LANES].astype(BF)


def left_first_kernel(place_ref, images_ref, masks_ref, basis_ref, left_ref, mask_ref, inputs_ref, part_ref):
    slots = left_ref.shape[0]
    count = masks_ref.shape[1]
    part = count // slots
    me = place_ref[0]
    fill_mask(masks_ref, mask_ref)
    fill_inputs(images_ref, mask_ref, inputs_ref)
    for step in range(slots):
        for pixel in range(PIX):
            base = pl.multiple_of(pixel * count + (me ^ step) * part, part)
            part_ref[pixel * part : (pixel + 1) * part, :] = inputs_ref[pl.ds(base, part), :]
        left_ref[step] = jnp.transpose(matmul(part_ref[...], basis_ref[...])).astype(BF)


def left_second_kernel(hidden_ref, basis_ref, left_ref):
    product = matmul(hidden_ref[...], basis_ref[...])
    for group in range(left_ref.shape[0]):
        left_ref[group] = product[:, group * LANES : (group + 1) * LANES].astype(BF)


def weight_kernel(place_ref, near_refs, far_refs, weight_ref):
    me, side = place_ref[0], place_ref[1]
    depth, half = near_refs[0].shape[1:]
    for refs, at in ((near_refs, side), (far_refs, 1 - side)):
        lanes = pl.ds(pl.multiple_of(at * half, half), half)
        for step, slot_ref in enumerate(refs):
            span = pl.ds(pl.multiple_of((me ^ step) * depth, depth), depth)
            for tap in range(TAPS):
                weight_ref[tap, span, lanes] = slot_ref[tap]


def taps_kernel(turned, sign, big_refs, small_refs, out_ref, left_ref, right_ref):
    rows, width = small_refs[0].shape
    channels = big_refs[0].shape[0]
    part = rows // PIX
    right_ref[...] = jnp.zeros_like(right_ref)
    for slot, (big_ref, small_ref) in enumerate(zip(big_refs, small_refs)):
        base = slot * rows
        left_ref[:, base : base + rows] = big_ref[...]
        for tap, (row_step, col_step) in enumerate(OFFSETS):
            for to_row, from_row, length in runs(sign * row_step, sign * col_step, part):
                right_ref[base + to_row : base + to_row + length, tap * width : (tap + 1) * width] = (
                    small_ref[from_row : from_row + length, :]
                )
    for tap in range(0, TAPS, 2):
        taps = min(2, TAPS - tap)
        product = matmul(left_ref[...], right_ref[:, tap * width : (tap + taps) * width])
        if turned:
            out_ref[tap * width : (tap + taps) * width, :] = jnp.transpose(product).astype(BF)
        else:
            for nth in range(taps):
                out_ref[(tap + nth) * channels : (tap + nth + 1) * channels, :] = product[
                    :, nth * width : (nth + 1) * width
                ].astype(BF)


def scales_kernel(place_ref, coeff_ref, scales_ref, scales_out_ref, ratio_ref):
    half = ratio_ref.shape[1]
    columns = pl.ds(pl.multiple_of(place_ref[1] * half, half), half)
    coeff = coeff_ref[...].astype(F32)
    scales_out_ref[...] = SCALE_DECAY * scales_ref[...] + (1.0 - SCALE_DECAY) * coeff * coeff
    ratio_ref[...] = (
        coeff_ref[:, columns].astype(F32) / (scales_out_ref[:, columns] + DAMPING)
    ).astype(BF)


def middle_second_kernel(basis_ref, slot_refs, out_ref, stack_ref):
    width = basis_ref.shape[0]
    for tap in range(TAPS):
        for step, slot_ref in enumerate(slot_refs):
            stack_ref[step * width : (step + 1) * width, :] = slot_ref[tap * width : (tap + 1) * width, :]
        out_ref[tap * width : (tap + 1) * width, :] = matmul(basis_ref[...], stack_ref[...]).astype(BF)


def add_squares(total, values):
    return total + jnp.sum((values * values).reshape(-1, 8, LANES), axis=0)


def restore_kernel(
    place_ref, basis_in_ref, middle_first_ref, basis_out_ref, near_ref, far_ref, sums_first_ref, sums_second_ref,
    head_ref, first_ref, second_ref, squares_ref, stack_ref, wide_ref,
):
    me, side = place_ref[0], place_ref[1]
    channels = basis_in_ref.shape[0]
    half = near_ref.shape[1]
    wide_ref[:, pl.ds(pl.multiple_of(side * half, half), half)] = near_ref[...]
    wide_ref[:, pl.ds(pl.multiple_of((1 - side) * half, half), half)] = far_ref[...]
    total = jnp.zeros((8, LANES), F32)
    for tap in range(TAPS):
        stack_ref[:, tap * LANES : (tap + 1) * LANES] = middle_first_ref[
            tap * channels : (tap + 1) * channels, :
        ]
    for tap in range(0, TAPS, 2):
        taps = min(2, TAPS - tap)
        product = matmul(basis_in_ref[...], stack_ref[:, tap * LANES : (tap + taps) * LANES])
        for nth in range(taps):
            block = product[:, nth * LANES : (nth + 1) * LANES]
            first_ref[tap + nth] = block.astype(BF)
            total = add_squares(total, block)
    for tap in range(TAPS):
        product = matmul(wide_ref[tap * LANES : (tap + 1) * LANES, :], basis_out_ref[...], NT)
        second_ref[tap] = product.astype(BF)
        for lane in range(0, channels, LANES):
            total = add_squares(total, product[:, lane : lane + LANES])
    groups = sums_first_ref.shape[0] // 2
    row = lax.broadcasted_iota(jnp.int32, (8, LANES), 0)
    mine = (row == me) | (row == me + groups)
    for ref in (sums_first_ref, sums_second_ref):
        total = total + jnp.where(mine, ref[...] * ref[...], 0.0)
    line = lax.broadcasted_iota(jnp.int32, (16, LANES), 0)
    lane = lax.broadcasted_iota(jnp.int32, (16, LANES), 1)
    counted = (line < CLASSES) | ((line == CLASSES) & (lane < CLASSES) & (me == 0))
    head = jnp.where(counted, head_ref[...], 0.0)
    squares_ref[...] = add_squares(total, head)


def update_kernel(
    place_ref, square_refs, weight_refs, mean_refs, square_moment_refs, grad_refs, small_refs,
    weight_outs, mean_outs, square_outs, small_outs, norm_out_ref,
):
    parts = [ref[...] for ref in square_refs]
    while len(parts) > 1:
        parts = [parts[at] + parts[at + 1] for at in range(0, len(parts), 2)]
    total = jnp.sum(jnp.sum(parts[0], axis=1, keepdims=True), axis=0, keepdims=True)
    grad_norm = jnp.sqrt(total)
    factor = CLIP_NORM / jnp.maximum(grad_norm, CLIP_NORM)

    def moments(gradient, mean_old, square_old):
        mean_new = BETA_ONE * mean_old + (1.0 - BETA_ONE) * gradient
        square_new = BETA_TWO * square_old + (1.0 - BETA_TWO) * gradient * gradient
        return mean_new, square_new

    for at in range(len(weight_refs)):
        gradient = grad_refs[at][...].astype(F32) * factor[None]
        mean_new, square_new = moments(gradient, mean_refs[at][...], square_moment_refs[at][...])
        mean_outs[at][...] = mean_new
        square_outs[at][...] = square_new
        step = (mean_new * (1.0 / (1.0 - BETA_ONE**STEP))) / (
            jnp.sqrt(square_new * (1.0 / (1.0 - BETA_TWO**STEP))) + ADAM_EPS
        )
        weight = weight_refs[at][...]
        weight_outs[at][...] = weight - LEARN_RATE * (step + WEIGHT_DECAY * weight)

    @pl.when(pl.program_id(0) == 0)
    def _():
        norm_out_ref[...] = jnp.broadcast_to(grad_norm, norm_out_ref.shape)
        norm_grad, norm_mean, norm_square, head_grad, head_mean, head_square, bias_grad, bias_mean, bias_square = small_refs
        (first_mean, first_square, second_mean, second_square, head_mean_out, head_square_out,
         bias_mean_out, bias_square_out) = small_outs
        mean_new, square_new = moments(norm_grad[...] * factor, norm_mean[...], norm_square[...])
        first_mean[...] = mean_new[0:2, :]
        second_mean[...] = mean_new[2:4, :]
        first_square[...] = square_new[0:2, :]
        second_square[...] = square_new[2:4, :]
        mean_new, square_new = moments(head_grad[...] * factor, head_mean[...], head_square[...])
        head_mean_out[...] = mean_new
        head_square_out[...] = square_new
        mean_new, square_new = moments(bias_grad[...] * factor, bias_mean[...], bias_square[...])
        bias_mean_out[...] = mean_new
        bias_square_out[...] = square_new


def swap(values, axis, step):
    count = lax.axis_size(axis)
    return lax.ppermute(values, axis, [(here, here ^ step) for here in range(count)])


def gathered(values, axis):
    return [values] + [swap(values, axis, step) for step in range(1, lax.axis_size(axis))]


def exchanged(block_of, axis):
    me = lax.axis_index(axis)
    return [block_of(me)] + [
        swap(block_of(me ^ step), axis, step) for step in range(1, lax.axis_size(axis))
    ]


def picked(values, index):
    return lax.dynamic_index_in_dim(values, index, 0, keepdims=False)


def in_order(slots, axis):
    me = lax.axis_index(axis)
    stacked = jnp.stack(slots)
    return jnp.stack([picked(stacked, me ^ place) for place in range(len(slots))])


def every_device(tiles):
    return lax.all_to_all(tiles, EVERY, 0, 0, tiled=True)


def batch_split(partial):
    count_dp, count_cin = lax.axis_size("dp"), lax.axis_size("cin")
    rows, width = partial.shape
    split = partial.reshape(count_cin, rows // count_cin, width)
    slots = exchanged(functools.partial(picked, split), "cin")
    near = sum(slot.astype(F32) for slot in slots).astype(BF)
    split = near.reshape(count_dp, -1, width)
    slots = exchanged(functools.partial(picked, split), "dp")
    return sum(slot.astype(F32) for slot in slots)


def batch_gather(block):
    far = in_order(gathered(block, "dp"), "dp").reshape(-1, block.shape[-1])
    return in_order(gathered(far, "cin"), "cin").reshape(-1, block.shape[-1])


def batch_rows(values):
    count_dp = lax.axis_size("dp")
    place = lax.axis_index("cin") * count_dp + lax.axis_index("dp")
    rows = values.shape[0] // (count_dp * lax.axis_size("cin"))
    return lax.dynamic_slice_in_dim(values, place * rows, rows, 0)


def local(
    images,
    masks,
    labels,
    w_first,
    w_second,
    norm_params,
    head_w,
    head_b,
    bases,
    scales_first,
    scales_second,
    w_first_mean,
    w_first_square,
    w_second_mean,
    w_second_square,
    norm_mean,
    norm_square,
    head_w_mean,
    head_w_square,
    head_b_mean,
    head_b_square,
):
    me = lax.axis_index("cout")
    side = lax.axis_index("cin") % 2
    place = jnp.stack([me, side]).astype(jnp.int32)
    sizes = tuple(lax.axis_size(name) for name in EVERY)
    groups = sizes[1]
    devices = sizes[0] * sizes[1] * sizes[2]
    channels = w_first.shape[1]
    width = w_first.shape[2]
    half = channels // 2
    count = images.shape[1]
    part = count // groups
    rows = PIX * part
    tile = shape((devices, 8, LANES), F32)
    wide = (rows, channels)
    basis_in_first, basis_out_first = bases[0, 0], bases[0, 1]
    basis_in_second, basis_out_second = bases[1, 0], bases[1, 1]

    piece = lax.dynamic_slice_in_dim(w_second, side * half, half, 2).astype(BF)
    near_weights = gathered(piece, "cout")
    head_rows = jnp.concatenate([head_w.T, jnp.zeros((16 - CLASSES, width), F32)], axis=0)
    head_full = lax.all_gather(head_rows, "cout")
    own_labels = lax.dynamic_slice_in_dim(labels, me * part, part, 0)[:, None]
    bias_row = jnp.pad(head_b, (0, LANES - CLASSES))[None]

    flat_images = images.reshape(PIX * count, channels)
    first_low, stats, mask = call(
        functools.partial(first_kernel, groups),
        [shape((groups, rows, width), BF), tile, shape((rows, LANES), F32)],
        [place, flat_images, masks, w_first, norm_params],
        [
            pltpu.VMEM((PIX * count, LANES), F32),
            pltpu.VMEM((PIX * count, channels), BF),
            pltpu.VMEM((channels, TAPS * width), BF),
            pltpu.VMEM((PIX * count, width), F32),
        ],
        flops=2 * PIX * count * channels * width * TAPS,
    )
    first_slots = exchanged(functools.partial(picked, first_low), "cout")
    got = every_device(stats)
    other_mask = swap(mask, "cin", 1)
    hidden, first_out, norm_first = call(
        lambda place_ref, *refs: first_norm_kernel(sizes, place_ref, refs[:groups], *refs[groups:]),
        [shape(wide, BF), shape(wide, BF), shape((8, channels), F32)],
        [place, *first_slots, got, mask],
    )
    other_hidden = swap(hidden, "cin", 1)
    mine, theirs, stats = call(
        lambda p, a, b, c, d, e, *refs: second_kernel(
            p, a, b, c, d, e, refs[:groups], *refs[groups:]
        ),
        [shape((rows, half), F32), shape((rows, half), F32), tile],
        [place, hidden, other_hidden, mask, other_mask, norm_params, *near_weights],
        [
            pltpu.VMEM((2 * rows, channels), BF),
            pltpu.VMEM((channels, TAPS * half), BF),
            pltpu.VMEM((2 * rows, half), F32),
        ],
        flops=4 * rows * channels * half * TAPS,
    )
    from_other = swap(theirs, "cin", 1)
    got = every_device(stats)
    second_out, norm_second, dz_second, sums, head_blocks = call(
        functools.partial(head_kernel, sizes),
        [
            shape(wide, F32),
            shape((8, channels), F32),
            shape(wide, F32),
            tile,
            shape((groups, 16, width), F32),
        ],
        [place, mine, from_other, got, norm_first, mask, head_full, bias_row, own_labels],
        [
            pltpu.VMEM(wide, F32),
            pltpu.VMEM((part, channels), F32),
            pltpu.VMEM((LANES, channels), F32),
        ],
    )
    got = every_device(sums)
    grad_second, right_turned, sums_second = call(
        second_back_kernel,
        [shape(wide, BF), shape((channels, rows), BF), shape((8, LANES), F32)],
        [dz_second, second_out, norm_second, got, mask, basis_out_second],
        scalars=0,
    )
    far_weights = [swap(slot, "cin", 1) for slot in near_weights]
    (weight_full,) = call(
        lambda p, *refs: weight_kernel(p, refs[:groups], refs[groups : 2 * groups], refs[-1]),
        [shape((TAPS, channels, channels), BF)],
        [place, *near_weights, *far_weights],
    )
    dz_first, sums = call(
        conv_back_kernel,
        [shape(wide, F32), tile],
        [grad_second, weight_full, first_out, norm_first, mask],
        [pltpu.VMEM(wide, F32)],
        flops=2 * rows * channels * channels * TAPS,
        scalars=0,
    )
    right_slots = gathered(right_turned, "cout")
    (left_blocks,) = call(
        left_second_kernel,
        [shape((groups, rows, width), BF)],
        [hidden, basis_in_second],
        scalars=0,
    )
    left_slots = exchanged(functools.partial(picked, left_blocks), "cout")
    (left_turned,) = call(
        left_first_kernel,
        [shape((groups, channels, rows), BF)],
        [place, flat_images, masks, basis_in_first],
        [
            pltpu.VMEM((PIX * count, LANES), F32),
            pltpu.VMEM((PIX * count, channels), BF),
            pltpu.VMEM((rows, channels), BF),
        ],
    )
    got = every_device(sums)
    right_blocks, sums_first = call(
        first_back_kernel,
        [shape((groups, rows, width), BF), shape((8, LANES), F32)],
        [dz_first, first_out, norm_first, got, mask, basis_out_first],
        [pltpu.VMEM(wide, BF)],
        scalars=0,
    )

    def products(turned, sign, big, small):
        (out,) = call(
            lambda *refs: taps_kernel(turned, sign, refs[:groups], refs[groups : 2 * groups], *refs[2 * groups :]),
            [shape((TAPS * width, channels) if turned else (TAPS * channels, width), BF)],
            [*big, *small],
            [
                pltpu.VMEM((channels, groups * rows), BF),
                pltpu.VMEM((groups * rows, TAPS * width), BF),
            ],
            flops=2 * groups * rows * channels * width * TAPS,
            scalars=0,
        )
        return out

    coeff_own = batch_split(products(True, 1, right_slots, left_slots)).astype(BF)
    coeff_second = batch_gather(coeff_own)
    flat_scales = scales_second.reshape(TAPS * width, channels)
    scales_second_new, ratio = call(
        scales_kernel,
        [shape(flat_scales.shape, F32), shape((TAPS * width, half), BF)],
        [place, coeff_second, flat_scales],
    )
    ratio_slots = gathered(ratio, "cout")
    basis_rows = lax.dynamic_slice_in_dim(basis_in_second, me * width, width, 0)

    def in_slots(values):
        return jnp.concatenate(
            [lax.dynamic_slice_in_dim(values, (me ^ step) * width, width, 1) for step in range(groups)], 1
        )

    (near_middle,) = call(
        lambda basis_ref, *refs: middle_second_kernel(basis_ref, refs[:groups], *refs[groups:]),
        [shape((TAPS * width, half), BF)],
        [in_slots(basis_rows), *ratio_slots],
        [pltpu.VMEM((channels, half), BF)],
        scalars=0,
    )
    far_middle = swap(near_middle, "cin", 1)

    right_parts = exchanged(functools.partial(picked, right_blocks), "cout")
    left_parts = [left_turned[step] for step in range(groups)]
    own = batch_split(products(False, -1, left_parts, right_parts))
    flat_scales = scales_first.reshape(TAPS * channels, width)
    scales_own = SCALE_DECAY * batch_rows(flat_scales) + (1.0 - SCALE_DECAY) * own * own
    ratio = jnp.concatenate(gathered((own / (scales_own + DAMPING)).astype(BF), "cout"), axis=1)
    basis_rows = lax.dynamic_slice_in_dim(basis_out_first, me * width, width, 0)
    middle = matmul(ratio, in_slots(basis_rows), NT).astype(BF)
    middle_first = batch_gather(middle)
    coeff_first = batch_gather(own.astype(BF)).astype(F32)
    scales_first_new = SCALE_DECAY * flat_scales + (1.0 - SCALE_DECAY) * coeff_first * coeff_first

    sent = jnp.broadcast_to(head_blocks[None, :, None], sizes + head_blocks.shape[1:])
    head_sums = jnp.sum(every_device(sent.reshape((devices,) + head_blocks.shape[1:])), axis=0)
    head_w_grad = head_sums[:CLASSES].T
    head_b_grad = head_sums[CLASSES : CLASSES + 1, :CLASSES]
    loss_total = head_sums[CLASSES, CLASSES]
    norm_grad = jnp.stack(
        [picked(total, at) for total in (sums_first, sums_second) for at in (me, groups + me)]
    )

    first_grad, second_grad, squares = call(
        restore_kernel,
        [shape((TAPS, channels, width), BF), shape((TAPS, width, channels), BF), shape((8, LANES), F32)],
        [
            place,
            basis_in_first,
            middle_first,
            basis_out_second,
            near_middle,
            far_middle,
            sums_first,
            sums_second,
            head_sums,
        ],
        [pltpu.VMEM((channels, TAPS * width), BF), pltpu.VMEM((TAPS * width, channels), BF)],
        flops=4 * TAPS * channels * channels * width,
    )
    square_slots = gathered(squares, "cout")

    smalls = [
        norm_grad, norm_mean, norm_square, head_w_grad, head_w_mean, head_w_square,
        head_b_grad, head_b_mean[None], head_b_square[None],
    ]
    small_outs = [shape((2, width), F32)] * 4 + [shape(head_w.shape, F32)] * 2 + [shape((1, CLASSES), F32)] * 2
    first_spec = pl.BlockSpec((1, channels, width), lambda tap: (tap, 0, 0))
    second_spec = pl.BlockSpec((1, width, channels), lambda tap: (tap, 0, 0))
    pair = [first_spec, second_spec]
    first_like, second_like = shape(w_first.shape, F32), shape(w_second.shape, F32)

    def whole(leaf):
        return pl.BlockSpec(leaf.shape, lambda tap: (0,) * len(leaf.shape))

    def update(*refs):
        at = [0]

        def take(number):
            at[0] += number
            return refs[at[0] - number : at[0]]

        update_kernel(
            None, take(groups), take(2), take(2), take(2), take(2), take(len(smalls)),
            take(2), take(2), take(2), take(len(small_outs)), take(1)[0],
        )

    results = pl.pallas_call(
        update,
        grid=(TAPS,),
        in_specs=[whole(leaf) for leaf in square_slots] + pair * 4 + [whole(leaf) for leaf in smalls],
        out_specs=pair * 3 + [whole(leaf) for leaf in small_outs] + [whole(shape((8, LANES), F32))],
        out_shape=[first_like, second_like] * 3 + small_outs + [shape((8, LANES), F32)],
        compiler_params=pltpu.CompilerParams(vmem_limit_bytes=VMEM_BYTES),
    )(
        *square_slots, w_first, w_second, w_first_mean, w_second_mean, w_first_square, w_second_square,
        first_grad, second_grad, *smalls,
    )
    (first_new, second_new, first_mean_new, second_mean_new, first_square_new, second_square_new,
     norm_first_mean, norm_first_square, norm_second_mean, norm_second_square,
     head_mean_new, head_square_new, bias_mean_new, bias_square_new, norm_tile) = results
    return (
        loss_total,
        norm_tile[0, 0],
        first_new,
        first_mean_new,
        first_square_new,
        second_new,
        second_mean_new,
        second_square_new,
        norm_first_mean,
        norm_first_square,
        norm_second_mean,
        norm_second_square,
        head_mean_new,
        head_square_new,
        bias_mean_new[0],
        bias_square_new[0],
        scales_first_new.reshape(scales_first.shape),
        scales_second_new.reshape(scales_second.shape),
    )


def solution(mesh):
    return jax.shard_map(
        local,
        mesh=mesh,
        in_specs=(
            P(None, ("dp", "cin"), None),
            P(None, ("dp", "cin")),
            P(("dp", "cin")),
            P(None, None, "cout"),
            P(None, "cout", None),
            P(None, "cout"),
            P("cout", None),
            P(),
            P(),
            P(None, None, "cout"),
            P(None, "cout", None),
            P(None, None, "cout"),
            P(None, None, "cout"),
            P(None, "cout", None),
            P(None, "cout", None),
            P(None, "cout"),
            P(None, "cout"),
            P("cout", None),
            P("cout", None),
            P(),
            P(),
        ),
        out_specs=(
            P(),
            P(),
            P(None, None, "cout"),
            P(None, None, "cout"),
            P(None, None, "cout"),
            P(None, "cout", None),
            P(None, "cout", None),
            P(None, "cout", None),
            P(None, "cout"),
            P(None, "cout"),
            P(None, "cout"),
            P(None, "cout"),
            P("cout", None),
            P("cout", None),
            P(),
            P(),
            P(None, None, "cout"),
            P(None, "cout", None),
        ),
        check_vma=False,
    )
```

time: 554 us -> 266 us (0.48); the launches traced: 544 us -> 265 us
  waiting for transfers between devices: 243 us -> 80.9 us
  starting transfers between devices: 0.94 us -> 94.1 us
  blocking collectives: 97.1 us -> 8.45 us
  matrix products: 76.3 us -> 0.32 us
  Pallas kernels: 0 us -> 40.5 us
  other arithmetic: 48.1 us -> 11.1 us
  local copies, waits for them, and re-layouts: 57.5 us -> 28.2 us
  between operations: 21.3 us -> 1.53 us
    psum x1 -> x0, waiting for transfers between devices: 106 us -> none  [over_batch(): return lax.psum(values, ('dp', 'cin'))]
    psum x6 -> x0, blocking collectives: 97.1 us -> none  [the longest x2 42.9 us: local(): lax.psum((jnp.sum(dz_second * scaled_second, axis=(0, 1)), jnp.sum(dz_sec...]
    reduce_scatter x1 -> x0, waiting for transfers between devices: 91.5 us -> none  [local(): lax.psum_scatter(rows_from(restore_block, block_rows, jnp.int32(0), lax.a...]
    ppermute x0 -> x52, waiting for transfers between devices: none -> 79.9 us  [swap(): lax.ppermute(values, axis, [(here, here ^ step) for here in range(count)])]
    dot_general x54 -> x1, matrix products: 70.6 us -> 0.32 us  [matmul(): lax.dot_general(left, right, dims, precision=precision, preferred_element...]
    ppermute x0 -> x52, starting transfers between devices: none -> 68.8 us  [swap(): lax.ppermute(values, axis, [(here, here ^ step) for here in range(count)])]
    pallas_call x0 -> x16, Pallas kernels: none -> 40.5 us  [the longest x15 29.2 us: call(): pl.pallas_call(kernel, out_shape=list(outs), in_specs=specs, out_specs=[p...]
    unnamed x7 -> x0, waiting for transfers between devices: 26.1 us -> none
  transfers between devices with their start and end apart: 6 -> 57, of which waited for: 5 -> 21; matrix products, arithmetic and copies ran while one was open for 7% -> 9% of each run, Pallas kernels for 0% -> 8%
where the time goes in v2:
time: 266 us; the launch traced here: 265 us
  starting transfers between devices  94.1 us (35%)
  waiting for transfers between devices  80.9 us (30%)
  Pallas kernels  40.5 us (15%)
  local copies, waits for them, and re-layouts  28.2 us (11%)
  other arithmetic  11.1 us (4%)
  blocking collectives  8.45 us (3%)
    ppermute x52, waiting for transfers between devices, swap(): lax.ppermute(values, axis, [(here, here ^ step) for here in range(count)])  79.9 us
    ppermute x52, starting transfers between devices, swap(): lax.ppermute(values, axis, [(here, here ^ step) for here in range(count)])  68.8 us
    pallas_call x15, Pallas kernels, call(): pl.pallas_call(kernel, out_shape=list(outs), in_specs=specs, out_specs=[p...  29.2 us
    all_to_all x5, starting transfers between devices, every_device(): return lax.all_to_all(tiles, EVERY, 0, 0, tiled=True)  25.3 us
    unnamed x114, local copies, waits for them, and re-layouts  15.3 us
    pallas_call x1, Pallas kernels, local(): pl.pallas_call(update, grid=(TAPS,), in_specs=[whole(leaf) for leaf in sq...  11.3 us
    all_gather x1, blocking collectives, local(): head_full = lax.all_gather(head_rows, 'cout')  8.45 us
  transfers between devices with their start and end apart: 57, of which 21 were waited for; matrix products, arithmetic and copies ran while one was open for 9% of the time, Pallas kernels for 8%

profile of v2, /device:TPU:0, one launch (start us, length us, event | category | flops | bytes accessed | tf_op | source)
XLA Modules:
  0.0 265.2 jit_solution(16114608753493690719)
XLA Ops:
  2.1 3.0 %collective-permute-start.5 = (bf16[9,128,256]{2,1,0:T(8,128)(2,1)S(1)}, bf16[9,128,256]{2,1,0:T(8,128)(2,1)}, u32[]{:S(2)}, u32[]{:S(2)}) collective-permute-start(bf16[9,128,256]{2,1,0:T(8,128)(2,1)S(1)} %dynamic-slice_convert_fusion.refs_0_), channel_id=1, source_target_pairs={{0,2},{2,0},{4,6},{6,4},{1,3},{3,1},{5,7},{7,5},{8,10},{10,8},{12,... | collective-permute-start | bytes 1769480 | tf_op jit(solution)/shard_map/ppermute | solution.py:516
  6.8 1.7 copy-done.3
  8.4 3.1 %shard_map.340 = (bf16[4,256,128]{2,1,0:T(8,128)(2,1)S(1)}, f32[32,8,128]{2,1,0:T(8,128)}, f32[256,128]{1,0:T(8,128)S(1)}) custom-call(s32[2]{0:T(128)S(1)} %pad_add_fusion.place_ref.p, bf16[1024,512]{1,0:T(8,128)(2,1)S(1)} %bitcast.145, s32[16,64]{1,0:T(8,128)S(1)} %copy-done.39, f32[9,512,128]{2,1,0:T(8,128)S(1)} %copy-done.3, f32[4,128]{1,0:T(4,128)S(1)} %copy-done.46), custom_call_target="tpu_custom_call" | custom-call | flops 1207959552 | bytes 3938312 | tf_op jit(solution)/shard_map/pallas_call | solution.py:63
  11.5 6.3 %all-to-all-start = ((f32[32,8,128]{2,1,0:T(8,128)}), f32[32,8,128]{2,1,0:T(8,128)S(1)}, u32[]{:S(2)}, u32[]{:S(2)}) async-start(f32[32,8,128]{2,1,0:T(8,128)} %get-tuple-element.60), calls=%async_computation | async-start | bytes 262144 | tf_op jit(solution)/shard_map/all_to_all | solution.py:541
  17.9 1.8 collective-permute-start
  21.2 12.8 %collective-permute-done.refs_1_ = bf16[256,128]{1,0:T(8,128)(2,1)S(1)} collective-permute-done((bf16[256,128]{1,0:T(8,128)(2,1)S(1)}, bf16[256,128]{1,0:T(8,128)(2,1)S(1)}, u32[]{:S(2)}, u32[]{:S(2)}) %collective-permute-start) | collective-permute-done | bytes 65568 | tf_op jit(solution)/shard_map/ppermute | solution.py:516
  34.0 2.7 %collective-permute-start.2 = (bf16[256,128]{1,0:T(8,128)(2,1)S(1)}, bf16[256,128]{1,0:T(8,128)(2,1)S(1)}, u32[]{:S(2)}, u32[]{:S(2)}) collective-permute-start(bf16[256,128]{1,0:T(8,128)(2,1)S(1)} %get-tuple-element.188), channel_id=1, source_target_pairs={{0,6},{2,4},{4,2},{6,0},{1,7},{3,5},{5,3},{7,1},{8,14},{10,12},{12... | collective-permute-start | bytes 196616 | tf_op jit(solution)/shard_map/ppermute | solution.py:516
  36.7 2.4 collective-permute-done.2.refs_3_
  42.5 3.7 %shard_map.342 = (f32[256,256]{1,0:T(8,128)S(1)}, f32[256,256]{1,0:T(8,128)S(1)}, f32[32,8,128]{2,1,0:T(8,128)}) custom-call(s32[2]{0:T(128)S(1)} %pad_add_fusion.place_ref.p, bf16[256,512]{1,0:T(8,128)(2,1)S(1)} %get-tuple-element.62.a.hidden_ref, bf16[256,512]{1,0:T(8,128)(2,1)S(1)} %collective-permute-done.3.b, ...), custom_call_target="tpu_custom_call" | custom-call | flops 1207959552 | bytes 3803144 | tf_op jit(solution)/shard_map/pallas_call | solution.py:63
  46.3 6.1 %all-to-all-start.1 = ((f32[32,8,128]{2,1,0:T(8,128)}), f32[32,8,128]{2,1,0:T(8,128)S(1)}, u32[]{:S(2)}, u32[]{:S(2)}) async-start(f32[32,8,128]{2,1,0:T(8,128)} %get-tuple-element.65), calls=%async_computation.1 | async-start | bytes 262144 | tf_op jit(solution)/shard_map/all_to_all | solution.py:541
  53.7 8.5 %all-gather = f32[64,128]{1,0:T(8,128)S(1)} all-gather(f32[16,128]{1,0:T(8,128)S(1)} %concatenate.12), channel_id=2, replica_groups=mesh['dp'=4,'cout'=4,'cin'=2] {'cout'}, dimensions={0}, use_global_device_ids=true | all-gather | bytes 40960 | tf_op jit(solution)/shard_map/all_gather | solution.py:610
  62.2 2.7 %shard_map.343 = (f32[256,512]{1,0:T(8,128)S(1)}, f32[8,512]{1,0:T(8,128)S(1)}, f32[256,512]{1,0:T(8,128)S(1)}, f32[32,8,128]{2,1,0:T(8,128)}, f32[4,16,128]{2,1,0:T(8,128)S(1)}) custom-call(s32[2]{0:T(128)S(1)} %pad_add_fusion.place_ref.p, f32[256,256]{1,0:T(8,128)S(1)} %get-tuple-element.63.mine_ref, f32[256,256]{1,0:T(8,128)S(1)} %collective-permute-done.8.got_ref_rows, ...), custom_call_target="tpu_custom_call" | custom-call | bytes 2064968 | tf_op jit(solution)/shard_map/pallas_call | solution.py:63
  67.1 4.6 %all-to-all-start.3 = ((f32[32,8,128]{2,1,0:T(8,128)}), f32[32,8,128]{2,1,0:T(8,128)S(1)}, u32[]{:S(2)}, u32[]{:S(2)}) async-start(f32[32,8,128]{2,1,0:T(8,128)} %get-tuple-element.71), calls=%async_computation.3 | async-start | bytes 262144 | tf_op jit(solution)/shard_map/all_to_all | solution.py:541
  71.7 2.8 %slice_bitcast_fusion.6 = (bf16[512,512]{1,0:T(8,128)(2,1)S(1)}, bf16[512,512]{1,0:T(8,128)(2,1)S(1)}, bf16[512,512]{1,0:T(8,128)(2,1)S(1)}, bf16[512,512]{1,0:T...) fusion(bf16[2,2,512,512]{3,2,1,0:T(8,128)(2,1)} %param.29), kind=kLoop, calls=%fused_computation.118 | loop fusion | bytes 5242880 | tf_op jit(solution)/shard_map/squeeze | solution.py:605
  74.5 1.6 shard_map.344
  77.1 1.8 collective-permute-start.30
  85.3 2.1 collective-permute-start.29
  87.4 2.5 shard_map.346.weight_ref
  90.0 1.6 shard_map.347
  92.2 3.8 %all-to-all-start.4 = ((f32[32,8,128]{2,1,0:T(8,128)}), f32[32,8,128]{2,1,0:T(8,128)S(1)}, u32[]{:S(2)}, u32[]{:S(2)}) async-start(f32[32,8,128]{2,1,0:T(8,128)} %copy-done.31), calls=%async_computation.4 | async-start | bytes 262144 | tf_op jit(solution)/shard_map/all_to_all | solution.py:541
  98.7 1.7 collective-permute-start.31
  101.8 1.7 dynamic-slice_bitcast_fusion.27
  105.5 3.1 %shard_map.351 = bf16[1152,512]{1,0:T(8,128)(2,1)S(1)} custom-call(bf16[512,256]{1,0:T(8,128)(2,1)} %get-tuple-element.77.refs_0_, bf16[512,256]{1,0:T(8,128)(2,1)} %collective-permute-done.27.refs_1_, bf16[512,256]{1,0:T(8,128)(2,1)} %collective-permute-done.28.refs_2_, bf16[512,256]{1,0:T(8,128)(2,1)} %collective-permute-done.29.refs_3_, ...), custom_call_target="tpu_custom_call" | custom-call | flops 1207959552 | bytes 2490368 | tf_op jit(solution)/shard_map/pallas_call | solution.py:63
  116.0 1.6 collective-permute-done.15.refs_7_
  117.7 1.7 shard_map.349
  123.2 4.5 %all-to-all-start.2 = ((f32[32,16,128]{2,1,0:T(8,128)}), f32[32,16,128]{2,1,0:T(8,128)S(1)}, u32[]{:S(2)}, u32[]{:S(2)}) async-start(f32[32,16,128]{2,1,0:T(8,128)} %bitcast.11), calls=%async_computation.2 | async-start | bytes 524288 | tf_op jit(solution)/shard_map/all_to_all | solution.py:541
  129.1 3.7 %collective-permute-start.36 = (bf16[144,512]{1,0:T(8,128)(2,1)S(1)}, bf16[144,512]{1,0:T(8,128)(2,1)S(1)}, u32[]{:S(2)}, u32[]{:S(2)}) collective-permute-start(bf16[144,512]{1,0:T(8,128)(2,1)S(1)} %get-tuple-element.163), channel_id=1, source_target_pairs={{0,24},{8,16},{16,8},{24,0},{1,25},{9,17},{17,9},{25,1},{2,26},{10... | collective-permute-start | bytes 442376 | tf_op jit(solution)/shard_map/ppermute | solution.py:516
  134.8 3.7 %collective-permute-start.19 = (bf16[576,128]{1,0:T(8,128)(2,1)S(1)}, bf16[576,128]{1,0:T(8,128)(2,1)S(1)}, u32[]{:S(2)}, u32[]{:S(2)}) collective-permute-start(bf16[576,128]{1,0:T(8,128)(2,1)S(1)} %get-tuple-element.170), channel_id=1, source_target_pairs={{0,24},{8,16},{16,8},{24,0},{1,25},{9,17},{17,9},{25,1},{2,26},{10... | collective-permute-start | bytes 442376 | tf_op jit(solution)/shard_map/ppermute | solution.py:516
  138.5 1.7 collective-permute-done.36
  140.3 13.7 %collective-permute-start.17 = (bf16[576,128]{1,0:T(8,128)(2,1)S(1)}, bf16[576,128]{1,0:T(8,128)(2,1)S(1)}, u32[]{:S(2)}, u32[]{:S(2)}) collective-permute-start(bf16[576,128]{1,0:T(8,128)(2,1)S(1)} %get-tuple-element.169), channel_id=1, source_target_pairs={{0,8},{8,0},{16,24},{24,16},{1,9},{9,1},{17,25},{25,17},{2,10},{10... | collective-permute-start | bytes 442376 | tf_op jit(solution)/shard_map/ppermute | solution.py:516
  153.9 2.6 collective-permute-done.35
  157.8 3.4 %collective-permute-start.37 = (bf16[144,512]{1,0:T(8,128)(2,1)S(1)}, bf16[144,512]{1,0:T(8,128)(2,1)S(1)}, u32[]{:S(2)}, u32[]{:S(2)}) collective-permute-start(bf16[144,512]{1,0:T(8,128)(2,1)S(1)} %fusion.21), channel_id=1, source_target_pairs={{0,8},{8,0},{16,24},{24,16},{1,9},{9,1},{17,25},{25,17},{2,10},{10... | collective-permute-start | bytes 442376 | tf_op jit(solution)/shard_map/ppermute | solution.py:516
  161.1 8.1 %collective-permute-done.18 = bf16[576,128]{1,0:T(8,128)(2,1)S(1)} collective-permute-done((bf16[576,128]{1,0:T(8,128)(2,1)S(1)}, bf16[576,128]{1,0:T(8,128)(2,1)S(1)}, u32[]{:S(2)}, u32[]{:S(2)}) %collective-permute-start.18) | collective-permute-done | bytes 147488 | tf_op jit(solution)/shard_map/ppermute | solution.py:516
  171.5 2.5 collective-permute-start.22
  173.9 7.9 %collective-permute-done.38 = bf16[144,512]{1,0:T(8,128)(2,1)S(1)} collective-permute-done((bf16[144,512]{1,0:T(8,128)(2,1)S(1)}, bf16[144,512]{1,0:T(8,128)(2,1)S(1)}, u32[]{:S(2)}, u32[]{:S(2)}) %collective-permute-start.38) | collective-permute-done | bytes 147488 | tf_op jit(solution)/shard_map/ppermute | solution.py:516
  190.1 3.2 %collective-permute-start.23 = (bf16[576,128]{1,0:T(8,128)(2,1)S(1)}, bf16[576,128]{1,0:T(8,128)(2,1)S(1)}, u32[]{:S(2)}, u32[]{:S(2)}) collective-permute-start(bf16[576,128]{1,0:T(8,128)(2,1)S(1)} %convolution_convert_fusion), channel_id=1, source_target_pairs={{0,8},{8,0},{16,24},{24,16},{1,9},{9,1},{17,25},{25,17},{2,10},{10... | collective-permute-start | bytes 442376 | tf_op jit(solution)/shard_map/ppermute | solution.py:516
  193.6 3.9 %collective-permute-done.25 = bf16[576,128]{1,0:T(8,128)(2,1)S(1)} collective-permute-done((bf16[576,128]{1,0:T(8,128)(2,1)S(1)}, bf16[576,128]{1,0:T(8,128)(2,1)S(1)}, u32[]{:S(2)}, u32[]{:S(2)}) %collective-permute-start.25) | collective-permute-done | bytes 147488 | tf_op jit(solution)/shard_map/ppermute | solution.py:516
  197.5 6.1 %collective-permute-done.24 = bf16[576,128]{1,0:T(8,128)(2,1)S(1)} collective-permute-done((bf16[576,128]{1,0:T(8,128)(2,1)S(1)}, bf16[576,128]{1,0:T(8,128)(2,1)S(1)}, u32[]{:S(2)}, u32[]{:S(2)}) %collective-permute-start.24) | collective-permute-done | bytes 147488 | tf_op jit(solution)/shard_map/ppermute | solution.py:516
  205.1 1.7 fusion.6
  208.5 3.0 %shard_map.352 = (f32[1152,512]{1,0:T(8,128)}, bf16[1152,256]{1,0:T(8,128)(2,1)S(1)}) custom-call(s32[2]{0:T(128)S(1)} %copy-done.38, bf16[1152,512]{1,0:T(8,128)(2,1)S(1)} %bitcast.138, f32[1152,512]{1,0:T(8,128)S(1)} %bitcast.139), custom_call_target="tpu_custom_call" | custom-call | bytes 6488072 | tf_op jit(solution)/shard_map/pallas_call | solution.py:63
  212.6 2.3 collective-permute-start.43
  215.0 2.1 fusion.4
  217.1 10.5 %collective-permute-done.41.refs_1_ = bf16[1152,256]{1,0:T(8,128)(2,1)S(1)} collective-permute-done((bf16[1152,256]{1,0:T(8,128)(2,1)S(1)}, bf16[1152,256]{1,0:T(8,128)(2,1)S(1)}, u32[]{:S(2)}, u32[]{:S(2)}) %collective-permute-start.41) | collective-permute-done | bytes 589856 | tf_op jit(solution)/shard_map/ppermute | solution.py:516
  227.6 12.0 %collective-permute-done.42.refs_2_ = bf16[1152,256]{1,0:T(8,128)(2,1)S(1)} collective-permute-done((bf16[1152,256]{1,0:T(8,128)(2,1)S(1)}, bf16[1152,256]{1,0:T(8,128)(2,1)S(1)}, u32[]{:S(2)}, u32[]{:S(2)}) %collective-permute-start.42) | collective-permute-done | bytes 589856 | tf_op jit(solution)/shard_map/ppermute | solution.py:516
  240.5 1.7 collective-permute-done.44.far_ref
  242.2 3.0 %shard_map.354 = (bf16[9,512,128]{2,1,0:T(8,128)(2,1)S(1)}, bf16[9,128,512]{2,1,0:T(8,128)(2,1)S(1)}, f32[8,128]{1,0:T(8,128)S(1)}) custom-call(s32[2]{0:T(128)S(1)} %copy-done.38, bf16[512,512]{1,0:T(8,128)(2,1)S(1)} %get-tuple-element.139.basis_ref.basis_in_ref, bf16[4608,128]{1,0:T(8,128)(2,1)S(1)} %bitcast.140, ...), custom_call_target="tpu_custom_call" | custom-call | flops 1207959552 | bytes 5787656 | tf_op jit(solution)/shard_map/pallas_call | solution.py:63
  248.8 1.8 fusion
  252.0 11.3 %shard_map.355 = (f32[9,512,128]{2,1,0:T(8,128)}, f32[9,128,512]{2,1,0:T(8,128)}, f32[9,512,128]{2,1,0:T(8,128)}, f32[9,128,512]{2,1,0:T(8,128)}, f32[9,512,128]...) custom-call(f32[8,128]{1,0:T(8,128)S(1)} %get-tuple-element.81.refs_, ...), custom_call_target="tpu_custom_call" | custom-call | tf_op jit(solution)/shard_map/pallas_call | solution.py:819
  (244 shorter events, 63.9 us)
Async XLA Ops:
  2.1 40.3 %collective-permute-start.5 = (bf16[9,128,256]{2,1,0:T(8,128)(2,1)S(1)}, bf16[9,128,256]{2,1,0:T(8,128)(2,1)}, u32[]{:S(2)}, u32[]{:S(2)}) collective-permute-start(bf16[9,128,256]{2,1,0:T(8,128)(2,1)S(1)} %dynamic-slice_convert_fusion.refs_0_), channel_id=1, source_target_pairs={{0,2},{2,0},{4,6},{6,4},{1,3},{3,1},{5,7},{7,5},{8,10},{10,8},{12,... | collective-permute-start | bytes 1769480 | tf_op jit(solution)/shard_map/ppermute | solution.py:516
  5.2 37.3 %collective-permute-start.6 = (bf16[9,128,256]{2,1,0:T(8,128)(2,1)S(1)}, bf16[9,128,256]{2,1,0:T(8,128)(2,1)}, u32[]{:S(2)}, u32[]{:S(2)}) collective-permute-start(bf16[9,128,256]{2,1,0:T(8,128)(2,1)S(1)} %dynamic-slice_convert_fusion.refs_0_), channel_id=1, source_target_pairs={{0,4},{2,6},{4,0},{6,2},{1,5},{3,7},{5,1},{7,3},{8,12},{10,14},{12... | collective-permute-start | bytes 1769480 | tf_op jit(solution)/shard_map/ppermute | solution.py:516
  6.7 35.8 %collective-permute-start.7 = (bf16[9,128,256]{2,1,0:T(8,128)(2,1)S(1)}, bf16[9,128,256]{2,1,0:T(8,128)(2,1)}, u32[]{:S(2)}, u32[]{:S(2)}) collective-permute-start(bf16[9,128,256]{2,1,0:T(8,128)(2,1)S(1)} %dynamic-slice_convert_fusion.refs_0_), channel_id=1, source_target_pairs={{0,6},{2,4},{4,2},{6,0},{1,7},{3,5},{5,3},{7,1},{8,14},{10,12},{12... | collective-permute-start | bytes 1769480 | tf_op jit(solution)/shard_map/ppermute | solution.py:516
  11.5 27.6 %all-to-all-start = ((f32[32,8,128]{2,1,0:T(8,128)}), f32[32,8,128]{2,1,0:T(8,128)S(1)}, u32[]{:S(2)}, u32[]{:S(2)}) async-start(f32[32,8,128]{2,1,0:T(8,128)} %get-tuple-element.60), calls=%async_computation | async-start | bytes 262144 | tf_op jit(solution)/shard_map/all_to_all | solution.py:541
  17.9 16.1 %collective-permute-start = (bf16[256,128]{1,0:T(8,128)(2,1)S(1)}, bf16[256,128]{1,0:T(8,128)(2,1)S(1)}, u32[]{:S(2)}, u32[]{:S(2)}) collective-permute-start(bf16[256,128]{1,0:T(8,128)(2,1)S(1)} %get-tuple-element.190), channel_id=1, source_target_pairs={{0,2},{2,0},{4,6},{6,4},{1,3},{3,1},{5,7},{7,5},{8,10},{10,8},{12,... | collective-permute-start | bytes 196616 | tf_op jit(solution)/shard_map/ppermute | solution.py:516
  19.7 17.0 %collective-permute-start.1 = (bf16[256,128]{1,0:T(8,128)(2,1)S(1)}, bf16[256,128]{1,0:T(8,128)(2,1)S(1)}, u32[]{:S(2)}, u32[]{:S(2)}) collective-permute-start(bf16[256,128]{1,0:T(8,128)(2,1)S(1)} %get-tuple-element.189), channel_id=1, source_target_pairs={{0,4},{2,6},{4,0},{6,2},{1,5},{3,7},{5,1},{7,3},{8,12},{10,14},{12... | collective-permute-start | bytes 196616 | tf_op jit(solution)/shard_map/ppermute | solution.py:516
  34.0 5.2 %collective-permute-start.2 = (bf16[256,128]{1,0:T(8,128)(2,1)S(1)}, bf16[256,128]{1,0:T(8,128)(2,1)S(1)}, u32[]{:S(2)}, u32[]{:S(2)}) collective-permute-start(bf16[256,128]{1,0:T(8,128)(2,1)S(1)} %get-tuple-element.188), channel_id=1, source_target_pairs={{0,6},{2,4},{4,2},{6,0},{1,7},{3,5},{5,3},{7,1},{8,14},{10,12},{12... | collective-permute-start | bytes 196616 | tf_op jit(solution)/shard_map/ppermute | solution.py:516
  46.2 16.0 %collective-permute-start.8 = (f32[256,256]{1,0:T(8,128)S(1)}, f32[256,256]{1,0:T(8,128)S(1)}, u32[]{:S(2)}, u32[]{:S(2)}) collective-permute-start(f32[256,256]{1,0:T(8,128)S(1)} %get-tuple-element.64), channel_id=1, source_target_pairs={{0,1},{1,0},{2,3},{3,2},{4,5},{5,4},{6,7},{7,6},{8,9},{9,8},{10,11... | collective-permute-start | bytes 786440 | tf_op jit(solution)/shard_map/ppermute | solution.py:516
  46.3 15.8 %all-to-all-start.1 = ((f32[32,8,128]{2,1,0:T(8,128)}), f32[32,8,128]{2,1,0:T(8,128)S(1)}, u32[]{:S(2)}, u32[]{:S(2)}) async-start(f32[32,8,128]{2,1,0:T(8,128)} %get-tuple-element.65), calls=%async_computation.1 | async-start | bytes 262144 | tf_op jit(solution)/shard_map/all_to_all | solution.py:541
  52.4 31.5 %collective-permute-start.9 = (bf16[9,128,256]{2,1,0:T(8,128)(2,1)S(1)}, bf16[9,128,256]{2,1,0:T(8,128)(2,1)}, u32[]{:S(2)}, u32[]{:S(2)}) collective-permute-start(bf16[9,128,256]{2,1,0:T(8,128)(2,1)S(1)} %dynamic-slice_convert_fusion.refs_0_), channel_id=1, source_target_pairs={{0,1},{1,0},{2,3},{3,2},{4,5},{5,4},{6,7},{7,6},{8,9},{9,8},{10,11... | collective-permute-start | bytes 1769480 | tf_op jit(solution)/shard_map/ppermute | solution.py:516
  52.7 31.6 %collective-permute-start.10 = (bf16[9,128,256]{2,1,0:T(8,128)(2,1)}, bf16[9,128,256]{2,1,0:T(8,128)(2,1)}, u32[]{:S(2)}, u32[]{:S(2)}) collective-permute-start(bf16[9,128,256]{2,1,0:T(8,128)(2,1)} %collective-permute-done.5.refs_1_), channel_id=1, source_target_pairs={{0,1},{1,0},{2,3},{3,2},{4,5},{5,4},{6,7},{7,6},{8,9},{9,8},{10,11... | collective-permute-start | bytes 1769480 | tf_op jit(solution)/shard_map/ppermute | solution.py:516
  53.0 32.4 %collective-permute-start.11 = (bf16[9,128,256]{2,1,0:T(8,128)(2,1)}, bf16[9,128,256]{2,1,0:T(8,128)(2,1)}, u32[]{:S(2)}, u32[]{:S(2)}) collective-permute-start(bf16[9,128,256]{2,1,0:T(8,128)(2,1)} %collective-permute-done.6.refs_2_), channel_id=1, source_target_pairs={{0,1},{1,0},{2,3},{3,2},{4,5},{5,4},{6,7},{7,6},{8,9},{9,8},{10,11... | collective-permute-start | bytes 1769480 | tf_op jit(solution)/shard_map/ppermute | solution.py:516
  53.2 34.2 %collective-permute-start.12 = (bf16[9,128,256]{2,1,0:T(8,128)(2,1)}, bf16[9,128,256]{2,1,0:T(8,128)(2,1)}, u32[]{:S(2)}, u32[]{:S(2)}) collective-permute-start(bf16[9,128,256]{2,1,0:T(8,128)(2,1)} %collective-permute-done.7.refs_3_), channel_id=1, source_target_pairs={{0,1},{1,0},{2,3},{3,2},{4,5},{5,4},{6,7},{7,6},{8,9},{9,8},{10,11... | collective-permute-start | bytes 1769480 | tf_op jit(solution)/shard_map/ppermute | solution.py:516
  67.1 12.8 %all-to-all-start.3 = ((f32[32,8,128]{2,1,0:T(8,128)}), f32[32,8,128]{2,1,0:T(8,128)S(1)}, u32[]{:S(2)}, u32[]{:S(2)}) async-start(f32[32,8,128]{2,1,0:T(8,128)} %get-tuple-element.71), calls=%async_computation.3 | async-start | bytes 262144 | tf_op jit(solution)/shard_map/all_to_all | solution.py:541
  77.1 23.2 %collective-permute-start.30 = (bf16[256,128]{1,0:T(8,128)(2,1)}, bf16[256,128]{1,0:T(8,128)(2,1)}, u32[]{:S(2)}, u32[]{:S(2)}) collective-permute-start(bf16[256,128]{1,0:T(8,128)(2,1)} %get-tuple-element.182), channel_id=1, source_target_pairs={{0,2},{2,0},{4,6},{6,4},{1,3},{3,1},{5,7},{7,5},{8,10},{10,8},{12,... | collective-permute-start | bytes 196616 | tf_op jit(solution)/shard_map/ppermute | solution.py:516
  83.9 21.6 %collective-permute-start.27 = (bf16[512,256]{1,0:T(8,128)(2,1)}, bf16[512,256]{1,0:T(8,128)(2,1)}, u32[]{:S(2)}, u32[]{:S(2)}) collective-permute-start(bf16[512,256]{1,0:T(8,128)(2,1)} %get-tuple-element.77.refs_0_), channel_id=1, source_target_pairs={{0,2},{2,0},{4,6},{6,4},{1,3},{3,1},{5,7},{7,5},{8,10},{10,8},{12,... | collective-permute-start | bytes 786440 | tf_op jit(solution)/shard_map/ppermute | solution.py:516
  84.4 21.2 %collective-permute-start.28 = (bf16[512,256]{1,0:T(8,128)(2,1)}, bf16[512,256]{1,0:T(8,128)(2,1)}, u32[]{:S(2)}, u32[]{:S(2)}) collective-permute-start(bf16[512,256]{1,0:T(8,128)(2,1)} %get-tuple-element.77.refs_0_), channel_id=1, source_target_pairs={{0,4},{2,6},{4,0},{6,2},{1,5},{3,7},{5,1},{7,3},{8,12},{10,14},{12... | collective-permute-start | bytes 786440 | tf_op jit(solution)/shard_map/ppermute | solution.py:516
  85.3 20.2 %collective-permute-start.29 = (bf16[512,256]{1,0:T(8,128)(2,1)}, bf16[512,256]{1,0:T(8,128)(2,1)}, u32[]{:S(2)}, u32[]{:S(2)}) collective-permute-start(bf16[512,256]{1,0:T(8,128)(2,1)} %get-tuple-element.77.refs_0_), channel_id=1, source_target_pairs={{0,6},{2,4},{4,2},{6,0},{1,7},{3,5},{5,3},{7,1},{8,14},{10,12},{12... | collective-permute-start | bytes 786440 | tf_op jit(solution)/shard_map/ppermute | solution.py:516
  92.2 17.5 %all-to-all-start.4 = ((f32[32,8,128]{2,1,0:T(8,128)}), f32[32,8,128]{2,1,0:T(8,128)S(1)}, u32[]{:S(2)}, u32[]{:S(2)}) async-start(f32[32,8,128]{2,1,0:T(8,128)} %copy-done.31), calls=%async_computation.4 | async-start | bytes 262144 | tf_op jit(solution)/shard_map/all_to_all | solution.py:541
  98.7 5.3 %collective-permute-start.31 = (bf16[256,128]{1,0:T(8,128)(2,1)}, bf16[256,128]{1,0:T(8,128)(2,1)S(1)}, u32[]{:S(2)}, u32[]{:S(2)}) collective-permute-start(bf16[256,128]{1,0:T(8,128)(2,1)} %get-tuple-element.181), channel_id=1, source_target_pairs={{0,4},{2,6},{4,0},{6,2},{1,5},{3,7},{5,1},{7,3},{8,12},{10,14},{12... | collective-permute-start | bytes 196616 | tf_op jit(solution)/shard_map/ppermute | solution.py:516
  100.3 5.2 %collective-permute-start.32 = (bf16[256,128]{1,0:T(8,128)(2,1)S(1)}, bf16[256,128]{1,0:T(8,128)(2,1)S(1)}, u32[]{:S(2)}, u32[]{:S(2)}) collective-permute-start(bf16[256,128]{1,0:T(8,128)(2,1)S(1)} %copy-done.48), channel_id=1, source_target_pairs={{0,6},{2,4},{4,2},{6,0},{1,7},{3,5},{5,3},{7,1},{8,14},{10,12},{12... | collective-permute-start | bytes 196616 | tf_op jit(solution)/shard_map/ppermute | solution.py:516
  112.5 5.2 %collective-permute-start.15 = (bf16[256,128]{1,0:T(8,128)(2,1)S(1)}, bf16[256,128]{1,0:T(8,128)(2,1)S(1)}, u32[]{:S(2)}, u32[]{:S(2)}) collective-permute-start(bf16[256,128]{1,0:T(8,128)(2,1)S(1)} %get-tuple-element.184), channel_id=1, source_target_pairs={{0,6},{2,4},{4,2},{6,0},{1,7},{3,5},{5,3},{7,1},{8,14},{10,12},{12... | collective-permute-start | bytes 196616 | tf_op jit(solution)/shard_map/ppermute | solution.py:516
  114.6 13.1 %collective-permute-start.33 = (bf16[576,512]{1,0:T(8,128)(2,1)}, bf16[576,512]{1,0:T(8,128)(2,1)}, u32[]{:S(2)}, u32[]{:S(2)}) collective-permute-start(bf16[576,512]{1,0:T(8,128)(2,1)} %dynamic-slice_bitcast_fusion), channel_id=1, source_target_pairs={{0,1},{1,0},{2,3},{3,2},{4,5},{5,4},{6,7},{7,6},{8,9},{9,8},{10,11... | collective-permute-start | bytes 1769480 | tf_op jit(solution)/shard_map/ppermute | solution.py:516
  121.3 12.3 %collective-permute-start.16 = (bf16[2304,128]{1,0:T(8,128)(2,1)}, bf16[2304,128]{1,0:T(8,128)(2,1)}, u32[]{:S(2)}, u32[]{:S(2)}) collective-permute-start(bf16[2304,128]{1,0:T(8,128)(2,1)} %dynamic-slice_bitcast_fusion.1), channel_id=1, source_target_pairs={{0,1},{1,0},{2,3},{3,2},{4,5},{5,4},{6,7},{7,6},{8,9},{9,8},{10,11... | collective-permute-start | bytes 1769480 | tf_op jit(solution)/shard_map/ppermute | solution.py:516
  123.2 81.2 %all-to-all-start.2 = ((f32[32,16,128]{2,1,0:T(8,128)}), f32[32,16,128]{2,1,0:T(8,128)S(1)}, u32[]{:S(2)}, u32[]{:S(2)}) async-start(f32[32,16,128]{2,1,0:T(8,128)} %bitcast.11), calls=%async_computation.2 | async-start | bytes 524288 | tf_op jit(solution)/shard_map/all_to_all | solution.py:541
  129.1 11.2 %collective-permute-start.36 = (bf16[144,512]{1,0:T(8,128)(2,1)S(1)}, bf16[144,512]{1,0:T(8,128)(2,1)S(1)}, u32[]{:S(2)}, u32[]{:S(2)}) collective-permute-start(bf16[144,512]{1,0:T(8,128)(2,1)S(1)} %get-tuple-element.163), channel_id=1, source_target_pairs={{0,24},{8,16},{16,8},{24,0},{1,25},{9,17},{17,9},{25,1},{2,26},{10... | collective-permute-start | bytes 442376 | tf_op jit(solution)/shard_map/ppermute | solution.py:516
  132.8 23.8 %collective-permute-start.35 = (bf16[144,512]{1,0:T(8,128)(2,1)S(1)}, bf16[144,512]{1,0:T(8,128)(2,1)S(1)}, u32[]{:S(2)}, u32[]{:S(2)}) collective-permute-start(bf16[144,512]{1,0:T(8,128)(2,1)S(1)} %get-tuple-element.164), channel_id=1, source_target_pairs={{0,16},{8,24},{16,0},{24,8},{1,17},{9,25},{17,1},{25,9},{2,18},{10... | collective-permute-start | bytes 442376 | tf_op jit(solution)/shard_map/ppermute | solution.py:516
  132.8 23.8 %collective-permute-start.34 = (bf16[144,512]{1,0:T(8,128)(2,1)S(1)}, bf16[144,512]{1,0:T(8,128)(2,1)S(1)}, u32[]{:S(2)}, u32[]{:S(2)}) collective-permute-start(bf16[144,512]{1,0:T(8,128)(2,1)S(1)} %get-tuple-element.162), channel_id=1, source_target_pairs={{0,8},{8,0},{16,24},{24,16},{1,9},{9,1},{17,25},{25,17},{2,10},{10... | collective-permute-start | bytes 442376 | tf_op jit(solution)/shard_map/ppermute | solution.py:516
  134.8 22.9 %collective-permute-start.19 = (bf16[576,128]{1,0:T(8,128)(2,1)S(1)}, bf16[576,128]{1,0:T(8,128)(2,1)S(1)}, u32[]{:S(2)}, u32[]{:S(2)}) collective-permute-start(bf16[576,128]{1,0:T(8,128)(2,1)S(1)} %get-tuple-element.170), channel_id=1, source_target_pairs={{0,24},{8,16},{16,8},{24,0},{1,25},{9,17},{17,9},{25,1},{2,26},{10... | collective-permute-start | bytes 442376 | tf_op jit(solution)/shard_map/ppermute | solution.py:516
  138.5 30.7 %collective-permute-start.18 = (bf16[576,128]{1,0:T(8,128)(2,1)S(1)}, bf16[576,128]{1,0:T(8,128)(2,1)S(1)}, u32[]{:S(2)}, u32[]{:S(2)}) collective-permute-start(bf16[576,128]{1,0:T(8,128)(2,1)S(1)} %get-tuple-element.171), channel_id=1, source_target_pairs={{0,16},{8,24},{16,0},{24,8},{1,17},{9,25},{17,1},{25,9},{2,18},{10... | collective-permute-start | bytes 442376 | tf_op jit(solution)/shard_map/ppermute | solution.py:516
  140.3 28.9 %collective-permute-start.17 = (bf16[576,128]{1,0:T(8,128)(2,1)S(1)}, bf16[576,128]{1,0:T(8,128)(2,1)S(1)}, u32[]{:S(2)}, u32[]{:S(2)}) collective-permute-start(bf16[576,128]{1,0:T(8,128)(2,1)S(1)} %get-tuple-element.169), channel_id=1, source_target_pairs={{0,8},{8,0},{16,24},{24,16},{1,9},{9,1},{17,25},{25,17},{2,10},{10... | collective-permute-start | bytes 442376 | tf_op jit(solution)/shard_map/ppermute | solution.py:516
  156.7 14.8 %collective-permute-start.39 = (bf16[144,512]{1,0:T(8,128)(2,1)S(1)}, bf16[144,512]{1,0:T(8,128)(2,1)S(1)}, u32[]{:S(2)}, u32[]{:S(2)}) collective-permute-start(bf16[144,512]{1,0:T(8,128)(2,1)S(1)} %fusion.21), channel_id=1, source_target_pairs={{0,24},{8,16},{16,8},{24,0},{1,25},{9,17},{17,9},{25,1},{2,26},{10... | collective-permute-start | bytes 442376 | tf_op jit(solution)/shard_map/ppermute | solution.py:516
  157.8 24.1 %collective-permute-start.38 = (bf16[144,512]{1,0:T(8,128)(2,1)S(1)}, bf16[144,512]{1,0:T(8,128)(2,1)S(1)}, u32[]{:S(2)}, u32[]{:S(2)}) collective-permute-start(bf16[144,512]{1,0:T(8,128)(2,1)S(1)} %fusion.21), channel_id=1, source_target_pairs={{0,16},{8,24},{16,0},{24,8},{1,17},{9,25},{17,1},{25,9},{2,18},{10... | collective-permute-start | bytes 442376 | tf_op jit(solution)/shard_map/ppermute | solution.py:516
  157.8 25.6 %collective-permute-start.37 = (bf16[144,512]{1,0:T(8,128)(2,1)S(1)}, bf16[144,512]{1,0:T(8,128)(2,1)S(1)}, u32[]{:S(2)}, u32[]{:S(2)}) collective-permute-start(bf16[144,512]{1,0:T(8,128)(2,1)S(1)} %fusion.21), channel_id=1, source_target_pairs={{0,8},{8,0},{16,24},{24,16},{1,9},{9,1},{17,25},{25,17},{2,10},{10... | collective-permute-start | bytes 442376 | tf_op jit(solution)/shard_map/ppermute | solution.py:516
  170.3 19.8 %collective-permute-start.50 = (bf16[576,128]{1,0:T(8,128)(2,1)S(1)}, bf16[576,128]{1,0:T(8,128)(2,1)S(1)}, u32[]{:S(2)}, u32[]{:S(2)}) collective-permute-start(bf16[576,128]{1,0:T(8,128)(2,1)S(1)} %get-tuple-element.152), channel_id=1, source_target_pairs={{0,24},{8,16},{16,8},{24,0},{1,25},{9,17},{17,9},{25,1},{2,26},{10... | collective-permute-start | bytes 442376 | tf_op jit(solution)/shard_map/ppermute | solution.py:516
  171.5 18.7 %collective-permute-start.49 = (bf16[576,128]{1,0:T(8,128)(2,1)S(1)}, bf16[576,128]{1,0:T(8,128)(2,1)S(1)}, u32[]{:S(2)}, u32[]{:S(2)}) collective-permute-start(bf16[576,128]{1,0:T(8,128)(2,1)S(1)} %get-tuple-element.152), channel_id=1, source_target_pairs={{0,16},{8,24},{16,0},{24,8},{1,17},{9,25},{17,1},{25,9},{2,18},{10... | collective-permute-start | bytes 442376 | tf_op jit(solution)/shard_map/ppermute | solution.py:516
  171.5 13.5 %collective-permute-start.22 = (bf16[576,128]{1,0:T(8,128)(2,1)S(1)}, bf16[576,128]{1,0:T(8,128)(2,1)S(1)}, u32[]{:S(2)}, u32[]{:S(2)}) collective-permute-start(bf16[576,128]{1,0:T(8,128)(2,1)S(1)} %get-tuple-element.153), channel_id=1, source_target_pairs={{0,6},{2,4},{4,2},{6,0},{1,7},{3,5},{5,3},{7,1},{8,14},{10,12},{12... | collective-permute-start | bytes 442376 | tf_op jit(solution)/shard_map/ppermute | solution.py:516
  185.0 8.3 %collective-permute-start.48 = (bf16[576,128]{1,0:T(8,128)(2,1)S(1)}, bf16[576,128]{1,0:T(8,128)(2,1)S(1)}, u32[]{:S(2)}, u32[]{:S(2)}) collective-permute-start(bf16[576,128]{1,0:T(8,128)(2,1)S(1)} %get-tuple-element.152), channel_id=1, source_target_pairs={{0,8},{8,0},{16,24},{24,16},{1,9},{9,1},{17,25},{25,17},{2,10},{10... | collective-permute-start | bytes 442376 | tf_op jit(solution)/shard_map/ppermute | solution.py:516
  187.0 18.1 %collective-permute-start.40 = (bf16[576,512]{1,0:T(8,128)(2,1)}, bf16[576,512]{1,0:T(8,128)(2,1)}, u32[]{:S(2)}, u32[]{:S(2)}) collective-permute-start(bf16[576,512]{1,0:T(8,128)(2,1)} %bitcast.67), channel_id=1, source_target_pairs={{0,1},{1,0},{2,3},{3,2},{4,5},{5,4},{6,7},{7,6},{8,9},{9,8},{10,11... | collective-permute-start | bytes 1769480 | tf_op jit(solution)/shard_map/ppermute | solution.py:516
  188.8 8.7 %collective-permute-start.25 = (bf16[576,128]{1,0:T(8,128)(2,1)S(1)}, bf16[576,128]{1,0:T(8,128)(2,1)S(1)}, u32[]{:S(2)}, u32[]{:S(2)}) collective-permute-start(bf16[576,128]{1,0:T(8,128)(2,1)S(1)} %convolution_convert_fusion), channel_id=1, source_target_pairs={{0,24},{8,16},{16,8},{24,0},{1,25},{9,17},{17,9},{25,1},{2,26},{10... | collective-permute-start | bytes 442376 | tf_op jit(solution)/shard_map/ppermute | solution.py:516
  190.1 13.5 %collective-permute-start.24 = (bf16[576,128]{1,0:T(8,128)(2,1)S(1)}, bf16[576,128]{1,0:T(8,128)(2,1)S(1)}, u32[]{:S(2)}, u32[]{:S(2)}) collective-permute-start(bf16[576,128]{1,0:T(8,128)(2,1)S(1)} %convolution_convert_fusion), channel_id=1, source_target_pairs={{0,16},{8,24},{16,0},{24,8},{1,17},{9,25},{17,1},{25,9},{2,18},{10... | collective-permute-start | bytes 442376 | tf_op jit(solution)/shard_map/ppermute | solution.py:516
  190.1 13.5 %collective-permute-start.23 = (bf16[576,128]{1,0:T(8,128)(2,1)S(1)}, bf16[576,128]{1,0:T(8,128)(2,1)S(1)}, u32[]{:S(2)}, u32[]{:S(2)}) collective-permute-start(bf16[576,128]{1,0:T(8,128)(2,1)S(1)} %convolution_convert_fusion), channel_id=1, source_target_pairs={{0,8},{8,0},{16,24},{24,16},{1,9},{9,1},{17,25},{25,17},{2,10},{10... | collective-permute-start | bytes 442376 | tf_op jit(solution)/shard_map/ppermute | solution.py:516
  193.5 21.4 %collective-permute-start.51 = (bf16[2304,128]{1,0:T(8,128)(2,1)S(1)}, bf16[2304,128]{1,0:T(8,128)(2,1)}, u32[]{:S(2)}, u32[]{:S(2)}) collective-permute-start(bf16[2304,128]{1,0:T(8,128)(2,1)S(1)} %bitcast.154), channel_id=1, source_target_pairs={{0,1},{1,0},{2,3},{3,2},{4,5},{5,4},{6,7},{7,6},{8,9},{9,8},{10,11... | collective-permute-start | bytes 1769480 | tf_op jit(solution)/shard_map/ppermute | solution.py:516
  203.8 11.1 %collective-permute-start.26 = (bf16[2304,128]{1,0:T(8,128)(2,1)S(1)}, bf16[2304,128]{1,0:T(8,128)(2,1)}, u32[]{:S(2)}, u32[]{:S(2)}) collective-permute-start(bf16[2304,128]{1,0:T(8,128)(2,1)S(1)} %bitcast.156), channel_id=1, source_target_pairs={{0,1},{1,0},{2,3},{3,2},{4,5},{5,4},{6,7},{7,6},{8,9},{9,8},{10,11... | collective-permute-start | bytes 1769480 | tf_op jit(solution)/shard_map/ppermute | solution.py:516
  211.4 16.2 %collective-permute-start.41 = (bf16[1152,256]{1,0:T(8,128)(2,1)S(1)}, bf16[1152,256]{1,0:T(8,128)(2,1)S(1)}, u32[]{:S(2)}, u32[]{:S(2)}) collective-permute-start(bf16[1152,256]{1,0:T(8,128)(2,1)S(1)} %get-tuple-element.78.refs_0_), channel_id=1, source_target_pairs={{0,2},{2,0},{4,6},{6,4},{1,3},{3,1},{5,7},{7,5},{8,10},{10,8},{12,... | collective-permute-start | bytes 1769480 | tf_op jit(solution)/shard_map/ppermute | solution.py:516
  212.0 27.7 %collective-permute-start.42 = (bf16[1152,256]{1,0:T(8,128)(2,1)S(1)}, bf16[1152,256]{1,0:T(8,128)(2,1)S(1)}, u32[]{:S(2)}, u32[]{:S(2)}) collective-permute-start(bf16[1152,256]{1,0:T(8,128)(2,1)S(1)} %get-tuple-element.78.refs_0_), channel_id=1, source_target_pairs={{0,4},{2,6},{4,0},{6,2},{1,5},{3,7},{5,1},{7,3},{8,12},{10,14},{12... | collective-permute-start | bytes 1769480 | tf_op jit(solution)/shard_map/ppermute | solution.py:516
  212.6 27.0 %collective-permute-start.43 = (bf16[1152,256]{1,0:T(8,128)(2,1)S(1)}, bf16[1152,256]{1,0:T(8,128)(2,1)S(1)}, u32[]{:S(2)}, u32[]{:S(2)}) collective-permute-start(bf16[1152,256]{1,0:T(8,128)(2,1)S(1)} %get-tuple-element.78.refs_0_), channel_id=1, source_target_pairs={{0,6},{2,4},{4,2},{6,0},{1,7},{3,5},{5,3},{7,1},{8,14},{10,12},{12... | collective-permute-start | bytes 1769480 | tf_op jit(solution)/shard_map/ppermute | solution.py:516
  245.2 5.4 %collective-permute-start.45 = (f32[8,128]{1,0:T(8,128)S(1)}, f32[8,128]{1,0:T(8,128)S(1)}, u32[]{:S(2)}, u32[]{:S(2)}) collective-permute-start(f32[8,128]{1,0:T(8,128)S(1)} %get-tuple-element.81.refs_0_), channel_id=1, source_target_pairs={{0,2},{2,0},{4,6},{6,4},{1,3},{3,1},{5,7},{7,5},{8,10},{10,8},{12,... | collective-permute-start | bytes 12296 | tf_op jit(solution)/shard_map/ppermute | solution.py:516
  (64 other events, 411.0 us)

commit v3 on v2

v3 whole, which is shorter than its diff:
```python
import functools
import math

import jax
import jax.numpy as jnp
from jax import lax
from jax.experimental import pallas as pl
from jax.experimental.pallas import tpu as pltpu
from jax.sharding import PartitionSpec as P

CLASSES = 10
SIDE = 4
PIX = 16
TAPS = 9
STEP = 10
LANES = 128

EPS_NORM = 1e-05
SCALE_DECAY = 0.95
DAMPING = 0.001
CLIP_NORM = 1.0
LEARN_RATE = 0.01
BETA_ONE = 0.9
BETA_TWO = 0.999
ADAM_EPS = 1e-08
WEIGHT_DECAY = 0.01
SMOOTH = 0.1
OFFSETS = [(row_step, col_step) for row_step in (-1, 0, 1) for col_step in (-1, 0, 1)]
EVERY = ("dp", "cout", "cin")
BF = jnp.bfloat16
F32 = jnp.float32
PRECISE = lax.Precision.HIGHEST
NN = (((1,), (0,)), ((), ()))
NT = (((1,), (1,)), ((), ()))
TN = (((0,), (0,)), ((), ()))


def matmul(left, right, dims=NN, precision=None):
    return lax.dot_general(
        left, right, dims, precision=precision, preferred_element_type=F32
    )


def runs(row_step, col_step, count):
    low, high = max(0, -col_step), min(SIDE, SIDE - col_step)
    found = []
    for row in range(max(0, -row_step), min(SIDE, SIDE - row_step)):
        to_row = (row * SIDE + low) * count
        from_row = ((row + row_step) * SIDE + low + col_step) * count
        length = (high - low) * count
        if found and found[-1][0] + found[-1][2] == to_row and found[-1][1] + found[-1][2] == from_row:
            found[-1] = (found[-1][0], found[-1][1], found[-1][2] + length)
        else:
            found.append((to_row, from_row, length))
    return found


class Late:
    def __init__(self, ref, copy):
        self.ref, self.copy, self.shape = ref, copy, ref.shape
        copy.start()

    def settle(self):
        if self.copy is not None:
            self.copy.wait()
        self.copy = None

    def __getitem__(self, index):
        self.settle()
        return self.ref[index]


class Result:
    def __init__(self, ref, copy):
        self.ref, self.copy, self.shape, self.sent = ref, copy, ref.shape, False

    def __getitem__(self, index):
        return self.ref[index]

    def __setitem__(self, index, values):
        self.ref[index] = values

    def send(self):
        if not self.sent:
            self.copy.start()
        self.sent = True


def call(kernel, outs, args, scratch=(), scalars=1, near=(), raw=(), near_out=(), flops=0, room=60):
    n_in, n_out = len(args), len(outs)
    copied = [at for at in range(scalars, n_in) if at not in near and at not in raw]
    copied_out = [at for at in range(n_out) if at not in near_out]

    def body(*refs):
        ins, results = list(refs[:n_in]), list(refs[n_in : n_in + n_out])
        rest = refs[n_in + n_out :]
        held, held_out = rest[: len(copied)], rest[len(copied) : len(copied) + len(copied_out)]
        own, arrived = rest[len(copied) + len(copied_out) : -1], rest[-1]
        for nth, at in enumerate(copied):
            ins[at] = Late(held[nth], pltpu.make_async_copy(ins[at], held[nth], arrived.at[nth]))
        for nth, at in enumerate(copied_out):
            copy = pltpu.make_async_copy(held_out[nth], results[at], arrived.at[len(copied) + nth])
            results[at] = Result(held_out[nth], copy)
        kernel(*ins, *results, *own)
        for at in copied:
            ins[at].settle()
        for at in copied_out:
            results[at].send()
        for at in copied_out:
            results[at].copy.wait()

    specs = [pl.BlockSpec(memory_space=pltpu.SMEM)] * scalars
    specs += [
        pl.BlockSpec(memory_space=pltpu.VMEM if at in near else pltpu.HBM) for at in range(scalars, n_in)
    ]
    moved = sum(math.prod(a.shape) * a.dtype.itemsize for a in list(args) + list(outs))
    return pl.pallas_call(
        body,
        out_shape=list(outs),
        in_specs=specs,
        out_specs=[
            pl.BlockSpec(memory_space=pltpu.VMEM if at in near_out else pltpu.HBM) for at in range(n_out)
        ],
        scratch_shapes=[pltpu.VMEM(args[at].shape, args[at].dtype) for at in copied]
        + [pltpu.VMEM(outs[at].shape, outs[at].dtype) for at in copied_out]
        + list(scratch)
        + [pltpu.SemaphoreType.DMA((max(1, len(copied) + len(copied_out)),))],
        compiler_params=pltpu.CompilerParams(vmem_limit_bytes=room * 1024 * 1024),
        cost_estimate=pl.CostEstimate(flops=flops, bytes_accessed=moved, transcendentals=0),
    )(*args)


def shape(dims, dtype):
    return jax.ShapeDtypeStruct(dims, dtype)


def gelu_parts(values):
    rate = math.sqrt(2.0 / math.pi)
    bend = jnp.tanh(rate * (values + 0.044715 * values * values * values))
    share = 0.5 * (1.0 + bend)
    slope = share + 0.5 * values * (1.0 - bend * bend) * rate * (1.0 + 0.134145 * values * values)
    return values * share, slope


def fill_mask(masks_ref, mask_ref):
    count = masks_ref.shape[1]
    same = lax.broadcasted_iota(jnp.int32, (count, count), 0) == lax.broadcasted_iota(
        jnp.int32, (count, count), 1
    )
    for pixel in range(PIX):
        row = masks_ref[pixel : pixel + 1, :].astype(F32)
        column = jnp.sum(jnp.where(same, row, 0.0), axis=1, keepdims=True)
        mask_ref[pixel * count : (pixel + 1) * count, :] = jnp.broadcast_to(column, (count, LANES))


def fill_inputs(images_ref, mask_ref, inputs_ref):
    low = mask_ref[...].astype(BF)
    for lane in range(0, images_ref.shape[1], LANES):
        inputs_ref[:, lane : lane + LANES] = images_ref[:, lane : lane + LANES] * low


def first_kernel(
    groups, place_ref, images_ref, masks_ref, weight_ref, params_ref, head_ref,
    send_refs, stats_ref, own_mask_ref, mask_ref, inputs_ref, low_ref, sum_ref, wide_ref, arrived,
):
    count = masks_ref.shape[1]
    part = count // groups
    me = place_ref[0]
    copies = [
        pltpu.make_async_copy(weight_ref.at[at : at + 3], wide_ref.at[at : at + 3], arrived.at[at // 3])
        for at in range(0, TAPS, 3)
    ]
    for copy in copies:
        copy.start()
    fill_mask(masks_ref, mask_ref)
    fill_inputs(images_ref, mask_ref, inputs_ref)
    for tap in range(TAPS):
        if tap % 3 == 0:
            copies[tap // 3].wait()
        low_ref[:, tap * LANES : (tap + 1) * LANES] = wide_ref[tap].astype(BF)
    sum_ref[...] = jnp.zeros_like(sum_ref)
    for tap in range(0, TAPS, 2):
        taps = min(2, TAPS - tap)
        product = matmul(inputs_ref[...], low_ref[:, tap * LANES : (tap + taps) * LANES])
        for nth in range(taps):
            for to_row, from_row, length in runs(*OFFSETS[tap + nth], count):
                sum_ref[to_row : to_row + length, :] += product[
                    from_row : from_row + length, nth * LANES : (nth + 1) * LANES
                ]
    mask = mask_ref[...]
    total = sum_ref[...]
    masked = total * mask
    tile = jnp.concatenate(
        [
            jnp.sum(masked, axis=0, keepdims=True),
            jnp.sum(masked * total, axis=0, keepdims=True),
            jnp.sum(mask, axis=0, keepdims=True),
            params_ref[0:2, :],
            jnp.zeros((3, LANES), F32),
        ],
        axis=0,
    )
    stats_ref[...] = jnp.broadcast_to(tile[None], stats_ref.shape)
    head = jnp.concatenate([head_ref[...], jnp.zeros((16 - CLASSES, LANES), F32)], axis=0).astype(BF)
    for step, send_ref in enumerate(send_refs):
        send_ref[PIX * part : PIX * part + 16, :] = head
        for pixel in range(PIX):
            base = pl.multiple_of(pixel * count + (me ^ step) * part, part)
            send_ref[pixel * part : (pixel + 1) * part, :] = sum_ref[pl.ds(base, part), :].astype(BF)
    for pixel in range(PIX):
        own = pl.multiple_of(pixel * count + me * part, part)
        own_mask_ref[pixel * part : (pixel + 1) * part, :] = mask_ref[pl.ds(own, part), :]


def first_norm_kernel(sizes, place_ref, slot_refs, got_ref, mask_ref, hidden_ref, first_ref, norm_ref, head_ref):
    rows = mask_ref.shape[0]
    count_dp, groups, count_cin = sizes
    me = place_ref[0]
    tiles = []
    for group in range(groups):
        total = None
        for far in range(count_dp):
            for near in range(count_cin):
                tile = got_ref[(far * groups + group) * count_cin + near]
                total = tile if total is None else total + tile
        tiles.append((total, got_ref[group * count_cin]))
    kept = tiles[0][0][2:3, :]
    for group, (total, single) in enumerate(tiles):
        lanes = slice(group * LANES, (group + 1) * LANES)
        mean = total[0:1, :] / kept
        norm_ref[0:1, lanes] = mean
        norm_ref[1:2, lanes] = lax.rsqrt(total[1:2, :] / kept - mean * mean + EPS_NORM)
        norm_ref[2:4, lanes] = single[3:5, :]
        norm_ref[4:5, lanes] = kept
        norm_ref[5:8, lanes] = jnp.zeros((3, LANES), F32)
    for step, slot_ref in enumerate(slot_refs):
        lanes = pl.ds(pl.multiple_of((me ^ step) * LANES, LANES), LANES)
        head_ref[:, lanes] = slot_ref[rows : rows + 16, :]
        low = slot_ref[0:rows, :]
        scaled = (low.astype(F32) - norm_ref[0:1, lanes]) * norm_ref[1:2, lanes]
        value, _ = gelu_parts(norm_ref[2:3, lanes] * scaled + norm_ref[3:4, lanes])
        hidden_ref[:, lanes] = (value * mask_ref[...]).astype(BF)
        first_ref[:, lanes] = low


def second_kernel(
    place_ref, own_ref, other_ref, own_mask_ref, other_mask_ref, params_ref, basis_ref, slot_refs,
    mine_ref, theirs_ref, stats_ref, left_refs, wide_ref, inputs_ref, weight_ref, sum_ref, arrived,
):
    me = place_ref[0]
    rows = own_ref.shape[0]
    part = rows // PIX
    depth, half = slot_refs[0].shape[1:]
    copies = []
    for step, slot_ref in enumerate(slot_refs):
        span = pl.ds(pl.multiple_of((me ^ step) * depth, depth), depth)
        copies.append(pltpu.make_async_copy(slot_ref, weight_ref.at[:, span, :], arrived.at[step]))
        copies[-1].start()
    inputs_ref[0:rows, :] = own_ref[...]
    wide_ref[...] = matmul(own_ref[...], basis_ref[...])
    send_columns(me, wide_ref, left_refs)
    for left_ref in left_refs:
        left_ref.send()
    inputs_ref[rows : 2 * rows, :] = other_ref[...]
    sum_ref[...] = jnp.zeros_like(sum_ref)
    for copy in copies:
        copy.wait()
    for tap in range(TAPS):
        product = matmul(inputs_ref[...], weight_ref[tap])
        for to_row, from_row, length in runs(*OFFSETS[tap], part):
            for base in (0, rows):
                sum_ref[base + to_row : base + to_row + length, :] += product[
                    base + from_row : base + from_row + length, :
                ]
    mine_ref[...] = sum_ref[0:rows, :]
    theirs_ref[...] = sum_ref[rows : 2 * rows, :]
    lines = [[], []]
    for lane in range(0, half, LANES):
        first = square = None
        for base, mask_ref in ((0, own_mask_ref), (rows, other_mask_ref)):
            total = sum_ref[base : base + rows, lane : lane + LANES]
            masked = total * mask_ref[...]
            first_part = jnp.sum(masked, axis=0, keepdims=True)
            square_part = jnp.sum(masked * total, axis=0, keepdims=True)
            first = first_part if first is None else first + first_part
            square = square_part if square is None else square + square_part
        lines[0].append(first)
        lines[1].append(square)
    spare = 8 - 2 * (half // LANES) - 2
    tile = jnp.concatenate(
        lines[0] + lines[1] + [params_ref[2:4, :], jnp.zeros((spare, LANES), F32)], axis=0
    )
    stats_ref[...] = jnp.broadcast_to(tile[None], stats_ref.shape)


def head_kernel(
    sizes, place_ref, mine_ref, got_ref_rows, got_ref, norm_first_ref, mask_ref, head_ref, bias_ref, labels_ref,
    wide_ref, norm_ref, dz_ref, sums_ref, head_out_ref, slope_ref, pooled_ref, weight_ref,
):
    count_dp, groups, count_cin = sizes
    side = place_ref[1]
    rows, half = mine_ref.shape
    part = rows // PIX
    blocks = half // LANES
    wide_ref[:, pl.ds(pl.multiple_of(side * half, half), half)] = mine_ref[...]
    wide_ref[:, pl.ds(pl.multiple_of((1 - side) * half, half), half)] = got_ref_rows[...]
    totals = [None, None]
    for source in range(count_dp * groups * count_cin):
        which = source % count_cin % 2
        tile = got_ref[source]
        totals[which] = tile if totals[which] is None else totals[which] + tile
    kept = norm_first_ref[4:5, 0:LANES]
    mask = mask_ref[...]
    for group in range(groups):
        lanes = slice(group * LANES, (group + 1) * LANES)
        total, line = totals[group // blocks], group % blocks
        mean = total[line : line + 1, :] / kept
        rstd = lax.rsqrt(total[blocks + line : blocks + line + 1, :] / kept - mean * mean + EPS_NORM)
        single = got_ref[group * count_cin]
        gain = single[2 * blocks : 2 * blocks + 1, :]
        shift = single[2 * blocks + 1 : 2 * blocks + 2, :]
        norm_ref[0:1, lanes] = mean
        norm_ref[1:2, lanes] = rstd
        norm_ref[2:3, lanes] = gain
        norm_ref[3:4, lanes] = shift
        norm_ref[4:8, lanes] = jnp.broadcast_to(kept, (4, LANES))
        value, slope = gelu_parts(gain * ((wide_ref[:, lanes] - mean) * rstd) + shift)
        slope_ref[:, lanes] = slope * mask * (1.0 / PIX)
        pooled_ref[:, lanes] = jnp.sum((value * mask).reshape(PIX, part, LANES), axis=0) * (1.0 / PIX)
    wide_ref.send()
    norm_ref.send()
    weight_ref[0:16, :] = head_ref[...]
    weight_ref[16:LANES, :] = jnp.zeros((LANES - 16, weight_ref.shape[1]), BF)
    pooled = pooled_ref[...].astype(BF)
    head = weight_ref[...]
    class_index = lax.broadcasted_iota(jnp.int32, (part, LANES), 1)
    logits = matmul(pooled, head, NT) + bias_ref[...]
    logits = jnp.where(class_index < CLASSES, logits, -1e30)
    logits = logits - jnp.max(logits, axis=1, keepdims=True)
    log_probs = logits - jnp.log(jnp.sum(jnp.exp(logits), axis=1, keepdims=True))
    wanted = jnp.where(class_index == labels_ref[...], 1.0 - SMOOTH, 0.0) + SMOOTH / CLASSES
    wanted = jnp.where(class_index < CLASSES, wanted, 0.0)
    loss = -jnp.sum(jnp.sum(wanted * log_probs, axis=1, keepdims=True), axis=0, keepdims=True)
    logit_grad = jnp.exp(log_probs) - wanted
    head_grad = matmul(logit_grad, pooled.astype(F32), TN, PRECISE)
    pooled_grad = matmul(logit_grad, head.astype(F32), NN, PRECISE)
    extra = jnp.sum(logit_grad, axis=0, keepdims=True)
    extra = jnp.where(class_index[0:1, :] == CLASSES, loss, extra)
    line = lax.broadcasted_iota(jnp.int32, (16, LANES), 0)
    gains, shifts = [], []
    for group in range(groups):
        lanes = slice(group * LANES, (group + 1) * LANES)
        head_out_ref[group] = jnp.where(line == CLASSES, extra, head_grad[0:16, lanes])
        spread = jnp.broadcast_to(pooled_grad[:, lanes][None], (PIX, part, LANES)).reshape(rows, LANES)
        dz = slope_ref[:, lanes] * spread
        dz_ref[:, lanes] = dz
        scaled = (wide_ref[:, lanes] - norm_ref[0:1, lanes]) * norm_ref[1:2, lanes]
        gains.append(jnp.sum(dz * scaled, axis=0, keepdims=True))
        shifts.append(jnp.sum(dz, axis=0, keepdims=True))
    sums_ref[...] = jnp.broadcast_to(jnp.concatenate(gains + shifts, axis=0)[None], sums_ref.shape)


def total_of(got_ref):
    total = got_ref[0]
    for source in range(1, got_ref.shape[0]):
        total = total + got_ref[source]
    return total


def norm_back(values, dz, norm, mask, gain_grad, shift_grad):
    scaled = (values - norm[0:1, :]) * norm[1:2, :]
    gain = norm[2:3, :]
    return norm[1:2, :] * (
        gain * dz - mask * (gain / norm[4:5, :]) * (shift_grad + scaled * gain_grad)
    )


def second_back_kernel(
    place_ref, dz_ref, wide_ref, norm_ref, got_ref, mask_ref, basis_ref, first_ref, norm_first_ref, head_ref, near_refs, far_refs,
    right_ref, sums_out_ref, dz_first_ref, sums_ref, grad_ref, weight_ref, sum_ref, arrived,
):
    me, side = place_ref[0], place_ref[1]
    depth, half = near_refs[0].shape[1:]
    copies = []
    for refs, at in ((near_refs, side), (far_refs, 1 - side)):
        lanes = pl.ds(pl.multiple_of(at * half, half), half)
        for step, slot_ref in enumerate(refs):
            span = pl.ds(pl.multiple_of((me ^ step) * depth, depth), depth)
            copies.append(
                pltpu.make_async_copy(slot_ref, weight_ref.at[:, span, lanes], arrived.at[len(copies)])
            )
            copies[-1].start()
    total = total_of(got_ref)
    sums_out_ref[...] = total
    groups = total.shape[0] // 2
    mask = mask_ref[...]
    for group in range(groups):
        lanes = slice(group * LANES, (group + 1) * LANES)
        grad_ref[:, lanes] = norm_back(
            wide_ref[:, lanes], dz_ref[:, lanes], norm_ref[:, lanes], mask,
            total[group : group + 1, :], total[groups + group : groups + group + 1, :],
        ).astype(BF)
    right_ref[...] = jnp.transpose(matmul(grad_ref[...], basis_ref[...])).astype(BF)
    right_ref.send()
    sums_out_ref.send()
    for copy in copies:
        copy.wait()
    rows, channels = grad_ref.shape
    part = rows // PIX
    sum_ref[...] = jnp.zeros_like(sum_ref)
    for tap in range(TAPS):
        product = matmul(grad_ref[...], weight_ref[tap], NT)
        row_step, col_step = OFFSETS[tap]
        for to_row, from_row, length in runs(-row_step, -col_step, part):
            sum_ref[to_row : to_row + length, :] += product[from_row : from_row + length, :]
    gains, shifts = [], []
    for lane in range(0, channels, LANES):
        lanes = slice(lane, lane + LANES)
        norm = norm_first_ref[:, lanes]
        scaled = (first_ref[:, lanes].astype(F32) - norm[0:1, :]) * norm[1:2, :]
        _, slope = gelu_parts(norm[2:3, :] * scaled + norm[3:4, :])
        dz = slope * mask * sum_ref[:, lanes]
        dz_first_ref[:, lanes] = dz
        gains.append(jnp.sum(dz * scaled, axis=0, keepdims=True))
        shifts.append(jnp.sum(dz, axis=0, keepdims=True))
    dz_first_ref.send()
    count_dp, _, count_cin = sums_ref.shape[:3]
    for group in range(groups):
        tile = jnp.concatenate(gains + shifts + [head_ref[group], jnp.zeros((8, LANES), F32)], axis=0)
        tile = tile.astype(BF)
        for far in range(count_dp):
            for near in range(count_cin):
                sums_ref[far, group, near] = tile


def first_back_kernel(
    place_ref, dz_ref, first_ref, norm_ref, got_ref, mask_ref, basis_ref, old_refs,
    send_refs, sums_ref, small_ref, grad_ref, product_ref,
):
    whole = got_ref[0].astype(F32)
    for source in range(1, got_ref.shape[0]):
        whole = whole + got_ref[source].astype(F32)
    total = whole[0:8, :]
    sums_ref[...] = total
    small_ref[...] = jnp.zeros(small_ref.shape, F32)
    small_ref[8:24, :] = whole[8:24, :]
    for at, row in enumerate((24, 28, 32, 48, 64, 65)):
        rows, lanes = old_refs[at].shape
        small_ref[row : row + rows, 0:lanes] = old_refs[at][...]
    groups = total.shape[0] // 2
    for group in range(groups):
        lanes = slice(group * LANES, (group + 1) * LANES)
        grad_ref[:, lanes] = norm_back(
            first_ref[:, lanes].astype(F32), dz_ref[:, lanes], norm_ref[:, lanes], mask_ref[...],
            total[group : group + 1, :], total[groups + group : groups + group + 1, :],
        ).astype(BF)
    product_ref[...] = matmul(grad_ref[...], basis_ref[...])
    send_columns(place_ref[0], product_ref, send_refs)


def send_columns(me, product_ref, send_refs):
    for step, send_ref in enumerate(send_refs):
        lanes = pl.ds(pl.multiple_of((me ^ step) * LANES, LANES), LANES)
        send_ref[...] = product_ref[:, lanes].astype(BF)


def left_first_kernel(place_ref, images_ref, masks_ref, basis_ref, left_ref, mask_ref, inputs_ref, part_ref):
    slots = left_ref.shape[0]
    count = masks_ref.shape[1]
    part = count // slots
    me = place_ref[0]
    fill_mask(masks_ref, mask_ref)
    fill_inputs(images_ref, mask_ref, inputs_ref)
    for step in range(slots):
        for pixel in range(PIX):
            base = pl.multiple_of(pixel * count + (me ^ step) * part, part)
            part_ref[pixel * part : (pixel + 1) * part, :] = inputs_ref[pl.ds(base, part), :]
        left_ref[step] = jnp.transpose(matmul(part_ref[...], basis_ref[...])).astype(BF)


def taps_kernel(sign, big_refs, small_refs, out_ref, left_ref, right_ref):
    rows, width = small_refs[0].shape
    channels = big_refs[0].shape[0]
    part = rows // PIX
    right_ref[...] = jnp.zeros_like(right_ref)
    for slot, (big_ref, small_ref) in enumerate(zip(big_refs, small_refs)):
        base = slot * rows
        left_ref[:, base : base + rows] = big_ref[...]
        for tap, (row_step, col_step) in enumerate(OFFSETS):
            for to_row, from_row, length in runs(sign * row_step, sign * col_step, part):
                right_ref[base + to_row : base + to_row + length, tap * width : (tap + 1) * width] = (
                    small_ref[from_row : from_row + length, :]
                )
    for tap in range(0, TAPS, 2):
        taps = min(2, TAPS - tap)
        product = matmul(left_ref[...], right_ref[:, tap * width : (tap + taps) * width])
        for nth in range(taps):
            out_ref[(tap + nth) * channels : (tap + nth + 1) * channels, :] = product[
                :, nth * width : (nth + 1) * width
            ].astype(BF)


def ratio_kernel(own_refs, scales_ref, coeff_ref, ratio_ref):
    coeff = None
    for ref in own_refs:
        coeff = ref[...].astype(F32) if coeff is None else coeff + ref[...].astype(F32)
    scales = SCALE_DECAY * scales_ref[...] + (1.0 - SCALE_DECAY) * coeff * coeff
    coeff_ref[...] = coeff.astype(BF)
    ratio_ref[...] = (coeff / (scales + DAMPING)).astype(BF)


def middle_kernel(basis_ref, slot_refs, out_ref):
    width = slot_refs[0].shape[1]
    ratio = jnp.concatenate([ref[...] for ref in slot_refs], axis=1)
    out_ref[...] = matmul(ratio, basis_ref[...], NT).astype(BF)


def scales_kernel(turned, coeff_ref, scales_ref, out_ref):
    taps = out_ref.shape[0]
    rows = coeff_ref.shape[0] // taps
    for tap in range(taps):
        coeff = coeff_ref[tap * rows : (tap + 1) * rows, :].astype(F32)
        if turned:
            coeff = jnp.transpose(coeff)
        out_ref[tap] = SCALE_DECAY * scales_ref[tap] + (1.0 - SCALE_DECAY) * coeff * coeff


def add_squares(total, values):
    return total + jnp.sum((values * values).reshape(-1, 8, LANES), axis=0)


def restore_kernel(
    place_ref, basis_in_ref, middle_first_ref, basis_out_ref, middle_second_ref, sums_first_ref, sums_second_ref,
    old_ref, first_ref, second_ref, squares_ref, small_ref, stack_ref,
):
    me = place_ref[0]
    channels = basis_in_ref.shape[0]
    total = jnp.zeros((8, LANES), F32)
    for tap in range(TAPS):
        product = matmul(
            middle_second_ref[tap * channels : (tap + 1) * channels, :], basis_out_ref[...], (((0,), (1,)), ((), ()))
        )
        second_ref[tap] = product.astype(BF)
        for lane in range(0, channels, LANES):
            total = add_squares(total, product[:, lane : lane + LANES])
    for tap in range(TAPS):
        stack_ref[:, tap * LANES : (tap + 1) * LANES] = middle_first_ref[
            tap * channels : (tap + 1) * channels, :
        ]
    for tap in range(0, TAPS, 2):
        taps = min(2, TAPS - tap)
        product = matmul(basis_in_ref[...], stack_ref[:, tap * LANES : (tap + taps) * LANES])
        for nth in range(taps):
            block = product[:, nth * LANES : (nth + 1) * LANES]
            first_ref[tap + nth] = block.astype(BF)
            total = add_squares(total, block)
    groups = sums_first_ref.shape[0] // 2
    row = lax.broadcasted_iota(jnp.int32, (8, LANES), 0)
    mine = (row == me) | (row == me + groups)
    for ref in (sums_first_ref, sums_second_ref):
        total = total + jnp.where(mine, ref[...] * ref[...], 0.0)
    line = lax.broadcasted_iota(jnp.int32, (16, LANES), 0)
    lane = lax.broadcasted_iota(jnp.int32, (16, LANES), 1)
    counted = (line < CLASSES) | ((line == CLASSES) & (lane < CLASSES) & (me == 0))
    head = jnp.where(counted, old_ref[8:24, :], 0.0)
    small_ref[...] = old_ref[...]
    for at, ref in enumerate((sums_first_ref, sums_second_ref)):
        small_ref[2 * at : 2 * at + 1, :] = ref[pl.ds(me, 1), :]
        small_ref[2 * at + 1 : 2 * at + 2, :] = ref[pl.ds(me + groups, 1), :]
    squares_ref[...] = add_squares(total, head)


def update_kernel(
    square_refs, weight_refs, mean_refs, square_moment_refs, grad_refs, small_refs,
    weight_outs, mean_outs, square_outs, small_outs, scalar_outs,
):
    parts = [ref[...] for ref in square_refs]
    while len(parts) > 1:
        parts = [parts[at] + parts[at + 1] for at in range(0, len(parts), 2)]
    total = jnp.sum(jnp.sum(parts[0], axis=1, keepdims=True), axis=0, keepdims=True)
    grad_norm = jnp.sqrt(total)
    factor = CLIP_NORM / jnp.maximum(grad_norm, CLIP_NORM)

    def moments(gradient, mean_old, square_old):
        mean_new = BETA_ONE * mean_old + (1.0 - BETA_ONE) * gradient
        square_new = BETA_TWO * square_old + (1.0 - BETA_TWO) * gradient * gradient
        return mean_new, square_new

    taps = mean_outs[0].shape[0]
    for at in range(len(weight_refs)):
        for nth in range(taps):
            tap = pl.program_id(0) * taps + nth
            gradient = grad_refs[at][tap].astype(F32) * factor
            mean_new, square_new = moments(gradient, mean_refs[at][tap], square_moment_refs[at][tap])
            mean_outs[at][nth] = mean_new
            square_outs[at][nth] = square_new
            square_hat = square_new * (1.0 / (1.0 - BETA_TWO**STEP))
            size = square_hat * lax.rsqrt(square_hat) + ADAM_EPS
            step = mean_new * (LEARN_RATE / (1.0 - BETA_ONE**STEP)) * pl.reciprocal(size, approx=True)
            weight_outs[at][nth] = weight_refs[at][tap] * (1.0 - LEARN_RATE * WEIGHT_DECAY) - step

    @pl.when(pl.program_id(0) == 0)
    def _():
        norm_out, loss_out = scalar_outs
        norm_out[...] = grad_norm
        (small,) = small_refs
        loss_out[...] = small[8 + CLASSES : 9 + CLASSES, CLASSES : CLASSES + 1]
        results = moments(small[0:4, :] * factor, small[24:28, :], small[28:32, :])
        for at in range(2):
            small_outs[at][...] = results[at][0:2, :]
            small_outs[2 + at][...] = results[at][2:4, :]
        results = moments(
            small[8 : 8 + CLASSES, :] * factor, small[32 : 32 + CLASSES, :], small[48 : 48 + CLASSES, :]
        )
        for at in range(2):
            small_outs[4 + at][...] = results[at]
        lanes = slice(0, CLASSES)
        results = moments(small[8 + CLASSES : 9 + CLASSES, lanes] * factor, small[64:65, lanes], small[65:66, lanes])
        for at in range(2):
            small_outs[6 + at][...] = results[at]


def swap(values, axis, step):
    count = lax.axis_size(axis)
    return lax.ppermute(values, axis, [(here, here ^ step) for here in range(count)])


def gathered(values, axis):
    return [values] + [swap(values, axis, step) for step in range(1, lax.axis_size(axis))]


def exchanged(sends, axis):
    return [sends[0]] + [swap(sends[step], axis, step) for step in range(1, len(sends))]


def picked(values, index):
    return lax.dynamic_index_in_dim(values, index, 0, keepdims=False)


def after(values, *others):
    return lax.optimization_barrier((values,) + others)[0]


def tree_sum(slots):
    while len(slots) > 1:
        slots = [slots[at] + slots[at + 1] for at in range(0, len(slots), 2)]
    return slots[0]


def every_device(tiles):
    return lax.all_to_all(tiles, EVERY, 0, 0, tiled=True)


def bits_of(axis):
    return range(lax.axis_size(axis).bit_length() - 1)


def halved(values, axis, bit):
    own = (lax.axis_index(axis) >> bit) & 1
    values = values.reshape(2, -1, values.shape[-1])
    return [picked(values, own), swap(picked(values, 1 - own), axis, 1 << bit)]


def doubled(values, axis, bit):
    own = (lax.axis_index(axis) >> bit) & 1
    other = swap(values, axis, 1 << bit)
    first = jnp.where(own == 0, values, other)
    return jnp.concatenate([first, jnp.where(own == 0, other, values)], axis=0)


def joined(terms):
    return terms[0] if len(terms) == 1 else (terms[0].astype(F32) + terms[1].astype(F32)).astype(BF)


def batch_gather(block, axes=("dp", "cin"), first=()):
    for order in reversed(first):
        block = doubled(block, *order)
    for axis in axes:
        for bit in reversed(bits_of(axis)):
            block = doubled(block, axis, bit)
    return block


def batch_rows(values):
    place = jnp.int32(0)
    for axis in ("cin", "dp"):
        for bit in bits_of(axis):
            place = place * 2 + ((lax.axis_index(axis) >> bit) & 1)
    rows = values.shape[0] // (lax.axis_size("dp") * lax.axis_size("cin"))
    return lax.dynamic_slice_in_dim(values, place * rows, rows, 0)


def local(
    images,
    masks,
    labels,
    w_first,
    w_second,
    norm_params,
    head_w,
    head_b,
    bases,
    scales_first,
    scales_second,
    w_first_mean,
    w_first_square,
    w_second_mean,
    w_second_square,
    norm_mean,
    norm_square,
    head_w_mean,
    head_w_square,
    head_b_mean,
    head_b_square,
):
    me = lax.axis_index("cout")
    side = lax.axis_index("cin") % 2
    place = jnp.stack([me, side]).astype(jnp.int32)
    sizes = tuple(lax.axis_size(name) for name in EVERY)
    groups = sizes[1]
    devices = sizes[0] * sizes[1] * sizes[2]
    channels = w_first.shape[1]
    width = w_first.shape[2]
    half = channels // 2
    count = images.shape[1]
    part = count // groups
    rows = PIX * part
    tile = shape((devices, 8, LANES), F32)
    wide = (rows, channels)
    basis_in_first, basis_out_first = bases[0, 0], bases[0, 1]
    basis_in_second, basis_out_second = bases[1, 0], bases[1, 1]
    bases_all = (basis_in_first, basis_out_first, basis_in_second, basis_out_second)

    piece = lax.dynamic_slice_in_dim(w_second, side * half, half, 2).astype(BF)
    own_labels = lax.dynamic_slice_in_dim(labels, me * part, part, 0)[:, None]
    bias_row = jnp.pad(head_b, (0, LANES - CLASSES))[None]

    flat_images = images.reshape(PIX * count, channels)
    sends = [shape((rows + 16, width), BF)] * groups
    *first_sends, stats, mask = call(
        lambda *refs: first_kernel(groups, *refs[:6], refs[6 : 6 + groups], *refs[6 + groups :]),
        sends + [tile, shape((rows, LANES), F32)],
        [place, flat_images, masks, w_first, norm_params, head_w.T],
        [
            pltpu.VMEM((PIX * count, LANES), F32),
            pltpu.VMEM((PIX * count, channels), BF),
            pltpu.VMEM((channels, TAPS * width), BF),
            pltpu.VMEM((PIX * count, width), F32),
            pltpu.VMEM((TAPS, channels, width), F32),
            pltpu.SemaphoreType.DMA((3,)),
        ],
        near=(1, 2, 4, 5),
        raw=(3,),
        room=56,
        flops=2 * PIX * count * channels * width * TAPS,
    )
    first_slots = exchanged(first_sends, "cout")
    got = every_device(after(stats, *first_slots))
    (left_turned,) = call(
        left_first_kernel,
        [shape((groups, channels, rows), BF)],
        [place, after(flat_images, stats), masks, basis_in_first],
        [
            pltpu.VMEM((PIX * count, LANES), F32),
            pltpu.VMEM((PIX * count, channels), BF),
            pltpu.VMEM((rows, channels), BF),
        ],
        near=(1, 2, 3),
        room=20,
    )
    near_weights = [piece]
    for step in range(1, groups):
        ready = piece if step < groups - 1 else after(piece, *first_slots)
        near_weights.append(swap(ready, "cout", step))
    other_mask = swap(mask, "cin", 1)
    first_mask = after(mask, left_turned, *near_weights[1:-1], *bases_all)
    hidden, first_out, norm_first, head_full = call(
        lambda place_ref, *refs: first_norm_kernel(sizes, place_ref, refs[:groups], *refs[groups:]),
        [shape(wide, BF), shape(wide, BF), shape((8, channels), F32), shape((16, channels), BF)],
        [place, *first_slots, got, first_mask],
        near_out=(0,),
    )
    other_hidden = swap(hidden, "cin", 1)
    mine, theirs, stats, *left_sends = call(
        lambda *refs: second_kernel(
            *refs[:7], refs[7 : 7 + groups], *refs[7 + groups : 10 + groups],
            refs[10 + groups : 10 + 2 * groups], *refs[10 + 2 * groups :],
        ),
        [shape((rows, half), F32), shape((rows, half), F32), tile] + [shape((rows, width), BF)] * groups,
        [place, hidden, other_hidden, mask, other_mask, norm_params, basis_in_second, *near_weights],
        [
            pltpu.VMEM(wide, F32),
            pltpu.VMEM((2 * rows, channels), BF),
            pltpu.VMEM((TAPS, channels, half), BF),
            pltpu.VMEM((2 * rows, half), F32),
            pltpu.SemaphoreType.DMA((groups,)),
        ],
        near=(1, 2),
        raw=tuple(range(7, 7 + groups)),
        flops=4 * rows * channels * half * TAPS,
    )
    from_other = swap(theirs, "cin", 1)
    got = every_device(stats)
    far_weights = [swap(after(slot, mine), "cin", 1) for slot in near_weights]
    left_slots = exchanged(left_sends, "cout")
    head_mask = after(mask, *far_weights)
    second_out, norm_second, dz_second, sums, head_blocks = call(
        functools.partial(head_kernel, sizes),
        [
            shape(wide, F32),
            shape((8, channels), F32),
            shape(wide, F32),
            tile,
            shape((groups, 16, width), F32),
        ],
        [place, mine, from_other, got, norm_first, head_mask, head_full, bias_row, own_labels],
        [
            pltpu.VMEM(wide, F32),
            pltpu.VMEM((part, channels), F32),
            pltpu.VMEM((LANES, channels), BF),
        ],
    )
    got = every_device(sums)
    right_turned, sums_second, dz_first, sums = call(
        lambda *refs: second_back_kernel(
            *refs[:10], refs[10 : 10 + groups], refs[10 + groups : 10 + 2 * groups], *refs[10 + 2 * groups :]
        ),
        [shape((channels, rows), BF), shape((8, LANES), F32), shape(wide, F32), shape(sizes + (32, LANES), BF)],
        [
            place, dz_second, second_out, norm_second, got, after(mask, *left_slots), basis_out_second, first_out, norm_first, head_blocks,
            *near_weights, *far_weights,
        ],
        [
            pltpu.VMEM(wide, BF),
            pltpu.VMEM((TAPS, channels, channels), BF),
            pltpu.VMEM(wide, F32),
            pltpu.SemaphoreType.DMA((2 * groups,)),
        ],
        raw=tuple(range(10, 10 + 2 * groups)),
        flops=2 * rows * channels * channels * TAPS,
    )
    right_slots = gathered(right_turned, "cout")
    def products(sign, big, small, near=()):
        (out,) = call(
            lambda *refs: taps_kernel(sign, refs[:groups], refs[groups : 2 * groups], *refs[2 * groups :]),
            [shape((TAPS * channels, width), BF)],
            [*big, *small],
            [
                pltpu.VMEM((channels, groups * rows), BF),
                pltpu.VMEM((groups * rows, TAPS * width), BF),
            ],
            scalars=0,
            near=near,
            near_out=(0,),
            room=56,
            flops=2 * groups * rows * channels * width * TAPS,
        )
        return out

    got = every_device(sums.reshape(devices, 32, LANES))
    orders = [(axis, bit) for axis in ("cin", "dp") for bit in bits_of(axis)]
    small_old = [norm_mean, norm_square, head_w_mean.T, head_w_square.T, head_b_mean[None], head_b_square[None]]
    *right_sends, sums_first, smalls = call(
        lambda *refs: first_back_kernel(*refs[:7], refs[7:13], refs[13 : 13 + groups], *refs[13 + groups :]),
        [shape((rows, width), BF)] * groups + [shape((8, LANES), F32), shape((72, LANES), F32)],
        [place, dz_first, first_out, norm_first, got, after(mask, *right_slots), basis_out_first, *small_old],
        [pltpu.VMEM(wide, BF), pltpu.VMEM(wide, F32)],
        near_out=tuple(range(groups)),
    )

    def hold(*values):
        def copy_in(*refs):
            arrived = refs[-1]
            copies = [
                pltpu.make_async_copy(refs[at], refs[len(values) + at], arrived.at[at])
                for at in range(len(values))
            ]
            for copy in copies:
                copy.start()
            for copy in copies:
                copy.wait()

        return call(
            lambda *refs: copy_in(*refs),
            [shape(value.shape, value.dtype) for value in values],
            values,
            [pltpu.SemaphoreType.DMA((len(values),))],
            scalars=0,
            raw=tuple(range(len(values))),
            near_out=tuple(range(len(values))),
            room=16,
        )

    def ratio_of(terms, scales_own):
        chunk = shape(scales_own.shape, BF)
        return call(
            lambda *refs: ratio_kernel(refs[: len(terms)], *refs[len(terms) :]),
            [chunk, chunk],
            [*terms, scales_own],
            scalars=0,
            near=tuple(range(len(terms) + 1)),
            near_out=(0, 1),
            room=16,
        )

    def middle_of(ratio, basis):
        slots = gathered(ratio, "cout")
        (out,) = call(
            lambda basis_ref, *refs: middle_kernel(basis_ref, refs[:groups], refs[-1]),
            [shape(ratio.shape, BF)],
            [basis, *slots],
            scalars=0,
            near=tuple(range(groups + 1)),
            near_out=(0,),
            room=16,
        )
        return out

    near_steps = len(bits_of("cin"))
    right_parts = exchanged(right_sends, "cout")
    left_parts = [left_turned[step] for step in range(groups)]
    products_first = products(-1, left_parts, right_parts, tuple(range(groups, 2 * groups)))
    terms_first = [products_first]
    for order in orders[:near_steps]:
        terms_first = halved(joined(terms_first), *order)
    near_first = joined(terms_first)
    products_second = products(1, [after(right_slots[0], near_first)] + right_slots[1:], left_slots)
    terms_first, terms_second = [near_first], [products_second]
    for order in orders[:near_steps]:
        terms_second = halved(joined(terms_second), *order)
    for order in orders[near_steps:-1]:
        terms_first = halved(joined(terms_first), *order)
        terms_second = halved(after(joined(terms_second), *terms_first), *order)
    filler = terms_first[1]
    terms_first = halved(joined(terms_first), *orders[-1])

    def in_slots(values):
        return jnp.concatenate(
            [lax.dynamic_slice_in_dim(values, (me ^ step) * width, width, 1) for step in range(groups)], 1
        )

    def basis_rows(basis):
        return in_slots(lax.dynamic_slice_in_dim(basis, me * width, width, 0))

    scales_turned = batch_rows(
        jnp.swapaxes(after(scales_second, filler), 1, 2).reshape(TAPS * channels, width)
    )
    scales_chunk = batch_rows(after(scales_first, filler).reshape(TAPS * channels, width))
    rows_first = basis_rows(after(basis_out_first, filler))
    rows_second = basis_rows(after(basis_in_second, filler))
    weights = hold(after(w_first, filler), w_second)
    own_first, ratio_first = ratio_of(terms_first, after(scales_chunk, *weights, *terms_second))
    means = hold(after(w_first_mean, own_first), w_second_mean)
    terms_second = halved(after(joined(terms_second), own_first), *orders[-1])
    own_second, ratio_second = ratio_of(terms_second, after(scales_turned, *means))
    coeff_first = doubled(own_first, *orders[-1])
    middle_first = middle_of(ratio_first, after(rows_first, own_second))
    gathered_first = doubled(middle_first, *orders[-1])
    middle_second = middle_of(ratio_second, after(rows_second, coeff_first, gathered_first))
    squares_old = hold(after(w_first_square, middle_second), w_second_square)
    gathered_second = doubled(middle_second, *orders[-1])
    coeff_second = own_second
    for order in reversed(orders[near_steps:-1]):
        gathered_first = doubled(gathered_first, *order)
        gathered_second = doubled(after(gathered_second, gathered_first), *order)
    gathered_first = batch_gather(gathered_first, ("cin",))
    gathered_second = batch_gather(gathered_second, ("cin",))
    coeff_first = batch_gather(coeff_first, ("cin",), orders[near_steps:-1])
    coeff_second = batch_gather(coeff_second)

    def scales_of(turned, coeff, scales):
        spec = pl.BlockSpec((3,) + scales.shape[1:], lambda tap: (tap, 0, 0))
        return pl.pallas_call(
            functools.partial(scales_kernel, turned),
            grid=(TAPS // 3,),
            in_specs=[pl.BlockSpec((3 * channels, width), lambda tap: (tap, 0)), spec],
            out_specs=spec,
            out_shape=shape(scales.shape, F32),
            compiler_params=pltpu.CompilerParams(vmem_limit_bytes=12 * 1024 * 1024),
        )(coeff, scales)

    scales_second_new = scales_of(True, coeff_second, scales_second)
    scales_first_new = scales_of(False, coeff_first, scales_first)

    first_grad, second_grad, squares, small_grads = call(
        restore_kernel,
        [shape((TAPS, channels, width), BF), shape((TAPS, width, channels), BF), shape((8, LANES), F32), shape((72, LANES), F32)],
        [
            place,
            basis_in_first,
            after(gathered_first, coeff_first),
            basis_out_second,
            gathered_second,
            sums_first,
            sums_second,
            smalls,
        ],
        [pltpu.VMEM((channels, TAPS * width), BF)],
        near=tuple(range(1, 8)),
        near_out=(0, 1, 2, 3),
        room=16,
        flops=4 * TAPS * channels * channels * width,
    )
    square_slots = gathered(squares, "cout")
    square_slots[0] = after(square_slots[0], coeff_second)

    smalls = [small_grads]
    small_outs = [shape((2, width), F32)] * 4 + [shape((CLASSES, width), F32)] * 2 + [shape((1, CLASSES), F32)] * 2
    small_outs += [shape((1, 1), F32)] * 2
    first_spec = pl.BlockSpec((1, channels, width), lambda tap: (tap, 0, 0))
    second_spec = pl.BlockSpec((1, width, channels), lambda tap: (tap, 0, 0))
    pair = [first_spec, second_spec]
    first_like, second_like = shape(w_first.shape, F32), shape(w_second.shape, F32)

    def whole(leaf):
        return pl.BlockSpec(leaf.shape, lambda tap: (0,) * len(leaf.shape))

    def update(*refs):
        at = [0]

        def take(number):
            at[0] += number
            return refs[at[0] - number : at[0]]

        update_kernel(
            take(groups), take(2), take(2), take(2), take(2), take(len(smalls)),
            take(2), take(2), take(2), take(len(small_outs) - 2), take(2),
        )

    results = pl.pallas_call(
        update,
        grid=(TAPS,),
        in_specs=[pl.BlockSpec(memory_space=pltpu.VMEM)] * (groups + 8 + len(smalls)),
        out_specs=pair * 3 + [whole(leaf) for leaf in small_outs],
        out_shape=[first_like, second_like] * 3 + small_outs,
        compiler_params=pltpu.CompilerParams(vmem_limit_bytes=16 * 1024 * 1024),
    )(
        *square_slots, *weights, *means, *squares_old,
        first_grad, second_grad, *smalls,
    )
    (first_new, second_new, first_mean_new, second_mean_new, first_square_new, second_square_new,
     norm_first_mean, norm_first_square, norm_second_mean, norm_second_square,
     head_mean_new, head_square_new, bias_mean_new, bias_square_new, grad_norm, loss_total) = results
    return (
        loss_total.reshape(()),
        grad_norm.reshape(()),
        first_new,
        first_mean_new,
        first_square_new,
        second_new,
        second_mean_new,
        second_square_new,
        norm_first_mean,
        norm_first_square,
        norm_second_mean,
        norm_second_square,
        head_mean_new.T,
        head_square_new.T,
        bias_mean_new[0],
        bias_square_new[0],
        scales_first_new,
        scales_second_new,
    )


def solution(mesh):
    return jax.shard_map(
        local,
        mesh=mesh,
        in_specs=(
            P(None, ("dp", "cin"), None),
            P(None, ("dp", "cin")),
            P(("dp", "cin")),
            P(None, None, "cout"),
            P(None, "cout", None),
            P(None, "cout"),
            P("cout", None),
            P(),
            P(),
            P(None, None, "cout"),
            P(None, "cout", None),
            P(None, None, "cout"),
            P(None, None, "cout"),
            P(None, "cout", None),
            P(None, "cout", None),
            P(None, "cout"),
            P(None, "cout"),
            P("cout", None),
            P("cout", None),
            P(),
            P(),
        ),
        out_specs=(
            P(),
            P(),
            P(None, None, "cout"),
            P(None, None, "cout"),
            P(None, None, "cout"),
            P(None, "cout", None),
            P(None, "cout", None),
            P(None, "cout", None),
            P(None, "cout"),
            P(None, "cout"),
            P(None, "cout"),
            P(None, "cout"),
            P("cout", None),
            P("cout", None),
            P(),
            P(),
            P(None, None, "cout"),
            P(None, "cout", None),
        ),
        check_vma=False,
    )
```

time: 266 us -> 246 us (0.925)
  starting transfers between devices: 94.1 us -> 66 us
  Pallas kernels: 40.5 us -> 60.6 us
  blocking collectives: 8.45 us -> 0 us
  other arithmetic: 11.1 us -> 3.99 us
  waiting for transfers between devices: 80.9 us -> 84.7 us
    pallas_call x16 -> x20, Pallas kernels: 40.5 us -> 60.6 us  [the longest x17 47.7 us: call(): pl.pallas_call(body, out_shape=list(outs), in_specs=specs, out_specs=[pl....]
    ppermute x52 -> x49, starting transfers between devices: 68.8 us -> 49.8 us  [swap(): lax.ppermute(values, axis, [(here, here ^ step) for here in range(count)])]
    all_to_all x5 -> x4, waiting for transfers between devices: 1.02 us -> 13.2 us  [every_device(): return lax.all_to_all(tiles, EVERY, 0, 0, tiled=True)]
    all_to_all x5 -> x4, starting transfers between devices: 25.3 us -> 16.2 us  [every_device(): return lax.all_to_all(tiles, EVERY, 0, 0, tiled=True)]
    all_gather x1 -> x0, blocking collectives: 8.45 us -> none  [local(): head_full = lax.all_gather(head_rows, 'cout')]
    ppermute x52 -> x49, waiting for transfers between devices: 79.9 us -> 71.5 us  [swap(): lax.ppermute(values, axis, [(here, here ^ step) for here in range(count)])]
    another operation x12 -> x0, other arithmetic: 5.4 us -> none  [the longest x5 4.01 us: in_order(): stacked = jnp.stack(slots)]
    convert_element_type x4, other arithmetic: 3.75 us -> 0.47 us  [joined(): (terms[0].astype(F32) + terms[1].astype(F32)).astype(BF)]
  transfers between devices with their start and end apart: 57 -> 53, of which waited for: 21 -> 24; matrix products, arithmetic and copies ran while one was open for 9% -> 6% of each run, Pallas kernels for 8% -> 9%
where the time goes in v3:
time: 246 us; the launch traced here: 245 us
  waiting for transfers between devices  84.7 us (34%)
  starting transfers between devices  66 us (27%)
  Pallas kernels  60.6 us (25%)
  local copies, waits for them, and re-layouts  28.4 us (12%)
  other arithmetic  3.99 us (2%)
    ppermute x49, waiting for transfers between devices, swap(): lax.ppermute(values, axis, [(here, here ^ step) for here in range(count)])  71.5 us
    ppermute x49, starting transfers between devices, swap(): lax.ppermute(values, axis, [(here, here ^ step) for here in range(count)])  49.8 us
    pallas_call x17, Pallas kernels, call(): pl.pallas_call(body, out_shape=list(outs), in_specs=specs, out_specs=[pl....  47.7 us
    all_to_all x4, starting transfers between devices, every_device(): return lax.all_to_all(tiles, EVERY, 0, 0, tiled=True)  16.2 us
    unnamed x96, local copies, waits for them, and re-layouts  14.4 us
    all_to_all x4, waiting for transfers between devices, every_device(): return lax.all_to_all(tiles, EVERY, 0, 0, tiled=True)  13.2 us
    pallas_call x1, Pallas kernels, local(): pl.pallas_call(update, grid=(TAPS,), in_specs=[pl.BlockSpec(memory_space=...  8.67 us
  transfers between devices with their start and end apart: 53, of which 24 were waited for; matrix products, arithmetic and copies ran while one was open for 6% of the time, Pallas kernels for 9%

profile of v3, /device:TPU:0, one launch (start us, length us, event | category | flops | bytes accessed | tf_op | source)
XLA Modules:
  0.0 245.4 jit_solution(5748514407373114220)
XLA Ops:
  0.7 2.2 dynamic-slice_convert_fusion.refs_7_.refs_10_
  2.8 2.9 %collective-permute-start.3 = (bf16[9,128,256]{2,1,0:T(8,128)(2,1)}, bf16[9,128,256]{2,1,0:T(8,128)(2,1)S(1)}, u32[]{:S(2)}, u32[]{:S(2)}) collective-permute-start(bf16[9,128,256]{2,1,0:T(8,128)(2,1)} %dynamic-slice_convert_fusion.refs_7_.refs_10_), channel_id=1, source_target_pairs={{0,2},{2,0},{4,6},{6,4},{1,3},{3,1},{5,7},{7,5},{8,10},{10,8},{12,... | collective-permute-start | bytes 1769480 | tf_op jit(solution)/shard_map/ppermute | solution.py:625
  7.9 5.5 %shard_map.340 = (bf16[272,128]{1,0:T(8,128)(2,1)}, bf16[272,128]{1,0:T(8,128)(2,1)}, bf16[272,128]{1,0:T(8,128)(2,1)}, bf16[272,128]{1,0:T(8,128)(2,1)}, f32[32,8,128]{2,1,0:T(8,128)}, /*index=5*/f32[256,128]{1,0:T(8,128)}) custom-call(s32[2]{0:T(128)} %pad_add_fusion.refs_0_, bf16[1024,512]{1,0:T(8,128)(2,1)} %bitcast.74, s32[16,64]{1,0:T(8,128)} %refs_2_.3, ...), custom_call_target="tpu_custom_call" | custom-call | flops 1207959552 | bytes 3959816 | tf_op jit(solution)/shard_map/pallas_call | solution.py:117
  14.1 2.9 %collective-permute-start.2 = (bf16[272,128]{1,0:T(8,128)(2,1)}, bf16[272,128]{1,0:T(8,128)(2,1)S(1)}, u32[]{:S(2)}, u32[]{:S(2)}) collective-permute-start(bf16[272,128]{1,0:T(8,128)(2,1)} %get-tuple-element.113), channel_id=1, source_target_pairs={{0,6},{2,4},{4,2},{6,0},{1,7},{3,5},{5,3},{7,1},{8,14},{10,12},{12... | collective-permute-start | bytes 208904 | tf_op jit(solution)/shard_map/ppermute | solution.py:625
  17.0 4.6 %collective-permute-done.refs_2_ = bf16[272,128]{1,0:T(8,128)(2,1)S(1)} collective-permute-done((bf16[272,128]{1,0:T(8,128)(2,1)}, bf16[272,128]{1,0:T(8,128)(2,1)S(1)}, u32[]{:S(2)}, u32[]{:S(2)}) %collective-permute-start) | collective-permute-done | bytes 69664 | tf_op jit(solution)/shard_map/ppermute | solution.py:625
  21.6 2.2 collective-permute-done.1.refs_3_
  25.3 4.9 %all-to-all-start = ((f32[32,8,128]{2,1,0:T(8,128)}), f32[32,8,128]{2,1,0:T(8,128)S(1)}, u32[]{:S(2)}, u32[]{:S(2)}) async-start(f32[32,8,128]{2,1,0:T(8,128)} %get-tuple-element.114), calls=%async_computation | async-start | bytes 262144 | tf_op jit(solution)/shard_map/all_to_all | solution.py:651
  32.0 1.7 shard_map.341
  33.7 6.3 %all-to-all-done.refs_5_ = f32[32,8,128]{2,1,0:T(8,128)S(1)} async-done(((f32[32,8,128]{2,1,0:T(8,128)}), f32[32,8,128]{2,1,0:T(8,128)S(1)}, u32[]{:S(2)}, u32[]{:S(2)}) %all-to-all-start) | async-done | bytes 131104 | tf_op jit(solution)/shard_map/all_to_all | solution.py:651
  40.7 3.5 %shard_map.342 = (bf16[256,512]{1,0:T(8,128)(2,1)}, bf16[256,512]{1,0:T(8,128)(2,1)}, f32[8,512]{1,0:T(8,128)}, bf16[16,512]{1,0:T(8,128)(2,1)}) custom-call(s32[2]{0:T(128)} %pad_add_fusion.refs_0_, bf16[272,128]{1,0:T(8,128)(2,1)} %get-tuple-element.110.refs_1_, bf16[272,128]{1,0:T(8,128)(2,1)} %copy-done.34, bf16[272,128]{1,0:T(8,128)(2,1)} %copy-done.35, ...), custom_call_target="tpu_custom_call" | custom-call | bytes 1097736 | tf_op jit(solution)/shard_map/pallas_call | solution.py:117
  47.4 5.7 %shard_map.343 = (f32[256,256]{1,0:T(8,128)}, f32[256,256]{1,0:T(8,128)}, f32[32,8,128]{2,1,0:T(8,128)}, bf16[256,128]{1,0:T(8,128)(2,1)}, bf16[256,128]{1,0:T(8...) custom-call(s32[2]{0:T(128)} %pad_add_fusion.refs_0_, bf16[256,512]{1,0:T(8,128)(2,1)} %get-tuple-element.117.refs_1_, ...), custom_call_target="tpu_custom_call" | custom-call | flops 1207959552 | bytes 4589576 | tf_op jit(solution)/shard_map/pallas_call | solution.py:117
  54.3 4.8 %all-to-all-start.1 = ((f32[32,8,128]{2,1,0:T(8,128)}), f32[32,8,128]{2,1,0:T(8,128)S(1)}, u32[]{:S(2)}, u32[]{:S(2)}) async-start(f32[32,8,128]{2,1,0:T(8,128)} %get-tuple-element.121), calls=%async_computation.1 | async-start | bytes 262144 | tf_op jit(solution)/shard_map/all_to_all | solution.py:651
  60.5 6.9 %all-to-all-done.1.refs_3_ = f32[32,8,128]{2,1,0:T(8,128)S(1)} async-done(((f32[32,8,128]{2,1,0:T(8,128)}), f32[32,8,128]{2,1,0:T(8,128)S(1)}, u32[]{:S(2)}, u32[]{:S(2)}) %all-to-all-start.1) | async-done | bytes 131104 | tf_op jit(solution)/shard_map/all_to_all | solution.py:651
  68.0 4.3 %shard_map.344 = (f32[256,512]{1,0:T(8,128)}, f32[8,512]{1,0:T(8,128)}, f32[256,512]{1,0:T(8,128)}, f32[32,8,128]{2,1,0:T(8,128)}, f32[4,16,128]{2,1,0:T(8,128)}) custom-call(s32[2]{0:T(128)} %pad_add_fusion.refs_0_, f32[256,256]{1,0:T(8,128)} %get-tuple-element.119.refs_1_, f32[256,256]{1,0:T(8,128)} %collective-permute-done.8.refs_2_, ...), custom_call_target="tpu_custom_call" | custom-call | bytes 2048584 | tf_op jit(solution)/shard_map/pallas_call | solution.py:117
  72.3 2.6 %all-to-all-start.2 = ((f32[32,8,128]{2,1,0:T(8,128)}), f32[32,8,128]{2,1,0:T(8,128)S(1)}, u32[]{:S(2)}, u32[]{:S(2)}) async-start(f32[32,8,128]{2,1,0:T(8,128)} %get-tuple-element.132), calls=%async_computation.2 | async-start | bytes 262144 | tf_op jit(solution)/shard_map/all_to_all | solution.py:651
  74.9 1.7 collective-permute-start.13
  79.9 2.1 collective-permute-done.14.refs_6_
  84.9 6.7 %shard_map.345 = (bf16[512,256]{1,0:T(8,128)(2,1)}, f32[8,128]{1,0:T(8,128)}, f32[256,512]{1,0:T(8,128)}, bf16[4,4,2,32,128]{4,3,2,1,0:T(8,128)(2,1)}) custom-call(s32[2]{0:T(128)} %pad_add_fusion.refs_0_, f32[256,512]{1,0:T(8,128)} %get-tuple-element.129.refs_1_, f32[256,512]{1,0:T(8,128)} %get-tuple-element.130.refs_2_, ...), custom_call_target="tpu_custom_call" | custom-call | flops 1207959552 | bytes 7933960 | tf_op jit(solution)/shard_map/pallas_call | solution.py:117
  91.7 3.9 %all-to-all-start.3 = ((bf16[32,32,128]{2,1,0:T(8,128)(2,1)}), bf16[32,32,128]{2,1,0:T(8,128)(2,1)S(1)}, u32[]{:S(2)}, u32[]{:S(2)}) async-start(bf16[32,32,128]{2,1,0:T(8,128)(2,1)} %bitcast.87), calls=%async_computation.3 | async-start | bytes 524288 | tf_op jit(solution)/shard_map/all_to_all | solution.py:651
  95.5 1.7 collective-permute-start.16
  99.1 8.0 %collective-permute-done.16.refs_1_ = bf16[512,256]{1,0:T(8,128)(2,1)S(1)} collective-permute-done((bf16[512,256]{1,0:T(8,128)(2,1)}, bf16[512,256]{1,0:T(8,128)(2,1)S(1)}, u32[]{:S(2)}, u32[]{:S(2)}) %collective-permute-start.16) | collective-permute-done | bytes 262176 | tf_op jit(solution)/shard_map/ppermute | solution.py:625
  107.1 4.6 %collective-permute-done.17.refs_2_ = bf16[512,256]{1,0:T(8,128)(2,1)S(1)} collective-permute-done((bf16[512,256]{1,0:T(8,128)(2,1)}, bf16[512,256]{1,0:T(8,128)(2,1)S(1)}, u32[]{:S(2)}, u32[]{:S(2)}) %collective-permute-start.17) | collective-permute-done | bytes 262176 | tf_op jit(solution)/shard_map/ppermute | solution.py:625
  114.1 3.7 %shard_map.346 = (bf16[256,128]{1,0:T(8,128)(2,1)}, bf16[256,128]{1,0:T(8,128)(2,1)}, bf16[256,128]{1,0:T(8,128)(2,1)}, bf16[256,128]{1,0:T(8,128)(2,1)}, f32[8,128]{1,0:T(8,128)}, /*index=5*/f32[72,128]{1,0:T(8,128)}) custom-call(s32[2]{0:T(128)} %pad_add_fusion.refs_0_, f32[256,512]{1,0:T(8,128)} %get-tuple-element.140.refs_1_, ...), custom_call_target="tpu_custom_call" | custom-call | bytes 2037848 | tf_op jit(solution)/shard_map/pallas_call | solution.py:117
  123.6 1.8 collective-permute-done.21.refs_7_
  126.0 4.7 %shard_map.347 = bf16[4608,128]{1,0:T(8,128)(2,1)} custom-call(bf16[512,256]{1,0:T(8,128)(2,1)} %get-tuple-element.217.refs_0_, bf16[512,256]{1,0:T(8,128)(2,1)} %get-tuple-element.216.refs_1_, bf16[512,256]{1,0:T(8,128)(2,1)} %get-tuple-element.215.refs_2_, bf16[512,256]{1,0:T(8,128)(2,1)} %get-tuple-element.214.refs_3_, ...), custom_call_target="tpu_custom_call" | custom-call | flops 1207959552 | bytes 2490368 | tf_op jit(solution)/shard_map/pallas_call | solution.py:117
  132.1 1.9 collective-permute-done.22
  134.9 4.1 %shard_map.348 = bf16[4608,128]{1,0:T(8,128)(2,1)} custom-call(bf16[512,256]{1,0:T(8,128)(2,1)} %get-tuple-element.149.refs_0_, bf16[512,256]{1,0:T(8,128)(2,1)} %copy-done.37, bf16[512,256]{1,0:T(8,128)(2,1)} %copy-done.38, bf16[512,256]{1,0:T(8,128)(2,1)} %collective-permute-done.18.refs_3_, bf16[256,128]{1,0:T(8,128)(2,1)} %get-tuple-element.133.refs_4_, ...), custom_call_target="tpu_custom_call" | custom-call | flops 1207959552 | bytes 2490368 | tf_op jit(solution)/shard_map/pallas_call | solution.py:117
  140.2 3.1 %collective-permute-done.23 = bf16[1152,128]{1,0:T(8,128)(2,1)S(1)} collective-permute-done((bf16[1152,128]{1,0:T(8,128)(2,1)S(1)}, bf16[1152,128]{1,0:T(8,128)(2,1)S(1)}, u32[]{:S(2)}, u32[]{:S(2)}) %collective-permute-start.23) | collective-permute-done | bytes 294944 | tf_op jit(solution)/shard_map/ppermute | solution.py:625
  145.2 2.2 collective-permute-start.26
  151.5 7.1 %collective-permute-done.25 = bf16[1152,128]{1,0:T(8,128)(2,1)S(1)} collective-permute-done((bf16[1152,128]{1,0:T(8,128)(2,1)S(1)}, bf16[1152,128]{1,0:T(8,128)(2,1)S(1)}, u32[]{:S(2)}, u32[]{:S(2)}) %collective-permute-start.25) | collective-permute-done | bytes 294944 | tf_op jit(solution)/shard_map/ppermute | solution.py:625
  160.9 2.1 collective-permute-start.30
  164.6 1.9 collective-permute-start.27
  166.6 1.9 copy.40
  169.6 1.7 copy-done.6
  171.2 1.7 copy-done.7
  173.2 3.4 %collective-permute-done.27.refs_1_ = bf16[576,128]{1,0:T(8,128)(2,1)} collective-permute-done((bf16[576,128]{1,0:T(8,128)(2,1)}, bf16[576,128]{1,0:T(8,128)(2,1)}, u32[]{:S(2)}, u32[]{:S(2)}) %collective-permute-start.27) | collective-permute-done | bytes 147488 | tf_op jit(solution)/shard_map/ppermute | solution.py:625
  183.0 2.9 %collective-permute-start.31 = (bf16[576,128]{1,0:T(8,128)(2,1)S(1)}, bf16[576,128]{1,0:T(8,128)(2,1)S(1)}, u32[]{:S(2)}, u32[]{:S(2)}) collective-permute-start(bf16[576,128]{1,0:T(8,128)(2,1)S(1)} %shard_map.353), channel_id=1, source_target_pairs={{0,16},{8,24},{16,0},{24,8},{1,17},{9,25},{17,1},{25,9},{2,18},{10... | collective-permute-start | bytes 442376 | tf_op jit(solution)/shard_map/ppermute | solution.py:625
  186.8 5.5 %collective-permute-done.31 = bf16[576,128]{1,0:T(8,128)(2,1)S(1)} collective-permute-done((bf16[576,128]{1,0:T(8,128)(2,1)S(1)}, bf16[576,128]{1,0:T(8,128)(2,1)S(1)}, u32[]{:S(2)}, u32[]{:S(2)}) %collective-permute-start.31) | collective-permute-done | bytes 147488 | tf_op jit(solution)/shard_map/ppermute | solution.py:625
  192.4 2.1 collective-permute-start.32
  195.4 2.1 collective-permute-start.44
  197.8 11.5 %collective-permute-done.40 = bf16[576,128]{1,0:T(8,128)(2,1)S(1)} collective-permute-done((bf16[576,128]{1,0:T(8,128)(2,1)S(1)}, bf16[576,128]{1,0:T(8,128)(2,1)S(1)}, u32[]{:S(2)}, u32[]{:S(2)}) %collective-permute-start.40) | collective-permute-done | bytes 147488 | tf_op jit(solution)/shard_map/ppermute | solution.py:625
  211.3 1.9 collective-permute-start.41
  214.4 6.3 %collective-permute-done.41 = bf16[1152,128]{1,0:T(8,128)(2,1)S(1)} collective-permute-done((bf16[1152,128]{1,0:T(8,128)(2,1)S(1)}, bf16[1152,128]{1,0:T(8,128)(2,1)S(1)}, u32[]{:S(2)}, u32[]{:S(2)}) %collective-permute-start.41) | collective-permute-done | bytes 294944 | tf_op jit(solution)/shard_map/ppermute | solution.py:625
  222.8 2.0 shard_map.358
  226.7 3.0 %shard_map.355 = (bf16[9,512,128]{2,1,0:T(8,128)(2,1)S(1)}, bf16[9,128,512]{2,1,0:T(8,128)(2,1)S(1)}, f32[8,128]{1,0:T(8,128)S(1)}, f32[72,128]{1,0:T(8,128)S(1)}) custom-call(s32[2]{0:T(128)S(1)} %copy-done.17, bf16[512,512]{1,0:T(8,128)(2,1)S(1)} %get-tuple-element.204.refs_3_.refs_1_, bf16[4608,128]{1,0:T(8,128)(2,1)S(1)} %pad_maximum_fusion.refs_2_, ...), custom_call_target="tpu_custom_call" | custom-call | flops 1207959552 | bytes 5853192 | tf_op jit(solution)/shard_map/pallas_call | solution.py:117
  231.6 1.7 collective-permute-start.48
  233.4 2.2 shard_map.359
  236.6 8.7 %shard_map.357 = (f32[9,512,128]{2,1,0:T(8,128)}, f32[9,128,512]{2,1,0:T(8,128)}, f32[9,512,128]{2,1,0:T(8,128)}, f32[9,128,512]{2,1,0:T(8,128)}, f32[9,512,128]...) custom-call(f32[8,128]{1,0:T(8,128)S(1)} %get-tuple-element.175.refs, ...), custom_call_target="tpu_custom_call" | custom-call | tf_op jit(solution)/shard_map/pallas_call | solution.py:1030
  (221 shorter events, 63.0 us)
Async XLA Ops:
  2.8 30.9 %collective-permute-start.3 = (bf16[9,128,256]{2,1,0:T(8,128)(2,1)}, bf16[9,128,256]{2,1,0:T(8,128)(2,1)S(1)}, u32[]{:S(2)}, u32[]{:S(2)}) collective-permute-start(bf16[9,128,256]{2,1,0:T(8,128)(2,1)} %dynamic-slice_convert_fusion.refs_7_.refs_10_), channel_id=1, source_target_pairs={{0,2},{2,0},{4,6},{6,4},{1,3},{3,1},{5,7},{7,5},{8,10},{10,8},{12,... | collective-permute-start | bytes 1769480 | tf_op jit(solution)/shard_map/ppermute | solution.py:625
  5.8 27.9 %collective-permute-start.4 = (bf16[9,128,256]{2,1,0:T(8,128)(2,1)}, bf16[9,128,256]{2,1,0:T(8,128)(2,1)}, u32[]{:S(2)}, u32[]{:S(2)}) collective-permute-start(bf16[9,128,256]{2,1,0:T(8,128)(2,1)} %dynamic-slice_convert_fusion.refs_7_.refs_10_), channel_id=1, source_target_pairs={{0,4},{2,6},{4,0},{6,2},{1,5},{3,7},{5,1},{7,3},{8,12},{10,14},{12... | collective-permute-start | bytes 1769480 | tf_op jit(solution)/shard_map/ppermute | solution.py:625
  13.4 8.2 %collective-permute-start = (bf16[272,128]{1,0:T(8,128)(2,1)}, bf16[272,128]{1,0:T(8,128)(2,1)S(1)}, u32[]{:S(2)}, u32[]{:S(2)}) collective-permute-start(bf16[272,128]{1,0:T(8,128)(2,1)} %get-tuple-element.111), channel_id=1, source_target_pairs={{0,2},{2,0},{4,6},{6,4},{1,3},{3,1},{5,7},{7,5},{8,10},{10,8},{12,... | collective-permute-start | bytes 208904 | tf_op jit(solution)/shard_map/ppermute | solution.py:625
  14.0 9.8 %collective-permute-start.1 = (bf16[272,128]{1,0:T(8,128)(2,1)}, bf16[272,128]{1,0:T(8,128)(2,1)S(1)}, u32[]{:S(2)}, u32[]{:S(2)}) collective-permute-start(bf16[272,128]{1,0:T(8,128)(2,1)} %get-tuple-element.112), channel_id=1, source_target_pairs={{0,4},{2,6},{4,0},{6,2},{1,5},{3,7},{5,1},{7,3},{8,12},{10,14},{12... | collective-permute-start | bytes 208904 | tf_op jit(solution)/shard_map/ppermute | solution.py:625
  14.1 9.7 %collective-permute-start.2 = (bf16[272,128]{1,0:T(8,128)(2,1)}, bf16[272,128]{1,0:T(8,128)(2,1)S(1)}, u32[]{:S(2)}, u32[]{:S(2)}) collective-permute-start(bf16[272,128]{1,0:T(8,128)(2,1)} %get-tuple-element.113), channel_id=1, source_target_pairs={{0,6},{2,4},{4,2},{6,0},{1,7},{3,5},{5,3},{7,1},{8,14},{10,12},{12... | collective-permute-start | bytes 208904 | tf_op jit(solution)/shard_map/ppermute | solution.py:625
  23.8 22.2 %collective-permute-start.7 = (bf16[9,128,256]{2,1,0:T(8,128)(2,1)}, bf16[9,128,256]{2,1,0:T(8,128)(2,1)}, u32[]{:S(2)}, u32[]{:S(2)}) collective-permute-start(bf16[9,128,256]{2,1,0:T(8,128)(2,1)} %dynamic-slice_convert_fusion.refs_7_.refs_10_), channel_id=1, source_target_pairs={{0,6},{2,4},{4,2},{6,0},{1,7},{3,5},{5,3},{7,1},{8,14},{10,12},{12... | collective-permute-start | bytes 1769480 | tf_op jit(solution)/shard_map/ppermute | solution.py:625
  25.3 14.7 %all-to-all-start = ((f32[32,8,128]{2,1,0:T(8,128)}), f32[32,8,128]{2,1,0:T(8,128)S(1)}, u32[]{:S(2)}, u32[]{:S(2)}) async-start(f32[32,8,128]{2,1,0:T(8,128)} %get-tuple-element.114), calls=%async_computation | async-start | bytes 262144 | tf_op jit(solution)/shard_map/all_to_all | solution.py:651
  53.1 7.4 %collective-permute-start.12 = (bf16[9,128,256]{2,1,0:T(8,128)(2,1)}, bf16[9,128,256]{2,1,0:T(8,128)(2,1)S(1)}, u32[]{:S(2)}, u32[]{:S(2)}) collective-permute-start(bf16[9,128,256]{2,1,0:T(8,128)(2,1)} %collective-permute-done.7.refs_10_.refs_13_), channel_id=1, source_target_pairs={{0,1},{1,0},{2,3},{3,2},{4,5},{5,4},{6,7},{7,6},{8,9},{9,8},{10,11... | collective-permute-start | bytes 1769480 | tf_op jit(solution)/shard_map/ppermute | solution.py:625
  53.3 7.2 %collective-permute-start.11 = (bf16[9,128,256]{2,1,0:T(8,128)(2,1)}, bf16[9,128,256]{2,1,0:T(8,128)(2,1)S(1)}, u32[]{:S(2)}, u32[]{:S(2)}) collective-permute-start(bf16[9,128,256]{2,1,0:T(8,128)(2,1)} %collective-permute-done.4.refs_9_.refs_12_), channel_id=1, source_target_pairs={{0,1},{1,0},{2,3},{3,2},{4,5},{5,4},{6,7},{7,6},{8,9},{9,8},{10,11... | collective-permute-start | bytes 1769480 | tf_op jit(solution)/shard_map/ppermute | solution.py:625
  53.6 6.8 %collective-permute-start.10 = (bf16[9,128,256]{2,1,0:T(8,128)(2,1)}, bf16[9,128,256]{2,1,0:T(8,128)(2,1)S(1)}, u32[]{:S(2)}, u32[]{:S(2)}) collective-permute-start(bf16[9,128,256]{2,1,0:T(8,128)(2,1)} %copy-done.27), channel_id=1, source_target_pairs={{0,1},{1,0},{2,3},{3,2},{4,5},{5,4},{6,7},{7,6},{8,9},{9,8},{10,11... | collective-permute-start | bytes 1769480 | tf_op jit(solution)/shard_map/ppermute | solution.py:625
  53.8 6.7 %collective-permute-start.9 = (bf16[9,128,256]{2,1,0:T(8,128)(2,1)}, bf16[9,128,256]{2,1,0:T(8,128)(2,1)}, u32[]{:S(2)}, u32[]{:S(2)}) collective-permute-start(bf16[9,128,256]{2,1,0:T(8,128)(2,1)} %dynamic-slice_convert_fusion.refs_7_.refs_10_), channel_id=1, source_target_pairs={{0,1},{1,0},{2,3},{3,2},{4,5},{5,4},{6,7},{7,6},{8,9},{9,8},{10,11... | collective-permute-start | bytes 1769480 | tf_op jit(solution)/shard_map/ppermute | solution.py:625
  54.1 13.2 %collective-permute-start.8 = (f32[256,256]{1,0:T(8,128)}, f32[256,256]{1,0:T(8,128)}, u32[]{:S(2)}, u32[]{:S(2)}) collective-permute-start(f32[256,256]{1,0:T(8,128)} %get-tuple-element.120), channel_id=1, source_target_pairs={{0,1},{1,0},{2,3},{3,2},{4,5},{5,4},{6,7},{7,6},{8,9},{9,8},{10,11... | collective-permute-start | bytes 786440 | tf_op jit(solution)/shard_map/ppermute | solution.py:625
  54.3 13.1 %all-to-all-start.1 = ((f32[32,8,128]{2,1,0:T(8,128)}), f32[32,8,128]{2,1,0:T(8,128)S(1)}, u32[]{:S(2)}, u32[]{:S(2)}) async-start(f32[32,8,128]{2,1,0:T(8,128)} %get-tuple-element.121), calls=%async_computation.1 | async-start | bytes 262144 | tf_op jit(solution)/shard_map/all_to_all | solution.py:651
  72.3 11.9 %all-to-all-start.2 = ((f32[32,8,128]{2,1,0:T(8,128)}), f32[32,8,128]{2,1,0:T(8,128)S(1)}, u32[]{:S(2)}, u32[]{:S(2)}) async-start(f32[32,8,128]{2,1,0:T(8,128)} %get-tuple-element.132), calls=%async_computation.2 | async-start | bytes 262144 | tf_op jit(solution)/shard_map/all_to_all | solution.py:651
  74.9 5.0 %collective-permute-start.13 = (bf16[256,128]{1,0:T(8,128)(2,1)}, bf16[256,128]{1,0:T(8,128)(2,1)S(1)}, u32[]{:S(2)}, u32[]{:S(2)}) collective-permute-start(bf16[256,128]{1,0:T(8,128)(2,1)} %get-tuple-element.134), channel_id=1, source_target_pairs={{0,2},{2,0},{4,6},{6,4},{1,3},{3,1},{5,7},{7,5},{8,10},{10,8},{12,... | collective-permute-start | bytes 196616 | tf_op jit(solution)/shard_map/ppermute | solution.py:625
  76.6 5.4 %collective-permute-start.14 = (bf16[256,128]{1,0:T(8,128)(2,1)}, bf16[256,128]{1,0:T(8,128)(2,1)S(1)}, u32[]{:S(2)}, u32[]{:S(2)}) collective-permute-start(bf16[256,128]{1,0:T(8,128)(2,1)} %get-tuple-element.135), channel_id=1, source_target_pairs={{0,4},{2,6},{4,0},{6,2},{1,5},{3,7},{5,1},{7,3},{8,12},{10,14},{12... | collective-permute-start | bytes 196616 | tf_op jit(solution)/shard_map/ppermute | solution.py:625
  78.1 5.5 %collective-permute-start.15 = (bf16[256,128]{1,0:T(8,128)(2,1)}, bf16[256,128]{1,0:T(8,128)(2,1)S(1)}, u32[]{:S(2)}, u32[]{:S(2)}) collective-permute-start(bf16[256,128]{1,0:T(8,128)(2,1)} %get-tuple-element.136), channel_id=1, source_target_pairs={{0,6},{2,4},{4,2},{6,0},{1,7},{3,5},{5,3},{7,1},{8,14},{10,12},{12... | collective-permute-start | bytes 196616 | tf_op jit(solution)/shard_map/ppermute | solution.py:625
  91.7 21.7 %all-to-all-start.3 = ((bf16[32,32,128]{2,1,0:T(8,128)(2,1)}), bf16[32,32,128]{2,1,0:T(8,128)(2,1)S(1)}, u32[]{:S(2)}, u32[]{:S(2)}) async-start(bf16[32,32,128]{2,1,0:T(8,128)(2,1)} %bitcast.87), calls=%async_computation.3 | async-start | bytes 524288 | tf_op jit(solution)/shard_map/all_to_all | solution.py:651
  95.5 11.6 %collective-permute-start.16 = (bf16[512,256]{1,0:T(8,128)(2,1)}, bf16[512,256]{1,0:T(8,128)(2,1)S(1)}, u32[]{:S(2)}, u32[]{:S(2)}) collective-permute-start(bf16[512,256]{1,0:T(8,128)(2,1)} %get-tuple-element.149.refs_0_), channel_id=1, source_target_pairs={{0,2},{2,0},{4,6},{6,4},{1,3},{3,1},{5,7},{7,5},{8,10},{10,8},{12,... | collective-permute-start | bytes 786440 | tf_op jit(solution)/shard_map/ppermute | solution.py:625
  97.2 14.5 %collective-permute-start.17 = (bf16[512,256]{1,0:T(8,128)(2,1)}, bf16[512,256]{1,0:T(8,128)(2,1)S(1)}, u32[]{:S(2)}, u32[]{:S(2)}) collective-permute-start(bf16[512,256]{1,0:T(8,128)(2,1)} %get-tuple-element.149.refs_0_), channel_id=1, source_target_pairs={{0,4},{2,6},{4,0},{6,2},{1,5},{3,7},{5,1},{7,3},{8,12},{10,14},{12... | collective-permute-start | bytes 786440 | tf_op jit(solution)/shard_map/ppermute | solution.py:625
  98.7 14.7 %collective-permute-start.18 = (bf16[512,256]{1,0:T(8,128)(2,1)}, bf16[512,256]{1,0:T(8,128)(2,1)}, u32[]{:S(2)}, u32[]{:S(2)}) collective-permute-start(bf16[512,256]{1,0:T(8,128)(2,1)} %get-tuple-element.149.refs_0_), channel_id=1, source_target_pairs={{0,6},{2,4},{4,2},{6,0},{1,7},{3,5},{5,3},{7,1},{8,14},{10,12},{12... | collective-permute-start | bytes 786440 | tf_op jit(solution)/shard_map/ppermute | solution.py:625
  117.8 4.7 %collective-permute-start.19 = (bf16[256,128]{1,0:T(8,128)(2,1)}, bf16[256,128]{1,0:T(8,128)(2,1)S(1)}, u32[]{:S(2)}, u32[]{:S(2)}) collective-permute-start(bf16[256,128]{1,0:T(8,128)(2,1)} %get-tuple-element.145), channel_id=1, source_target_pairs={{0,2},{2,0},{4,6},{6,4},{1,3},{3,1},{5,7},{7,5},{8,10},{10,8},{12,... | collective-permute-start | bytes 196616 | tf_op jit(solution)/shard_map/ppermute | solution.py:625
  118.8 4.8 %collective-permute-start.20 = (bf16[256,128]{1,0:T(8,128)(2,1)}, bf16[256,128]{1,0:T(8,128)(2,1)S(1)}, u32[]{:S(2)}, u32[]{:S(2)}) collective-permute-start(bf16[256,128]{1,0:T(8,128)(2,1)} %get-tuple-element.146), channel_id=1, source_target_pairs={{0,4},{2,6},{4,0},{6,2},{1,5},{3,7},{5,1},{7,3},{8,12},{10,14},{12... | collective-permute-start | bytes 196616 | tf_op jit(solution)/shard_map/ppermute | solution.py:625
  120.0 5.4 %collective-permute-start.21 = (bf16[256,128]{1,0:T(8,128)(2,1)}, bf16[256,128]{1,0:T(8,128)(2,1)S(1)}, u32[]{:S(2)}, u32[]{:S(2)}) collective-permute-start(bf16[256,128]{1,0:T(8,128)(2,1)} %get-tuple-element.147), channel_id=1, source_target_pairs={{0,6},{2,4},{4,2},{6,0},{1,7},{3,5},{5,3},{7,1},{8,14},{10,12},{12... | collective-permute-start | bytes 196616 | tf_op jit(solution)/shard_map/ppermute | solution.py:625
  134.2 9.1 %collective-permute-start.23 = (bf16[1152,128]{1,0:T(8,128)(2,1)S(1)}, bf16[1152,128]{1,0:T(8,128)(2,1)S(1)}, u32[]{:S(2)}, u32[]{:S(2)}) collective-permute-start(bf16[1152,128]{1,0:T(8,128)(2,1)S(1)} %dynamic-slice_bitcast_fusion.5), channel_id=1, source_target_pairs={{0,8},{8,0},{16,24},{24,16},{1,9},{9,1},{17,25},{25,17},{2,10},{10... | collective-permute-start | bytes 884744 | tf_op jit(solution)/shard_map/ppermute | solution.py:625
  140.2 7.2 %collective-permute-start.24 = (bf16[2304,128]{1,0:T(8,128)(2,1)S(1)}, bf16[2304,128]{1,0:T(8,128)(2,1)S(1)}, u32[]{:S(2)}, u32[]{:S(2)}) collective-permute-start(bf16[2304,128]{1,0:T(8,128)(2,1)S(1)} %dynamic-slice_bitcast_fusion), channel_id=1, source_target_pairs={{0,1},{1,0},{2,3},{3,2},{4,5},{5,4},{6,7},{7,6},{8,9},{9,8},{10,11... | collective-permute-start | bytes 1769480 | tf_op jit(solution)/shard_map/ppermute | solution.py:625
  145.2 13.4 %collective-permute-start.26 = (bf16[576,128]{1,0:T(8,128)(2,1)S(1)}, bf16[576,128]{1,0:T(8,128)(2,1)S(1)}, u32[]{:S(2)}, u32[]{:S(2)}) collective-permute-start(bf16[576,128]{1,0:T(8,128)(2,1)S(1)} %get-tuple-element.244), channel_id=1, source_target_pairs={{0,16},{8,24},{16,0},{24,8},{1,17},{9,25},{17,1},{25,9},{2,18},{10... | collective-permute-start | bytes 442376 | tf_op jit(solution)/shard_map/ppermute | solution.py:625
  147.6 10.9 %collective-permute-start.25 = (bf16[1152,128]{1,0:T(8,128)(2,1)S(1)}, bf16[1152,128]{1,0:T(8,128)(2,1)S(1)}, u32[]{:S(2)}, u32[]{:S(2)}) collective-permute-start(bf16[1152,128]{1,0:T(8,128)(2,1)S(1)} %dynamic-slice_bitcast_fusion.2), channel_id=1, source_target_pairs={{0,8},{8,0},{16,24},{24,16},{1,9},{9,1},{17,25},{25,17},{2,10},{10... | collective-permute-start | bytes 884744 | tf_op jit(solution)/shard_map/ppermute | solution.py:625
  159.4 18.4 %collective-permute-start.28 = (bf16[576,128]{1,0:T(8,128)(2,1)}, bf16[576,128]{1,0:T(8,128)(2,1)}, u32[]{:S(2)}, u32[]{:S(2)}) collective-permute-start(bf16[576,128]{1,0:T(8,128)(2,1)} %get-tuple-element.165.refs_1_), channel_id=1, source_target_pairs={{0,2},{2,0},{4,6},{6,4},{1,3},{3,1},{5,7},{7,5},{8,10},{10,8},{12,... | collective-permute-start | bytes 442376 | tf_op jit(solution)/shard_map/ppermute | solution.py:625
  160.3 18.4 %collective-permute-start.29 = (bf16[576,128]{1,0:T(8,128)(2,1)}, bf16[576,128]{1,0:T(8,128)(2,1)}, u32[]{:S(2)}, u32[]{:S(2)}) collective-permute-start(bf16[576,128]{1,0:T(8,128)(2,1)} %get-tuple-element.165.refs_1_), channel_id=1, source_target_pairs={{0,4},{2,6},{4,0},{6,2},{1,5},{3,7},{5,1},{7,3},{8,12},{10,14},{12... | collective-permute-start | bytes 442376 | tf_op jit(solution)/shard_map/ppermute | solution.py:625
  160.9 18.8 %collective-permute-start.30 = (bf16[576,128]{1,0:T(8,128)(2,1)}, bf16[576,128]{1,0:T(8,128)(2,1)}, u32[]{:S(2)}, u32[]{:S(2)}) collective-permute-start(bf16[576,128]{1,0:T(8,128)(2,1)} %get-tuple-element.165.refs_1_), channel_id=1, source_target_pairs={{0,6},{2,4},{4,2},{6,0},{1,7},{3,5},{5,3},{7,1},{8,14},{10,12},{12... | collective-permute-start | bytes 442376 | tf_op jit(solution)/shard_map/ppermute | solution.py:625
  163.0 20.0 %collective-permute-start.34 = (bf16[576,128]{1,0:T(8,128)(2,1)S(1)}, bf16[576,128]{1,0:T(8,128)(2,1)}, u32[]{:S(2)}, u32[]{:S(2)}) collective-permute-start(bf16[576,128]{1,0:T(8,128)(2,1)S(1)} %get-tuple-element.156), channel_id=1, source_target_pairs={{0,16},{8,24},{16,0},{24,8},{1,17},{9,25},{17,1},{25,9},{2,18},{10... | collective-permute-start | bytes 442376 | tf_op jit(solution)/shard_map/ppermute | solution.py:625
  164.6 12.0 %collective-permute-start.27 = (bf16[576,128]{1,0:T(8,128)(2,1)}, bf16[576,128]{1,0:T(8,128)(2,1)}, u32[]{:S(2)}, u32[]{:S(2)}) collective-permute-start(bf16[576,128]{1,0:T(8,128)(2,1)} %get-tuple-element.242), channel_id=1, source_target_pairs={{0,16},{8,24},{16,0},{24,8},{1,17},{9,25},{17,1},{25,9},{2,18},{10... | collective-permute-start | bytes 442376 | tf_op jit(solution)/shard_map/ppermute | solution.py:625
  177.7 17.6 %collective-permute-start.43 = (bf16[576,128]{1,0:T(8,128)(2,1)S(1)}, bf16[576,128]{1,0:T(8,128)(2,1)S(1)}, u32[]{:S(2)}, u32[]{:S(2)}) collective-permute-start(bf16[576,128]{1,0:T(8,128)(2,1)S(1)} %get-tuple-element.163), channel_id=1, source_target_pairs={{0,16},{8,24},{16,0},{24,8},{1,17},{9,25},{17,1},{25,9},{2,18},{10... | collective-permute-start | bytes 442376 | tf_op jit(solution)/shard_map/ppermute | solution.py:625
  177.8 14.6 %collective-permute-start.37 = (bf16[576,128]{1,0:T(8,128)(2,1)S(1)}, bf16[576,128]{1,0:T(8,128)(2,1)S(1)}, u32[]{:S(2)}, u32[]{:S(2)}) collective-permute-start(bf16[576,128]{1,0:T(8,128)(2,1)S(1)} %get-tuple-element.169.refs_1_), channel_id=1, source_target_pairs={{0,2},{2,0},{4,6},{6,4},{1,3},{3,1},{5,7},{7,5},{8,10},{10,8},{12,... | collective-permute-start | bytes 442376 | tf_op jit(solution)/shard_map/ppermute | solution.py:625
  178.7 15.8 %collective-permute-start.38 = (bf16[576,128]{1,0:T(8,128)(2,1)S(1)}, bf16[576,128]{1,0:T(8,128)(2,1)S(1)}, u32[]{:S(2)}, u32[]{:S(2)}) collective-permute-start(bf16[576,128]{1,0:T(8,128)(2,1)S(1)} %get-tuple-element.169.refs_1_), channel_id=1, source_target_pairs={{0,4},{2,6},{4,0},{6,2},{1,5},{3,7},{5,1},{7,3},{8,12},{10,14},{12... | collective-permute-start | bytes 442376 | tf_op jit(solution)/shard_map/ppermute | solution.py:625
  179.8 14.8 %collective-permute-start.39 = (bf16[576,128]{1,0:T(8,128)(2,1)S(1)}, bf16[576,128]{1,0:T(8,128)(2,1)S(1)}, u32[]{:S(2)}, u32[]{:S(2)}) collective-permute-start(bf16[576,128]{1,0:T(8,128)(2,1)S(1)} %get-tuple-element.169.refs_1_), channel_id=1, source_target_pairs={{0,6},{2,4},{4,2},{6,0},{1,7},{3,5},{5,3},{7,1},{8,14},{10,12},{12... | collective-permute-start | bytes 442376 | tf_op jit(solution)/shard_map/ppermute | solution.py:625
  183.0 9.4 %collective-permute-start.31 = (bf16[576,128]{1,0:T(8,128)(2,1)S(1)}, bf16[576,128]{1,0:T(8,128)(2,1)S(1)}, u32[]{:S(2)}, u32[]{:S(2)}) collective-permute-start(bf16[576,128]{1,0:T(8,128)(2,1)S(1)} %shard_map.353), channel_id=1, source_target_pairs={{0,16},{8,24},{16,0},{24,8},{1,17},{9,25},{17,1},{25,9},{2,18},{10... | collective-permute-start | bytes 442376 | tf_op jit(solution)/shard_map/ppermute | solution.py:625
  192.3 17.0 %collective-permute-start.35 = (bf16[1152,128]{1,0:T(8,128)(2,1)S(1)}, bf16[1152,128]{1,0:T(8,128)(2,1)S(1)}, u32[]{:S(2)}, u32[]{:S(2)}) collective-permute-start(bf16[1152,128]{1,0:T(8,128)(2,1)S(1)} %pad_maximum_fusion.9), channel_id=1, source_target_pairs={{0,8},{8,0},{16,24},{24,16},{1,9},{9,1},{17,25},{25,17},{2,10},{10... | collective-permute-start | bytes 884744 | tf_op jit(solution)/shard_map/ppermute | solution.py:625
  192.4 18.6 %collective-permute-start.32 = (bf16[1152,128]{1,0:T(8,128)(2,1)S(1)}, bf16[1152,128]{1,0:T(8,128)(2,1)S(1)}, u32[]{:S(2)}, u32[]{:S(2)}) collective-permute-start(bf16[1152,128]{1,0:T(8,128)(2,1)S(1)} %pad_maximum_fusion.8), channel_id=1, source_target_pairs={{0,8},{8,0},{16,24},{24,16},{1,9},{9,1},{17,25},{25,17},{2,10},{10... | collective-permute-start | bytes 884744 | tf_op jit(solution)/shard_map/ppermute | solution.py:625
  194.9 14.4 %collective-permute-start.40 = (bf16[576,128]{1,0:T(8,128)(2,1)S(1)}, bf16[576,128]{1,0:T(8,128)(2,1)S(1)}, u32[]{:S(2)}, u32[]{:S(2)}) collective-permute-start(bf16[576,128]{1,0:T(8,128)(2,1)S(1)} %shard_map.354), channel_id=1, source_target_pairs={{0,16},{8,24},{16,0},{24,8},{1,17},{9,25},{17,1},{25,9},{2,18},{10... | collective-permute-start | bytes 442376 | tf_op jit(solution)/shard_map/ppermute | solution.py:625
  195.4 18.8 %collective-permute-start.44 = (bf16[1152,128]{1,0:T(8,128)(2,1)S(1)}, bf16[1152,128]{1,0:T(8,128)(2,1)S(1)}, u32[]{:S(2)}, u32[]{:S(2)}) collective-permute-start(bf16[1152,128]{1,0:T(8,128)(2,1)S(1)} %pad_maximum_fusion.11), channel_id=1, source_target_pairs={{0,8},{8,0},{16,24},{24,16},{1,9},{9,1},{17,25},{25,17},{2,10},{10... | collective-permute-start | bytes 884744 | tf_op jit(solution)/shard_map/ppermute | solution.py:625
  209.5 11.3 %collective-permute-start.36 = (bf16[2304,128]{1,0:T(8,128)(2,1)S(1)}, bf16[2304,128]{1,0:T(8,128)(2,1)S(1)}, u32[]{:S(2)}, u32[]{:S(2)}) collective-permute-start(bf16[2304,128]{1,0:T(8,128)(2,1)S(1)} %pad_maximum_fusion.5), channel_id=1, source_target_pairs={{0,1},{1,0},{2,3},{3,2},{4,5},{5,4},{6,7},{7,6},{8,9},{9,8},{10,11... | collective-permute-start | bytes 1769480 | tf_op jit(solution)/shard_map/ppermute | solution.py:625
  211.2 13.6 %collective-permute-start.33 = (bf16[2304,128]{1,0:T(8,128)(2,1)S(1)}, bf16[2304,128]{1,0:T(8,128)(2,1)S(1)}, u32[]{:S(2)}, u32[]{:S(2)}) collective-permute-start(bf16[2304,128]{1,0:T(8,128)(2,1)S(1)} %pad_maximum_fusion.4), channel_id=1, source_target_pairs={{0,1},{1,0},{2,3},{3,2},{4,5},{5,4},{6,7},{7,6},{8,9},{9,8},{10,11... | collective-permute-start | bytes 1769480 | tf_op jit(solution)/shard_map/ppermute | solution.py:625
  211.3 9.4 %collective-permute-start.41 = (bf16[1152,128]{1,0:T(8,128)(2,1)S(1)}, bf16[1152,128]{1,0:T(8,128)(2,1)S(1)}, u32[]{:S(2)}, u32[]{:S(2)}) collective-permute-start(bf16[1152,128]{1,0:T(8,128)(2,1)S(1)} %pad_maximum_fusion.10), channel_id=1, source_target_pairs={{0,8},{8,0},{16,24},{24,16},{1,9},{9,1},{17,25},{25,17},{2,10},{10... | collective-permute-start | bytes 884744 | tf_op jit(solution)/shard_map/ppermute | solution.py:625
  214.4 10.8 %collective-permute-start.45 = (bf16[2304,128]{1,0:T(8,128)(2,1)S(1)}, bf16[2304,128]{1,0:T(8,128)(2,1)S(1)}, u32[]{:S(2)}, u32[]{:S(2)}) collective-permute-start(bf16[2304,128]{1,0:T(8,128)(2,1)S(1)} %pad_maximum_fusion.7), channel_id=1, source_target_pairs={{0,1},{1,0},{2,3},{3,2},{4,5},{5,4},{6,7},{7,6},{8,9},{9,8},{10,11... | collective-permute-start | bytes 1769480 | tf_op jit(solution)/shard_map/ppermute | solution.py:625
  229.7 5.9 %collective-permute-start.46 = (f32[8,128]{1,0:T(8,128)S(1)}, f32[8,128]{1,0:T(8,128)S(1)}, u32[]{:S(2)}, u32[]{:S(2)}) collective-permute-start(f32[8,128]{1,0:T(8,128)S(1)} %get-tuple-element.175.refs_0_), channel_id=1, source_target_pairs={{0,2},{2,0},{4,6},{6,4},{1,3},{3,1},{5,7},{7,5},{8,10},{10,8},{12,... | collective-permute-start | bytes 12296 | tf_op jit(solution)/shard_map/ppermute | solution.py:625
  230.8 4.8 %collective-permute-start.47 = (f32[8,128]{1,0:T(8,128)S(1)}, f32[8,128]{1,0:T(8,128)S(1)}, u32[]{:S(2)}, u32[]{:S(2)}) collective-permute-start(f32[8,128]{1,0:T(8,128)S(1)} %get-tuple-element.175.refs_0_), channel_id=1, source_target_pairs={{0,4},{2,6},{4,0},{6,2},{1,5},{3,7},{5,1},{7,3},{8,12},{10,14},{12... | collective-permute-start | bytes 12296 | tf_op jit(solution)/shard_map/ppermute | solution.py:625
  (53 other events, 355.1 us)

commit v4 on v3

--- a/solution.py
+++ b/solution.py
@@ -160,8 +160,8 @@
 
 
 def first_kernel(
-    groups, place_ref, images_ref, masks_ref, weight_ref, params_ref, head_ref,
-    send_refs, stats_ref, own_mask_ref, mask_ref, inputs_ref, low_ref, sum_ref, wide_ref, arrived,
+    groups, place_ref, images_ref, masks_ref, weight_ref,
+    sum_ref, all_mask_ref, stats_ref, own_mask_ref, mask_ref, inputs_ref, low_ref, wide_ref, arrived,
 ):
     count = masks_ref.shape[1]
     part = count // groups
@@ -174,11 +174,17 @@
         copy.start()
     fill_mask(masks_ref, mask_ref)
     fill_inputs(images_ref, mask_ref, inputs_ref)
+    all_mask_ref[...] = mask_ref[...].astype(BF)
+    all_mask_ref.send()
+    for pixel in range(PIX):
+        own = pl.multiple_of(pixel * count + me * part, part)
+        own_mask_ref[pixel * part : (pixel + 1) * part, :] = mask_ref[pl.ds(own, part), :]
+    own_mask_ref.send()
     for tap in range(TAPS):
         if tap % 3 == 0:
             copies[tap // 3].wait()
         low_ref[:, tap * LANES : (tap + 1) * LANES] = wide_ref[tap].astype(BF)
-    sum_ref[...] = jnp.zeros_like(sum_ref)
+    sum_ref[...] = jnp.zeros(sum_ref.shape, F32)
     for tap in range(0, TAPS, 2):
         taps = min(2, TAPS - tap)
         product = matmul(inputs_ref[...], low_ref[:, tap * LANES : (tap + taps) * LANES])
@@ -187,6 +193,7 @@
                 sum_ref[to_row : to_row + length, :] += product[
                     from_row : from_row + length, nth * LANES : (nth + 1) * LANES
                 ]
+    sum_ref.send()
     mask = mask_ref[...]
     total = sum_ref[...]
     masked = total * mask
@@ -195,57 +202,70 @@
             jnp.sum(masked, axis=0, keepdims=True),
             jnp.sum(masked * total, axis=0, keepdims=True),
             jnp.sum(mask, axis=0, keepdims=True),
-            params_ref[0:2, :],
-            jnp.zeros((3, LANES), F32),
+            jnp.zeros((5, LANES), F32),
         ],
         axis=0,
     )
     stats_ref[...] = jnp.broadcast_to(tile[None], stats_ref.shape)
-    head = jnp.concatenate([head_ref[...], jnp.zeros((16 - CLASSES, LANES), F32)], axis=0).astype(BF)
+
+
+def first_norm_kernel(
+    place_ref, got_ref, first_ref, mask_ref, params_ref, head_ref, send_refs, kept_ref, hidden_ref, scaled_ref
+):
+    total = total_of(got_ref)
+    kept = total[2:3, :]
+    mean = total[0:1, :] / kept
+    rstd = lax.rsqrt(total[1:2, :] / kept - mean * mean + EPS_NORM)
+    kept_ref[...] = jnp.broadcast_to(kept, kept_ref.shape)
+    gain, shift = params_ref[0:1, :], params_ref[1:2, :]
+    count = first_ref.shape[0] // PIX
+    part = count // len(send_refs)
+    scaled = (first_ref[...] - mean) * rstd
+    value, _ = gelu_parts(gain * scaled + shift)
+    hidden_ref[...] = (value * mask_ref[...].astype(F32)).astype(BF)
+    scaled_ref[...] = scaled.astype(BF)
+    lines = [head_ref[...]]
+    for line in (rstd, gain, shift):
+        high = line.astype(BF).astype(F32)
+        lines += [high, line - high]
+    extra = jnp.concatenate(lines, axis=0).astype(BF)
+    rows = PIX * part
     for step, send_ref in enumerate(send_refs):
-        send_ref[PIX * part : PIX * part + 16, :] = head
         for pixel in range(PIX):
-            base = pl.multiple_of(pixel * count + (me ^ step) * part, part)
-            send_ref[pixel * part : (pixel + 1) * part, :] = sum_ref[pl.ds(base, part), :].astype(BF)
-    for pixel in range(PIX):
-        own = pl.multiple_of(pixel * count + me * part, part)
-        own_mask_ref[pixel * part : (pixel + 1) * part, :] = mask_ref[pl.ds(own, part), :]
-
-
-def first_norm_kernel(sizes, place_ref, slot_refs, got_ref, mask_ref, hidden_ref, first_ref, norm_ref, head_ref):
-    rows = mask_ref.shape[0]
-    count_dp, groups, count_cin = sizes
-    me = place_ref[0]
-    tiles = []
-    for group in range(groups):
-        total = None
-        for far in range(count_dp):
-            for near in range(count_cin):
-                tile = got_ref[(far * groups + group) * count_cin + near]
-                total = tile if total is None else total + tile
-        tiles.append((total, got_ref[group * count_cin]))
-    kept = tiles[0][0][2:3, :]
-    for group, (total, single) in enumerate(tiles):
-        lanes = slice(group * LANES, (group + 1) * LANES)
-        mean = total[0:1, :] / kept
-        norm_ref[0:1, lanes] = mean
-        norm_ref[1:2, lanes] = lax.rsqrt(total[1:2, :] / kept - mean * mean + EPS_NORM)
-        norm_ref[2:4, lanes] = single[3:5, :]
-        norm_ref[4:5, lanes] = kept
-        norm_ref[5:8, lanes] = jnp.zeros((3, LANES), F32)
+            base = pl.ds(pl.multiple_of(pixel * count + (place_ref[0] ^ step) * part, part), part)
+            send_ref[pixel * part : (pixel + 1) * part, :] = hidden_ref[base, :]
+            send_ref[rows + pixel * part : rows + (pixel + 1) * part, :] = scaled_ref[base, :]
+        send_ref[2 * rows : 2 * rows + 16, :] = extra
+
+
+def hidden_kernel(place_ref, slot_refs, mask_ref, hidden_ref):
+    rows = hidden_ref.shape[0]
     for step, slot_ref in enumerate(slot_refs):
-        lanes = pl.ds(pl.multiple_of((me ^ step) * LANES, LANES), LANES)
-        head_ref[:, lanes] = slot_ref[rows : rows + 16, :]
-        low = slot_ref[0:rows, :]
-        scaled = (low.astype(F32) - norm_ref[0:1, lanes]) * norm_ref[1:2, lanes]
-        value, _ = gelu_parts(norm_ref[2:3, lanes] * scaled + norm_ref[3:4, lanes])
-        hidden_ref[:, lanes] = (value * mask_ref[...]).astype(BF)
-        first_ref[:, lanes] = low
+        lanes = pl.ds(pl.multiple_of((place_ref[0] ^ step) * LANES, LANES), LANES)
+        hidden_ref[:, lanes] = slot_ref[0:rows, :]
+    hidden_ref[:, len(slot_refs) * LANES :] = mask_ref[...].astype(BF)
+
+
+def gather_kernel(place_ref, slot_refs, kept_ref, scaled_ref, norm_ref, head_ref):
+    rows = scaled_ref.shape[0]
+    norm_ref[0:1, :] = jnp.zeros((1, norm_ref.shape[1]), F32)
+    norm_ref[5:8, :] = jnp.zeros((3, norm_ref.shape[1]), F32)
+    for step, slot_ref in enumerate(slot_refs):
+        lanes = pl.ds(pl.multiple_of((place_ref[0] ^ step) * LANES, LANES), LANES)
+        scaled_ref[:, lanes] = slot_ref[rows : 2 * rows, :]
+        extra = slot_ref[2 * rows : 2 * rows + 16, :].astype(F32)
+        line = lax.broadcasted_iota(jnp.int32, (16, LANES), 0)
+        head_ref[:, lanes] = jnp.where(line < CLASSES, extra, 0.0).astype(BF)
+        for at in range(3):
+            norm_ref[at + 1 : at + 2, lanes] = (
+                extra[CLASSES + 2 * at : CLASSES + 2 * at + 1, :] + extra[CLASSES + 2 * at + 1 : CLASSES + 2 * at + 2, :]
+            )
+        norm_ref[4:5, lanes] = kept_ref[0:1, :]
 
 
 def second_kernel(
-    place_ref, own_ref, other_ref, own_mask_ref, other_mask_ref, params_ref, basis_ref, slot_refs,
-    mine_ref, theirs_ref, stats_ref, left_refs, wide_ref, inputs_ref, weight_ref, sum_ref, arrived,
+    place_ref, own_ref, other_ref, params_ref, slot_refs,
+    mine_ref, theirs_ref, stats_ref, inputs_ref, weight_ref, sum_ref, arrived,
 ):
     me = place_ref[0]
     rows = own_ref.shape[0]
@@ -256,12 +276,9 @@
         span = pl.ds(pl.multiple_of((me ^ step) * depth, depth), depth)
         copies.append(pltpu.make_async_copy(slot_ref, weight_ref.at[:, span, :], arrived.at[step]))
         copies[-1].start()
-    inputs_ref[0:rows, :] = own_ref[...]
-    wide_ref[...] = matmul(own_ref[...], basis_ref[...])
-    send_columns(me, wide_ref, left_refs)
-    for left_ref in left_refs:
-        left_ref.send()
-    inputs_ref[rows : 2 * rows, :] = other_ref[...]
+    channels = inputs_ref.shape[1]
+    inputs_ref[0:rows, :] = own_ref[:, 0:channels]
+    inputs_ref[rows : 2 * rows, :] = other_ref[:, 0:channels]
     sum_ref[...] = jnp.zeros_like(sum_ref)
     for copy in copies:
         copy.wait()
@@ -277,9 +294,9 @@
     lines = [[], []]
     for lane in range(0, half, LANES):
         first = square = None
-        for base, mask_ref in ((0, own_mask_ref), (rows, other_mask_ref)):
+        for base, ref in ((0, own_ref), (rows, other_ref)):
             total = sum_ref[base : base + rows, lane : lane + LANES]
-            masked = total * mask_ref[...]
+            masked = total * ref[:, channels : channels + LANES].astype(F32)
             first_part = jnp.sum(masked, axis=0, keepdims=True)
             square_part = jnp.sum(masked * total, axis=0, keepdims=True)
             first = first_part if first is None else first + first_part
@@ -367,8 +384,7 @@
     return total
 
 
-def norm_back(values, dz, norm, mask, gain_grad, shift_grad):
-    scaled = (values - norm[0:1, :]) * norm[1:2, :]
+def norm_back(scaled, dz, norm, mask, gain_grad, shift_grad):
     gain = norm[2:3, :]
     return norm[1:2, :] * (
         gain * dz - mask * (gain / norm[4:5, :]) * (shift_grad + scaled * gain_grad)
@@ -376,8 +392,8 @@
 
 
 def second_back_kernel(
-    place_ref, dz_ref, wide_ref, norm_ref, got_ref, mask_ref, basis_ref, first_ref, norm_first_ref, head_ref, near_refs, far_refs,
-    right_ref, sums_out_ref, dz_first_ref, sums_ref, grad_ref, weight_ref, sum_ref, arrived,
+    place_ref, dz_ref, wide_ref, norm_ref, got_ref, mask_ref, first_ref, norm_first_ref, head_ref, basis_ref, near_refs, far_refs,
+    grad_ref, sums_out_ref, sums_ref, send_refs, part_ref, weight_ref, sum_ref, arrived,
 ):
     me, side = place_ref[0], place_ref[1]
     depth, half = near_refs[0].shape[1:]
@@ -396,12 +412,12 @@
     mask = mask_ref[...]
     for group in range(groups):
         lanes = slice(group * LANES, (group + 1) * LANES)
+        norm = norm_ref[:, lanes]
         grad_ref[:, lanes] = norm_back(
-            wide_ref[:, lanes], dz_ref[:, lanes], norm_ref[:, lanes], mask,
+            (wide_ref[:, lanes] - norm[0:1, :]) * norm[1:2, :], dz_ref[:, lanes], norm, mask,
             total[group : group + 1, :], total[groups + group : groups + group + 1, :],
         ).astype(BF)
-    right_ref[...] = jnp.transpose(matmul(grad_ref[...], basis_ref[...])).astype(BF)
-    right_ref.send()
+    grad_ref.send()
     sums_out_ref.send()
     for copy in copies:
         copy.wait()
@@ -417,13 +433,14 @@
     for lane in range(0, channels, LANES):
         lanes = slice(lane, lane + LANES)
         norm = norm_first_ref[:, lanes]
-        scaled = (first_ref[:, lanes].astype(F32) - norm[0:1, :]) * norm[1:2, :]
+        scaled = first_ref[:, lanes].astype(F32)
         _, slope = gelu_parts(norm[2:3, :] * scaled + norm[3:4, :])
         dz = slope * mask * sum_ref[:, lanes]
-        dz_first_ref[:, lanes] = dz
+        part_ref[:, lanes] = (norm[1:2, :] * norm[2:3, :] * dz).astype(BF)
         gains.append(jnp.sum(dz * scaled, axis=0, keepdims=True))
         shifts.append(jnp.sum(dz, axis=0, keepdims=True))
-    dz_first_ref.send()
+    sum_ref[...] = matmul(part_ref[...], basis_ref[...])
+    send_columns(me, sum_ref, send_refs)
     count_dp, _, count_cin = sums_ref.shape[:3]
     for group in range(groups):
         tile = jnp.concatenate(gains + shifts + [head_ref[group], jnp.zeros((8, LANES), F32)], axis=0)
@@ -433,29 +450,70 @@
                 sums_ref[far, group, near] = tile
 
 
-def first_back_kernel(
-    place_ref, dz_ref, first_ref, norm_ref, got_ref, mask_ref, basis_ref, old_refs,
-    send_refs, sums_ref, small_ref, grad_ref, product_ref,
+def first_products_kernel(
+    place_ref, got_ref, norm_ref, mask_ref, basis_ref, old_refs, big_refs, part_refs, scaled_refs,
+    out_ref, sums_ref, small_ref, left_ref, right_ref, slot_ref, column_ref, mask_slot_ref,
 ):
+    me = place_ref[0]
+    rows, width = part_refs[0].shape
+    part = rows // PIX
+    count = mask_ref.shape[0] // PIX
     whole = got_ref[0].astype(F32)
     for source in range(1, got_ref.shape[0]):
         whole = whole + got_ref[source].astype(F32)
-    total = whole[0:8, :]
-    sums_ref[...] = total
+    sums_ref[...] = whole[0:8, :]
     small_ref[...] = jnp.zeros(small_ref.shape, F32)
     small_ref[8:24, :] = whole[8:24, :]
     for at, row in enumerate((24, 28, 32, 48, 64, 65)):
-        rows, lanes = old_refs[at].shape
-        small_ref[row : row + rows, 0:lanes] = old_refs[at][...]
-    groups = total.shape[0] // 2
+        lines, lanes = old_refs[at].shape
+        small_ref[row : row + lines, 0:lanes] = old_refs[at][...]
+    groups = len(part_refs)
+    column_ref[...] = basis_ref[:, pl.ds(pl.multiple_of(me * width, width), width)]
+    rates, shifts = [], []
     for group in range(groups):
         lanes = slice(group * LANES, (group + 1) * LANES)
-        grad_ref[:, lanes] = norm_back(
-            first_ref[:, lanes].astype(F32), dz_ref[:, lanes], norm_ref[:, lanes], mask_ref[...],
-            total[group : group + 1, :], total[groups + group : groups + group + 1, :],
+        scale = norm_ref[1:2, lanes] * norm_ref[2:3, lanes] / norm_ref[4:5, lanes]
+        rates.append(scale * whole[group : group + 1, :])
+        shifts.append(scale * whole[groups + group : groups + group + 1, :])
+    rate = jnp.concatenate(rates, axis=1)
+    shift = jnp.broadcast_to(jnp.concatenate(shifts, axis=1), (8, groups * LANES))
+    fixed = matmul(shift, column_ref[...].astype(F32), NN, PRECISE)[0:1, :]
+    for step in range(groups):
+        for pixel in range(PIX):
+            base = pl.ds(pl.multiple_of(pixel * count + (me ^ step) * part, part), part)
+            mask_slot_ref[pixel * part : (pixel + 1) * part, :] = mask_ref[base, :]
+        moved = matmul((scaled_refs[step][...].astype(F32) * rate).astype(BF), column_ref[...])
+        slot_ref[step] = (
+            part_refs[step][...].astype(F32) - mask_slot_ref[...].astype(F32) * (fixed + moved)
         ).astype(BF)
-    product_ref[...] = matmul(grad_ref[...], basis_ref[...])
-    send_columns(place_ref[0], product_ref, send_refs)
+    taps_kernel(-1, big_refs, [slot_ref.at[step] for step in range(groups)], out_ref, left_ref, right_ref)
+
+
+def left_second_kernel(place_ref, norm_ref, mask_ref, basis_ref, scaled_refs, left_refs, column_ref, wide_ref):
+    me = place_ref[0]
+    rows, width = left_refs[0].shape
+    part = rows // PIX
+    count = mask_ref.shape[0] // PIX
+    column_ref[...] = basis_ref[:, pl.ds(pl.multiple_of(me * width, width), width)]
+    for step, scaled_ref in enumerate(scaled_refs):
+        mask = jnp.concatenate(
+            [
+                mask_ref[pl.ds(pl.multiple_of(pixel * count + (me ^ step) * part, part), part), :]
+                for pixel in range(PIX)
+            ],
+            axis=0,
+        ).astype(F32)
+        for lane in range(0, wide_ref.shape[1], LANES):
+            lanes = slice(lane, lane + LANES)
+            value, _ = gelu_parts(
+                norm_ref[2:3, lanes] * scaled_ref[:, lanes].astype(F32) + norm_ref[3:4, lanes]
+            )
+            wide_ref[:, lanes] = (value * mask).astype(BF)
+        left_refs[step][...] = matmul(wide_ref[...], column_ref[...]).astype(BF)
+
+
+def right_kernel(grad_ref, basis_ref, right_ref):
+    right_ref[...] = jnp.transpose(matmul(grad_ref[...], basis_ref[...])).astype(BF)
 
 
 def send_columns(me, product_ref, send_refs):
@@ -523,6 +581,15 @@
         if turned:
             coeff = jnp.transpose(coeff)
         out_ref[tap] = SCALE_DECAY * scales_ref[tap] + (1.0 - SCALE_DECAY) * coeff * coeff
+
+
+def wide_ratio_kernel(place_ref, coeff_ref, scales_ref, scales_out_ref, ratio_ref):
+    half = ratio_ref.shape[0]
+    rows = pl.ds(pl.multiple_of(place_ref[1] * half, half), half)
+    coeff = coeff_ref[...].astype(F32)
+    scales_out_ref[...] = SCALE_DECAY * scales_ref[...] + (1.0 - SCALE_DECAY) * coeff * coeff
+    scales_out_ref.send()
+    ratio_ref[...] = (coeff_ref[rows, :].astype(F32) / (scales_out_ref[rows, :] + DAMPING)).astype(BF)
 
 
 def add_squares(total, values):
@@ -736,26 +803,28 @@
     bias_row = jnp.pad(head_b, (0, LANES - CLASSES))[None]
 
     flat_images = images.reshape(PIX * count, channels)
-    sends = [shape((rows + 16, width), BF)] * groups
-    *first_sends, stats, mask = call(
-        lambda *refs: first_kernel(groups, *refs[:6], refs[6 : 6 + groups], *refs[6 + groups :]),
-        sends + [tile, shape((rows, LANES), F32)],
-        [place, flat_images, masks, w_first, norm_params, head_w.T],
+    first_out, all_mask, stats, mask = call(
+        functools.partial(first_kernel, groups),
+        [
+            shape((PIX * count, width), F32),
+            shape((PIX * count, LANES), BF),
+            shape((sizes[0] * sizes[2], 8, LANES), F32),
+            shape((rows, LANES), F32),
+        ],
+        [place, flat_images, masks, w_first],
         [
             pltpu.VMEM((PIX * count, LANES), F32),
             pltpu.VMEM((PIX * count, channels), BF),
             pltpu.VMEM((channels, TAPS * width), BF),
-            pltpu.VMEM((PIX * count, width), F32),
             pltpu.VMEM((TAPS, channels, width), F32),
             pltpu.SemaphoreType.DMA((3,)),
         ],
-        near=(1, 2, 4, 5),
+        near=(1, 2),
         raw=(3,),
         room=56,
         flops=2 * PIX * count * channels * width * TAPS,
     )
-    first_slots = exchanged(first_sends, "cout")
-    got = every_device(after(stats, *first_slots))
+    got = lax.all_to_all(stats, ("dp", "cin"), 0, 0, tiled=True)
     (left_turned,) = call(
         left_first_kernel,
         [shape((groups, channels, rows), BF)],
@@ -770,39 +839,61 @@
     )
     near_weights = [piece]
     for step in range(1, groups):
-        ready = piece if step < groups - 1 else after(piece, *first_slots)
+        ready = piece if step < groups - 1 else after(piece, stats)
         near_weights.append(swap(ready, "cout", step))
-    other_mask = swap(mask, "cin", 1)
-    first_mask = after(mask, left_turned, *near_weights[1:-1], *bases_all)
-    hidden, first_out, norm_first, head_full = call(
-        lambda place_ref, *refs: first_norm_kernel(sizes, place_ref, refs[:groups], *refs[groups:]),
-        [shape(wide, BF), shape(wide, BF), shape((8, channels), F32), shape((16, channels), BF)],
-        [place, *first_slots, got, first_mask],
+    first_mask = after(all_mask, left_turned, *near_weights[1:-1], *bases_all)
+    *first_sends, kept = call(
+        lambda *refs: first_norm_kernel(*refs[:6], refs[6 : 6 + groups], *refs[6 + groups :]),
+        [shape((2 * rows + 16, width), BF)] * groups + [shape((8, LANES), F32)],
+        [place, got, first_out, first_mask, norm_params, head_w.T],
+        [pltpu.VMEM((PIX * count, LANES), BF), pltpu.VMEM((PIX * count, LANES), BF)],
+        near_out=tuple(range(groups)),
+    )
+    def in_slots(values):
+        return jnp.concatenate(
+            [lax.dynamic_slice_in_dim(values, (me ^ step) * width, width, 1) for step in range(groups)], 1
+        )
+
+    def basis_rows(basis):
+        return in_slots(lax.dynamic_slice_in_dim(basis, me * width, width, 0))
+
+    scales_turned = batch_rows(
+        jnp.swapaxes(after(scales_second, kept), 1, 2).reshape(TAPS * channels, width)
+    )
+    rows_first = basis_rows(after(basis_out_first, kept))
+    rows_second = basis_rows(after(basis_in_second, kept))
+    kept = after(kept, scales_turned, rows_first, rows_second)
+    first_slots = exchanged(first_sends, "cout")
+    (hidden,) = call(
+        lambda *refs: hidden_kernel(refs[0], refs[1 : 1 + groups], *refs[1 + groups :]),
+        [shape((rows, channels + LANES), BF)],
+        [place, *first_slots, after(mask, kept)],
+        near=tuple(range(1, 1 + groups)),
         near_out=(0,),
     )
     other_hidden = swap(hidden, "cin", 1)
-    mine, theirs, stats, *left_sends = call(
-        lambda *refs: second_kernel(
-            *refs[:7], refs[7 : 7 + groups], *refs[7 + groups : 10 + groups],
-            refs[10 + groups : 10 + 2 * groups], *refs[10 + 2 * groups :],
-        ),
-        [shape((rows, half), F32), shape((rows, half), F32), tile] + [shape((rows, width), BF)] * groups,
-        [place, hidden, other_hidden, mask, other_mask, norm_params, basis_in_second, *near_weights],
+    mine, theirs, stats = call(
+        lambda *refs: second_kernel(*refs[:4], refs[4 : 4 + groups], *refs[4 + groups :]),
+        [shape((rows, half), F32), shape((rows, half), F32), tile],
+        [place, hidden, other_hidden, norm_params, *near_weights],
         [
-            pltpu.VMEM(wide, F32),
             pltpu.VMEM((2 * rows, channels), BF),
             pltpu.VMEM((TAPS, channels, half), BF),
             pltpu.VMEM((2 * rows, half), F32),
             pltpu.SemaphoreType.DMA((groups,)),
         ],
         near=(1, 2),
-        raw=tuple(range(7, 7 + groups)),
+        raw=tuple(range(4, 4 + groups)),
         flops=4 * rows * channels * half * TAPS,
     )
+    scaled_first, norm_first, head_full = call(
+        lambda *refs: gather_kernel(refs[0], refs[1 : 1 + groups], *refs[1 + groups :]),
+        [shape(wide, BF), shape((8, channels), F32), shape((16, channels), BF)],
+        [place, *first_slots, after(kept, mine)],
+    )
     from_other = swap(theirs, "cin", 1)
-    got = every_device(stats)
+    got_second = every_device(stats)
     far_weights = [swap(after(slot, mine), "cin", 1) for slot in near_weights]
-    left_slots = exchanged(left_sends, "cout")
     head_mask = after(mask, *far_weights)
     second_out, norm_second, dz_second, sums, head_blocks = call(
         functools.partial(head_kernel, sizes),
@@ -813,7 +904,7 @@
             tile,
             shape((groups, 16, width), F32),
         ],
-        [place, mine, from_other, got, norm_first, head_mask, head_full, bias_row, own_labels],
+        [place, mine, from_other, got_second, norm_first, head_mask, head_full, bias_row, own_labels],
         [
             pltpu.VMEM(wide, F32),
             pltpu.VMEM((part, channels), F32),
@@ -821,14 +912,16 @@
         ],
     )
     got = every_device(sums)
-    right_turned, sums_second, dz_first, sums = call(
+    scaled_slots = gathered(after(scaled_first, got_second), "cout")
+    grad_second, sums_second, sums, *right_sends = call(
         lambda *refs: second_back_kernel(
-            *refs[:10], refs[10 : 10 + groups], refs[10 + groups : 10 + 2 * groups], *refs[10 + 2 * groups :]
+            *refs[:10], refs[10 : 10 + groups], refs[10 + groups : 10 + 2 * groups],
+            *refs[10 + 2 * groups : 13 + 2 * groups], refs[13 + 2 * groups : 13 + 3 * groups], *refs[13 + 3 * groups :]
         ),
-        [shape((channels, rows), BF), shape((8, LANES), F32), shape(wide, F32), shape(sizes + (32, LANES), BF)],
+        [shape(wide, BF), shape((8, LANES), F32), shape(sizes + (32, LANES), BF)] + [shape((rows, width), BF)] * groups,
         [
-            place, dz_second, second_out, norm_second, got, after(mask, *left_slots), basis_out_second, first_out, norm_first, head_blocks,
-            *near_weights, *far_weights,
+            place, dz_second, second_out, norm_second, got, after(mask, *scaled_slots), scaled_first,
+            norm_first, head_blocks, basis_out_first, *near_weights, *far_weights,
         ],
         [
             pltpu.VMEM(wide, BF),
@@ -839,7 +932,16 @@
         raw=tuple(range(10, 10 + 2 * groups)),
         flops=2 * rows * channels * channels * TAPS,
     )
-    right_slots = gathered(right_turned, "cout")
+    left_slots = call(
+        lambda *refs: left_second_kernel(*refs[:4], refs[4 : 4 + groups], refs[4 + groups : 4 + 2 * groups], *refs[4 + 2 * groups :]),
+        [shape((rows, width), BF)] * groups,
+        [place, norm_first, after(all_mask, sums_second), basis_in_second, *scaled_slots],
+        [pltpu.VMEM((channels, width), BF), pltpu.VMEM(wide, BF)],
+    )
+    (right_turned,) = call(
+        right_kernel, [shape((channels, rows), BF)], [grad_second, basis_out_second], scalars=0
+    )
+
     def products(sign, big, small, near=()):
         (out,) = call(
             lambda *refs: taps_kernel(sign, refs[:groups], refs[groups : 2 * groups], *refs[2 * groups :]),
@@ -857,17 +959,11 @@
         )
         return out
 
+    right_parts = exchanged(right_sends, "cout")
     got = every_device(sums.reshape(devices, 32, LANES))
+    right_slots = gathered(after(right_turned, got), "cout")
     orders = [(axis, bit) for axis in ("cin", "dp") for bit in bits_of(axis)]
     small_old = [norm_mean, norm_square, head_w_mean.T, head_w_square.T, head_b_mean[None], head_b_square[None]]
-    *right_sends, sums_first, smalls = call(
-        lambda *refs: first_back_kernel(*refs[:7], refs[7:13], refs[13 : 13 + groups], *refs[13 + groups :]),
-        [shape((rows, width), BF)] * groups + [shape((8, LANES), F32), shape((72, LANES), F32)],
-        [place, dz_first, first_out, norm_first, got, after(mask, *right_slots), basis_out_first, *small_old],
-        [pltpu.VMEM(wide, BF), pltpu.VMEM(wide, F32)],
-        near_out=tuple(range(groups)),
-    )
-
     def hold(*values):
         def copy_in(*refs):
             arrived = refs[-1]
@@ -903,11 +999,10 @@
             room=16,
         )
 
-    def middle_of(ratio, basis):
-        slots = gathered(ratio, "cout")
+    def middle_of(slots, basis):
         (out,) = call(
             lambda basis_ref, *refs: middle_kernel(basis_ref, refs[:groups], refs[-1]),
-            [shape(ratio.shape, BF)],
+            [shape(slots[0].shape, BF)],
             [basis, *slots],
             scalars=0,
             near=tuple(range(groups + 1)),
@@ -917,56 +1012,72 @@
         return out
 
     near_steps = len(bits_of("cin"))
-    right_parts = exchanged(right_sends, "cout")
     left_parts = [left_turned[step] for step in range(groups)]
-    products_first = products(-1, left_parts, right_parts, tuple(range(groups, 2 * groups)))
+    products_first, sums_first, smalls = call(
+        lambda *refs: first_products_kernel(
+            *refs[:5], refs[5:11], *[refs[11 + at * groups : 11 + (at + 1) * groups] for at in range(3)],
+            *refs[11 + 3 * groups :]
+        ),
+        [shape((TAPS * channels, width), BF), shape((8, LANES), F32), shape((72, LANES), F32)],
+        [
+            place, after(got, right_turned, *left_slots), norm_first, all_mask, basis_out_first, *small_old, *left_parts, *right_parts, *scaled_slots,
+        ],
+        [
+            pltpu.VMEM((channels, groups * rows), BF),
+            pltpu.VMEM((groups * rows, TAPS * width), BF),
+            pltpu.VMEM((groups, rows, width), BF),
+            pltpu.VMEM((channels, width), BF),
+            pltpu.VMEM((rows, LANES), BF),
+        ],
+        near_out=(0,),
+        room=56,
+        flops=2 * groups * rows * channels * width * TAPS,
+    )
     terms_first = [products_first]
-    for order in orders[:near_steps]:
+    for order in orders[:-1]:
         terms_first = halved(joined(terms_first), *order)
     near_first = joined(terms_first)
-    products_second = products(1, [after(right_slots[0], near_first)] + right_slots[1:], left_slots)
-    terms_first, terms_second = [near_first], [products_second]
+    terms_first = halved(near_first, *orders[-1])
+
+    own_first = joined([after(terms_first[0], *right_slots), terms_first[1]])
+    coeff_first = doubled(own_first, *orders[-1])
+    products_second = products(1, [after(right_slots[0], own_first)] + right_slots[1:], left_slots)
+    terms_second = [products_second]
     for order in orders[:near_steps]:
         terms_second = halved(joined(terms_second), *order)
+    near_second = joined(terms_second)
+    terms_second = [near_second]
     for order in orders[near_steps:-1]:
-        terms_first = halved(joined(terms_first), *order)
-        terms_second = halved(after(joined(terms_second), *terms_first), *order)
-    filler = terms_first[1]
-    terms_first = halved(joined(terms_first), *orders[-1])
-
-    def in_slots(values):
-        return jnp.concatenate(
-            [lax.dynamic_slice_in_dim(values, (me ^ step) * width, width, 1) for step in range(groups)], 1
-        )
-
-    def basis_rows(basis):
-        return in_slots(lax.dynamic_slice_in_dim(basis, me * width, width, 0))
-
-    scales_turned = batch_rows(
-        jnp.swapaxes(after(scales_second, filler), 1, 2).reshape(TAPS * channels, width)
-    )
-    scales_chunk = batch_rows(after(scales_first, filler).reshape(TAPS * channels, width))
-    rows_first = basis_rows(after(basis_out_first, filler))
-    rows_second = basis_rows(after(basis_in_second, filler))
-    weights = hold(after(w_first, filler), w_second)
-    own_first, ratio_first = ratio_of(terms_first, after(scales_chunk, *weights, *terms_second))
-    means = hold(after(w_first_mean, own_first), w_second_mean)
-    terms_second = halved(after(joined(terms_second), own_first), *orders[-1])
-    own_second, ratio_second = ratio_of(terms_second, after(scales_turned, *means))
-    coeff_first = doubled(own_first, *orders[-1])
-    middle_first = middle_of(ratio_first, after(rows_first, own_second))
-    gathered_first = doubled(middle_first, *orders[-1])
-    middle_second = middle_of(ratio_second, after(rows_second, coeff_first, gathered_first))
+        terms_second = halved(joined(terms_second), *order)
+    terms_far = terms_second
+    for order in reversed(orders[near_steps:-1]):
+        coeff_first = doubled(after(coeff_first, near_second), *order)
+    coeff_first = batch_gather(coeff_first, ("cin",))
+    flat_scales = scales_first.reshape(TAPS * channels, width)
+    scales_first_new, ratio_first = call(
+        wide_ratio_kernel,
+        [shape(flat_scales.shape, F32), shape((TAPS * channels // 2, width), BF)],
+        [place, coeff_first, flat_scales],
+        near=(1, 2),
+        near_out=(1,),
+        room=16,
+    )
+    slots_first = gathered(ratio_first, "cout")
+    terms_second = halved(joined(terms_second), *orders[-1])
+    own_second, ratio_second = ratio_of(terms_second, after(scales_turned, ratio_first))
+    weights = hold(after(w_first, own_second), w_second)
+    coeff_second = doubled(own_second, *orders[-1])
+    middle_second = middle_of(gathered(ratio_second, "cout"), after(rows_second, coeff_second, ratio_first))
+    means = hold(after(w_first_mean, weights[0]), w_second_mean)
+    middle_first = middle_of(slots_first, after(rows_first, *means))
+    gathered_first = doubled(middle_first, "cin", 0)
     squares_old = hold(after(w_first_square, middle_second), w_second_square)
     gathered_second = doubled(middle_second, *orders[-1])
-    coeff_second = own_second
     for order in reversed(orders[near_steps:-1]):
-        gathered_first = doubled(gathered_first, *order)
-        gathered_second = doubled(after(gathered_second, gathered_first), *order)
-    gathered_first = batch_gather(gathered_first, ("cin",))
+        coeff_second = doubled(coeff_second, *order)
+        gathered_second = doubled(after(gathered_second, *squares_old), *order)
     gathered_second = batch_gather(gathered_second, ("cin",))
-    coeff_first = batch_gather(coeff_first, ("cin",), orders[near_steps:-1])
-    coeff_second = batch_gather(coeff_second)
+    coeff_second = batch_gather(coeff_second, ("cin",))
 
     def scales_of(turned, coeff, scales):
         spec = pl.BlockSpec((3,) + scales.shape[1:], lambda tap: (tap, 0, 0))
@@ -980,7 +1091,6 @@
         )(coeff, scales)
 
     scales_second_new = scales_of(True, coeff_second, scales_second)
-    scales_first_new = scales_of(False, coeff_first, scales_first)
 
     first_grad, second_grad, squares, small_grads = call(
         restore_kernel,
@@ -988,7 +1098,7 @@
         [
             place,
             basis_in_first,
-            after(gathered_first, coeff_first),
+            gathered_first,
             basis_out_second,
             gathered_second,
             sums_first,
@@ -1058,7 +1168,7 @@
         head_square_new.T,
         bias_mean_new[0],
         bias_square_new[0],
-        scales_first_new,
+        scales_first_new.reshape(scales_first.shape),
         scales_second_new,
     )
 

time: 246 us -> 236 us (0.959)
  waiting for transfers between devices: 84.7 us -> 76 us
  Pallas kernels: 60.6 us -> 69 us
  starting transfers between devices: 66 us -> 57.9 us
  local copies, waits for them, and re-layouts: 28.4 us -> 24 us
  other arithmetic: 3.99 us -> 6.61 us
    pallas_call x17 -> x20, Pallas kernels: 47.7 us -> 58.2 us  [call(): pl.pallas_call(body, out_shape=list(outs), in_specs=specs, out_specs=[pl....]
    ppermute x49 -> x46, starting transfers between devices: 49.8 us -> 42.3 us  [swap(): lax.ppermute(values, axis, [(here, here ^ step) for here in range(count)])]
    ppermute x49 -> x46, waiting for transfers between devices: 71.5 us -> 65.5 us  [swap(): lax.ppermute(values, axis, [(here, here ^ step) for here in range(count)])]
    all_to_all x4 -> x3, starting transfers between devices: 16.2 us -> 10.7 us  [every_device(): return lax.all_to_all(tiles, EVERY, 0, 0, tiled=True)]
    all_to_all x0 -> x1, starting transfers between devices: none -> 4.89 us  [local(): got = lax.all_to_all(stats, ('dp', 'cin'), 0, 0, tiled=True)]
    unnamed x96 -> x60, local copies, waits for them, and re-layouts: 14.4 us -> 10.3 us
    all_to_all x4 -> x3, waiting for transfers between devices: 13.2 us -> 10.5 us  [every_device(): return lax.all_to_all(tiles, EVERY, 0, 0, tiled=True)]
  transfers between devices with their start and end apart: 53 -> 50, of which waited for: 24 -> 21; matrix products, arithmetic and copies ran while one was open for 6% -> 6% of each run, Pallas kernels for 9% -> 16%
where the time goes in v4:
time: 236 us; the launch traced here: 235 us
  waiting for transfers between devices  76 us (32%)
  Pallas kernels  69 us (29%)
  starting transfers between devices  57.9 us (25%)
  local copies, waits for them, and re-layouts  24 us (10%)
  other arithmetic  6.61 us (3%)
    ppermute x46, waiting for transfers between devices, swap(): lax.ppermute(values, axis, [(here, here ^ step) for here in range(count)])  65.5 us
    pallas_call x20, Pallas kernels, call(): pl.pallas_call(body, out_shape=list(outs), in_specs=specs, out_specs=[pl....  58.2 us
    ppermute x46, starting transfers between devices, swap(): lax.ppermute(values, axis, [(here, here ^ step) for here in range(count)])  42.3 us
    all_to_all x3, starting transfers between devices, every_device(): return lax.all_to_all(tiles, EVERY, 0, 0, tiled=True)  10.7 us
    all_to_all x3, waiting for transfers between devices, every_device(): return lax.all_to_all(tiles, EVERY, 0, 0, tiled=True)  10.5 us
    unnamed x60, local copies, waits for them, and re-layouts  10.3 us
    pallas_call x1, Pallas kernels, local(): pl.pallas_call(update, grid=(TAPS,), in_specs=[pl.BlockSpec(memory_space=...  8.57 us
    all_to_all x1, starting transfers between devices, local(): got = lax.all_to_all(stats, ('dp', 'cin'), 0, 0, tiled=True)  4.89 us
  transfers between devices with their start and end apart: 50, of which 21 were waited for; matrix products, arithmetic and copies ran while one was open for 6% of the time, Pallas kernels for 16%

profile of v4, /device:TPU:0, one launch (start us, length us, event | category | flops | bytes accessed | tf_op | source)
XLA Modules:
  0.0 235.1 jit_solution(15788646235228940655)
XLA Ops:
  0.7 2.2 dynamic-slice_convert_fusion.refs_4_.refs_10_
  2.8 2.9 %collective-permute-start = (bf16[9,128,256]{2,1,0:T(8,128)(2,1)}, bf16[9,128,256]{2,1,0:T(8,128)(2,1)}, u32[]{:S(2)}, u32[]{:S(2)}) collective-permute-start(bf16[9,128,256]{2,1,0:T(8,128)(2,1)} %dynamic-slice_convert_fusion.refs_4_.refs_10_), channel_id=1, source_target_pairs={{0,2},{2,0},{4,6},{6,4},{1,3},{3,1},{5,7},{7,5},{8,10},{10,8},{12,... | collective-permute-start | bytes 1769480 | tf_op jit(solution)/shard_map/ppermute | solution.py:692
  7.9 5.6 %shard_map.340 = (f32[1024,128]{1,0:T(8,128)}, bf16[1024,128]{1,0:T(8,128)(2,1)}, f32[8,8,128]{2,1,0:T(8,128)}, f32[256,128]{1,0:T(8,128)}) custom-call(s32[2]{0:T(128)} %pad_add_fusion.refs_0_, bf16[1024,512]{1,0:T(8,128)(2,1)} %bitcast.75, s32[16,64]{1,0:T(8,128)} %refs_2_.3, f32[9,512,128]{2,1,0:T(8,128)} %refs_0_), custom_call_target="tpu_custom_call" | custom-call | flops 1207959552 | bytes 4362248 | tf_op jit(solution)/shard_map/pallas_call | solution.py:117
  13.5 4.9 %all-to-all-start = ((f32[8,8,128]{2,1,0:T(8,128)}), f32[8,8,128]{2,1,0:T(8,128)S(1)}, u32[]{:S(2)}, u32[]{:S(2)}) async-start(f32[8,8,128]{2,1,0:T(8,128)} %get-tuple-element.112), calls=%async_computation | async-start | bytes 65536 | tf_op jit(solution)/shard_map/all_to_all | solution.py:827
  22.6 1.7 shard_map.341
  24.9 3.7 %shard_map.342 = (bf16[528,128]{1,0:T(8,128)(2,1)}, bf16[528,128]{1,0:T(8,128)(2,1)}, bf16[528,128]{1,0:T(8,128)(2,1)}, bf16[528,128]{1,0:T(8,128)(2,1)}, f32[8,128]{1,0:T(8,128)}) custom-call(s32[2]{0:T(128)} %pad_add_fusion.refs_0_, f32[8,8,128]{2,1,0:T(8,128)} %copy-done.24, f32[1024,128]{1,0:T(8,128)} %get-tuple-element.113.refs_2_, ...), custom_call_target="tpu_custom_call" | custom-call | bytes 1371144 | tf_op jit(solution)/shard_map/pallas_call | solution.py:117
  34.1 1.9 copy.39
  36.0 1.7 constant_dynamic-slice_fusion.refs_2_
  38.7 2.5 %collective-permute-done.4.refs_4_ = bf16[528,128]{1,0:T(8,128)(2,1)} collective-permute-done((bf16[528,128]{1,0:T(8,128)(2,1)}, bf16[528,128]{1,0:T(8,128)(2,1)}, u32[]{:S(2)}, u32[]{:S(2)}) %collective-permute-start.4) | collective-permute-done | bytes 135200 | tf_op jit(solution)/shard_map/ppermute | solution.py:692
  41.2 2.8 %shard_map.343.refs_1_ = bf16[256,640]{1,0:T(8,128)(2,1)} custom-call(s32[2]{0:T(128)} %pad_add_fusion.refs_0_, bf16[528,128]{1,0:T(8,128)(2,1)} %get-tuple-element.119.refs_1_, bf16[528,128]{1,0:T(8,128)(2,1)} %collective-permute-done.2.refs_2_, bf16[528,128]{1,0:T(8,128)(2,1)} %collective-permute-done.3.refs_3_, ...), custom_call_target="tpu_custom_call" | custom-call | bytes 999432 | tf_op jit(solution)/shard_map/pallas_call | solution.py:117
  44.1 1.8 collective-permute-done.5.refs_2_
  46.6 5.0 %shard_map.344 = (f32[256,256]{1,0:T(8,128)}, f32[256,256]{1,0:T(8,128)}, f32[32,8,128]{2,1,0:T(8,128)}) custom-call(s32[2]{0:T(128)} %pad_add_fusion.refs_0_, bf16[256,640]{1,0:T(8,128)(2,1)} %shard_map.343.refs_1_, bf16[256,640]{1,0:T(8,128)(2,1)} %copy-done.25, f32[4,128]{1,0:T(4,128)} %refs_3_.3, ...), custom_call_target="tpu_custom_call" | custom-call | flops 1207959552 | bytes 3672072 | tf_op jit(solution)/shard_map/pallas_call | solution.py:117
  52.7 3.9 %all-to-all-start.1 = ((f32[32,8,128]{2,1,0:T(8,128)}), f32[32,8,128]{2,1,0:T(8,128)}, u32[]{:S(2)}, u32[]{:S(2)}) async-start(f32[32,8,128]{2,1,0:T(8,128)} %get-tuple-element.131), calls=%async_computation.1 | async-start | bytes 262144 | tf_op jit(solution)/shard_map/all_to_all | solution.py:718
  57.4 2.6 %shard_map.345 = (bf16[256,512]{1,0:T(8,128)(2,1)}, f32[8,512]{1,0:T(8,128)}, bf16[16,512]{1,0:T(8,128)(2,1)}) custom-call(s32[2]{0:T(128)} %pad_add_fusion.refs_0_, bf16[528,128]{1,0:T(8,128)(2,1)} %get-tuple-element.119.refs_1_, bf16[528,128]{1,0:T(8,128)(2,1)} %collective-permute-done.2.refs_2_, bf16[528,128]{1,0:T(8,128)(2,1)} %collective-permute-done.3.refs_3_, ...), custom_call_target="tpu_custom_call" | custom-call | bytes 839688 | tf_op jit(solution)/shard_map/pallas_call | solution.py:117
  60.0 4.9 %all-to-all-done.1.refs_3_ = f32[32,8,128]{2,1,0:T(8,128)} async-done(((f32[32,8,128]{2,1,0:T(8,128)}), f32[32,8,128]{2,1,0:T(8,128)}, u32[]{:S(2)}, u32[]{:S(2)}) %all-to-all-start.1) | async-done | bytes 131104 | tf_op jit(solution)/shard_map/all_to_all | solution.py:718
  66.3 2.1 collective-permute-start.14
  69.1 4.2 %shard_map.346 = (f32[256,512]{1,0:T(8,128)}, f32[8,512]{1,0:T(8,128)}, f32[256,512]{1,0:T(8,128)}, f32[32,8,128]{2,1,0:T(8,128)}, f32[4,16,128]{2,1,0:T(8,128)}) custom-call(s32[2]{0:T(128)} %pad_add_fusion.refs_0_, f32[256,256]{1,0:T(8,128)} %get-tuple-element.129.refs_1_, f32[256,256]{1,0:T(8,128)} %collective-permute-done.7.refs_2_, ...), custom_call_target="tpu_custom_call" | custom-call | bytes 2048584 | tf_op jit(solution)/shard_map/pallas_call | solution.py:117
  73.4 3.3 %all-to-all-start.2 = ((f32[32,8,128]{2,1,0:T(8,128)}), f32[32,8,128]{2,1,0:T(8,128)}, u32[]{:S(2)}, u32[]{:S(2)}) async-start(f32[32,8,128]{2,1,0:T(8,128)} %get-tuple-element.143), calls=%async_computation.2 | async-start | bytes 262144 | tf_op jit(solution)/shard_map/all_to_all | solution.py:718
  76.7 2.6 %collective-permute-done.13.refs_6_.refs_21_ = bf16[256,512]{1,0:T(8,128)(2,1)} collective-permute-done((bf16[256,512]{1,0:T(8,128)(2,1)}, bf16[256,512]{1,0:T(8,128)(2,1)}, u32[]{:S(2)}, u32[]{:S(2)}) %collective-permute-start.13) | collective-permute-done | bytes 262176 | tf_op jit(solution)/shard_map/ppermute | solution.py:692
  79.3 5.6 %all-to-all-done.2.refs_4_ = f32[32,8,128]{2,1,0:T(8,128)} async-done(((f32[32,8,128]{2,1,0:T(8,128)}), f32[32,8,128]{2,1,0:T(8,128)}, u32[]{:S(2)}, u32[]{:S(2)}) %all-to-all-start.2) | async-done | bytes 131104 | tf_op jit(solution)/shard_map/all_to_all | solution.py:718
  84.9 7.2 %shard_map.347 = (bf16[256,512]{1,0:T(8,128)(2,1)}, f32[8,128]{1,0:T(8,128)}, bf16[4,4,2,32,128]{4,3,2,1,0:T(8,128)(2,1)}, bf16[256,128]{1,0:T(8,128)(2,1)}, bf1...) custom-call(s32[2]{0:T(128)} %pad_add_fusion.refs_0_, ...), custom_call_target="tpu_custom_call" | custom-call | flops 1207959552 | bytes 7671816 | tf_op jit(solution)/shard_map/pallas_call | solution.py:117
  92.1 3.5 %all-to-all-start.3 = ((bf16[32,32,128]{2,1,0:T(8,128)(2,1)}), bf16[32,32,128]{2,1,0:T(8,128)(2,1)}, u32[]{:S(2)}, u32[]{:S(2)}) async-start(bf16[32,32,128]{2,1,0:T(8,128)(2,1)} %bitcast.88), calls=%async_computation.3 | async-start | bytes 524288 | tf_op jit(solution)/shard_map/all_to_all | solution.py:718
  100.1 2.2 shard_map.348.refs_0_
  102.4 4.4 %shard_map.349 = (bf16[256,128]{1,0:T(8,128)(2,1)}, bf16[256,128]{1,0:T(8,128)(2,1)}, bf16[256,128]{1,0:T(8,128)(2,1)}, bf16[256,128]{1,0:T(8,128)(2,1)}) custom-call(s32[2]{0:T(128)} %pad_add_fusion.refs_0_, f32[8,512]{1,0:T(8,128)} %get-tuple-element.133.refs_4_.refs_7_.refs_1_.refs_2_, bf16[1024,128]{1,0:T(8,128)(2,1)} %get-tuple-element.152.refs_3_.refs_2_, ...), custom_call_target="tpu_custom_call" | custom-call | bytes 2113544 | tf_op jit(solution)/shard_map/pallas_call | solution.py:117
  106.8 6.6 %shard_map.350 = (bf16[4608,128]{1,0:T(8,128)(2,1)}, f32[8,128]{1,0:T(8,128)}, f32[72,128]{1,0:T(8,128)}) custom-call(s32[2]{0:T(128)} %pad_add_fusion.refs_0_, bf16[32,32,128]{2,1,0:T(8,128)(2,1)} %all-to-all-done.3.refs_1_, f32[8,512]{1,0:T(8,128)} %get-tuple-element.133.refs_4_.refs_7_.refs_1_.refs_2_, ...), custom_call_target="tpu_custom_call" | custom-call | flops 1207959552 | bytes 4659288 | tf_op jit(solution)/shard_map/pallas_call | solution.py:117
  114.6 2.1 collective-permute-done.18
  123.7 4.3 %collective-permute-done.19 = bf16[1152,128]{1,0:T(8,128)(2,1)S(1)} collective-permute-done((bf16[1152,128]{1,0:T(8,128)(2,1)}, bf16[1152,128]{1,0:T(8,128)(2,1)S(1)}, u32[]{:S(2)}, u32[]{:S(2)}) %collective-permute-start.19) | collective-permute-done | bytes 294944 | tf_op jit(solution)/shard_map/ppermute | solution.py:692
  128.2 2.5 %collective-permute-start.23 = (bf16[576,128]{1,0:T(8,128)(2,1)S(1)}, bf16[576,128]{1,0:T(8,128)(2,1)S(1)}, u32[]{:S(2)}, u32[]{:S(2)}) collective-permute-start(bf16[576,128]{1,0:T(8,128)(2,1)S(1)} %get-tuple-element.245), channel_id=1, source_target_pairs={{0,16},{8,24},{16,0},{24,8},{1,17},{9,25},{17,1},{25,9},{2,18},{10... | collective-permute-start | bytes 442376 | tf_op jit(solution)/shard_map/ppermute | solution.py:692
  130.7 4.7 %collective-permute-done.21.refs_2_ = bf16[512,256]{1,0:T(8,128)(2,1)S(1)} collective-permute-done((bf16[512,256]{1,0:T(8,128)(2,1)}, bf16[512,256]{1,0:T(8,128)(2,1)S(1)}, u32[]{:S(2)}, u32[]{:S(2)}) %collective-permute-start.21) | collective-permute-done | bytes 262176 | tf_op jit(solution)/shard_map/ppermute | solution.py:692
  135.4 2.0 collective-permute-done.23
  138.0 4.0 %shard_map.351 = bf16[4608,128]{1,0:T(8,128)(2,1)} custom-call(bf16[512,256]{1,0:T(8,128)(2,1)} %shard_map.348.refs_0_, bf16[512,256]{1,0:T(8,128)(2,1)} %copy-done.26, bf16[512,256]{1,0:T(8,128)(2,1)} %copy-done.27, bf16[512,256]{1,0:T(8,128)(2,1)} %copy-done.28, bf16[256,128]{1,0:T(8,128)(2,1)} %get-tuple-element.153.refs_4_, ...), custom_call_target="tpu_custom_call" | custom-call | flops 1207959552 | bytes 2490368 | tf_op jit(solution)/shard_map/pallas_call | solution.py:117
  143.2 3.2 %collective-permute-done.27 = bf16[576,128]{1,0:T(8,128)(2,1)S(1)} collective-permute-done((bf16[576,128]{1,0:T(8,128)(2,1)S(1)}, bf16[576,128]{1,0:T(8,128)(2,1)S(1)}, u32[]{:S(2)}, u32[]{:S(2)}) %collective-permute-start.27) | collective-permute-done | bytes 147488 | tf_op jit(solution)/shard_map/ppermute | solution.py:692
  147.7 2.3 collective-permute-start.28
  150.1 7.8 %collective-permute-done.28 = bf16[1152,128]{1,0:T(8,128)(2,1)} collective-permute-done((bf16[1152,128]{1,0:T(8,128)(2,1)S(1)}, bf16[1152,128]{1,0:T(8,128)(2,1)}, u32[]{:S(2)}, u32[]{:S(2)}) %collective-permute-start.28) | collective-permute-done | bytes 294944 | tf_op jit(solution)/shard_map/ppermute | solution.py:692
  159.0 4.6 %collective-permute-done.25 = bf16[1152,128]{1,0:T(8,128)(2,1)S(1)} collective-permute-done((bf16[1152,128]{1,0:T(8,128)(2,1)S(1)}, bf16[1152,128]{1,0:T(8,128)(2,1)S(1)}, u32[]{:S(2)}, u32[]{:S(2)}) %collective-permute-start.25) | collective-permute-done | bytes 294944 | tf_op jit(solution)/shard_map/ppermute | solution.py:692
  166.5 2.9 %shard_map.352 = (f32[4608,128]{1,0:T(8,128)}, bf16[2304,128]{1,0:T(8,128)(2,1)S(1)}) custom-call(s32[2]{0:T(128)S(1)} %copy-done.17, bf16[4608,128]{1,0:T(8,128)(2,1)S(1)} %pad_maximum_fusion.refs_1_, f32[4608,128]{1,0:T(8,128)S(1)} %bitcast.74), custom_call_target="tpu_custom_call" | custom-call | bytes 6488072 | tf_op jit(solution)/shard_map/pallas_call | solution.py:117
  169.4 3.8 %collective-permute-done.26.refs_1_ = bf16[576,128]{1,0:T(8,128)(2,1)S(1)} collective-permute-done((bf16[576,128]{1,0:T(8,128)(2,1)S(1)}, bf16[576,128]{1,0:T(8,128)(2,1)S(1)}, u32[]{:S(2)}, u32[]{:S(2)}) %collective-permute-start.26) | collective-permute-done | bytes 147488 | tf_op jit(solution)/shard_map/ppermute | solution.py:692
  177.0 4.5 %collective-permute-done.34 = bf16[576,128]{1,0:T(8,128)(2,1)S(1)} collective-permute-done((bf16[576,128]{1,0:T(8,128)(2,1)S(1)}, bf16[576,128]{1,0:T(8,128)(2,1)S(1)}, u32[]{:S(2)}, u32[]{:S(2)}) %collective-permute-start.34) | collective-permute-done | bytes 147488 | tf_op jit(solution)/shard_map/ppermute | solution.py:692
  181.6 1.7 collective-permute-done.36.refs_3_
  183.6 2.8 %collective-permute-start.38 = (bf16[576,128]{1,0:T(8,128)(2,1)S(1)}, bf16[576,128]{1,0:T(8,128)(2,1)S(1)}, u32[]{:S(2)}, u32[]{:S(2)}) collective-permute-start(bf16[576,128]{1,0:T(8,128)(2,1)S(1)} %shard_map.357), channel_id=1, source_target_pairs={{0,16},{8,24},{16,0},{24,8},{1,17},{9,25},{17,1},{25,9},{2,18},{10... | collective-permute-start | bytes 442376 | tf_op jit(solution)/shard_map/ppermute | solution.py:692
  187.8 2.1 collective-permute-start.32
  195.4 6.5 %collective-permute-done.41 = bf16[1152,128]{1,0:T(8,128)(2,1)S(1)} collective-permute-done((bf16[1152,128]{1,0:T(8,128)(2,1)S(1)}, bf16[1152,128]{1,0:T(8,128)(2,1)S(1)}, u32[]{:S(2)}, u32[]{:S(2)}) %collective-permute-start.41) | collective-permute-done | bytes 294944 | tf_op jit(solution)/shard_map/ppermute | solution.py:692
  202.2 2.9 %collective-permute-done.39 = bf16[1152,128]{1,0:T(8,128)(2,1)S(1)} collective-permute-done((bf16[1152,128]{1,0:T(8,128)(2,1)S(1)}, bf16[1152,128]{1,0:T(8,128)(2,1)S(1)}, u32[]{:S(2)}, u32[]{:S(2)}) %collective-permute-start.39) | collective-permute-done | bytes 294944 | tf_op jit(solution)/shard_map/ppermute | solution.py:692
  205.3 7.0 %collective-permute-done.32.refs_4_ = bf16[2304,128]{1,0:T(8,128)(2,1)S(1)} collective-permute-done((bf16[2304,128]{1,0:T(8,128)(2,1)S(1)}, bf16[2304,128]{1,0:T(8,128)(2,1)S(1)}, u32[]{:S(2)}, u32[]{:S(2)}) %collective-permute-start.32) | collective-permute-done | bytes 589856 | tf_op jit(solution)/shard_map/ppermute | solution.py:692
  216.5 3.0 %shard_map.359 = (bf16[9,512,128]{2,1,0:T(8,128)(2,1)S(1)}, bf16[9,128,512]{2,1,0:T(8,128)(2,1)S(1)}, f32[8,128]{1,0:T(8,128)S(1)}, f32[72,128]{1,0:T(8,128)S(1)}) custom-call(s32[2]{0:T(128)S(1)} %copy-done.17, bf16[512,512]{1,0:T(8,128)(2,1)S(1)} %copy-done.12, bf16[4608,128]{1,0:T(8,128)(2,1)S(1)} %pad_maximum_fusion.1.refs_2_, ...), custom_call_target="tpu_custom_call" | custom-call | flops 1207959552 | bytes 5853192 | tf_op jit(solution)/shard_map/pallas_call | solution.py:117
  219.4 1.8 collective-permute-start.43
  223.1 2.2 shard_map.361
  226.3 8.6 %shard_map.360 = (f32[9,512,128]{2,1,0:T(8,128)}, f32[9,128,512]{2,1,0:T(8,128)}, f32[9,512,128]{2,1,0:T(8,128)}, f32[9,128,512]{2,1,0:T(8,128)}, f32[9,512,128]...) custom-call(f32[8,128]{1,0:T(8,128)S(1)} %get-tuple-element.184.refs, ...), custom_call_target="tpu_custom_call" | custom-call | tf_op jit(solution)/shard_map/pallas_call | solution.py:1140
  (177 shorter events, 56.5 us)
Async XLA Ops:
  2.8 21.4 %collective-permute-start = (bf16[9,128,256]{2,1,0:T(8,128)(2,1)}, bf16[9,128,256]{2,1,0:T(8,128)(2,1)}, u32[]{:S(2)}, u32[]{:S(2)}) collective-permute-start(bf16[9,128,256]{2,1,0:T(8,128)(2,1)} %dynamic-slice_convert_fusion.refs_4_.refs_10_), channel_id=1, source_target_pairs={{0,2},{2,0},{4,6},{6,4},{1,3},{3,1},{5,7},{7,5},{8,10},{10,8},{12,... | collective-permute-start | bytes 1769480 | tf_op jit(solution)/shard_map/ppermute | solution.py:692
  5.8 18.5 %collective-permute-start.1 = (bf16[9,128,256]{2,1,0:T(8,128)(2,1)}, bf16[9,128,256]{2,1,0:T(8,128)(2,1)}, u32[]{:S(2)}, u32[]{:S(2)}) collective-permute-start(bf16[9,128,256]{2,1,0:T(8,128)(2,1)} %dynamic-slice_convert_fusion.refs_4_.refs_10_), channel_id=1, source_target_pairs={{0,4},{2,6},{4,0},{6,2},{1,5},{3,7},{5,1},{7,3},{8,12},{10,14},{12... | collective-permute-start | bytes 1769480 | tf_op jit(solution)/shard_map/ppermute | solution.py:692
  13.5 10.8 %all-to-all-start = ((f32[8,8,128]{2,1,0:T(8,128)}), f32[8,8,128]{2,1,0:T(8,128)S(1)}, u32[]{:S(2)}, u32[]{:S(2)}) async-start(f32[8,8,128]{2,1,0:T(8,128)} %get-tuple-element.112), calls=%async_computation | async-start | bytes 65536 | tf_op jit(solution)/shard_map/all_to_all | solution.py:827
  18.4 25.7 %collective-permute-start.6 = (bf16[9,128,256]{2,1,0:T(8,128)(2,1)}, bf16[9,128,256]{2,1,0:T(8,128)(2,1)}, u32[]{:S(2)}, u32[]{:S(2)}) collective-permute-start(bf16[9,128,256]{2,1,0:T(8,128)(2,1)} %dynamic-slice_convert_fusion.refs_4_.refs_10_), channel_id=1, source_target_pairs={{0,6},{2,4},{4,2},{6,0},{1,7},{3,5},{5,3},{7,1},{8,14},{10,12},{12... | collective-permute-start | bytes 1769480 | tf_op jit(solution)/shard_map/ppermute | solution.py:692
  28.6 9.2 %collective-permute-start.2 = (bf16[528,128]{1,0:T(8,128)(2,1)}, bf16[528,128]{1,0:T(8,128)(2,1)}, u32[]{:S(2)}, u32[]{:S(2)}) collective-permute-start(bf16[528,128]{1,0:T(8,128)(2,1)} %get-tuple-element.120), channel_id=1, source_target_pairs={{0,2},{2,0},{4,6},{6,4},{1,3},{3,1},{5,7},{7,5},{8,10},{10,8},{12,... | collective-permute-start | bytes 405512 | tf_op jit(solution)/shard_map/ppermute | solution.py:692
  30.1 8.5 %collective-permute-start.3 = (bf16[528,128]{1,0:T(8,128)(2,1)}, bf16[528,128]{1,0:T(8,128)(2,1)}, u32[]{:S(2)}, u32[]{:S(2)}) collective-permute-start(bf16[528,128]{1,0:T(8,128)(2,1)} %get-tuple-element.121), channel_id=1, source_target_pairs={{0,4},{2,6},{4,0},{6,2},{1,5},{3,7},{5,1},{7,3},{8,12},{10,14},{12... | collective-permute-start | bytes 405512 | tf_op jit(solution)/shard_map/ppermute | solution.py:692
  31.6 9.6 %collective-permute-start.4 = (bf16[528,128]{1,0:T(8,128)(2,1)}, bf16[528,128]{1,0:T(8,128)(2,1)}, u32[]{:S(2)}, u32[]{:S(2)}) collective-permute-start(bf16[528,128]{1,0:T(8,128)(2,1)} %get-tuple-element.122), channel_id=1, source_target_pairs={{0,6},{2,4},{4,2},{6,0},{1,7},{3,5},{5,3},{7,1},{8,14},{10,12},{12... | collective-permute-start | bytes 405512 | tf_op jit(solution)/shard_map/ppermute | solution.py:692
  51.6 13.2 %collective-permute-start.11 = (bf16[9,128,256]{2,1,0:T(8,128)(2,1)}, bf16[9,128,256]{2,1,0:T(8,128)(2,1)}, u32[]{:S(2)}, u32[]{:S(2)}) collective-permute-start(bf16[9,128,256]{2,1,0:T(8,128)(2,1)} %collective-permute-done.6.refs_7_.refs_13_), channel_id=1, source_target_pairs={{0,1},{1,0},{2,3},{3,2},{4,5},{5,4},{6,7},{7,6},{8,9},{9,8},{10,11... | collective-permute-start | bytes 1769480 | tf_op jit(solution)/shard_map/ppermute | solution.py:692
  51.8 13.5 %collective-permute-start.10 = (bf16[9,128,256]{2,1,0:T(8,128)(2,1)}, bf16[9,128,256]{2,1,0:T(8,128)(2,1)}, u32[]{:S(2)}, u32[]{:S(2)}) collective-permute-start(bf16[9,128,256]{2,1,0:T(8,128)(2,1)} %collective-permute-done.1.refs_6_.refs_12_), channel_id=1, source_target_pairs={{0,1},{1,0},{2,3},{3,2},{4,5},{5,4},{6,7},{7,6},{8,9},{9,8},{10,11... | collective-permute-start | bytes 1769480 | tf_op jit(solution)/shard_map/ppermute | solution.py:692
  52.2 14.1 %collective-permute-start.9 = (bf16[9,128,256]{2,1,0:T(8,128)(2,1)}, bf16[9,128,256]{2,1,0:T(8,128)(2,1)}, u32[]{:S(2)}, u32[]{:S(2)}) collective-permute-start(bf16[9,128,256]{2,1,0:T(8,128)(2,1)} %collective-permute-done.refs_5_.refs_11_), channel_id=1, source_target_pairs={{0,1},{1,0},{2,3},{3,2},{4,5},{5,4},{6,7},{7,6},{8,9},{9,8},{10,11... | collective-permute-start | bytes 1769480 | tf_op jit(solution)/shard_map/ppermute | solution.py:692
  52.4 16.8 %collective-permute-start.8 = (bf16[9,128,256]{2,1,0:T(8,128)(2,1)}, bf16[9,128,256]{2,1,0:T(8,128)(2,1)}, u32[]{:S(2)}, u32[]{:S(2)}) collective-permute-start(bf16[9,128,256]{2,1,0:T(8,128)(2,1)} %dynamic-slice_convert_fusion.refs_4_.refs_10_), channel_id=1, source_target_pairs={{0,1},{1,0},{2,3},{3,2},{4,5},{5,4},{6,7},{7,6},{8,9},{9,8},{10,11... | collective-permute-start | bytes 1769480 | tf_op jit(solution)/shard_map/ppermute | solution.py:692
  52.7 12.1 %all-to-all-start.1 = ((f32[32,8,128]{2,1,0:T(8,128)}), f32[32,8,128]{2,1,0:T(8,128)}, u32[]{:S(2)}, u32[]{:S(2)}) async-start(f32[32,8,128]{2,1,0:T(8,128)} %get-tuple-element.131), calls=%async_computation.1 | async-start | bytes 262144 | tf_op jit(solution)/shard_map/all_to_all | solution.py:718
  56.7 12.5 %collective-permute-start.7 = (f32[256,256]{1,0:T(8,128)}, f32[256,256]{1,0:T(8,128)}, u32[]{:S(2)}, u32[]{:S(2)}) collective-permute-start(f32[256,256]{1,0:T(8,128)} %get-tuple-element.130), channel_id=1, source_target_pairs={{0,1},{1,0},{2,3},{3,2},{4,5},{5,4},{6,7},{7,6},{8,9},{9,8},{10,11... | collective-permute-start | bytes 786440 | tf_op jit(solution)/shard_map/ppermute | solution.py:692
  64.9 11.8 %collective-permute-start.12 = (bf16[256,512]{1,0:T(8,128)(2,1)}, bf16[256,512]{1,0:T(8,128)(2,1)}, u32[]{:S(2)}, u32[]{:S(2)}) collective-permute-start(bf16[256,512]{1,0:T(8,128)(2,1)} %get-tuple-element.145.refs_6_.refs_4_.refs_19_), channel_id=1, source_target_pairs={{0,2},{2,0},{4,6},{6,4},{1,3},{3,1},{5,7},{7,5},{8,10},{10,8},{12,... | collective-permute-start | bytes 786440 | tf_op jit(solution)/shard_map/ppermute | solution.py:692
  65.3 14.0 %collective-permute-start.13 = (bf16[256,512]{1,0:T(8,128)(2,1)}, bf16[256,512]{1,0:T(8,128)(2,1)}, u32[]{:S(2)}, u32[]{:S(2)}) collective-permute-start(bf16[256,512]{1,0:T(8,128)(2,1)} %get-tuple-element.145.refs_6_.refs_4_.refs_19_), channel_id=1, source_target_pairs={{0,4},{2,6},{4,0},{6,2},{1,5},{3,7},{5,1},{7,3},{8,12},{10,14},{12... | collective-permute-start | bytes 786440 | tf_op jit(solution)/shard_map/ppermute | solution.py:692
  66.3 13.0 %collective-permute-start.14 = (bf16[256,512]{1,0:T(8,128)(2,1)}, bf16[256,512]{1,0:T(8,128)(2,1)}, u32[]{:S(2)}, u32[]{:S(2)}) collective-permute-start(bf16[256,512]{1,0:T(8,128)(2,1)} %get-tuple-element.145.refs_6_.refs_4_.refs_19_), channel_id=1, source_target_pairs={{0,6},{2,4},{4,2},{6,0},{1,7},{3,5},{5,3},{7,1},{8,14},{10,12},{12... | collective-permute-start | bytes 786440 | tf_op jit(solution)/shard_map/ppermute | solution.py:692
  73.4 11.5 %all-to-all-start.2 = ((f32[32,8,128]{2,1,0:T(8,128)}), f32[32,8,128]{2,1,0:T(8,128)}, u32[]{:S(2)}, u32[]{:S(2)}) async-start(f32[32,8,128]{2,1,0:T(8,128)} %get-tuple-element.143), calls=%async_computation.2 | async-start | bytes 262144 | tf_op jit(solution)/shard_map/all_to_all | solution.py:718
  92.1 14.6 %all-to-all-start.3 = ((bf16[32,32,128]{2,1,0:T(8,128)(2,1)}), bf16[32,32,128]{2,1,0:T(8,128)(2,1)}, u32[]{:S(2)}, u32[]{:S(2)}) async-start(bf16[32,32,128]{2,1,0:T(8,128)(2,1)} %bitcast.88), calls=%async_computation.3 | async-start | bytes 524288 | tf_op jit(solution)/shard_map/all_to_all | solution.py:718
  95.6 11.1 %collective-permute-start.15 = (bf16[256,128]{1,0:T(8,128)(2,1)}, bf16[256,128]{1,0:T(8,128)(2,1)}, u32[]{:S(2)}, u32[]{:S(2)}) collective-permute-start(bf16[256,128]{1,0:T(8,128)(2,1)} %get-tuple-element.159), channel_id=1, source_target_pairs={{0,2},{2,0},{4,6},{6,4},{1,3},{3,1},{5,7},{7,5},{8,10},{10,8},{12,... | collective-permute-start | bytes 196616 | tf_op jit(solution)/shard_map/ppermute | solution.py:692
  97.1 9.7 %collective-permute-start.16 = (bf16[256,128]{1,0:T(8,128)(2,1)}, bf16[256,128]{1,0:T(8,128)(2,1)}, u32[]{:S(2)}, u32[]{:S(2)}) collective-permute-start(bf16[256,128]{1,0:T(8,128)(2,1)} %get-tuple-element.160), channel_id=1, source_target_pairs={{0,4},{2,6},{4,0},{6,2},{1,5},{3,7},{5,1},{7,3},{8,12},{10,14},{12... | collective-permute-start | bytes 196616 | tf_op jit(solution)/shard_map/ppermute | solution.py:692
  98.6 8.2 %collective-permute-start.17 = (bf16[256,128]{1,0:T(8,128)(2,1)}, bf16[256,128]{1,0:T(8,128)(2,1)}, u32[]{:S(2)}, u32[]{:S(2)}) collective-permute-start(bf16[256,128]{1,0:T(8,128)(2,1)} %get-tuple-element.161), channel_id=1, source_target_pairs={{0,6},{2,4},{4,2},{6,0},{1,7},{3,5},{5,3},{7,1},{8,14},{10,12},{12... | collective-permute-start | bytes 196616 | tf_op jit(solution)/shard_map/ppermute | solution.py:692
  114.5 2.2 collective-permute-start.18
  118.8 9.3 %collective-permute-start.19 = (bf16[1152,128]{1,0:T(8,128)(2,1)}, bf16[1152,128]{1,0:T(8,128)(2,1)S(1)}, u32[]{:S(2)}, u32[]{:S(2)}) collective-permute-start(bf16[1152,128]{1,0:T(8,128)(2,1)} %dynamic-slice_bitcast_fusion.3), channel_id=1, source_target_pairs={{0,8},{8,0},{16,24},{24,16},{1,9},{9,1},{17,25},{25,17},{2,10},{10... | collective-permute-start | bytes 884744 | tf_op jit(solution)/shard_map/ppermute | solution.py:692
  120.3 10.4 %collective-permute-start.20 = (bf16[512,256]{1,0:T(8,128)(2,1)}, bf16[512,256]{1,0:T(8,128)(2,1)S(1)}, u32[]{:S(2)}, u32[]{:S(2)}) collective-permute-start(bf16[512,256]{1,0:T(8,128)(2,1)} %shard_map.348.refs_0_), channel_id=1, source_target_pairs={{0,2},{2,0},{4,6},{6,4},{1,3},{3,1},{5,7},{7,5},{8,10},{10,8},{12,... | collective-permute-start | bytes 786440 | tf_op jit(solution)/shard_map/ppermute | solution.py:692
  121.7 13.6 %collective-permute-start.21 = (bf16[512,256]{1,0:T(8,128)(2,1)}, bf16[512,256]{1,0:T(8,128)(2,1)S(1)}, u32[]{:S(2)}, u32[]{:S(2)}) collective-permute-start(bf16[512,256]{1,0:T(8,128)(2,1)} %shard_map.348.refs_0_), channel_id=1, source_target_pairs={{0,4},{2,6},{4,0},{6,2},{1,5},{3,7},{5,1},{7,3},{8,12},{10,14},{12... | collective-permute-start | bytes 786440 | tf_op jit(solution)/shard_map/ppermute | solution.py:692
  123.2 12.1 %collective-permute-start.22 = (bf16[512,256]{1,0:T(8,128)(2,1)}, bf16[512,256]{1,0:T(8,128)(2,1)S(1)}, u32[]{:S(2)}, u32[]{:S(2)}) collective-permute-start(bf16[512,256]{1,0:T(8,128)(2,1)} %shard_map.348.refs_0_), channel_id=1, source_target_pairs={{0,6},{2,4},{4,2},{6,0},{1,7},{3,5},{5,3},{7,1},{8,14},{10,12},{12... | collective-permute-start | bytes 786440 | tf_op jit(solution)/shard_map/ppermute | solution.py:692
  128.2 9.2 %collective-permute-start.23 = (bf16[576,128]{1,0:T(8,128)(2,1)S(1)}, bf16[576,128]{1,0:T(8,128)(2,1)S(1)}, u32[]{:S(2)}, u32[]{:S(2)}) collective-permute-start(bf16[576,128]{1,0:T(8,128)(2,1)S(1)} %get-tuple-element.245), channel_id=1, source_target_pairs={{0,16},{8,24},{16,0},{24,8},{1,17},{9,25},{17,1},{25,9},{2,18},{10... | collective-permute-start | bytes 442376 | tf_op jit(solution)/shard_map/ppermute | solution.py:692
  137.4 9.0 %collective-permute-start.27 = (bf16[576,128]{1,0:T(8,128)(2,1)S(1)}, bf16[576,128]{1,0:T(8,128)(2,1)S(1)}, u32[]{:S(2)}, u32[]{:S(2)}) collective-permute-start(bf16[576,128]{1,0:T(8,128)(2,1)S(1)} %add_convert_fusion), channel_id=1, source_target_pairs={{0,16},{8,24},{16,0},{24,8},{1,17},{9,25},{17,1},{25,9},{2,18},{10... | collective-permute-start | bytes 442376 | tf_op jit(solution)/shard_map/ppermute | solution.py:692
  143.1 3.4 %collective-permute-start.24 = (bf16[2304,128]{1,0:T(8,128)(2,1)S(1)}, bf16[2304,128]{1,0:T(8,128)(2,1)}, u32[]{:S(2)}, u32[]{:S(2)}) collective-permute-start(bf16[2304,128]{1,0:T(8,128)(2,1)S(1)} %dynamic-slice_bitcast_fusion), channel_id=1, source_target_pairs={{0,1},{1,0},{2,3},{3,2},{4,5},{5,4},{6,7},{7,6},{8,9},{9,8},{10,11... | collective-permute-start | bytes 1769480 | tf_op jit(solution)/shard_map/ppermute | solution.py:692
  147.7 10.2 %collective-permute-start.28 = (bf16[1152,128]{1,0:T(8,128)(2,1)S(1)}, bf16[1152,128]{1,0:T(8,128)(2,1)}, u32[]{:S(2)}, u32[]{:S(2)}) collective-permute-start(bf16[1152,128]{1,0:T(8,128)(2,1)S(1)} %pad_maximum_fusion.7), channel_id=1, source_target_pairs={{0,8},{8,0},{16,24},{24,16},{1,9},{9,1},{17,25},{25,17},{2,10},{10... | collective-permute-start | bytes 884744 | tf_op jit(solution)/shard_map/ppermute | solution.py:692
  150.0 13.6 %collective-permute-start.25 = (bf16[1152,128]{1,0:T(8,128)(2,1)S(1)}, bf16[1152,128]{1,0:T(8,128)(2,1)S(1)}, u32[]{:S(2)}, u32[]{:S(2)}) collective-permute-start(bf16[1152,128]{1,0:T(8,128)(2,1)S(1)} %dynamic-slice_bitcast_fusion.2), channel_id=1, source_target_pairs={{0,8},{8,0},{16,24},{24,16},{1,9},{9,1},{17,25},{25,17},{2,10},{10... | collective-permute-start | bytes 884744 | tf_op jit(solution)/shard_map/ppermute | solution.py:692
  159.0 5.6 %collective-permute-start.29 = (bf16[2304,128]{1,0:T(8,128)(2,1)S(1)}, bf16[2304,128]{1,0:T(8,128)(2,1)S(1)}, u32[]{:S(2)}, u32[]{:S(2)}) collective-permute-start(bf16[2304,128]{1,0:T(8,128)(2,1)S(1)} %pad_maximum_fusion.4), channel_id=1, source_target_pairs={{0,1},{1,0},{2,3},{3,2},{4,5},{5,4},{6,7},{7,6},{8,9},{9,8},{10,11... | collective-permute-start | bytes 1769480 | tf_op jit(solution)/shard_map/ppermute | solution.py:692
  163.7 9.5 %collective-permute-start.26 = (bf16[576,128]{1,0:T(8,128)(2,1)S(1)}, bf16[576,128]{1,0:T(8,128)(2,1)S(1)}, u32[]{:S(2)}, u32[]{:S(2)}) collective-permute-start(bf16[576,128]{1,0:T(8,128)(2,1)S(1)} %get-tuple-element.242), channel_id=1, source_target_pairs={{0,16},{8,24},{16,0},{24,8},{1,17},{9,25},{17,1},{25,9},{2,18},{10... | collective-permute-start | bytes 442376 | tf_op jit(solution)/shard_map/ppermute | solution.py:692
  173.4 8.2 %collective-permute-start.34 = (bf16[576,128]{1,0:T(8,128)(2,1)S(1)}, bf16[576,128]{1,0:T(8,128)(2,1)S(1)}, u32[]{:S(2)}, u32[]{:S(2)}) collective-permute-start(bf16[576,128]{1,0:T(8,128)(2,1)S(1)} %get-tuple-element.168), channel_id=1, source_target_pairs={{0,16},{8,24},{16,0},{24,8},{1,17},{9,25},{17,1},{25,9},{2,18},{10... | collective-permute-start | bytes 442376 | tf_op jit(solution)/shard_map/ppermute | solution.py:692
  173.5 8.2 %collective-permute-start.35 = (bf16[576,128]{1,0:T(8,128)(2,1)S(1)}, bf16[576,128]{1,0:T(8,128)(2,1)S(1)}, u32[]{:S(2)}, u32[]{:S(2)}) collective-permute-start(bf16[576,128]{1,0:T(8,128)(2,1)S(1)} %get-tuple-element.176.refs_1_), channel_id=1, source_target_pairs={{0,2},{2,0},{4,6},{6,4},{1,3},{3,1},{5,7},{7,5},{8,10},{10,8},{12,... | collective-permute-start | bytes 442376 | tf_op jit(solution)/shard_map/ppermute | solution.py:692
  175.0 8.3 %collective-permute-start.36 = (bf16[576,128]{1,0:T(8,128)(2,1)S(1)}, bf16[576,128]{1,0:T(8,128)(2,1)S(1)}, u32[]{:S(2)}, u32[]{:S(2)}) collective-permute-start(bf16[576,128]{1,0:T(8,128)(2,1)S(1)} %get-tuple-element.176.refs_1_), channel_id=1, source_target_pairs={{0,4},{2,6},{4,0},{6,2},{1,5},{3,7},{5,1},{7,3},{8,12},{10,14},{12... | collective-permute-start | bytes 442376 | tf_op jit(solution)/shard_map/ppermute | solution.py:692
  176.5 6.8 %collective-permute-start.37 = (bf16[576,128]{1,0:T(8,128)(2,1)S(1)}, bf16[576,128]{1,0:T(8,128)(2,1)S(1)}, u32[]{:S(2)}, u32[]{:S(2)}) collective-permute-start(bf16[576,128]{1,0:T(8,128)(2,1)S(1)} %get-tuple-element.176.refs_1_), channel_id=1, source_target_pairs={{0,6},{2,4},{4,2},{6,0},{1,7},{3,5},{5,3},{7,1},{8,14},{10,12},{12... | collective-permute-start | bytes 442376 | tf_op jit(solution)/shard_map/ppermute | solution.py:692
  183.6 11.6 %collective-permute-start.38 = (bf16[576,128]{1,0:T(8,128)(2,1)S(1)}, bf16[576,128]{1,0:T(8,128)(2,1)S(1)}, u32[]{:S(2)}, u32[]{:S(2)}) collective-permute-start(bf16[576,128]{1,0:T(8,128)(2,1)S(1)} %shard_map.357), channel_id=1, source_target_pairs={{0,16},{8,24},{16,0},{24,8},{1,17},{9,25},{17,1},{25,9},{2,18},{10... | collective-permute-start | bytes 442376 | tf_op jit(solution)/shard_map/ppermute | solution.py:692
  186.4 18.9 %collective-permute-start.30 = (bf16[2304,128]{1,0:T(8,128)(2,1)S(1)}, bf16[2304,128]{1,0:T(8,128)(2,1)S(1)}, u32[]{:S(2)}, u32[]{:S(2)}) collective-permute-start(bf16[2304,128]{1,0:T(8,128)(2,1)S(1)} %get-tuple-element.166.refs_1_), channel_id=1, source_target_pairs={{0,2},{2,0},{4,6},{6,4},{1,3},{3,1},{5,7},{7,5},{8,10},{10,8},{12,... | collective-permute-start | bytes 1769480 | tf_op jit(solution)/shard_map/ppermute | solution.py:692
  186.9 18.3 %collective-permute-start.31 = (bf16[2304,128]{1,0:T(8,128)(2,1)S(1)}, bf16[2304,128]{1,0:T(8,128)(2,1)S(1)}, u32[]{:S(2)}, u32[]{:S(2)}) collective-permute-start(bf16[2304,128]{1,0:T(8,128)(2,1)S(1)} %get-tuple-element.166.refs_1_), channel_id=1, source_target_pairs={{0,4},{2,6},{4,0},{6,2},{1,5},{3,7},{5,1},{7,3},{8,12},{10,14},{12... | collective-permute-start | bytes 1769480 | tf_op jit(solution)/shard_map/ppermute | solution.py:692
  187.8 24.5 %collective-permute-start.32 = (bf16[2304,128]{1,0:T(8,128)(2,1)S(1)}, bf16[2304,128]{1,0:T(8,128)(2,1)S(1)}, u32[]{:S(2)}, u32[]{:S(2)}) collective-permute-start(bf16[2304,128]{1,0:T(8,128)(2,1)S(1)} %get-tuple-element.166.refs_1_), channel_id=1, source_target_pairs={{0,6},{2,4},{4,2},{6,0},{1,7},{3,5},{5,3},{7,1},{8,14},{10,12},{12... | collective-permute-start | bytes 1769480 | tf_op jit(solution)/shard_map/ppermute | solution.py:692
  192.6 9.3 %collective-permute-start.41 = (bf16[1152,128]{1,0:T(8,128)(2,1)S(1)}, bf16[1152,128]{1,0:T(8,128)(2,1)S(1)}, u32[]{:S(2)}, u32[]{:S(2)}) collective-permute-start(bf16[1152,128]{1,0:T(8,128)(2,1)S(1)} %pad_maximum_fusion.8), channel_id=1, source_target_pairs={{0,8},{8,0},{16,24},{24,16},{1,9},{9,1},{17,25},{25,17},{2,10},{10... | collective-permute-start | bytes 884744 | tf_op jit(solution)/shard_map/ppermute | solution.py:692
  195.3 9.8 %collective-permute-start.39 = (bf16[1152,128]{1,0:T(8,128)(2,1)S(1)}, bf16[1152,128]{1,0:T(8,128)(2,1)S(1)}, u32[]{:S(2)}, u32[]{:S(2)}) collective-permute-start(bf16[1152,128]{1,0:T(8,128)(2,1)S(1)} %pad_maximum_fusion.9), channel_id=1, source_target_pairs={{0,8},{8,0},{16,24},{24,16},{1,9},{9,1},{17,25},{25,17},{2,10},{10... | collective-permute-start | bytes 884744 | tf_op jit(solution)/shard_map/ppermute | solution.py:692
  202.1 11.1 %collective-permute-start.42 = (bf16[2304,128]{1,0:T(8,128)(2,1)S(1)}, bf16[2304,128]{1,0:T(8,128)(2,1)S(1)}, u32[]{:S(2)}, u32[]{:S(2)}) collective-permute-start(bf16[2304,128]{1,0:T(8,128)(2,1)S(1)} %pad_maximum_fusion.6), channel_id=1, source_target_pairs={{0,1},{1,0},{2,3},{3,2},{4,5},{5,4},{6,7},{7,6},{8,9},{9,8},{10,11... | collective-permute-start | bytes 1769480 | tf_op jit(solution)/shard_map/ppermute | solution.py:692
  205.2 8.2 %collective-permute-start.40 = (bf16[2304,128]{1,0:T(8,128)(2,1)S(1)}, bf16[2304,128]{1,0:T(8,128)(2,1)S(1)}, u32[]{:S(2)}, u32[]{:S(2)}) collective-permute-start(bf16[2304,128]{1,0:T(8,128)(2,1)S(1)} %pad_maximum_fusion.5), channel_id=1, source_target_pairs={{0,1},{1,0},{2,3},{3,2},{4,5},{5,4},{6,7},{7,6},{8,9},{9,8},{10,11... | collective-permute-start | bytes 1769480 | tf_op jit(solution)/shard_map/ppermute | solution.py:692
  219.4 5.8 %collective-permute-start.43 = (f32[8,128]{1,0:T(8,128)S(1)}, f32[8,128]{1,0:T(8,128)S(1)}, u32[]{:S(2)}, u32[]{:S(2)}) collective-permute-start(f32[8,128]{1,0:T(8,128)S(1)} %get-tuple-element.184.refs_0_), channel_id=1, source_target_pairs={{0,2},{2,0},{4,6},{6,4},{1,3},{3,1},{5,7},{7,5},{8,10},{10,8},{12,... | collective-permute-start | bytes 12296 | tf_op jit(solution)/shard_map/ppermute | solution.py:692
  221.2 4.0 %collective-permute-start.44 = (f32[8,128]{1,0:T(8,128)S(1)}, f32[8,128]{1,0:T(8,128)S(1)}, u32[]{:S(2)}, u32[]{:S(2)}) collective-permute-start(f32[8,128]{1,0:T(8,128)S(1)} %get-tuple-element.184.refs_0_), channel_id=1, source_target_pairs={{0,4},{2,6},{4,0},{6,2},{1,5},{3,7},{5,1},{7,3},{8,12},{10,14},{12... | collective-permute-start | bytes 12296 | tf_op jit(solution)/shard_map/ppermute | solution.py:692
  221.8 4.5 %collective-permute-start.45 = (f32[8,128]{1,0:T(8,128)S(1)}, f32[8,128]{1,0:T(8,128)S(1)}, u32[]{:S(2)}, u32[]{:S(2)}) collective-permute-start(f32[8,128]{1,0:T(8,128)S(1)} %get-tuple-element.184.refs_0_), channel_id=1, source_target_pairs={{0,6},{2,4},{4,2},{6,0},{1,7},{3,5},{5,3},{7,1},{8,14},{10,12},{12... | collective-permute-start | bytes 12296 | tf_op jit(solution)/shard_map/ppermute | solution.py:692
  (32 other events, 216.9 us)

commit v5 on v4

--- a/solution.py
+++ b/solution.py
@@ -536,6 +536,29 @@
         left_ref[step] = jnp.transpose(matmul(part_ref[...], basis_ref[...])).astype(BF)
 
 
+def pick_kernel(own_ref, full_ref, kept_ref, sent_ref):
+    half = kept_ref.shape[0]
+    kept_ref[...] = full_ref[pl.ds(pl.multiple_of(own_ref[0] * half, half), half), :]
+    sent_ref[...] = full_ref[pl.ds(pl.multiple_of((1 - own_ref[0]) * half, half), half), :]
+
+
+def split_kernel(own_ref, here_ref, came_ref, kept_ref, sent_ref):
+    half = kept_ref.shape[0]
+    for which, ref in ((own_ref[0], kept_ref), (1 - own_ref[0], sent_ref)):
+        rows = pl.ds(pl.multiple_of(which * half, half), half)
+        ref[...] = (here_ref[rows, :].astype(F32) + came_ref[rows, :].astype(F32)).astype(BF)
+
+
+def merge_kernel(own_ref, here_ref, came_ref, out_ref):
+    rows = here_ref.shape[0]
+    for choice in range(2):
+
+        @pl.when(own_ref[0] == choice)
+        def _():
+            out_ref[choice * rows : (choice + 1) * rows, :] = here_ref[...]
+            out_ref[(1 - choice) * rows : (2 - choice) * rows, :] = came_ref[...]
+
+
 def taps_kernel(sign, big_refs, small_refs, out_ref, left_ref, right_ref):
     rows, width = small_refs[0].shape
     channels = big_refs[0].shape[0]
@@ -722,17 +745,40 @@
     return range(lax.axis_size(axis).bit_length() - 1)
 
 
-def halved(values, axis, bit):
-    own = (lax.axis_index(axis) >> bit) & 1
-    values = values.reshape(2, -1, values.shape[-1])
-    return [picked(values, own), swap(picked(values, 1 - own), axis, 1 << bit)]
+def bit_of(axis, bit):
+    return (lax.axis_index(axis) >> bit) & 1
+
+
+def crossed(parts, axis, bit):
+    return [parts[0], swap(parts[1], axis, 1 << bit)]
+
+
+def halved(terms, axis, bit):
+    rows, width = terms[0].shape
+    own = bit_of(axis, bit)
+    if rows // 2 % 16:
+        total = joined(terms).reshape(2, rows // 2, width)
+        return crossed([picked(total, own), picked(total, 1 - own)], axis, bit)
+    half = shape((rows // 2, width), BF)
+    parts = call(
+        pick_kernel if len(terms) == 1 else split_kernel,
+        [half, half],
+        [own[None], *terms],
+        near=tuple(range(1, 1 + len(terms))),
+        near_out=(0, 1),
+        room=16,
+    )
+    return crossed(parts, axis, bit)
 
 
 def doubled(values, axis, bit):
-    own = (lax.axis_index(axis) >> bit) & 1
+    own = bit_of(axis, bit)
+    rows, width = values.shape
     other = swap(values, axis, 1 << bit)
-    first = jnp.where(own == 0, values, other)
-    return jnp.concatenate([first, jnp.where(own == 0, other, values)], axis=0)
+    (out,) = call(
+        merge_kernel, [shape((2 * rows, width), BF)], [own[None], values, other], near=(1, 2), near_out=(0,), room=16
+    )
+    return out
 
 
 def joined(terms):
@@ -954,7 +1000,7 @@
             scalars=0,
             near=near,
             near_out=(0,),
-            room=56,
+            room=44,
             flops=2 * groups * rows * channels * width * TAPS,
         )
         return out
@@ -1034,24 +1080,15 @@
         flops=2 * groups * rows * channels * width * TAPS,
     )
     terms_first = [products_first]
-    for order in orders[:-1]:
-        terms_first = halved(joined(terms_first), *order)
-    near_first = joined(terms_first)
-    terms_first = halved(near_first, *orders[-1])
-
+    for order in orders:
+        terms_first = halved(terms_first, *order)
     own_first = joined([after(terms_first[0], *right_slots), terms_first[1]])
     coeff_first = doubled(own_first, *orders[-1])
-    products_second = products(1, [after(right_slots[0], own_first)] + right_slots[1:], left_slots)
-    terms_second = [products_second]
-    for order in orders[:near_steps]:
-        terms_second = halved(joined(terms_second), *order)
-    near_second = joined(terms_second)
-    terms_second = [near_second]
-    for order in orders[near_steps:-1]:
-        terms_second = halved(joined(terms_second), *order)
-    terms_far = terms_second
+    terms_second = [products(1, [after(right_slots[0], own_first)] + right_slots[1:], left_slots)]
+    for order in orders:
+        terms_second = halved(terms_second, *order)
     for order in reversed(orders[near_steps:-1]):
-        coeff_first = doubled(after(coeff_first, near_second), *order)
+        coeff_first = doubled(coeff_first, *order)
     coeff_first = batch_gather(coeff_first, ("cin",))
     flat_scales = scales_first.reshape(TAPS * channels, width)
     scales_first_new, ratio_first = call(
@@ -1063,7 +1100,6 @@
         room=16,
     )
     slots_first = gathered(ratio_first, "cout")
-    terms_second = halved(joined(terms_second), *orders[-1])
     own_second, ratio_second = ratio_of(terms_second, after(scales_turned, ratio_first))
     weights = hold(after(w_first, own_second), w_second)
     coeff_second = doubled(own_second, *orders[-1])

time: 236 us -> 231 us (0.979)
  local copies, waits for them, and re-layouts: 24 us -> 16 us
  waiting for transfers between devices: 76 us -> 81.5 us
  other arithmetic: 6.61 us -> 1.31 us
  starting transfers between devices: 57.9 us -> 61.4 us
    ppermute x46, waiting for transfers between devices: 65.5 us -> 71 us  [swap(): lax.ppermute(values, axis, [(here, here ^ step) for here in range(count)])]
    unnamed x60 -> x64, local copies, waits for them, and re-layouts: 10.3 us -> 5.3 us
    ppermute x46, starting transfers between devices: 42.3 us -> 45.8 us  [swap(): lax.ppermute(values, axis, [(here, here ^ step) for here in range(count)])]
    squeeze x6 -> x0, local copies, waits for them, and re-layouts: 3.04 us -> none  [picked(): return lax.dynamic_index_in_dim(values, index, 0, keepdims=False)]
    convert_element_type x5 -> x1, other arithmetic: 2.83 us -> 0.04 us  [joined(): (terms[0].astype(F32) + terms[1].astype(F32)).astype(BF)]
    pallas_call x20 -> x36, Pallas kernels: 58.2 us -> 57.9 us  [call(): pl.pallas_call(body, out_shape=list(outs), in_specs=specs, out_specs=[pl....]
  transfers between devices with their start and end apart: 50 -> 50, of which waited for: 21 -> 21; matrix products, arithmetic and copies ran while one was open for 6% -> 4% of each run, Pallas kernels for 16% -> 18%
where the time goes in v5:
time: 231 us
  waiting for transfers between devices  81.5 us (35%)
  Pallas kernels  68.7 us (30%)
  starting transfers between devices  61.4 us (27%)
  local copies, waits for them, and re-layouts  16 us (7%)
    ppermute x46, waiting for transfers between devices, swap(): lax.ppermute(values, axis, [(here, here ^ step) for here in range(count)])  71 us
    pallas_call x36, Pallas kernels, call(): pl.pallas_call(body, out_shape=list(outs), in_specs=specs, out_specs=[pl....  57.9 us
    ppermute x46, starting transfers between devices, swap(): lax.ppermute(values, axis, [(here, here ^ step) for here in range(count)])  45.8 us
    all_to_all x3, starting transfers between devices, every_device(): return lax.all_to_all(tiles, EVERY, 0, 0, tiled=True)  10.7 us
    all_to_all x3, waiting for transfers between devices, every_device(): return lax.all_to_all(tiles, EVERY, 0, 0, tiled=True)  10.5 us
    pallas_call x1, Pallas kernels, local(): pl.pallas_call(update, grid=(TAPS,), in_specs=[pl.BlockSpec(memory_space=...  8.65 us
    unnamed x64, local copies, waits for them, and re-layouts  5.3 us
    all_to_all x1, starting transfers between devices, local(): got = lax.all_to_all(stats, ('dp', 'cin'), 0, 0, tiled=True)  4.89 us
  transfers between devices with their start and end apart: 50, of which 21 were waited for; matrix products, arithmetic and copies ran while one was open for 4% of the time, Pallas kernels for 18%

profile of v5, /device:TPU:0, one launch (start us, length us, event | category | flops | bytes accessed | tf_op | source)
XLA Modules:
  0.0 230.6 jit_solution(4751959021002147354)
XLA Ops:
  0.7 2.2 dynamic-slice_convert_fusion.refs_4_.refs_10_
  2.8 2.9 %collective-permute-start = (bf16[9,128,256]{2,1,0:T(8,128)(2,1)}, bf16[9,128,256]{2,1,0:T(8,128)(2,1)}, u32[]{:S(2)}, u32[]{:S(2)}) collective-permute-start(bf16[9,128,256]{2,1,0:T(8,128)(2,1)} %dynamic-slice_convert_fusion.refs_4_.refs_10_), channel_id=1, source_target_pairs={{0,2},{2,0},{4,6},{6,4},{1,3},{3,1},{5,7},{7,5},{8,10},{10,8},{12,... | collective-permute-start | bytes 1769480 | tf_op jit(solution)/shard_map/ppermute | solution.py:715
  7.9 5.4 %shard_map.340 = (f32[1024,128]{1,0:T(8,128)}, bf16[1024,128]{1,0:T(8,128)(2,1)}, f32[8,8,128]{2,1,0:T(8,128)}, f32[256,128]{1,0:T(8,128)}) custom-call(s32[2]{0:T(128)} %pad_add_fusion.refs_0_, bf16[1024,512]{1,0:T(8,128)(2,1)} %bitcast.44, s32[16,64]{1,0:T(8,128)} %refs_2_.3, f32[9,512,128]{2,1,0:T(8,128)} %refs_0_), custom_call_target="tpu_custom_call" | custom-call | flops 1207959552 | bytes 4362248 | tf_op jit(solution)/shard_map/pallas_call | solution.py:117
  13.4 4.9 %all-to-all-start = ((f32[8,8,128]{2,1,0:T(8,128)}), f32[8,8,128]{2,1,0:T(8,128)S(1)}, u32[]{:S(2)}, u32[]{:S(2)}) async-start(f32[8,8,128]{2,1,0:T(8,128)} %get-tuple-element.123), calls=%async_computation | async-start | bytes 65536 | tf_op jit(solution)/shard_map/all_to_all | solution.py:873
  24.8 3.7 %shard_map.342 = (bf16[528,128]{1,0:T(8,128)(2,1)}, bf16[528,128]{1,0:T(8,128)(2,1)}, bf16[528,128]{1,0:T(8,128)(2,1)}, bf16[528,128]{1,0:T(8,128)(2,1)}, f32[8,128]{1,0:T(8,128)}) custom-call(s32[2]{0:T(128)} %pad_add_fusion.refs_0_, f32[8,8,128]{2,1,0:T(8,128)} %copy-done.29, f32[1024,128]{1,0:T(8,128)} %get-tuple-element.124.refs_2_, ...), custom_call_target="tpu_custom_call" | custom-call | bytes 1371144 | tf_op jit(solution)/shard_map/pallas_call | solution.py:117
  34.1 1.9 copy.39
  36.0 1.7 constant_dynamic-slice_fusion.refs_2_
  38.4 2.6 %collective-permute-done.4.refs_4_ = bf16[528,128]{1,0:T(8,128)(2,1)} collective-permute-done((bf16[528,128]{1,0:T(8,128)(2,1)}, bf16[528,128]{1,0:T(8,128)(2,1)}, u32[]{:S(2)}, u32[]{:S(2)}) %collective-permute-start.4) | collective-permute-done | bytes 135200 | tf_op jit(solution)/shard_map/ppermute | solution.py:715
  41.0 2.8 %shard_map.343.refs_1_ = bf16[256,640]{1,0:T(8,128)(2,1)} custom-call(s32[2]{0:T(128)} %pad_add_fusion.refs_0_, bf16[528,128]{1,0:T(8,128)(2,1)} %get-tuple-element.130.refs_1_, bf16[528,128]{1,0:T(8,128)(2,1)} %collective-permute-done.2.refs_2_, bf16[528,128]{1,0:T(8,128)(2,1)} %collective-permute-done.3.refs_3_, ...), custom_call_target="tpu_custom_call" | custom-call | bytes 999432 | tf_op jit(solution)/shard_map/pallas_call | solution.py:117
  43.9 1.8 collective-permute-done.5.refs_2_
  46.5 5.0 %shard_map.344 = (f32[256,256]{1,0:T(8,128)}, f32[256,256]{1,0:T(8,128)}, f32[32,8,128]{2,1,0:T(8,128)}) custom-call(s32[2]{0:T(128)} %pad_add_fusion.refs_0_, bf16[256,640]{1,0:T(8,128)(2,1)} %shard_map.343.refs_1_, bf16[256,640]{1,0:T(8,128)(2,1)} %copy-done.30, f32[4,128]{1,0:T(4,128)} %refs_3_.3, ...), custom_call_target="tpu_custom_call" | custom-call | flops 1207959552 | bytes 3672072 | tf_op jit(solution)/shard_map/pallas_call | solution.py:117
  52.6 3.9 %all-to-all-start.1 = ((f32[32,8,128]{2,1,0:T(8,128)}), f32[32,8,128]{2,1,0:T(8,128)}, u32[]{:S(2)}, u32[]{:S(2)}) async-start(f32[32,8,128]{2,1,0:T(8,128)} %get-tuple-element.142), calls=%async_computation.1 | async-start | bytes 262144 | tf_op jit(solution)/shard_map/all_to_all | solution.py:741
  57.3 2.6 %shard_map.345 = (bf16[256,512]{1,0:T(8,128)(2,1)}, f32[8,512]{1,0:T(8,128)}, bf16[16,512]{1,0:T(8,128)(2,1)}) custom-call(s32[2]{0:T(128)} %pad_add_fusion.refs_0_, bf16[528,128]{1,0:T(8,128)(2,1)} %get-tuple-element.130.refs_1_, bf16[528,128]{1,0:T(8,128)(2,1)} %collective-permute-done.2.refs_2_, bf16[528,128]{1,0:T(8,128)(2,1)} %collective-permute-done.3.refs_3_, ...), custom_call_target="tpu_custom_call" | custom-call | bytes 839688 | tf_op jit(solution)/shard_map/pallas_call | solution.py:117
  59.8 4.9 %all-to-all-done.1.refs_3_ = f32[32,8,128]{2,1,0:T(8,128)} async-done(((f32[32,8,128]{2,1,0:T(8,128)}), f32[32,8,128]{2,1,0:T(8,128)}, u32[]{:S(2)}, u32[]{:S(2)}) %all-to-all-start.1) | async-done | bytes 131104 | tf_op jit(solution)/shard_map/all_to_all | solution.py:741
  66.2 2.1 collective-permute-start.14
  69.0 4.2 %shard_map.346 = (f32[256,512]{1,0:T(8,128)}, f32[8,512]{1,0:T(8,128)}, f32[256,512]{1,0:T(8,128)}, f32[32,8,128]{2,1,0:T(8,128)}, f32[4,16,128]{2,1,0:T(8,128)}) custom-call(s32[2]{0:T(128)} %pad_add_fusion.refs_0_, f32[256,256]{1,0:T(8,128)} %get-tuple-element.140.refs_1_, f32[256,256]{1,0:T(8,128)} %collective-permute-done.7.refs_2_, ...), custom_call_target="tpu_custom_call" | custom-call | bytes 2048584 | tf_op jit(solution)/shard_map/pallas_call | solution.py:117
  73.2 3.3 %all-to-all-start.2 = ((f32[32,8,128]{2,1,0:T(8,128)}), f32[32,8,128]{2,1,0:T(8,128)}, u32[]{:S(2)}, u32[]{:S(2)}) async-start(f32[32,8,128]{2,1,0:T(8,128)} %get-tuple-element.154), calls=%async_computation.2 | async-start | bytes 262144 | tf_op jit(solution)/shard_map/all_to_all | solution.py:741
  76.5 2.6 %collective-permute-done.13.refs_6_.refs_21_ = bf16[256,512]{1,0:T(8,128)(2,1)} collective-permute-done((bf16[256,512]{1,0:T(8,128)(2,1)}, bf16[256,512]{1,0:T(8,128)(2,1)}, u32[]{:S(2)}, u32[]{:S(2)}) %collective-permute-start.13) | collective-permute-done | bytes 262176 | tf_op jit(solution)/shard_map/ppermute | solution.py:715
  79.1 5.6 %all-to-all-done.2.refs_4_ = f32[32,8,128]{2,1,0:T(8,128)} async-done(((f32[32,8,128]{2,1,0:T(8,128)}), f32[32,8,128]{2,1,0:T(8,128)}, u32[]{:S(2)}, u32[]{:S(2)}) %all-to-all-start.2) | async-done | bytes 131104 | tf_op jit(solution)/shard_map/all_to_all | solution.py:741
  84.7 7.2 %shard_map.347 = (bf16[256,512]{1,0:T(8,128)(2,1)}, f32[8,128]{1,0:T(8,128)}, bf16[4,4,2,32,128]{4,3,2,1,0:T(8,128)(2,1)}, bf16[256,128]{1,0:T(8,128)(2,1)}, bf1...) custom-call(s32[2]{0:T(128)} %pad_add_fusion.refs_0_, ...), custom_call_target="tpu_custom_call" | custom-call | flops 1207959552 | bytes 7671816 | tf_op jit(solution)/shard_map/pallas_call | solution.py:117
  91.9 3.5 %all-to-all-start.3 = ((bf16[32,32,128]{2,1,0:T(8,128)(2,1)}), bf16[32,32,128]{2,1,0:T(8,128)(2,1)}, u32[]{:S(2)}, u32[]{:S(2)}) async-start(bf16[32,32,128]{2,1,0:T(8,128)(2,1)} %bitcast.47), calls=%async_computation.3 | async-start | bytes 524288 | tf_op jit(solution)/shard_map/all_to_all | solution.py:741
  100.0 2.2 shard_map.348.refs_0_
  102.2 4.4 %shard_map.349 = (bf16[256,128]{1,0:T(8,128)(2,1)}, bf16[256,128]{1,0:T(8,128)(2,1)}, bf16[256,128]{1,0:T(8,128)(2,1)}, bf16[256,128]{1,0:T(8,128)(2,1)}) custom-call(s32[2]{0:T(128)} %pad_add_fusion.refs_0_, f32[8,512]{1,0:T(8,128)} %get-tuple-element.144.refs_4_.refs_7_.refs_1_.refs_2_, bf16[1024,128]{1,0:T(8,128)(2,1)} %get-tuple-element.163.refs_3_.refs_2_, ...), custom_call_target="tpu_custom_call" | custom-call | bytes 2113544 | tf_op jit(solution)/shard_map/pallas_call | solution.py:117
  106.6 6.7 %shard_map.350 = (bf16[4608,128]{1,0:T(8,128)(2,1)}, f32[8,128]{1,0:T(8,128)}, f32[72,128]{1,0:T(8,128)}) custom-call(s32[2]{0:T(128)} %pad_add_fusion.refs_0_, bf16[32,32,128]{2,1,0:T(8,128)(2,1)} %all-to-all-done.3.refs_1_, f32[8,512]{1,0:T(8,128)} %get-tuple-element.144.refs_4_.refs_7_.refs_1_.refs_2_, ...), custom_call_target="tpu_custom_call" | custom-call | flops 1207959552 | bytes 4659288 | tf_op jit(solution)/shard_map/pallas_call | solution.py:117
  114.8 2.0 collective-permute-done.18.refs_2_
  121.9 4.1 %collective-permute-done.19.refs_2_ = bf16[1152,128]{1,0:T(8,128)(2,1)S(1)} collective-permute-done((bf16[1152,128]{1,0:T(8,128)(2,1)S(1)}, bf16[1152,128]{1,0:T(8,128)(2,1)S(1)}, u32[]{:S(2)}, u32[]{:S(2)}) %collective-permute-start.19) | collective-permute-done | bytes 294944 | tf_op jit(solution)/shard_map/ppermute | solution.py:715
  126.2 2.5 %collective-permute-start.23 = (bf16[576,128]{1,0:T(8,128)(2,1)S(1)}, bf16[576,128]{1,0:T(8,128)(2,1)S(1)}, u32[]{:S(2)}, u32[]{:S(2)}) collective-permute-start(bf16[576,128]{1,0:T(8,128)(2,1)S(1)} %get-tuple-element.180), channel_id=1, source_target_pairs={{0,16},{8,24},{16,0},{24,8},{1,17},{9,25},{17,1},{25,9},{2,18},{10... | collective-permute-start | bytes 442376 | tf_op jit(solution)/shard_map/ppermute | solution.py:715
  128.6 4.7 %collective-permute-done.21.refs_2_ = bf16[512,256]{1,0:T(8,128)(2,1)S(1)} collective-permute-done((bf16[512,256]{1,0:T(8,128)(2,1)S(1)}, bf16[512,256]{1,0:T(8,128)(2,1)S(1)}, u32[]{:S(2)}, u32[]{:S(2)}) %collective-permute-start.21) | collective-permute-done | bytes 262176 | tf_op jit(solution)/shard_map/ppermute | solution.py:715
  133.3 2.0 collective-permute-done.23
  136.0 2.4 %shard_map.354.refs_1_ = bf16[4608,128]{1,0:T(8,128)(2,1)S(1)} custom-call(bf16[512,256]{1,0:T(8,128)(2,1)S(1)} %copy-done.17, bf16[512,256]{1,0:T(8,128)(2,1)S(1)} %collective-permute-done.20.refs_1_, bf16[512,256]{1,0:T(8,128)(2,1)S(1)} %collective-permute-done.21.refs_2_, bf16[512,256]{1,0:T(8,128)(2,1)S(1)} %collective-permute-done.22.refs_3_, ...), custom_call_target="tpu_custom_call" | custom-call | flops 1207959552 | bytes 2490368 | tf_op jit(solution)/shard_map/pallas_call | solution.py:117
  138.6 5.8 %collective-permute-done.27.refs_2_ = bf16[576,128]{1,0:T(8,128)(2,1)S(1)} collective-permute-done((bf16[576,128]{1,0:T(8,128)(2,1)S(1)}, bf16[576,128]{1,0:T(8,128)(2,1)S(1)}, u32[]{:S(2)}, u32[]{:S(2)}) %collective-permute-start.27) | collective-permute-done | bytes 147488 | tf_op jit(solution)/shard_map/ppermute | solution.py:715
  144.5 6.7 %collective-permute-done.28.refs_2_ = bf16[1152,128]{1,0:T(8,128)(2,1)S(1)} collective-permute-done((bf16[1152,128]{1,0:T(8,128)(2,1)S(1)}, bf16[1152,128]{1,0:T(8,128)(2,1)S(1)}, u32[]{:S(2)}, u32[]{:S(2)}) %collective-permute-start.28) | collective-permute-done | bytes 294944 | tf_op jit(solution)/shard_map/ppermute | solution.py:715
  152.4 8.6 %collective-permute-done.25.refs_2_ = bf16[1152,128]{1,0:T(8,128)(2,1)S(1)} collective-permute-done((bf16[1152,128]{1,0:T(8,128)(2,1)S(1)}, bf16[1152,128]{1,0:T(8,128)(2,1)S(1)}, u32[]{:S(2)}, u32[]{:S(2)}) %collective-permute-start.25) | collective-permute-done | bytes 294944 | tf_op jit(solution)/shard_map/ppermute | solution.py:715
  161.1 2.5 %collective-permute-start.26 = (bf16[576,128]{1,0:T(8,128)(2,1)S(1)}, bf16[576,128]{1,0:T(8,128)(2,1)S(1)}, u32[]{:S(2)}, u32[]{:S(2)}) collective-permute-start(bf16[576,128]{1,0:T(8,128)(2,1)S(1)} %get-tuple-element.187), channel_id=1, source_target_pairs={{0,16},{8,24},{16,0},{24,8},{1,17},{9,25},{17,1},{25,9},{2,18},{10... | collective-permute-start | bytes 442376 | tf_op jit(solution)/shard_map/ppermute | solution.py:715
  163.8 2.9 %shard_map.361 = (f32[4608,128]{1,0:T(8,128)}, bf16[2304,128]{1,0:T(8,128)(2,1)S(1)}) custom-call(s32[2]{0:T(128)S(1)} %copy-done.19, bf16[4608,128]{1,0:T(8,128)(2,1)S(1)} %shard_map.360.refs_1_, f32[4608,128]{1,0:T(8,128)S(1)} %bitcast.43), custom_call_target="tpu_custom_call" | custom-call | bytes 6488072 | tf_op jit(solution)/shard_map/pallas_call | solution.py:117
  166.7 4.0 %collective-permute-done.26.refs_1_ = bf16[576,128]{1,0:T(8,128)(2,1)S(1)} collective-permute-done((bf16[576,128]{1,0:T(8,128)(2,1)S(1)}, bf16[576,128]{1,0:T(8,128)(2,1)S(1)}, u32[]{:S(2)}, u32[]{:S(2)}) %collective-permute-start.26) | collective-permute-done | bytes 147488 | tf_op jit(solution)/shard_map/ppermute | solution.py:715
  176.0 3.9 %collective-permute-done.34.refs_2_ = bf16[576,128]{1,0:T(8,128)(2,1)S(1)} collective-permute-done((bf16[576,128]{1,0:T(8,128)(2,1)S(1)}, bf16[576,128]{1,0:T(8,128)(2,1)S(1)}, u32[]{:S(2)}, u32[]{:S(2)}) %collective-permute-start.34) | collective-permute-done | bytes 147488 | tf_op jit(solution)/shard_map/ppermute | solution.py:715
  181.4 1.8 collective-permute-start.32
  185.3 7.4 %collective-permute-done.38.refs_2_ = bf16[576,128]{1,0:T(8,128)(2,1)S(1)} collective-permute-done((bf16[576,128]{1,0:T(8,128)(2,1)S(1)}, bf16[576,128]{1,0:T(8,128)(2,1)S(1)}, u32[]{:S(2)}, u32[]{:S(2)}) %collective-permute-start.38) | collective-permute-done | bytes 147488 | tf_op jit(solution)/shard_map/ppermute | solution.py:715
  192.9 2.0 collective-permute-start.41
  195.6 7.1 %collective-permute-done.39.refs_2_ = bf16[1152,128]{1,0:T(8,128)(2,1)S(1)} collective-permute-done((bf16[1152,128]{1,0:T(8,128)(2,1)S(1)}, bf16[1152,128]{1,0:T(8,128)(2,1)S(1)}, u32[]{:S(2)}, u32[]{:S(2)}) %collective-permute-start.39) | collective-permute-done | bytes 294944 | tf_op jit(solution)/shard_map/ppermute | solution.py:715
  202.9 3.1 %collective-permute-done.31.refs_3_ = bf16[2304,128]{1,0:T(8,128)(2,1)S(1)} collective-permute-done((bf16[2304,128]{1,0:T(8,128)(2,1)S(1)}, bf16[2304,128]{1,0:T(8,128)(2,1)S(1)}, u32[]{:S(2)}, u32[]{:S(2)}) %collective-permute-start.31) | collective-permute-done | bytes 589856 | tf_op jit(solution)/shard_map/ppermute | solution.py:715
  209.2 3.0 %shard_map.373 = (bf16[9,512,128]{2,1,0:T(8,128)(2,1)S(1)}, bf16[9,128,512]{2,1,0:T(8,128)(2,1)S(1)}, f32[8,128]{1,0:T(8,128)S(1)}, f32[72,128]{1,0:T(8,128)S(1)}) custom-call(s32[2]{0:T(128)S(1)} %copy-done.19, bf16[512,512]{1,0:T(8,128)(2,1)S(1)} %copy-done.12, bf16[4608,128]{1,0:T(8,128)(2,1)S(1)} %shard_map.366.refs_2_, bf16[512,512]{1,0:T(8,128)(2,1)S(1)} %copy-done.10, ...), custom_call_target="tpu_custom_call" | custom-call | flops 1207959552 | bytes 5853192 | tf_op jit(solution)/shard_map/pallas_call | solution.py:117
  212.2 3.3 %collective-permute-start.43 = (f32[8,128]{1,0:T(8,128)S(1)}, f32[8,128]{1,0:T(8,128)S(1)}, u32[]{:S(2)}, u32[]{:S(2)}) collective-permute-start(f32[8,128]{1,0:T(8,128)S(1)} %get-tuple-element.206.refs_0_), channel_id=1, source_target_pairs={{0,2},{2,0},{4,6},{6,4},{1,3},{3,1},{5,7},{7,5},{8,10},{10,8},{12,... | collective-permute-start | bytes 12296 | tf_op jit(solution)/shard_map/ppermute | solution.py:715
  215.5 1.8 collective-permute-start.44
  217.3 2.2 shard_map.377
  219.5 2.2 collective-permute-done.45.refs_3_
  221.7 8.6 %shard_map.376 = (f32[9,512,128]{2,1,0:T(8,128)}, f32[9,128,512]{2,1,0:T(8,128)}, f32[9,512,128]{2,1,0:T(8,128)}, f32[9,128,512]{2,1,0:T(8,128)}, f32[9,512,128]...) custom-call(f32[8,128]{1,0:T(8,128)S(1)} %get-tuple-element.206.refs, ...), custom_call_target="tpu_custom_call" | custom-call | tf_op jit(solution)/shard_map/pallas_call | solution.py:1176
  (167 shorter events, 46.1 us)
Async XLA Ops:
  2.8 21.3 %collective-permute-start = (bf16[9,128,256]{2,1,0:T(8,128)(2,1)}, bf16[9,128,256]{2,1,0:T(8,128)(2,1)}, u32[]{:S(2)}, u32[]{:S(2)}) collective-permute-start(bf16[9,128,256]{2,1,0:T(8,128)(2,1)} %dynamic-slice_convert_fusion.refs_4_.refs_10_), channel_id=1, source_target_pairs={{0,2},{2,0},{4,6},{6,4},{1,3},{3,1},{5,7},{7,5},{8,10},{10,8},{12,... | collective-permute-start | bytes 1769480 | tf_op jit(solution)/shard_map/ppermute | solution.py:715
  5.8 18.4 %collective-permute-start.1 = (bf16[9,128,256]{2,1,0:T(8,128)(2,1)}, bf16[9,128,256]{2,1,0:T(8,128)(2,1)}, u32[]{:S(2)}, u32[]{:S(2)}) collective-permute-start(bf16[9,128,256]{2,1,0:T(8,128)(2,1)} %dynamic-slice_convert_fusion.refs_4_.refs_10_), channel_id=1, source_target_pairs={{0,4},{2,6},{4,0},{6,2},{1,5},{3,7},{5,1},{7,3},{8,12},{10,14},{12... | collective-permute-start | bytes 1769480 | tf_op jit(solution)/shard_map/ppermute | solution.py:715
  13.4 10.8 %all-to-all-start = ((f32[8,8,128]{2,1,0:T(8,128)}), f32[8,8,128]{2,1,0:T(8,128)S(1)}, u32[]{:S(2)}, u32[]{:S(2)}) async-start(f32[8,8,128]{2,1,0:T(8,128)} %get-tuple-element.123), calls=%async_computation | async-start | bytes 65536 | tf_op jit(solution)/shard_map/all_to_all | solution.py:873
  18.3 25.7 %collective-permute-start.6 = (bf16[9,128,256]{2,1,0:T(8,128)(2,1)}, bf16[9,128,256]{2,1,0:T(8,128)(2,1)}, u32[]{:S(2)}, u32[]{:S(2)}) collective-permute-start(bf16[9,128,256]{2,1,0:T(8,128)(2,1)} %dynamic-slice_convert_fusion.refs_4_.refs_10_), channel_id=1, source_target_pairs={{0,6},{2,4},{4,2},{6,0},{1,7},{3,5},{5,3},{7,1},{8,14},{10,12},{12... | collective-permute-start | bytes 1769480 | tf_op jit(solution)/shard_map/ppermute | solution.py:715
  28.5 9.2 %collective-permute-start.2 = (bf16[528,128]{1,0:T(8,128)(2,1)}, bf16[528,128]{1,0:T(8,128)(2,1)}, u32[]{:S(2)}, u32[]{:S(2)}) collective-permute-start(bf16[528,128]{1,0:T(8,128)(2,1)} %get-tuple-element.131), channel_id=1, source_target_pairs={{0,2},{2,0},{4,6},{6,4},{1,3},{3,1},{5,7},{7,5},{8,10},{10,8},{12,... | collective-permute-start | bytes 405512 | tf_op jit(solution)/shard_map/ppermute | solution.py:715
  30.1 8.4 %collective-permute-start.3 = (bf16[528,128]{1,0:T(8,128)(2,1)}, bf16[528,128]{1,0:T(8,128)(2,1)}, u32[]{:S(2)}, u32[]{:S(2)}) collective-permute-start(bf16[528,128]{1,0:T(8,128)(2,1)} %get-tuple-element.132), channel_id=1, source_target_pairs={{0,4},{2,6},{4,0},{6,2},{1,5},{3,7},{5,1},{7,3},{8,12},{10,14},{12... | collective-permute-start | bytes 405512 | tf_op jit(solution)/shard_map/ppermute | solution.py:715
  31.6 9.5 %collective-permute-start.4 = (bf16[528,128]{1,0:T(8,128)(2,1)}, bf16[528,128]{1,0:T(8,128)(2,1)}, u32[]{:S(2)}, u32[]{:S(2)}) collective-permute-start(bf16[528,128]{1,0:T(8,128)(2,1)} %get-tuple-element.133), channel_id=1, source_target_pairs={{0,6},{2,4},{4,2},{6,0},{1,7},{3,5},{5,3},{7,1},{8,14},{10,12},{12... | collective-permute-start | bytes 405512 | tf_op jit(solution)/shard_map/ppermute | solution.py:715
  51.5 13.2 %collective-permute-start.11 = (bf16[9,128,256]{2,1,0:T(8,128)(2,1)}, bf16[9,128,256]{2,1,0:T(8,128)(2,1)}, u32[]{:S(2)}, u32[]{:S(2)}) collective-permute-start(bf16[9,128,256]{2,1,0:T(8,128)(2,1)} %collective-permute-done.6.refs_7_.refs_13_), channel_id=1, source_target_pairs={{0,1},{1,0},{2,3},{3,2},{4,5},{5,4},{6,7},{7,6},{8,9},{9,8},{10,11... | collective-permute-start | bytes 1769480 | tf_op jit(solution)/shard_map/ppermute | solution.py:715
  51.7 13.5 %collective-permute-start.10 = (bf16[9,128,256]{2,1,0:T(8,128)(2,1)}, bf16[9,128,256]{2,1,0:T(8,128)(2,1)}, u32[]{:S(2)}, u32[]{:S(2)}) collective-permute-start(bf16[9,128,256]{2,1,0:T(8,128)(2,1)} %collective-permute-done.1.refs_6_.refs_12_), channel_id=1, source_target_pairs={{0,1},{1,0},{2,3},{3,2},{4,5},{5,4},{6,7},{7,6},{8,9},{9,8},{10,11... | collective-permute-start | bytes 1769480 | tf_op jit(solution)/shard_map/ppermute | solution.py:715
  52.1 14.1 %collective-permute-start.9 = (bf16[9,128,256]{2,1,0:T(8,128)(2,1)}, bf16[9,128,256]{2,1,0:T(8,128)(2,1)}, u32[]{:S(2)}, u32[]{:S(2)}) collective-permute-start(bf16[9,128,256]{2,1,0:T(8,128)(2,1)} %collective-permute-done.refs_5_.refs_11_), channel_id=1, source_target_pairs={{0,1},{1,0},{2,3},{3,2},{4,5},{5,4},{6,7},{7,6},{8,9},{9,8},{10,11... | collective-permute-start | bytes 1769480 | tf_op jit(solution)/shard_map/ppermute | solution.py:715
  52.2 16.8 %collective-permute-start.8 = (bf16[9,128,256]{2,1,0:T(8,128)(2,1)}, bf16[9,128,256]{2,1,0:T(8,128)(2,1)}, u32[]{:S(2)}, u32[]{:S(2)}) collective-permute-start(bf16[9,128,256]{2,1,0:T(8,128)(2,1)} %dynamic-slice_convert_fusion.refs_4_.refs_10_), channel_id=1, source_target_pairs={{0,1},{1,0},{2,3},{3,2},{4,5},{5,4},{6,7},{7,6},{8,9},{9,8},{10,11... | collective-permute-start | bytes 1769480 | tf_op jit(solution)/shard_map/ppermute | solution.py:715
  52.6 12.1 %all-to-all-start.1 = ((f32[32,8,128]{2,1,0:T(8,128)}), f32[32,8,128]{2,1,0:T(8,128)}, u32[]{:S(2)}, u32[]{:S(2)}) async-start(f32[32,8,128]{2,1,0:T(8,128)} %get-tuple-element.142), calls=%async_computation.1 | async-start | bytes 262144 | tf_op jit(solution)/shard_map/all_to_all | solution.py:741
  56.5 12.5 %collective-permute-start.7 = (f32[256,256]{1,0:T(8,128)}, f32[256,256]{1,0:T(8,128)}, u32[]{:S(2)}, u32[]{:S(2)}) collective-permute-start(f32[256,256]{1,0:T(8,128)} %get-tuple-element.141), channel_id=1, source_target_pairs={{0,1},{1,0},{2,3},{3,2},{4,5},{5,4},{6,7},{7,6},{8,9},{9,8},{10,11... | collective-permute-start | bytes 786440 | tf_op jit(solution)/shard_map/ppermute | solution.py:715
  64.7 11.8 %collective-permute-start.12 = (bf16[256,512]{1,0:T(8,128)(2,1)}, bf16[256,512]{1,0:T(8,128)(2,1)}, u32[]{:S(2)}, u32[]{:S(2)}) collective-permute-start(bf16[256,512]{1,0:T(8,128)(2,1)} %get-tuple-element.156.refs_6_.refs_4_.refs_19_), channel_id=1, source_target_pairs={{0,2},{2,0},{4,6},{6,4},{1,3},{3,1},{5,7},{7,5},{8,10},{10,8},{12,... | collective-permute-start | bytes 786440 | tf_op jit(solution)/shard_map/ppermute | solution.py:715
  65.2 14.0 %collective-permute-start.13 = (bf16[256,512]{1,0:T(8,128)(2,1)}, bf16[256,512]{1,0:T(8,128)(2,1)}, u32[]{:S(2)}, u32[]{:S(2)}) collective-permute-start(bf16[256,512]{1,0:T(8,128)(2,1)} %get-tuple-element.156.refs_6_.refs_4_.refs_19_), channel_id=1, source_target_pairs={{0,4},{2,6},{4,0},{6,2},{1,5},{3,7},{5,1},{7,3},{8,12},{10,14},{12... | collective-permute-start | bytes 786440 | tf_op jit(solution)/shard_map/ppermute | solution.py:715
  66.2 13.0 %collective-permute-start.14 = (bf16[256,512]{1,0:T(8,128)(2,1)}, bf16[256,512]{1,0:T(8,128)(2,1)}, u32[]{:S(2)}, u32[]{:S(2)}) collective-permute-start(bf16[256,512]{1,0:T(8,128)(2,1)} %get-tuple-element.156.refs_6_.refs_4_.refs_19_), channel_id=1, source_target_pairs={{0,6},{2,4},{4,2},{6,0},{1,7},{3,5},{5,3},{7,1},{8,14},{10,12},{12... | collective-permute-start | bytes 786440 | tf_op jit(solution)/shard_map/ppermute | solution.py:715
  73.2 11.5 %all-to-all-start.2 = ((f32[32,8,128]{2,1,0:T(8,128)}), f32[32,8,128]{2,1,0:T(8,128)}, u32[]{:S(2)}, u32[]{:S(2)}) async-start(f32[32,8,128]{2,1,0:T(8,128)} %get-tuple-element.154), calls=%async_computation.2 | async-start | bytes 262144 | tf_op jit(solution)/shard_map/all_to_all | solution.py:741
  91.9 14.6 %all-to-all-start.3 = ((bf16[32,32,128]{2,1,0:T(8,128)(2,1)}), bf16[32,32,128]{2,1,0:T(8,128)(2,1)}, u32[]{:S(2)}, u32[]{:S(2)}) async-start(bf16[32,32,128]{2,1,0:T(8,128)(2,1)} %bitcast.47), calls=%async_computation.3 | async-start | bytes 524288 | tf_op jit(solution)/shard_map/all_to_all | solution.py:741
  95.4 11.1 %collective-permute-start.15 = (bf16[256,128]{1,0:T(8,128)(2,1)}, bf16[256,128]{1,0:T(8,128)(2,1)}, u32[]{:S(2)}, u32[]{:S(2)}) collective-permute-start(bf16[256,128]{1,0:T(8,128)(2,1)} %get-tuple-element.170), channel_id=1, source_target_pairs={{0,2},{2,0},{4,6},{6,4},{1,3},{3,1},{5,7},{7,5},{8,10},{10,8},{12,... | collective-permute-start | bytes 196616 | tf_op jit(solution)/shard_map/ppermute | solution.py:715
  96.9 9.7 %collective-permute-start.16 = (bf16[256,128]{1,0:T(8,128)(2,1)}, bf16[256,128]{1,0:T(8,128)(2,1)}, u32[]{:S(2)}, u32[]{:S(2)}) collective-permute-start(bf16[256,128]{1,0:T(8,128)(2,1)} %get-tuple-element.171), channel_id=1, source_target_pairs={{0,4},{2,6},{4,0},{6,2},{1,5},{3,7},{5,1},{7,3},{8,12},{10,14},{12... | collective-permute-start | bytes 196616 | tf_op jit(solution)/shard_map/ppermute | solution.py:715
  98.4 8.2 %collective-permute-start.17 = (bf16[256,128]{1,0:T(8,128)(2,1)}, bf16[256,128]{1,0:T(8,128)(2,1)}, u32[]{:S(2)}, u32[]{:S(2)}) collective-permute-start(bf16[256,128]{1,0:T(8,128)(2,1)} %get-tuple-element.172), channel_id=1, source_target_pairs={{0,6},{2,4},{4,2},{6,0},{1,7},{3,5},{5,3},{7,1},{8,14},{10,12},{12... | collective-permute-start | bytes 196616 | tf_op jit(solution)/shard_map/ppermute | solution.py:715
  114.7 2.1 collective-permute-start.18
  116.9 9.1 %collective-permute-start.19 = (bf16[1152,128]{1,0:T(8,128)(2,1)S(1)}, bf16[1152,128]{1,0:T(8,128)(2,1)S(1)}, u32[]{:S(2)}, u32[]{:S(2)}) collective-permute-start(bf16[1152,128]{1,0:T(8,128)(2,1)S(1)} %get-tuple-element.177), channel_id=1, source_target_pairs={{0,8},{8,0},{16,24},{24,16},{1,9},{9,1},{17,25},{25,17},{2,10},{10... | collective-permute-start | bytes 884744 | tf_op jit(solution)/shard_map/ppermute | solution.py:715
  118.5 10.2 %collective-permute-start.20 = (bf16[512,256]{1,0:T(8,128)(2,1)S(1)}, bf16[512,256]{1,0:T(8,128)(2,1)S(1)}, u32[]{:S(2)}, u32[]{:S(2)}) collective-permute-start(bf16[512,256]{1,0:T(8,128)(2,1)S(1)} %copy-done.17), channel_id=1, source_target_pairs={{0,2},{2,0},{4,6},{6,4},{1,3},{3,1},{5,7},{7,5},{8,10},{10,8},{12,... | collective-permute-start | bytes 786440 | tf_op jit(solution)/shard_map/ppermute | solution.py:715
  119.9 13.4 %collective-permute-start.21 = (bf16[512,256]{1,0:T(8,128)(2,1)S(1)}, bf16[512,256]{1,0:T(8,128)(2,1)S(1)}, u32[]{:S(2)}, u32[]{:S(2)}) collective-permute-start(bf16[512,256]{1,0:T(8,128)(2,1)S(1)} %copy-done.17), channel_id=1, source_target_pairs={{0,4},{2,6},{4,0},{6,2},{1,5},{3,7},{5,1},{7,3},{8,12},{10,14},{12... | collective-permute-start | bytes 786440 | tf_op jit(solution)/shard_map/ppermute | solution.py:715
  121.4 11.9 %collective-permute-start.22 = (bf16[512,256]{1,0:T(8,128)(2,1)S(1)}, bf16[512,256]{1,0:T(8,128)(2,1)S(1)}, u32[]{:S(2)}, u32[]{:S(2)}) collective-permute-start(bf16[512,256]{1,0:T(8,128)(2,1)S(1)} %copy-done.17), channel_id=1, source_target_pairs={{0,6},{2,4},{4,2},{6,0},{1,7},{3,5},{5,3},{7,1},{8,14},{10,12},{12... | collective-permute-start | bytes 786440 | tf_op jit(solution)/shard_map/ppermute | solution.py:715
  126.2 9.2 %collective-permute-start.23 = (bf16[576,128]{1,0:T(8,128)(2,1)S(1)}, bf16[576,128]{1,0:T(8,128)(2,1)S(1)}, u32[]{:S(2)}, u32[]{:S(2)}) collective-permute-start(bf16[576,128]{1,0:T(8,128)(2,1)S(1)} %get-tuple-element.180), channel_id=1, source_target_pairs={{0,16},{8,24},{16,0},{24,8},{1,17},{9,25},{17,1},{25,9},{2,18},{10... | collective-permute-start | bytes 442376 | tf_op jit(solution)/shard_map/ppermute | solution.py:715
  135.4 9.0 %collective-permute-start.27 = (bf16[576,128]{1,0:T(8,128)(2,1)S(1)}, bf16[576,128]{1,0:T(8,128)(2,1)S(1)}, u32[]{:S(2)}, u32[]{:S(2)}) collective-permute-start(bf16[576,128]{1,0:T(8,128)(2,1)S(1)} %add_convert_fusion.refs_1_), channel_id=1, source_target_pairs={{0,16},{8,24},{16,0},{24,8},{1,17},{9,25},{17,1},{25,9},{2,18},{10... | collective-permute-start | bytes 442376 | tf_op jit(solution)/shard_map/ppermute | solution.py:715
  138.5 12.9 %collective-permute-start.24 = (bf16[2304,128]{1,0:T(8,128)(2,1)S(1)}, bf16[2304,128]{1,0:T(8,128)(2,1)S(1)}, u32[]{:S(2)}, u32[]{:S(2)}) collective-permute-start(bf16[2304,128]{1,0:T(8,128)(2,1)S(1)} %get-tuple-element.183), channel_id=1, source_target_pairs={{0,1},{1,0},{2,3},{3,2},{4,5},{5,4},{6,7},{7,6},{8,9},{9,8},{10,11... | collective-permute-start | bytes 1769480 | tf_op jit(solution)/shard_map/ppermute | solution.py:715
  144.4 6.8 %collective-permute-start.28 = (bf16[1152,128]{1,0:T(8,128)(2,1)S(1)}, bf16[1152,128]{1,0:T(8,128)(2,1)S(1)}, u32[]{:S(2)}, u32[]{:S(2)}) collective-permute-start(bf16[1152,128]{1,0:T(8,128)(2,1)S(1)} %shard_map.358.refs_1_), channel_id=1, source_target_pairs={{0,8},{8,0},{16,24},{24,16},{1,9},{9,1},{17,25},{25,17},{2,10},{10... | collective-permute-start | bytes 884744 | tf_op jit(solution)/shard_map/ppermute | solution.py:715
  151.3 12.3 %collective-permute-start.29 = (bf16[2304,128]{1,0:T(8,128)(2,1)S(1)}, bf16[2304,128]{1,0:T(8,128)(2,1)S(1)}, u32[]{:S(2)}, u32[]{:S(2)}) collective-permute-start(bf16[2304,128]{1,0:T(8,128)(2,1)S(1)} %shard_map.359.refs_1_), channel_id=1, source_target_pairs={{0,1},{1,0},{2,3},{3,2},{4,5},{5,4},{6,7},{7,6},{8,9},{9,8},{10,11... | collective-permute-start | bytes 1769480 | tf_op jit(solution)/shard_map/ppermute | solution.py:715
  151.6 9.5 %collective-permute-start.25 = (bf16[1152,128]{1,0:T(8,128)(2,1)S(1)}, bf16[1152,128]{1,0:T(8,128)(2,1)S(1)}, u32[]{:S(2)}, u32[]{:S(2)}) collective-permute-start(bf16[1152,128]{1,0:T(8,128)(2,1)S(1)} %get-tuple-element.185), channel_id=1, source_target_pairs={{0,8},{8,0},{16,24},{24,16},{1,9},{9,1},{17,25},{25,17},{2,10},{10... | collective-permute-start | bytes 884744 | tf_op jit(solution)/shard_map/ppermute | solution.py:715
  161.1 9.6 %collective-permute-start.26 = (bf16[576,128]{1,0:T(8,128)(2,1)S(1)}, bf16[576,128]{1,0:T(8,128)(2,1)S(1)}, u32[]{:S(2)}, u32[]{:S(2)}) collective-permute-start(bf16[576,128]{1,0:T(8,128)(2,1)S(1)} %get-tuple-element.187), channel_id=1, source_target_pairs={{0,16},{8,24},{16,0},{24,8},{1,17},{9,25},{17,1},{25,9},{2,18},{10... | collective-permute-start | bytes 442376 | tf_op jit(solution)/shard_map/ppermute | solution.py:715
  170.8 9.0 %collective-permute-start.34 = (bf16[576,128]{1,0:T(8,128)(2,1)S(1)}, bf16[576,128]{1,0:T(8,128)(2,1)S(1)}, u32[]{:S(2)}, u32[]{:S(2)}) collective-permute-start(bf16[576,128]{1,0:T(8,128)(2,1)S(1)} %get-tuple-element.190.refs_1_), channel_id=1, source_target_pairs={{0,16},{8,24},{16,0},{24,8},{1,17},{9,25},{17,1},{25,9},{2,18},{10... | collective-permute-start | bytes 442376 | tf_op jit(solution)/shard_map/ppermute | solution.py:715
  170.9 10.5 %collective-permute-start.35 = (bf16[576,128]{1,0:T(8,128)(2,1)S(1)}, bf16[576,128]{1,0:T(8,128)(2,1)S(1)}, u32[]{:S(2)}, u32[]{:S(2)}) collective-permute-start(bf16[576,128]{1,0:T(8,128)(2,1)S(1)} %get-tuple-element.198.refs_1_), channel_id=1, source_target_pairs={{0,2},{2,0},{4,6},{6,4},{1,3},{3,1},{5,7},{7,5},{8,10},{10,8},{12,... | collective-permute-start | bytes 442376 | tf_op jit(solution)/shard_map/ppermute | solution.py:715
  172.5 10.7 %collective-permute-start.36 = (bf16[576,128]{1,0:T(8,128)(2,1)S(1)}, bf16[576,128]{1,0:T(8,128)(2,1)S(1)}, u32[]{:S(2)}, u32[]{:S(2)}) collective-permute-start(bf16[576,128]{1,0:T(8,128)(2,1)S(1)} %get-tuple-element.198.refs_1_), channel_id=1, source_target_pairs={{0,4},{2,6},{4,0},{6,2},{1,5},{3,7},{5,1},{7,3},{8,12},{10,14},{12... | collective-permute-start | bytes 442376 | tf_op jit(solution)/shard_map/ppermute | solution.py:715
  174.0 9.3 %collective-permute-start.37 = (bf16[576,128]{1,0:T(8,128)(2,1)S(1)}, bf16[576,128]{1,0:T(8,128)(2,1)S(1)}, u32[]{:S(2)}, u32[]{:S(2)}) collective-permute-start(bf16[576,128]{1,0:T(8,128)(2,1)S(1)} %get-tuple-element.198.refs_1_), channel_id=1, source_target_pairs={{0,6},{2,4},{4,2},{6,0},{1,7},{3,5},{5,3},{7,1},{8,14},{10,12},{12... | collective-permute-start | bytes 442376 | tf_op jit(solution)/shard_map/ppermute | solution.py:715
  174.5 28.5 %collective-permute-start.30 = (bf16[2304,128]{1,0:T(8,128)(2,1)S(1)}, bf16[2304,128]{1,0:T(8,128)(2,1)S(1)}, u32[]{:S(2)}, u32[]{:S(2)}) collective-permute-start(bf16[2304,128]{1,0:T(8,128)(2,1)S(1)} %get-tuple-element.188.refs_1_), channel_id=1, source_target_pairs={{0,2},{2,0},{4,6},{6,4},{1,3},{3,1},{5,7},{7,5},{8,10},{10,8},{12,... | collective-permute-start | bytes 1769480 | tf_op jit(solution)/shard_map/ppermute | solution.py:715
  179.9 26.2 %collective-permute-start.31 = (bf16[2304,128]{1,0:T(8,128)(2,1)S(1)}, bf16[2304,128]{1,0:T(8,128)(2,1)S(1)}, u32[]{:S(2)}, u32[]{:S(2)}) collective-permute-start(bf16[2304,128]{1,0:T(8,128)(2,1)S(1)} %get-tuple-element.188.refs_1_), channel_id=1, source_target_pairs={{0,4},{2,6},{4,0},{6,2},{1,5},{3,7},{5,1},{7,3},{8,12},{10,14},{12... | collective-permute-start | bytes 1769480 | tf_op jit(solution)/shard_map/ppermute | solution.py:715
  181.4 24.7 %collective-permute-start.32 = (bf16[2304,128]{1,0:T(8,128)(2,1)S(1)}, bf16[2304,128]{1,0:T(8,128)(2,1)S(1)}, u32[]{:S(2)}, u32[]{:S(2)}) collective-permute-start(bf16[2304,128]{1,0:T(8,128)(2,1)S(1)} %get-tuple-element.188.refs_1_), channel_id=1, source_target_pairs={{0,6},{2,4},{4,2},{6,0},{1,7},{3,5},{5,3},{7,1},{8,14},{10,12},{12... | collective-permute-start | bytes 1769480 | tf_op jit(solution)/shard_map/ppermute | solution.py:715
  183.6 9.1 %collective-permute-start.38 = (bf16[576,128]{1,0:T(8,128)(2,1)S(1)}, bf16[576,128]{1,0:T(8,128)(2,1)S(1)}, u32[]{:S(2)}, u32[]{:S(2)}) collective-permute-start(bf16[576,128]{1,0:T(8,128)(2,1)S(1)} %shard_map.368.refs_1_), channel_id=1, source_target_pairs={{0,16},{8,24},{16,0},{24,8},{1,17},{9,25},{17,1},{25,9},{2,18},{10... | collective-permute-start | bytes 442376 | tf_op jit(solution)/shard_map/ppermute | solution.py:715
  192.8 10.0 %collective-permute-start.39 = (bf16[1152,128]{1,0:T(8,128)(2,1)S(1)}, bf16[1152,128]{1,0:T(8,128)(2,1)S(1)}, u32[]{:S(2)}, u32[]{:S(2)}) collective-permute-start(bf16[1152,128]{1,0:T(8,128)(2,1)S(1)} %shard_map.369.refs_1_), channel_id=1, source_target_pairs={{0,8},{8,0},{16,24},{24,16},{1,9},{9,1},{17,25},{25,17},{2,10},{10... | collective-permute-start | bytes 884744 | tf_op jit(solution)/shard_map/ppermute | solution.py:715
  192.9 15.0 %collective-permute-start.41 = (bf16[1152,128]{1,0:T(8,128)(2,1)S(1)}, bf16[1152,128]{1,0:T(8,128)(2,1)S(1)}, u32[]{:S(2)}, u32[]{:S(2)}) collective-permute-start(bf16[1152,128]{1,0:T(8,128)(2,1)S(1)} %shard_map.367.refs_1_), channel_id=1, source_target_pairs={{0,8},{8,0},{16,24},{24,16},{1,9},{9,1},{17,25},{25,17},{2,10},{10... | collective-permute-start | bytes 884744 | tf_op jit(solution)/shard_map/ppermute | solution.py:715
  202.8 5.3 %collective-permute-start.40 = (bf16[2304,128]{1,0:T(8,128)(2,1)S(1)}, bf16[2304,128]{1,0:T(8,128)(2,1)S(1)}, u32[]{:S(2)}, u32[]{:S(2)}) collective-permute-start(bf16[2304,128]{1,0:T(8,128)(2,1)S(1)} %shard_map.371.refs_1_), channel_id=1, source_target_pairs={{0,1},{1,0},{2,3},{3,2},{4,5},{5,4},{6,7},{7,6},{8,9},{9,8},{10,11... | collective-permute-start | bytes 1769480 | tf_op jit(solution)/shard_map/ppermute | solution.py:715
  208.0 9.2 %collective-permute-start.42 = (bf16[2304,128]{1,0:T(8,128)(2,1)S(1)}, bf16[2304,128]{1,0:T(8,128)(2,1)S(1)}, u32[]{:S(2)}, u32[]{:S(2)}) collective-permute-start(bf16[2304,128]{1,0:T(8,128)(2,1)S(1)} %shard_map.374.refs_1_), channel_id=1, source_target_pairs={{0,1},{1,0},{2,3},{3,2},{4,5},{5,4},{6,7},{7,6},{8,9},{9,8},{10,11... | collective-permute-start | bytes 1769480 | tf_op jit(solution)/shard_map/ppermute | solution.py:715
  212.2 7.3 %collective-permute-start.43 = (f32[8,128]{1,0:T(8,128)S(1)}, f32[8,128]{1,0:T(8,128)S(1)}, u32[]{:S(2)}, u32[]{:S(2)}) collective-permute-start(f32[8,128]{1,0:T(8,128)S(1)} %get-tuple-element.206.refs_0_), channel_id=1, source_target_pairs={{0,2},{2,0},{4,6},{6,4},{1,3},{3,1},{5,7},{7,5},{8,10},{10,8},{12,... | collective-permute-start | bytes 12296 | tf_op jit(solution)/shard_map/ppermute | solution.py:715
  215.5 4.1 %collective-permute-start.44 = (f32[8,128]{1,0:T(8,128)S(1)}, f32[8,128]{1,0:T(8,128)S(1)}, u32[]{:S(2)}, u32[]{:S(2)}) collective-permute-start(f32[8,128]{1,0:T(8,128)S(1)} %get-tuple-element.206.refs_0_), channel_id=1, source_target_pairs={{0,4},{2,6},{4,0},{6,2},{1,5},{3,7},{5,1},{7,3},{8,12},{10,14},{12... | collective-permute-start | bytes 12296 | tf_op jit(solution)/shard_map/ppermute | solution.py:715
  217.2 4.5 %collective-permute-start.45 = (f32[8,128]{1,0:T(8,128)S(1)}, f32[8,128]{1,0:T(8,128)S(1)}, u32[]{:S(2)}, u32[]{:S(2)}) collective-permute-start(f32[8,128]{1,0:T(8,128)S(1)} %get-tuple-element.206.refs_0_), channel_id=1, source_target_pairs={{0,6},{2,4},{4,2},{6,0},{1,7},{3,5},{5,3},{7,1},{8,14},{10,12},{12... | collective-permute-start | bytes 12296 | tf_op jit(solution)/shard_map/ppermute | solution.py:715
  (34 other events, 398.0 us)

commit v6 on v5

--- a/solution.py
+++ b/solution.py
@@ -397,15 +397,17 @@
 ):
     me, side = place_ref[0], place_ref[1]
     depth, half = near_refs[0].shape[1:]
-    copies = []
-    for refs, at in ((near_refs, side), (far_refs, 1 - side)):
-        lanes = pl.ds(pl.multiple_of(at * half, half), half)
-        for step, slot_ref in enumerate(refs):
-            span = pl.ds(pl.multiple_of((me ^ step) * depth, depth), depth)
-            copies.append(
-                pltpu.make_async_copy(slot_ref, weight_ref.at[:, span, lanes], arrived.at[len(copies)])
-            )
-            copies[-1].start()
+    copies = {}
+    for tap in range(0, TAPS, 3):
+        for which, (refs, at) in enumerate(((near_refs, side), (far_refs, 1 - side))):
+            lanes = pl.ds(pl.multiple_of(at * half, half), half)
+            for step, slot_ref in enumerate(refs):
+                span = pl.ds(pl.multiple_of((me ^ step) * depth, depth), depth)
+                number = which * len(refs) + step
+                copies[tap, number] = pltpu.make_async_copy(
+                    slot_ref.at[tap : tap + 3], weight_ref.at[tap : tap + 3, span, lanes], arrived.at[tap // 3, number]
+                )
+                copies[tap, number].start()
     total = total_of(got_ref)
     sums_out_ref[...] = total
     groups = total.shape[0] // 2
@@ -419,12 +421,13 @@
         ).astype(BF)
     grad_ref.send()
     sums_out_ref.send()
-    for copy in copies:
-        copy.wait()
     rows, channels = grad_ref.shape
     part = rows // PIX
     sum_ref[...] = jnp.zeros_like(sum_ref)
     for tap in range(TAPS):
+        if tap % 3 == 0:
+            for number in range(2 * len(near_refs)):
+                copies[tap, number].wait()
         product = matmul(grad_ref[...], weight_ref[tap], NT)
         row_step, col_step = OFFSETS[tap]
         for to_row, from_row, length in runs(-row_step, -col_step, part):
@@ -452,7 +455,7 @@
 
 def first_products_kernel(
     place_ref, got_ref, norm_ref, mask_ref, basis_ref, old_refs, big_refs, part_refs, scaled_refs,
-    out_ref, sums_ref, small_ref, left_ref, right_ref, slot_ref, column_ref, mask_slot_ref,
+    kept_ref, sent_ref, sums_ref, small_ref, left_ref, right_ref, slot_ref, column_ref, mask_slot_ref, out_ref,
 ):
     me = place_ref[0]
     rows, width = part_refs[0].shape
@@ -487,6 +490,9 @@
             part_refs[step][...].astype(F32) - mask_slot_ref[...].astype(F32) * (fixed + moved)
         ).astype(BF)
     taps_kernel(-1, big_refs, [slot_ref.at[step] for step in range(groups)], out_ref, left_ref, right_ref)
+    half = kept_ref.shape[0]
+    sent_ref[...] = out_ref[pl.ds(pl.multiple_of((1 - place_ref[1]) * half, half), half), :]
+    kept_ref[...] = out_ref[pl.ds(pl.multiple_of(place_ref[1] * half, half), half), :]
 
 
 def left_second_kernel(place_ref, norm_ref, mask_ref, basis_ref, scaled_refs, left_refs, column_ref, wide_ref):
@@ -662,14 +668,19 @@
 
 def update_kernel(
     square_refs, weight_refs, mean_refs, square_moment_refs, grad_refs, small_refs,
-    weight_outs, mean_outs, square_outs, small_outs, scalar_outs,
+    weight_outs, mean_outs, square_outs, small_outs, scalar_outs, norm_ref,
 ):
-    parts = [ref[...] for ref in square_refs]
-    while len(parts) > 1:
-        parts = [parts[at] + parts[at + 1] for at in range(0, len(parts), 2)]
-    total = jnp.sum(jnp.sum(parts[0], axis=1, keepdims=True), axis=0, keepdims=True)
-    grad_norm = jnp.sqrt(total)
-    factor = CLIP_NORM / jnp.maximum(grad_norm, CLIP_NORM)
+    @pl.when(pl.program_id(0) == 0)
+    def _():
+        parts = [ref[...] for ref in square_refs]
+        while len(parts) > 1:
+            parts = [parts[at] + parts[at + 1] for at in range(0, len(parts), 2)]
+        total = jnp.sum(jnp.sum(parts[0], axis=1, keepdims=True), axis=0, keepdims=True)
+        found = jnp.sqrt(total)
+        norm_ref[0:1, :] = jnp.broadcast_to(found, (1, LANES))
+        norm_ref[1:2, :] = jnp.broadcast_to(CLIP_NORM / jnp.maximum(found, CLIP_NORM), (1, LANES))
+
+    grad_norm, factor = norm_ref[0:1, 0:1], norm_ref[1:2, 0:1]
 
     def moments(gradient, mean_old, square_old):
         mean_new = BETA_ONE * mean_old + (1.0 - BETA_ONE) * gradient
@@ -973,7 +984,7 @@
             pltpu.VMEM(wide, BF),
             pltpu.VMEM((TAPS, channels, channels), BF),
             pltpu.VMEM(wide, F32),
-            pltpu.SemaphoreType.DMA((2 * groups,)),
+            pltpu.SemaphoreType.DMA((3, 2 * groups)),
         ],
         raw=tuple(range(10, 10 + 2 * groups)),
         flops=2 * rows * channels * channels * TAPS,
@@ -1059,12 +1070,12 @@
 
     near_steps = len(bits_of("cin"))
     left_parts = [left_turned[step] for step in range(groups)]
-    products_first, sums_first, smalls = call(
+    *products_first, sums_first, smalls = call(
         lambda *refs: first_products_kernel(
             *refs[:5], refs[5:11], *[refs[11 + at * groups : 11 + (at + 1) * groups] for at in range(3)],
             *refs[11 + 3 * groups :]
         ),
-        [shape((TAPS * channels, width), BF), shape((8, LANES), F32), shape((72, LANES), F32)],
+        [shape((TAPS * channels // 2, width), BF)] * 2 + [shape((8, LANES), F32), shape((72, LANES), F32)],
         [
             place, after(got, right_turned, *left_slots), norm_first, all_mask, basis_out_first, *small_old, *left_parts, *right_parts, *scaled_slots,
         ],
@@ -1074,13 +1085,14 @@
             pltpu.VMEM((groups, rows, width), BF),
             pltpu.VMEM((channels, width), BF),
             pltpu.VMEM((rows, LANES), BF),
+            pltpu.VMEM((TAPS * channels, width), BF),
         ],
-        near_out=(0,),
+        near_out=(0, 1),
         room=56,
         flops=2 * groups * rows * channels * width * TAPS,
     )
-    terms_first = [products_first]
-    for order in orders:
+    terms_first = crossed(products_first, *orders[0])
+    for order in orders[1:]:
         terms_first = halved(terms_first, *order)
     own_first = joined([after(terms_first[0], *right_slots), terms_first[1]])
     coeff_first = doubled(own_first, *orders[-1])
@@ -1153,8 +1165,8 @@
     smalls = [small_grads]
     small_outs = [shape((2, width), F32)] * 4 + [shape((CLASSES, width), F32)] * 2 + [shape((1, CLASSES), F32)] * 2
     small_outs += [shape((1, 1), F32)] * 2
-    first_spec = pl.BlockSpec((1, channels, width), lambda tap: (tap, 0, 0))
-    second_spec = pl.BlockSpec((1, width, channels), lambda tap: (tap, 0, 0))
+    first_spec = pl.BlockSpec((3, channels, width), lambda tap: (tap, 0, 0))
+    second_spec = pl.BlockSpec((3, width, channels), lambda tap: (tap, 0, 0))
     pair = [first_spec, second_spec]
     first_like, second_like = shape(w_first.shape, F32), shape(w_second.shape, F32)
 
@@ -1170,12 +1182,13 @@
 
         update_kernel(
             take(groups), take(2), take(2), take(2), take(2), take(len(smalls)),
-            take(2), take(2), take(2), take(len(small_outs) - 2), take(2),
+            take(2), take(2), take(2), take(len(small_outs) - 2), take(2), take(1)[0],
         )
 
     results = pl.pallas_call(
         update,
-        grid=(TAPS,),
+        grid=(TAPS // 3,),
+        scratch_shapes=[pltpu.VMEM((8, LANES), F32)],
         in_specs=[pl.BlockSpec(memory_space=pltpu.VMEM)] * (groups + 8 + len(smalls)),
         out_specs=pair * 3 + [whole(leaf) for leaf in small_outs],
         out_shape=[first_like, second_like] * 3 + small_outs,

time: 231 us -> 230 us (level)
    pallas_call x36 -> x35, Pallas kernels: 57.9 us -> 57.5 us  [call(): pl.pallas_call(body, out_shape=list(outs), in_specs=specs, out_specs=[pl....]
where the time goes in v6:
time: 230 us; the launch traced here: 229 us
  waiting for transfers between devices  81.6 us (35%)
  Pallas kernels  67.5 us (29%)
  starting transfers between devices  61.4 us (27%)
  local copies, waits for them, and re-layouts  15.8 us (7%)
    ppermute x46, waiting for transfers between devices, swap(): lax.ppermute(values, axis, [(here, here ^ step) for here in range(count)])  71.2 us
    pallas_call x35, Pallas kernels, call(): pl.pallas_call(body, out_shape=list(outs), in_specs=specs, out_specs=[pl....  57.5 us
    ppermute x46, starting transfers between devices, swap(): lax.ppermute(values, axis, [(here, here ^ step) for here in range(count)])  45.8 us
    all_to_all x3, starting transfers between devices, every_device(): return lax.all_to_all(tiles, EVERY, 0, 0, tiled=True)  10.7 us
    all_to_all x3, waiting for transfers between devices, every_device(): return lax.all_to_all(tiles, EVERY, 0, 0, tiled=True)  10.5 us
    pallas_call x1, Pallas kernels, local(): pl.pallas_call(update, grid=(TAPS // 3,), scratch_shapes=[pltpu.VMEM((8,...  7.79 us
    unnamed x64, local copies, waits for them, and re-layouts  5.08 us
    all_to_all x1, starting transfers between devices, local(): got = lax.all_to_all(stats, ('dp', 'cin'), 0, 0, tiled=True)  4.89 us
  transfers between devices with their start and end apart: 50, of which 21 were waited for; matrix products, arithmetic and copies ran while one was open for 4% of the time, Pallas kernels for 18%

profile of v6, /device:TPU:0, one launch (start us, length us, event | category | flops | bytes accessed | tf_op | source)
XLA Modules:
  0.0 229.3 jit_solution(3880641856031731475)
XLA Ops:
  0.7 2.2 dynamic-slice_convert_fusion.refs_4_.refs_10_
  2.8 2.9 %collective-permute-start = (bf16[9,128,256]{2,1,0:T(8,128)(2,1)}, bf16[9,128,256]{2,1,0:T(8,128)(2,1)}, u32[]{:S(2)}, u32[]{:S(2)}) collective-permute-start(bf16[9,128,256]{2,1,0:T(8,128)(2,1)} %dynamic-slice_convert_fusion.refs_4_.refs_10_), channel_id=1, source_target_pairs={{0,2},{2,0},{4,6},{6,4},{1,3},{3,1},{5,7},{7,5},{8,10},{10,8},{12,... | collective-permute-start | bytes 1769480 | tf_op jit(solution)/shard_map/ppermute | solution.py:726
  7.9 5.4 %shard_map.340 = (f32[1024,128]{1,0:T(8,128)}, bf16[1024,128]{1,0:T(8,128)(2,1)}, f32[8,8,128]{2,1,0:T(8,128)}, f32[256,128]{1,0:T(8,128)}) custom-call(s32[2]{0:T(128)} %pad_add_fusion.refs_0_, bf16[1024,512]{1,0:T(8,128)(2,1)} %bitcast.44, s32[16,64]{1,0:T(8,128)} %refs_2_.3, f32[9,512,128]{2,1,0:T(8,128)} %refs_0_), custom_call_target="tpu_custom_call" | custom-call | flops 1207959552 | bytes 4362248 | tf_op jit(solution)/shard_map/pallas_call | solution.py:117
  13.4 4.9 %all-to-all-start = ((f32[8,8,128]{2,1,0:T(8,128)}), f32[8,8,128]{2,1,0:T(8,128)S(1)}, u32[]{:S(2)}, u32[]{:S(2)}) async-start(f32[8,8,128]{2,1,0:T(8,128)} %get-tuple-element.122), calls=%async_computation | async-start | bytes 65536 | tf_op jit(solution)/shard_map/all_to_all | solution.py:884
  24.8 3.7 %shard_map.342 = (bf16[528,128]{1,0:T(8,128)(2,1)}, bf16[528,128]{1,0:T(8,128)(2,1)}, bf16[528,128]{1,0:T(8,128)(2,1)}, bf16[528,128]{1,0:T(8,128)(2,1)}, f32[8,128]{1,0:T(8,128)}) custom-call(s32[2]{0:T(128)} %pad_add_fusion.refs_0_, f32[8,8,128]{2,1,0:T(8,128)} %copy-done.29, f32[1024,128]{1,0:T(8,128)} %get-tuple-element.123.refs_2_, ...), custom_call_target="tpu_custom_call" | custom-call | bytes 1371144 | tf_op jit(solution)/shard_map/pallas_call | solution.py:117
  34.1 1.9 copy.39
  36.0 1.7 constant_dynamic-slice_fusion.refs_2_
  38.4 2.6 %collective-permute-done.4.refs_4_ = bf16[528,128]{1,0:T(8,128)(2,1)} collective-permute-done((bf16[528,128]{1,0:T(8,128)(2,1)}, bf16[528,128]{1,0:T(8,128)(2,1)}, u32[]{:S(2)}, u32[]{:S(2)}) %collective-permute-start.4) | collective-permute-done | bytes 135200 | tf_op jit(solution)/shard_map/ppermute | solution.py:726
  41.0 2.8 %shard_map.343.refs_1_ = bf16[256,640]{1,0:T(8,128)(2,1)} custom-call(s32[2]{0:T(128)} %pad_add_fusion.refs_0_, bf16[528,128]{1,0:T(8,128)(2,1)} %get-tuple-element.129.refs_1_, bf16[528,128]{1,0:T(8,128)(2,1)} %collective-permute-done.2.refs_2_, bf16[528,128]{1,0:T(8,128)(2,1)} %collective-permute-done.3.refs_3_, ...), custom_call_target="tpu_custom_call" | custom-call | bytes 999432 | tf_op jit(solution)/shard_map/pallas_call | solution.py:117
  43.9 1.8 collective-permute-done.5.refs_2_
  46.5 5.0 %shard_map.344 = (f32[256,256]{1,0:T(8,128)}, f32[256,256]{1,0:T(8,128)}, f32[32,8,128]{2,1,0:T(8,128)}) custom-call(s32[2]{0:T(128)} %pad_add_fusion.refs_0_, bf16[256,640]{1,0:T(8,128)(2,1)} %shard_map.343.refs_1_, bf16[256,640]{1,0:T(8,128)(2,1)} %copy-done.30, f32[4,128]{1,0:T(4,128)} %refs_3_.3, ...), custom_call_target="tpu_custom_call" | custom-call | flops 1207959552 | bytes 3672072 | tf_op jit(solution)/shard_map/pallas_call | solution.py:117
  52.6 3.9 %all-to-all-start.1 = ((f32[32,8,128]{2,1,0:T(8,128)}), f32[32,8,128]{2,1,0:T(8,128)}, u32[]{:S(2)}, u32[]{:S(2)}) async-start(f32[32,8,128]{2,1,0:T(8,128)} %get-tuple-element.141), calls=%async_computation.1 | async-start | bytes 262144 | tf_op jit(solution)/shard_map/all_to_all | solution.py:752
  57.3 2.6 %shard_map.345 = (bf16[256,512]{1,0:T(8,128)(2,1)}, f32[8,512]{1,0:T(8,128)}, bf16[16,512]{1,0:T(8,128)(2,1)}) custom-call(s32[2]{0:T(128)} %pad_add_fusion.refs_0_, bf16[528,128]{1,0:T(8,128)(2,1)} %get-tuple-element.129.refs_1_, bf16[528,128]{1,0:T(8,128)(2,1)} %collective-permute-done.2.refs_2_, bf16[528,128]{1,0:T(8,128)(2,1)} %collective-permute-done.3.refs_3_, ...), custom_call_target="tpu_custom_call" | custom-call | bytes 839688 | tf_op jit(solution)/shard_map/pallas_call | solution.py:117
  59.8 4.9 %all-to-all-done.1.refs_3_ = f32[32,8,128]{2,1,0:T(8,128)} async-done(((f32[32,8,128]{2,1,0:T(8,128)}), f32[32,8,128]{2,1,0:T(8,128)}, u32[]{:S(2)}, u32[]{:S(2)}) %all-to-all-start.1) | async-done | bytes 131104 | tf_op jit(solution)/shard_map/all_to_all | solution.py:752
  66.2 2.1 collective-permute-start.14
  69.0 4.3 %shard_map.346 = (f32[256,512]{1,0:T(8,128)}, f32[8,512]{1,0:T(8,128)}, f32[256,512]{1,0:T(8,128)}, f32[32,8,128]{2,1,0:T(8,128)}, f32[4,16,128]{2,1,0:T(8,128)}) custom-call(s32[2]{0:T(128)} %pad_add_fusion.refs_0_, f32[256,256]{1,0:T(8,128)} %get-tuple-element.139.refs_1_, f32[256,256]{1,0:T(8,128)} %collective-permute-done.7.refs_2_, ...), custom_call_target="tpu_custom_call" | custom-call | bytes 2048584 | tf_op jit(solution)/shard_map/pallas_call | solution.py:117
  73.2 3.3 %all-to-all-start.2 = ((f32[32,8,128]{2,1,0:T(8,128)}), f32[32,8,128]{2,1,0:T(8,128)}, u32[]{:S(2)}, u32[]{:S(2)}) async-start(f32[32,8,128]{2,1,0:T(8,128)} %get-tuple-element.153), calls=%async_computation.2 | async-start | bytes 262144 | tf_op jit(solution)/shard_map/all_to_all | solution.py:752
  76.6 2.6 %collective-permute-done.13.refs_6_.refs_21_ = bf16[256,512]{1,0:T(8,128)(2,1)} collective-permute-done((bf16[256,512]{1,0:T(8,128)(2,1)}, bf16[256,512]{1,0:T(8,128)(2,1)}, u32[]{:S(2)}, u32[]{:S(2)}) %collective-permute-start.13) | collective-permute-done | bytes 262176 | tf_op jit(solution)/shard_map/ppermute | solution.py:726
  79.2 5.6 %all-to-all-done.2.refs_4_ = f32[32,8,128]{2,1,0:T(8,128)} async-done(((f32[32,8,128]{2,1,0:T(8,128)}), f32[32,8,128]{2,1,0:T(8,128)}, u32[]{:S(2)}, u32[]{:S(2)}) %all-to-all-start.2) | async-done | bytes 131104 | tf_op jit(solution)/shard_map/all_to_all | solution.py:752
  84.8 6.7 %shard_map.347 = (bf16[256,512]{1,0:T(8,128)(2,1)}, f32[8,128]{1,0:T(8,128)}, bf16[4,4,2,32,128]{4,3,2,1,0:T(8,128)(2,1)}, bf16[256,128]{1,0:T(8,128)(2,1)}, bf1...) custom-call(s32[2]{0:T(128)} %pad_add_fusion.refs_0_, ...), custom_call_target="tpu_custom_call" | custom-call | flops 1207959552 | bytes 7671816 | tf_op jit(solution)/shard_map/pallas_call | solution.py:117
  91.5 3.5 %all-to-all-start.3 = ((bf16[32,32,128]{2,1,0:T(8,128)(2,1)}), bf16[32,32,128]{2,1,0:T(8,128)(2,1)}, u32[]{:S(2)}, u32[]{:S(2)}) async-start(bf16[32,32,128]{2,1,0:T(8,128)(2,1)} %bitcast.47), calls=%async_computation.3 | async-start | bytes 524288 | tf_op jit(solution)/shard_map/all_to_all | solution.py:752
  99.5 2.2 shard_map.348.refs_0_
  101.7 4.4 %shard_map.349 = (bf16[256,128]{1,0:T(8,128)(2,1)}, bf16[256,128]{1,0:T(8,128)(2,1)}, bf16[256,128]{1,0:T(8,128)(2,1)}, bf16[256,128]{1,0:T(8,128)(2,1)}) custom-call(s32[2]{0:T(128)} %pad_add_fusion.refs_0_, f32[8,512]{1,0:T(8,128)} %get-tuple-element.143.refs_4_.refs_7_.refs_1_.refs_2_, bf16[1024,128]{1,0:T(8,128)(2,1)} %get-tuple-element.162.refs_3_.refs_2_, ...), custom_call_target="tpu_custom_call" | custom-call | bytes 2113544 | tf_op jit(solution)/shard_map/pallas_call | solution.py:117
  106.2 6.8 %shard_map.350 = (bf16[2304,128]{1,0:T(8,128)(2,1)}, bf16[2304,128]{1,0:T(8,128)(2,1)}, f32[8,128]{1,0:T(8,128)}, f32[72,128]{1,0:T(8,128)}) custom-call(s32[2]{0:T(128)} %pad_add_fusion.refs_0_, bf16[32,32,128]{2,1,0:T(8,128)(2,1)} %all-to-all-done.3.refs_1_, f32[8,512]{1,0:T(8,128)} %get-tuple-element.143.refs_4_.refs_7_.refs_1_.refs_2_, ...), custom_call_target="tpu_custom_call" | custom-call | flops 1207959552 | bytes 4659288 | tf_op jit(solution)/shard_map/pallas_call | solution.py:117
  113.1 2.2 collective-permute-done.18.refs_2_
  121.5 4.1 %collective-permute-done.19.refs_2_ = bf16[1152,128]{1,0:T(8,128)(2,1)S(1)} collective-permute-done((bf16[1152,128]{1,0:T(8,128)(2,1)S(1)}, bf16[1152,128]{1,0:T(8,128)(2,1)S(1)}, u32[]{:S(2)}, u32[]{:S(2)}) %collective-permute-start.19) | collective-permute-done | bytes 294944 | tf_op jit(solution)/shard_map/ppermute | solution.py:726
  125.7 2.5 %collective-permute-start.23 = (bf16[576,128]{1,0:T(8,128)(2,1)S(1)}, bf16[576,128]{1,0:T(8,128)(2,1)S(1)}, u32[]{:S(2)}, u32[]{:S(2)}) collective-permute-start(bf16[576,128]{1,0:T(8,128)(2,1)S(1)} %get-tuple-element.178), channel_id=1, source_target_pairs={{0,16},{8,24},{16,0},{24,8},{1,17},{9,25},{17,1},{25,9},{2,18},{10... | collective-permute-start | bytes 442376 | tf_op jit(solution)/shard_map/ppermute | solution.py:726
  128.2 4.7 %collective-permute-done.21.refs_2_ = bf16[512,256]{1,0:T(8,128)(2,1)S(1)} collective-permute-done((bf16[512,256]{1,0:T(8,128)(2,1)S(1)}, bf16[512,256]{1,0:T(8,128)(2,1)S(1)}, u32[]{:S(2)}, u32[]{:S(2)}) %collective-permute-start.21) | collective-permute-done | bytes 262176 | tf_op jit(solution)/shard_map/ppermute | solution.py:726
  132.9 2.0 collective-permute-done.23
  135.5 2.4 %shard_map.353.refs_1_ = bf16[4608,128]{1,0:T(8,128)(2,1)S(1)} custom-call(bf16[512,256]{1,0:T(8,128)(2,1)S(1)} %copy-done.17, bf16[512,256]{1,0:T(8,128)(2,1)S(1)} %collective-permute-done.20.refs_1_, bf16[512,256]{1,0:T(8,128)(2,1)S(1)} %collective-permute-done.21.refs_2_, bf16[512,256]{1,0:T(8,128)(2,1)S(1)} %collective-permute-done.22.refs_3_, ...), custom_call_target="tpu_custom_call" | custom-call | flops 1207959552 | bytes 2490368 | tf_op jit(solution)/shard_map/pallas_call | solution.py:117
  138.1 5.8 %collective-permute-done.27.refs_2_ = bf16[576,128]{1,0:T(8,128)(2,1)S(1)} collective-permute-done((bf16[576,128]{1,0:T(8,128)(2,1)S(1)}, bf16[576,128]{1,0:T(8,128)(2,1)S(1)}, u32[]{:S(2)}, u32[]{:S(2)}) %collective-permute-start.27) | collective-permute-done | bytes 147488 | tf_op jit(solution)/shard_map/ppermute | solution.py:726
  144.1 6.7 %collective-permute-done.28.refs_2_ = bf16[1152,128]{1,0:T(8,128)(2,1)S(1)} collective-permute-done((bf16[1152,128]{1,0:T(8,128)(2,1)S(1)}, bf16[1152,128]{1,0:T(8,128)(2,1)S(1)}, u32[]{:S(2)}, u32[]{:S(2)}) %collective-permute-start.28) | collective-permute-done | bytes 294944 | tf_op jit(solution)/shard_map/ppermute | solution.py:726
  152.0 8.6 %collective-permute-done.25.refs_2_ = bf16[1152,128]{1,0:T(8,128)(2,1)S(1)} collective-permute-done((bf16[1152,128]{1,0:T(8,128)(2,1)S(1)}, bf16[1152,128]{1,0:T(8,128)(2,1)S(1)}, u32[]{:S(2)}, u32[]{:S(2)}) %collective-permute-start.25) | collective-permute-done | bytes 294944 | tf_op jit(solution)/shard_map/ppermute | solution.py:726
  160.7 2.5 %collective-permute-start.26 = (bf16[576,128]{1,0:T(8,128)(2,1)S(1)}, bf16[576,128]{1,0:T(8,128)(2,1)S(1)}, u32[]{:S(2)}, u32[]{:S(2)}) collective-permute-start(bf16[576,128]{1,0:T(8,128)(2,1)S(1)} %get-tuple-element.185), channel_id=1, source_target_pairs={{0,16},{8,24},{16,0},{24,8},{1,17},{9,25},{17,1},{25,9},{2,18},{10... | collective-permute-start | bytes 442376 | tf_op jit(solution)/shard_map/ppermute | solution.py:726
  163.3 2.9 %shard_map.360 = (f32[4608,128]{1,0:T(8,128)}, bf16[2304,128]{1,0:T(8,128)(2,1)S(1)}) custom-call(s32[2]{0:T(128)S(1)} %copy-done.19, bf16[4608,128]{1,0:T(8,128)(2,1)S(1)} %shard_map.359.refs_1_, f32[4608,128]{1,0:T(8,128)S(1)} %bitcast.43), custom_call_target="tpu_custom_call" | custom-call | bytes 6488072 | tf_op jit(solution)/shard_map/pallas_call | solution.py:117
  166.2 4.0 %collective-permute-done.26.refs_1_ = bf16[576,128]{1,0:T(8,128)(2,1)S(1)} collective-permute-done((bf16[576,128]{1,0:T(8,128)(2,1)S(1)}, bf16[576,128]{1,0:T(8,128)(2,1)S(1)}, u32[]{:S(2)}, u32[]{:S(2)}) %collective-permute-start.26) | collective-permute-done | bytes 147488 | tf_op jit(solution)/shard_map/ppermute | solution.py:726
  175.5 3.9 %collective-permute-done.34.refs_2_ = bf16[576,128]{1,0:T(8,128)(2,1)S(1)} collective-permute-done((bf16[576,128]{1,0:T(8,128)(2,1)S(1)}, bf16[576,128]{1,0:T(8,128)(2,1)S(1)}, u32[]{:S(2)}, u32[]{:S(2)}) %collective-permute-start.34) | collective-permute-done | bytes 147488 | tf_op jit(solution)/shard_map/ppermute | solution.py:726
  180.9 1.8 collective-permute-start.32
  184.9 7.4 %collective-permute-done.38.refs_2_ = bf16[576,128]{1,0:T(8,128)(2,1)S(1)} collective-permute-done((bf16[576,128]{1,0:T(8,128)(2,1)S(1)}, bf16[576,128]{1,0:T(8,128)(2,1)S(1)}, u32[]{:S(2)}, u32[]{:S(2)}) %collective-permute-start.38) | collective-permute-done | bytes 147488 | tf_op jit(solution)/shard_map/ppermute | solution.py:726
  192.4 2.0 collective-permute-start.41
  195.2 7.1 %collective-permute-done.39.refs_2_ = bf16[1152,128]{1,0:T(8,128)(2,1)S(1)} collective-permute-done((bf16[1152,128]{1,0:T(8,128)(2,1)S(1)}, bf16[1152,128]{1,0:T(8,128)(2,1)S(1)}, u32[]{:S(2)}, u32[]{:S(2)}) %collective-permute-start.39) | collective-permute-done | bytes 294944 | tf_op jit(solution)/shard_map/ppermute | solution.py:726
  202.5 3.1 %collective-permute-done.31.refs_3_ = bf16[2304,128]{1,0:T(8,128)(2,1)S(1)} collective-permute-done((bf16[2304,128]{1,0:T(8,128)(2,1)S(1)}, bf16[2304,128]{1,0:T(8,128)(2,1)S(1)}, u32[]{:S(2)}, u32[]{:S(2)}) %collective-permute-start.31) | collective-permute-done | bytes 589856 | tf_op jit(solution)/shard_map/ppermute | solution.py:726
  208.7 3.0 %shard_map.372 = (bf16[9,512,128]{2,1,0:T(8,128)(2,1)S(1)}, bf16[9,128,512]{2,1,0:T(8,128)(2,1)S(1)}, f32[8,128]{1,0:T(8,128)S(1)}, f32[72,128]{1,0:T(8,128)S(1)}) custom-call(s32[2]{0:T(128)S(1)} %copy-done.19, bf16[512,512]{1,0:T(8,128)(2,1)S(1)} %copy-done.12, bf16[4608,128]{1,0:T(8,128)(2,1)S(1)} %shard_map.365.refs_2_, bf16[512,512]{1,0:T(8,128)(2,1)S(1)} %copy-done.10, ...), custom_call_target="tpu_custom_call" | custom-call | flops 1207959552 | bytes 5853192 | tf_op jit(solution)/shard_map/pallas_call | solution.py:117
  211.8 3.3 %collective-permute-start.43 = (f32[8,128]{1,0:T(8,128)S(1)}, f32[8,128]{1,0:T(8,128)S(1)}, u32[]{:S(2)}, u32[]{:S(2)}) collective-permute-start(f32[8,128]{1,0:T(8,128)S(1)} %get-tuple-element.204.refs_0_), channel_id=1, source_target_pairs={{0,2},{2,0},{4,6},{6,4},{1,3},{3,1},{5,7},{7,5},{8,10},{10,8},{12,... | collective-permute-start | bytes 12296 | tf_op jit(solution)/shard_map/ppermute | solution.py:726
  215.1 1.7 collective-permute-start.44
  216.9 2.2 shard_map.376
  219.1 2.2 collective-permute-done.45.refs_3_
  221.3 7.8 %shard_map.375 = (f32[9,512,128]{2,1,0:T(8,128)}, f32[9,128,512]{2,1,0:T(8,128)}, f32[9,512,128]{2,1,0:T(8,128)}, f32[9,128,512]{2,1,0:T(8,128)}, f32[9,512,128]...) custom-call(f32[8,128]{1,0:T(8,128)S(1)} %get-tuple-element.204.refs, ...), custom_call_target="tpu_custom_call" | custom-call | tf_op jit(solution)/shard_map/pallas_call | solution.py:1188
  (166 shorter events, 45.9 us)
Async XLA Ops:
  2.8 21.3 %collective-permute-start = (bf16[9,128,256]{2,1,0:T(8,128)(2,1)}, bf16[9,128,256]{2,1,0:T(8,128)(2,1)}, u32[]{:S(2)}, u32[]{:S(2)}) collective-permute-start(bf16[9,128,256]{2,1,0:T(8,128)(2,1)} %dynamic-slice_convert_fusion.refs_4_.refs_10_), channel_id=1, source_target_pairs={{0,2},{2,0},{4,6},{6,4},{1,3},{3,1},{5,7},{7,5},{8,10},{10,8},{12,... | collective-permute-start | bytes 1769480 | tf_op jit(solution)/shard_map/ppermute | solution.py:726
  5.8 18.4 %collective-permute-start.1 = (bf16[9,128,256]{2,1,0:T(8,128)(2,1)}, bf16[9,128,256]{2,1,0:T(8,128)(2,1)}, u32[]{:S(2)}, u32[]{:S(2)}) collective-permute-start(bf16[9,128,256]{2,1,0:T(8,128)(2,1)} %dynamic-slice_convert_fusion.refs_4_.refs_10_), channel_id=1, source_target_pairs={{0,4},{2,6},{4,0},{6,2},{1,5},{3,7},{5,1},{7,3},{8,12},{10,14},{12... | collective-permute-start | bytes 1769480 | tf_op jit(solution)/shard_map/ppermute | solution.py:726
  13.4 10.8 %all-to-all-start = ((f32[8,8,128]{2,1,0:T(8,128)}), f32[8,8,128]{2,1,0:T(8,128)S(1)}, u32[]{:S(2)}, u32[]{:S(2)}) async-start(f32[8,8,128]{2,1,0:T(8,128)} %get-tuple-element.122), calls=%async_computation | async-start | bytes 65536 | tf_op jit(solution)/shard_map/all_to_all | solution.py:884
  18.3 25.7 %collective-permute-start.6 = (bf16[9,128,256]{2,1,0:T(8,128)(2,1)}, bf16[9,128,256]{2,1,0:T(8,128)(2,1)}, u32[]{:S(2)}, u32[]{:S(2)}) collective-permute-start(bf16[9,128,256]{2,1,0:T(8,128)(2,1)} %dynamic-slice_convert_fusion.refs_4_.refs_10_), channel_id=1, source_target_pairs={{0,6},{2,4},{4,2},{6,0},{1,7},{3,5},{5,3},{7,1},{8,14},{10,12},{12... | collective-permute-start | bytes 1769480 | tf_op jit(solution)/shard_map/ppermute | solution.py:726
  28.5 9.2 %collective-permute-start.2 = (bf16[528,128]{1,0:T(8,128)(2,1)}, bf16[528,128]{1,0:T(8,128)(2,1)}, u32[]{:S(2)}, u32[]{:S(2)}) collective-permute-start(bf16[528,128]{1,0:T(8,128)(2,1)} %get-tuple-element.130), channel_id=1, source_target_pairs={{0,2},{2,0},{4,6},{6,4},{1,3},{3,1},{5,7},{7,5},{8,10},{10,8},{12,... | collective-permute-start | bytes 405512 | tf_op jit(solution)/shard_map/ppermute | solution.py:726
  30.1 8.4 %collective-permute-start.3 = (bf16[528,128]{1,0:T(8,128)(2,1)}, bf16[528,128]{1,0:T(8,128)(2,1)}, u32[]{:S(2)}, u32[]{:S(2)}) collective-permute-start(bf16[528,128]{1,0:T(8,128)(2,1)} %get-tuple-element.131), channel_id=1, source_target_pairs={{0,4},{2,6},{4,0},{6,2},{1,5},{3,7},{5,1},{7,3},{8,12},{10,14},{12... | collective-permute-start | bytes 405512 | tf_op jit(solution)/shard_map/ppermute | solution.py:726
  31.6 9.5 %collective-permute-start.4 = (bf16[528,128]{1,0:T(8,128)(2,1)}, bf16[528,128]{1,0:T(8,128)(2,1)}, u32[]{:S(2)}, u32[]{:S(2)}) collective-permute-start(bf16[528,128]{1,0:T(8,128)(2,1)} %get-tuple-element.132), channel_id=1, source_target_pairs={{0,6},{2,4},{4,2},{6,0},{1,7},{3,5},{5,3},{7,1},{8,14},{10,12},{12... | collective-permute-start | bytes 405512 | tf_op jit(solution)/shard_map/ppermute | solution.py:726
  51.5 13.2 %collective-permute-start.11 = (bf16[9,128,256]{2,1,0:T(8,128)(2,1)}, bf16[9,128,256]{2,1,0:T(8,128)(2,1)}, u32[]{:S(2)}, u32[]{:S(2)}) collective-permute-start(bf16[9,128,256]{2,1,0:T(8,128)(2,1)} %collective-permute-done.6.refs_7_.refs_13_), channel_id=1, source_target_pairs={{0,1},{1,0},{2,3},{3,2},{4,5},{5,4},{6,7},{7,6},{8,9},{9,8},{10,11... | collective-permute-start | bytes 1769480 | tf_op jit(solution)/shard_map/ppermute | solution.py:726
  51.7 13.5 %collective-permute-start.10 = (bf16[9,128,256]{2,1,0:T(8,128)(2,1)}, bf16[9,128,256]{2,1,0:T(8,128)(2,1)}, u32[]{:S(2)}, u32[]{:S(2)}) collective-permute-start(bf16[9,128,256]{2,1,0:T(8,128)(2,1)} %collective-permute-done.1.refs_6_.refs_12_), channel_id=1, source_target_pairs={{0,1},{1,0},{2,3},{3,2},{4,5},{5,4},{6,7},{7,6},{8,9},{9,8},{10,11... | collective-permute-start | bytes 1769480 | tf_op jit(solution)/shard_map/ppermute | solution.py:726
  52.1 14.1 %collective-permute-start.9 = (bf16[9,128,256]{2,1,0:T(8,128)(2,1)}, bf16[9,128,256]{2,1,0:T(8,128)(2,1)}, u32[]{:S(2)}, u32[]{:S(2)}) collective-permute-start(bf16[9,128,256]{2,1,0:T(8,128)(2,1)} %collective-permute-done.refs_5_.refs_11_), channel_id=1, source_target_pairs={{0,1},{1,0},{2,3},{3,2},{4,5},{5,4},{6,7},{7,6},{8,9},{9,8},{10,11... | collective-permute-start | bytes 1769480 | tf_op jit(solution)/shard_map/ppermute | solution.py:726
  52.2 16.8 %collective-permute-start.8 = (bf16[9,128,256]{2,1,0:T(8,128)(2,1)}, bf16[9,128,256]{2,1,0:T(8,128)(2,1)}, u32[]{:S(2)}, u32[]{:S(2)}) collective-permute-start(bf16[9,128,256]{2,1,0:T(8,128)(2,1)} %dynamic-slice_convert_fusion.refs_4_.refs_10_), channel_id=1, source_target_pairs={{0,1},{1,0},{2,3},{3,2},{4,5},{5,4},{6,7},{7,6},{8,9},{9,8},{10,11... | collective-permute-start | bytes 1769480 | tf_op jit(solution)/shard_map/ppermute | solution.py:726
  52.6 12.1 %all-to-all-start.1 = ((f32[32,8,128]{2,1,0:T(8,128)}), f32[32,8,128]{2,1,0:T(8,128)}, u32[]{:S(2)}, u32[]{:S(2)}) async-start(f32[32,8,128]{2,1,0:T(8,128)} %get-tuple-element.141), calls=%async_computation.1 | async-start | bytes 262144 | tf_op jit(solution)/shard_map/all_to_all | solution.py:752
  56.5 12.5 %collective-permute-start.7 = (f32[256,256]{1,0:T(8,128)}, f32[256,256]{1,0:T(8,128)}, u32[]{:S(2)}, u32[]{:S(2)}) collective-permute-start(f32[256,256]{1,0:T(8,128)} %get-tuple-element.140), channel_id=1, source_target_pairs={{0,1},{1,0},{2,3},{3,2},{4,5},{5,4},{6,7},{7,6},{8,9},{9,8},{10,11... | collective-permute-start | bytes 786440 | tf_op jit(solution)/shard_map/ppermute | solution.py:726
  64.7 11.8 %collective-permute-start.12 = (bf16[256,512]{1,0:T(8,128)(2,1)}, bf16[256,512]{1,0:T(8,128)(2,1)}, u32[]{:S(2)}, u32[]{:S(2)}) collective-permute-start(bf16[256,512]{1,0:T(8,128)(2,1)} %get-tuple-element.155.refs_6_.refs_4_.refs_19_), channel_id=1, source_target_pairs={{0,2},{2,0},{4,6},{6,4},{1,3},{3,1},{5,7},{7,5},{8,10},{10,8},{12,... | collective-permute-start | bytes 786440 | tf_op jit(solution)/shard_map/ppermute | solution.py:726
  65.2 14.0 %collective-permute-start.13 = (bf16[256,512]{1,0:T(8,128)(2,1)}, bf16[256,512]{1,0:T(8,128)(2,1)}, u32[]{:S(2)}, u32[]{:S(2)}) collective-permute-start(bf16[256,512]{1,0:T(8,128)(2,1)} %get-tuple-element.155.refs_6_.refs_4_.refs_19_), channel_id=1, source_target_pairs={{0,4},{2,6},{4,0},{6,2},{1,5},{3,7},{5,1},{7,3},{8,12},{10,14},{12... | collective-permute-start | bytes 786440 | tf_op jit(solution)/shard_map/ppermute | solution.py:726
  66.2 13.0 %collective-permute-start.14 = (bf16[256,512]{1,0:T(8,128)(2,1)}, bf16[256,512]{1,0:T(8,128)(2,1)}, u32[]{:S(2)}, u32[]{:S(2)}) collective-permute-start(bf16[256,512]{1,0:T(8,128)(2,1)} %get-tuple-element.155.refs_6_.refs_4_.refs_19_), channel_id=1, source_target_pairs={{0,6},{2,4},{4,2},{6,0},{1,7},{3,5},{5,3},{7,1},{8,14},{10,12},{12... | collective-permute-start | bytes 786440 | tf_op jit(solution)/shard_map/ppermute | solution.py:726
  73.2 11.5 %all-to-all-start.2 = ((f32[32,8,128]{2,1,0:T(8,128)}), f32[32,8,128]{2,1,0:T(8,128)}, u32[]{:S(2)}, u32[]{:S(2)}) async-start(f32[32,8,128]{2,1,0:T(8,128)} %get-tuple-element.153), calls=%async_computation.2 | async-start | bytes 262144 | tf_op jit(solution)/shard_map/all_to_all | solution.py:752
  91.5 14.7 %all-to-all-start.3 = ((bf16[32,32,128]{2,1,0:T(8,128)(2,1)}), bf16[32,32,128]{2,1,0:T(8,128)(2,1)}, u32[]{:S(2)}, u32[]{:S(2)}) async-start(bf16[32,32,128]{2,1,0:T(8,128)(2,1)} %bitcast.47), calls=%async_computation.3 | async-start | bytes 524288 | tf_op jit(solution)/shard_map/all_to_all | solution.py:752
  95.0 11.2 %collective-permute-start.15 = (bf16[256,128]{1,0:T(8,128)(2,1)}, bf16[256,128]{1,0:T(8,128)(2,1)}, u32[]{:S(2)}, u32[]{:S(2)}) collective-permute-start(bf16[256,128]{1,0:T(8,128)(2,1)} %get-tuple-element.169), channel_id=1, source_target_pairs={{0,2},{2,0},{4,6},{6,4},{1,3},{3,1},{5,7},{7,5},{8,10},{10,8},{12,... | collective-permute-start | bytes 196616 | tf_op jit(solution)/shard_map/ppermute | solution.py:726
  96.4 9.7 %collective-permute-start.16 = (bf16[256,128]{1,0:T(8,128)(2,1)}, bf16[256,128]{1,0:T(8,128)(2,1)}, u32[]{:S(2)}, u32[]{:S(2)}) collective-permute-start(bf16[256,128]{1,0:T(8,128)(2,1)} %get-tuple-element.170), channel_id=1, source_target_pairs={{0,4},{2,6},{4,0},{6,2},{1,5},{3,7},{5,1},{7,3},{8,12},{10,14},{12... | collective-permute-start | bytes 196616 | tf_op jit(solution)/shard_map/ppermute | solution.py:726
  97.9 8.2 %collective-permute-start.17 = (bf16[256,128]{1,0:T(8,128)(2,1)}, bf16[256,128]{1,0:T(8,128)(2,1)}, u32[]{:S(2)}, u32[]{:S(2)}) collective-permute-start(bf16[256,128]{1,0:T(8,128)(2,1)} %get-tuple-element.171), channel_id=1, source_target_pairs={{0,6},{2,4},{4,2},{6,0},{1,7},{3,5},{5,3},{7,1},{8,14},{10,12},{12... | collective-permute-start | bytes 196616 | tf_op jit(solution)/shard_map/ppermute | solution.py:726
  113.0 2.3 collective-permute-start.18
  116.5 9.1 %collective-permute-start.19 = (bf16[1152,128]{1,0:T(8,128)(2,1)S(1)}, bf16[1152,128]{1,0:T(8,128)(2,1)S(1)}, u32[]{:S(2)}, u32[]{:S(2)}) collective-permute-start(bf16[1152,128]{1,0:T(8,128)(2,1)S(1)} %get-tuple-element.175), channel_id=1, source_target_pairs={{0,8},{8,0},{16,24},{24,16},{1,9},{9,1},{17,25},{25,17},{2,10},{10... | collective-permute-start | bytes 884744 | tf_op jit(solution)/shard_map/ppermute | solution.py:726
  118.0 10.2 %collective-permute-start.20 = (bf16[512,256]{1,0:T(8,128)(2,1)S(1)}, bf16[512,256]{1,0:T(8,128)(2,1)S(1)}, u32[]{:S(2)}, u32[]{:S(2)}) collective-permute-start(bf16[512,256]{1,0:T(8,128)(2,1)S(1)} %copy-done.17), channel_id=1, source_target_pairs={{0,2},{2,0},{4,6},{6,4},{1,3},{3,1},{5,7},{7,5},{8,10},{10,8},{12,... | collective-permute-start | bytes 786440 | tf_op jit(solution)/shard_map/ppermute | solution.py:726
  119.5 13.4 %collective-permute-start.21 = (bf16[512,256]{1,0:T(8,128)(2,1)S(1)}, bf16[512,256]{1,0:T(8,128)(2,1)S(1)}, u32[]{:S(2)}, u32[]{:S(2)}) collective-permute-start(bf16[512,256]{1,0:T(8,128)(2,1)S(1)} %copy-done.17), channel_id=1, source_target_pairs={{0,4},{2,6},{4,0},{6,2},{1,5},{3,7},{5,1},{7,3},{8,12},{10,14},{12... | collective-permute-start | bytes 786440 | tf_op jit(solution)/shard_map/ppermute | solution.py:726
  121.0 11.9 %collective-permute-start.22 = (bf16[512,256]{1,0:T(8,128)(2,1)S(1)}, bf16[512,256]{1,0:T(8,128)(2,1)S(1)}, u32[]{:S(2)}, u32[]{:S(2)}) collective-permute-start(bf16[512,256]{1,0:T(8,128)(2,1)S(1)} %copy-done.17), channel_id=1, source_target_pairs={{0,6},{2,4},{4,2},{6,0},{1,7},{3,5},{5,3},{7,1},{8,14},{10,12},{12... | collective-permute-start | bytes 786440 | tf_op jit(solution)/shard_map/ppermute | solution.py:726
  125.7 9.2 %collective-permute-start.23 = (bf16[576,128]{1,0:T(8,128)(2,1)S(1)}, bf16[576,128]{1,0:T(8,128)(2,1)S(1)}, u32[]{:S(2)}, u32[]{:S(2)}) collective-permute-start(bf16[576,128]{1,0:T(8,128)(2,1)S(1)} %get-tuple-element.178), channel_id=1, source_target_pairs={{0,16},{8,24},{16,0},{24,8},{1,17},{9,25},{17,1},{25,9},{2,18},{10... | collective-permute-start | bytes 442376 | tf_op jit(solution)/shard_map/ppermute | solution.py:726
  134.9 9.0 %collective-permute-start.27 = (bf16[576,128]{1,0:T(8,128)(2,1)S(1)}, bf16[576,128]{1,0:T(8,128)(2,1)S(1)}, u32[]{:S(2)}, u32[]{:S(2)}) collective-permute-start(bf16[576,128]{1,0:T(8,128)(2,1)S(1)} %add_convert_fusion.refs_1_), channel_id=1, source_target_pairs={{0,16},{8,24},{16,0},{24,8},{1,17},{9,25},{17,1},{25,9},{2,18},{10... | collective-permute-start | bytes 442376 | tf_op jit(solution)/shard_map/ppermute | solution.py:726
  138.1 12.9 %collective-permute-start.24 = (bf16[2304,128]{1,0:T(8,128)(2,1)S(1)}, bf16[2304,128]{1,0:T(8,128)(2,1)S(1)}, u32[]{:S(2)}, u32[]{:S(2)}) collective-permute-start(bf16[2304,128]{1,0:T(8,128)(2,1)S(1)} %get-tuple-element.181), channel_id=1, source_target_pairs={{0,1},{1,0},{2,3},{3,2},{4,5},{5,4},{6,7},{7,6},{8,9},{9,8},{10,11... | collective-permute-start | bytes 1769480 | tf_op jit(solution)/shard_map/ppermute | solution.py:726
  144.0 6.8 %collective-permute-start.28 = (bf16[1152,128]{1,0:T(8,128)(2,1)S(1)}, bf16[1152,128]{1,0:T(8,128)(2,1)S(1)}, u32[]{:S(2)}, u32[]{:S(2)}) collective-permute-start(bf16[1152,128]{1,0:T(8,128)(2,1)S(1)} %shard_map.357.refs_1_), channel_id=1, source_target_pairs={{0,8},{8,0},{16,24},{24,16},{1,9},{9,1},{17,25},{25,17},{2,10},{10... | collective-permute-start | bytes 884744 | tf_op jit(solution)/shard_map/ppermute | solution.py:726
  150.9 12.3 %collective-permute-start.29 = (bf16[2304,128]{1,0:T(8,128)(2,1)S(1)}, bf16[2304,128]{1,0:T(8,128)(2,1)S(1)}, u32[]{:S(2)}, u32[]{:S(2)}) collective-permute-start(bf16[2304,128]{1,0:T(8,128)(2,1)S(1)} %shard_map.358.refs_1_), channel_id=1, source_target_pairs={{0,1},{1,0},{2,3},{3,2},{4,5},{5,4},{6,7},{7,6},{8,9},{9,8},{10,11... | collective-permute-start | bytes 1769480 | tf_op jit(solution)/shard_map/ppermute | solution.py:726
  151.1 9.5 %collective-permute-start.25 = (bf16[1152,128]{1,0:T(8,128)(2,1)S(1)}, bf16[1152,128]{1,0:T(8,128)(2,1)S(1)}, u32[]{:S(2)}, u32[]{:S(2)}) collective-permute-start(bf16[1152,128]{1,0:T(8,128)(2,1)S(1)} %get-tuple-element.183), channel_id=1, source_target_pairs={{0,8},{8,0},{16,24},{24,16},{1,9},{9,1},{17,25},{25,17},{2,10},{10... | collective-permute-start | bytes 884744 | tf_op jit(solution)/shard_map/ppermute | solution.py:726
  160.7 9.6 %collective-permute-start.26 = (bf16[576,128]{1,0:T(8,128)(2,1)S(1)}, bf16[576,128]{1,0:T(8,128)(2,1)S(1)}, u32[]{:S(2)}, u32[]{:S(2)}) collective-permute-start(bf16[576,128]{1,0:T(8,128)(2,1)S(1)} %get-tuple-element.185), channel_id=1, source_target_pairs={{0,16},{8,24},{16,0},{24,8},{1,17},{9,25},{17,1},{25,9},{2,18},{10... | collective-permute-start | bytes 442376 | tf_op jit(solution)/shard_map/ppermute | solution.py:726
  170.4 9.0 %collective-permute-start.34 = (bf16[576,128]{1,0:T(8,128)(2,1)S(1)}, bf16[576,128]{1,0:T(8,128)(2,1)S(1)}, u32[]{:S(2)}, u32[]{:S(2)}) collective-permute-start(bf16[576,128]{1,0:T(8,128)(2,1)S(1)} %get-tuple-element.188.refs_1_), channel_id=1, source_target_pairs={{0,16},{8,24},{16,0},{24,8},{1,17},{9,25},{17,1},{25,9},{2,18},{10... | collective-permute-start | bytes 442376 | tf_op jit(solution)/shard_map/ppermute | solution.py:726
  170.5 10.5 %collective-permute-start.35 = (bf16[576,128]{1,0:T(8,128)(2,1)S(1)}, bf16[576,128]{1,0:T(8,128)(2,1)S(1)}, u32[]{:S(2)}, u32[]{:S(2)}) collective-permute-start(bf16[576,128]{1,0:T(8,128)(2,1)S(1)} %get-tuple-element.196.refs_1_), channel_id=1, source_target_pairs={{0,2},{2,0},{4,6},{6,4},{1,3},{3,1},{5,7},{7,5},{8,10},{10,8},{12,... | collective-permute-start | bytes 442376 | tf_op jit(solution)/shard_map/ppermute | solution.py:726
  172.0 10.7 %collective-permute-start.36 = (bf16[576,128]{1,0:T(8,128)(2,1)S(1)}, bf16[576,128]{1,0:T(8,128)(2,1)S(1)}, u32[]{:S(2)}, u32[]{:S(2)}) collective-permute-start(bf16[576,128]{1,0:T(8,128)(2,1)S(1)} %get-tuple-element.196.refs_1_), channel_id=1, source_target_pairs={{0,4},{2,6},{4,0},{6,2},{1,5},{3,7},{5,1},{7,3},{8,12},{10,14},{12... | collective-permute-start | bytes 442376 | tf_op jit(solution)/shard_map/ppermute | solution.py:726
  173.5 9.3 %collective-permute-start.37 = (bf16[576,128]{1,0:T(8,128)(2,1)S(1)}, bf16[576,128]{1,0:T(8,128)(2,1)S(1)}, u32[]{:S(2)}, u32[]{:S(2)}) collective-permute-start(bf16[576,128]{1,0:T(8,128)(2,1)S(1)} %get-tuple-element.196.refs_1_), channel_id=1, source_target_pairs={{0,6},{2,4},{4,2},{6,0},{1,7},{3,5},{5,3},{7,1},{8,14},{10,12},{12... | collective-permute-start | bytes 442376 | tf_op jit(solution)/shard_map/ppermute | solution.py:726
  174.0 28.5 %collective-permute-start.30 = (bf16[2304,128]{1,0:T(8,128)(2,1)S(1)}, bf16[2304,128]{1,0:T(8,128)(2,1)S(1)}, u32[]{:S(2)}, u32[]{:S(2)}) collective-permute-start(bf16[2304,128]{1,0:T(8,128)(2,1)S(1)} %get-tuple-element.186.refs_1_), channel_id=1, source_target_pairs={{0,2},{2,0},{4,6},{6,4},{1,3},{3,1},{5,7},{7,5},{8,10},{10,8},{12,... | collective-permute-start | bytes 1769480 | tf_op jit(solution)/shard_map/ppermute | solution.py:726
  179.4 26.2 %collective-permute-start.31 = (bf16[2304,128]{1,0:T(8,128)(2,1)S(1)}, bf16[2304,128]{1,0:T(8,128)(2,1)S(1)}, u32[]{:S(2)}, u32[]{:S(2)}) collective-permute-start(bf16[2304,128]{1,0:T(8,128)(2,1)S(1)} %get-tuple-element.186.refs_1_), channel_id=1, source_target_pairs={{0,4},{2,6},{4,0},{6,2},{1,5},{3,7},{5,1},{7,3},{8,12},{10,14},{12... | collective-permute-start | bytes 1769480 | tf_op jit(solution)/shard_map/ppermute | solution.py:726
  180.9 24.7 %collective-permute-start.32 = (bf16[2304,128]{1,0:T(8,128)(2,1)S(1)}, bf16[2304,128]{1,0:T(8,128)(2,1)S(1)}, u32[]{:S(2)}, u32[]{:S(2)}) collective-permute-start(bf16[2304,128]{1,0:T(8,128)(2,1)S(1)} %get-tuple-element.186.refs_1_), channel_id=1, source_target_pairs={{0,6},{2,4},{4,2},{6,0},{1,7},{3,5},{5,3},{7,1},{8,14},{10,12},{12... | collective-permute-start | bytes 1769480 | tf_op jit(solution)/shard_map/ppermute | solution.py:726
  183.2 9.1 %collective-permute-start.38 = (bf16[576,128]{1,0:T(8,128)(2,1)S(1)}, bf16[576,128]{1,0:T(8,128)(2,1)S(1)}, u32[]{:S(2)}, u32[]{:S(2)}) collective-permute-start(bf16[576,128]{1,0:T(8,128)(2,1)S(1)} %shard_map.367.refs_1_), channel_id=1, source_target_pairs={{0,16},{8,24},{16,0},{24,8},{1,17},{9,25},{17,1},{25,9},{2,18},{10... | collective-permute-start | bytes 442376 | tf_op jit(solution)/shard_map/ppermute | solution.py:726
  192.4 10.0 %collective-permute-start.39 = (bf16[1152,128]{1,0:T(8,128)(2,1)S(1)}, bf16[1152,128]{1,0:T(8,128)(2,1)S(1)}, u32[]{:S(2)}, u32[]{:S(2)}) collective-permute-start(bf16[1152,128]{1,0:T(8,128)(2,1)S(1)} %shard_map.368.refs_1_), channel_id=1, source_target_pairs={{0,8},{8,0},{16,24},{24,16},{1,9},{9,1},{17,25},{25,17},{2,10},{10... | collective-permute-start | bytes 884744 | tf_op jit(solution)/shard_map/ppermute | solution.py:726
  192.4 15.0 %collective-permute-start.41 = (bf16[1152,128]{1,0:T(8,128)(2,1)S(1)}, bf16[1152,128]{1,0:T(8,128)(2,1)S(1)}, u32[]{:S(2)}, u32[]{:S(2)}) collective-permute-start(bf16[1152,128]{1,0:T(8,128)(2,1)S(1)} %shard_map.366.refs_1_), channel_id=1, source_target_pairs={{0,8},{8,0},{16,24},{24,16},{1,9},{9,1},{17,25},{25,17},{2,10},{10... | collective-permute-start | bytes 884744 | tf_op jit(solution)/shard_map/ppermute | solution.py:726
  202.4 5.3 %collective-permute-start.40 = (bf16[2304,128]{1,0:T(8,128)(2,1)S(1)}, bf16[2304,128]{1,0:T(8,128)(2,1)S(1)}, u32[]{:S(2)}, u32[]{:S(2)}) collective-permute-start(bf16[2304,128]{1,0:T(8,128)(2,1)S(1)} %shard_map.370.refs_1_), channel_id=1, source_target_pairs={{0,1},{1,0},{2,3},{3,2},{4,5},{5,4},{6,7},{7,6},{8,9},{9,8},{10,11... | collective-permute-start | bytes 1769480 | tf_op jit(solution)/shard_map/ppermute | solution.py:726
  207.6 9.2 %collective-permute-start.42 = (bf16[2304,128]{1,0:T(8,128)(2,1)S(1)}, bf16[2304,128]{1,0:T(8,128)(2,1)S(1)}, u32[]{:S(2)}, u32[]{:S(2)}) collective-permute-start(bf16[2304,128]{1,0:T(8,128)(2,1)S(1)} %shard_map.373.refs_1_), channel_id=1, source_target_pairs={{0,1},{1,0},{2,3},{3,2},{4,5},{5,4},{6,7},{7,6},{8,9},{9,8},{10,11... | collective-permute-start | bytes 1769480 | tf_op jit(solution)/shard_map/ppermute | solution.py:726
  211.8 7.3 %collective-permute-start.43 = (f32[8,128]{1,0:T(8,128)S(1)}, f32[8,128]{1,0:T(8,128)S(1)}, u32[]{:S(2)}, u32[]{:S(2)}) collective-permute-start(f32[8,128]{1,0:T(8,128)S(1)} %get-tuple-element.204.refs_0_), channel_id=1, source_target_pairs={{0,2},{2,0},{4,6},{6,4},{1,3},{3,1},{5,7},{7,5},{8,10},{10,8},{12,... | collective-permute-start | bytes 12296 | tf_op jit(solution)/shard_map/ppermute | solution.py:726
  215.1 4.0 %collective-permute-start.44 = (f32[8,128]{1,0:T(8,128)S(1)}, f32[8,128]{1,0:T(8,128)S(1)}, u32[]{:S(2)}, u32[]{:S(2)}) collective-permute-start(f32[8,128]{1,0:T(8,128)S(1)} %get-tuple-element.204.refs_0_), channel_id=1, source_target_pairs={{0,4},{2,6},{4,0},{6,2},{1,5},{3,7},{5,1},{7,3},{8,12},{10,14},{12... | collective-permute-start | bytes 12296 | tf_op jit(solution)/shard_map/ppermute | solution.py:726
  216.8 4.5 %collective-permute-start.45 = (f32[8,128]{1,0:T(8,128)S(1)}, f32[8,128]{1,0:T(8,128)S(1)}, u32[]{:S(2)}, u32[]{:S(2)}) collective-permute-start(f32[8,128]{1,0:T(8,128)S(1)} %get-tuple-element.204.refs_0_), channel_id=1, source_target_pairs={{0,6},{2,4},{4,2},{6,0},{1,7},{3,5},{5,3},{7,1},{8,14},{10,12},{12... | collective-permute-start | bytes 12296 | tf_op jit(solution)/shard_map/ppermute | solution.py:726
  (34 other events, 396.8 us)

commit v7 on v6

--- a/solution.py
+++ b/solution.py
@@ -697,7 +697,7 @@
             square_outs[at][nth] = square_new
             square_hat = square_new * (1.0 / (1.0 - BETA_TWO**STEP))
             size = square_hat * lax.rsqrt(square_hat) + ADAM_EPS
-            step = mean_new * (LEARN_RATE / (1.0 - BETA_ONE**STEP)) * pl.reciprocal(size, approx=True)
+            step = mean_new * (LEARN_RATE / (1.0 - BETA_ONE**STEP)) / size
             weight_outs[at][nth] = weight_refs[at][tap] * (1.0 - LEARN_RATE * WEIGHT_DECAY) - step
 
     @pl.when(pl.program_id(0) == 0)

time: 230 us -> 230 us (level)
  no operation moved by 1% of the time
where the time goes in v7:
time: 230 us; the launch traced here: 229 us
  waiting for transfers between devices  81.6 us (35%)
  Pallas kernels  67.5 us (29%)
  starting transfers between devices  61.4 us (27%)
  local copies, waits for them, and re-layouts  15.8 us (7%)
    ppermute x46, waiting for transfers between devices, swap(): lax.ppermute(values, axis, [(here, here ^ step) for here in range(count)])  71.2 us
    pallas_call x35, Pallas kernels, call(): pl.pallas_call(body, out_shape=list(outs), in_specs=specs, out_specs=[pl....  57.5 us
    ppermute x46, starting transfers between devices, swap(): lax.ppermute(values, axis, [(here, here ^ step) for here in range(count)])  45.8 us
    all_to_all x3, starting transfers between devices, every_device(): return lax.all_to_all(tiles, EVERY, 0, 0, tiled=True)  10.7 us
    all_to_all x3, waiting for transfers between devices, every_device(): return lax.all_to_all(tiles, EVERY, 0, 0, tiled=True)  10.5 us
    pallas_call x1, Pallas kernels, local(): pl.pallas_call(update, grid=(TAPS // 3,), scratch_shapes=[pltpu.VMEM((8,...  7.8 us
    unnamed x64, local copies, waits for them, and re-layouts  5.08 us
    all_to_all x1, starting transfers between devices, local(): got = lax.all_to_all(stats, ('dp', 'cin'), 0, 0, tiled=True)  4.89 us
  transfers between devices with their start and end apart: 50, of which 21 were waited for; matrix products, arithmetic and copies ran while one was open for 4% of the time, Pallas kernels for 18%

profile of v7, /device:TPU:0, one launch (start us, length us, event | category | flops | bytes accessed | tf_op | source)
XLA Modules:
  0.0 229.3 jit_solution(15936807890624124324)
XLA Ops:
  0.7 2.2 dynamic-slice_convert_fusion.refs_4_.refs_10_
  2.8 2.9 %collective-permute-start = (bf16[9,128,256]{2,1,0:T(8,128)(2,1)}, bf16[9,128,256]{2,1,0:T(8,128)(2,1)}, u32[]{:S(2)}, u32[]{:S(2)}) collective-permute-start(bf16[9,128,256]{2,1,0:T(8,128)(2,1)} %dynamic-slice_convert_fusion.refs_4_.refs_10_), channel_id=1, source_target_pairs={{0,2},{2,0},{4,6},{6,4},{1,3},{3,1},{5,7},{7,5},{8,10},{10,8},{12,... | collective-permute-start | bytes 1769480 | tf_op jit(solution)/shard_map/ppermute | solution.py:726
  7.9 5.4 %shard_map.340 = (f32[1024,128]{1,0:T(8,128)}, bf16[1024,128]{1,0:T(8,128)(2,1)}, f32[8,8,128]{2,1,0:T(8,128)}, f32[256,128]{1,0:T(8,128)}) custom-call(s32[2]{0:T(128)} %pad_add_fusion.refs_0_, bf16[1024,512]{1,0:T(8,128)(2,1)} %bitcast.44, s32[16,64]{1,0:T(8,128)} %refs_2_.3, f32[9,512,128]{2,1,0:T(8,128)} %refs_0_), custom_call_target="tpu_custom_call" | custom-call | flops 1207959552 | bytes 4362248 | tf_op jit(solution)/shard_map/pallas_call | solution.py:117
  13.4 4.9 %all-to-all-start = ((f32[8,8,128]{2,1,0:T(8,128)}), f32[8,8,128]{2,1,0:T(8,128)S(1)}, u32[]{:S(2)}, u32[]{:S(2)}) async-start(f32[8,8,128]{2,1,0:T(8,128)} %get-tuple-element.122), calls=%async_computation | async-start | bytes 65536 | tf_op jit(solution)/shard_map/all_to_all | solution.py:884
  24.8 3.7 %shard_map.342 = (bf16[528,128]{1,0:T(8,128)(2,1)}, bf16[528,128]{1,0:T(8,128)(2,1)}, bf16[528,128]{1,0:T(8,128)(2,1)}, bf16[528,128]{1,0:T(8,128)(2,1)}, f32[8,128]{1,0:T(8,128)}) custom-call(s32[2]{0:T(128)} %pad_add_fusion.refs_0_, f32[8,8,128]{2,1,0:T(8,128)} %copy-done.29, f32[1024,128]{1,0:T(8,128)} %get-tuple-element.123.refs_2_, ...), custom_call_target="tpu_custom_call" | custom-call | bytes 1371144 | tf_op jit(solution)/shard_map/pallas_call | solution.py:117
  34.1 1.9 copy.39
  36.0 1.7 constant_dynamic-slice_fusion.refs_2_
  38.4 2.6 %collective-permute-done.4.refs_4_ = bf16[528,128]{1,0:T(8,128)(2,1)} collective-permute-done((bf16[528,128]{1,0:T(8,128)(2,1)}, bf16[528,128]{1,0:T(8,128)(2,1)}, u32[]{:S(2)}, u32[]{:S(2)}) %collective-permute-start.4) | collective-permute-done | bytes 135200 | tf_op jit(solution)/shard_map/ppermute | solution.py:726
  41.0 2.8 %shard_map.343.refs_1_ = bf16[256,640]{1,0:T(8,128)(2,1)} custom-call(s32[2]{0:T(128)} %pad_add_fusion.refs_0_, bf16[528,128]{1,0:T(8,128)(2,1)} %get-tuple-element.129.refs_1_, bf16[528,128]{1,0:T(8,128)(2,1)} %collective-permute-done.2.refs_2_, bf16[528,128]{1,0:T(8,128)(2,1)} %collective-permute-done.3.refs_3_, ...), custom_call_target="tpu_custom_call" | custom-call | bytes 999432 | tf_op jit(solution)/shard_map/pallas_call | solution.py:117
  43.9 1.8 collective-permute-done.5.refs_2_
  46.5 5.0 %shard_map.344 = (f32[256,256]{1,0:T(8,128)}, f32[256,256]{1,0:T(8,128)}, f32[32,8,128]{2,1,0:T(8,128)}) custom-call(s32[2]{0:T(128)} %pad_add_fusion.refs_0_, bf16[256,640]{1,0:T(8,128)(2,1)} %shard_map.343.refs_1_, bf16[256,640]{1,0:T(8,128)(2,1)} %copy-done.30, f32[4,128]{1,0:T(4,128)} %refs_3_.3, ...), custom_call_target="tpu_custom_call" | custom-call | flops 1207959552 | bytes 3672072 | tf_op jit(solution)/shard_map/pallas_call | solution.py:117
  52.6 3.9 %all-to-all-start.1 = ((f32[32,8,128]{2,1,0:T(8,128)}), f32[32,8,128]{2,1,0:T(8,128)}, u32[]{:S(2)}, u32[]{:S(2)}) async-start(f32[32,8,128]{2,1,0:T(8,128)} %get-tuple-element.141), calls=%async_computation.1 | async-start | bytes 262144 | tf_op jit(solution)/shard_map/all_to_all | solution.py:752
  57.3 2.6 %shard_map.345 = (bf16[256,512]{1,0:T(8,128)(2,1)}, f32[8,512]{1,0:T(8,128)}, bf16[16,512]{1,0:T(8,128)(2,1)}) custom-call(s32[2]{0:T(128)} %pad_add_fusion.refs_0_, bf16[528,128]{1,0:T(8,128)(2,1)} %get-tuple-element.129.refs_1_, bf16[528,128]{1,0:T(8,128)(2,1)} %collective-permute-done.2.refs_2_, bf16[528,128]{1,0:T(8,128)(2,1)} %collective-permute-done.3.refs_3_, ...), custom_call_target="tpu_custom_call" | custom-call | bytes 839688 | tf_op jit(solution)/shard_map/pallas_call | solution.py:117
  59.8 4.9 %all-to-all-done.1.refs_3_ = f32[32,8,128]{2,1,0:T(8,128)} async-done(((f32[32,8,128]{2,1,0:T(8,128)}), f32[32,8,128]{2,1,0:T(8,128)}, u32[]{:S(2)}, u32[]{:S(2)}) %all-to-all-start.1) | async-done | bytes 131104 | tf_op jit(solution)/shard_map/all_to_all | solution.py:752
  66.2 2.1 collective-permute-start.14
  69.0 4.3 %shard_map.346 = (f32[256,512]{1,0:T(8,128)}, f32[8,512]{1,0:T(8,128)}, f32[256,512]{1,0:T(8,128)}, f32[32,8,128]{2,1,0:T(8,128)}, f32[4,16,128]{2,1,0:T(8,128)}) custom-call(s32[2]{0:T(128)} %pad_add_fusion.refs_0_, f32[256,256]{1,0:T(8,128)} %get-tuple-element.139.refs_1_, f32[256,256]{1,0:T(8,128)} %collective-permute-done.7.refs_2_, ...), custom_call_target="tpu_custom_call" | custom-call | bytes 2048584 | tf_op jit(solution)/shard_map/pallas_call | solution.py:117
  73.2 3.3 %all-to-all-start.2 = ((f32[32,8,128]{2,1,0:T(8,128)}), f32[32,8,128]{2,1,0:T(8,128)}, u32[]{:S(2)}, u32[]{:S(2)}) async-start(f32[32,8,128]{2,1,0:T(8,128)} %get-tuple-element.153), calls=%async_computation.2 | async-start | bytes 262144 | tf_op jit(solution)/shard_map/all_to_all | solution.py:752
  76.6 2.6 %collective-permute-done.13.refs_6_.refs_21_ = bf16[256,512]{1,0:T(8,128)(2,1)} collective-permute-done((bf16[256,512]{1,0:T(8,128)(2,1)}, bf16[256,512]{1,0:T(8,128)(2,1)}, u32[]{:S(2)}, u32[]{:S(2)}) %collective-permute-start.13) | collective-permute-done | bytes 262176 | tf_op jit(solution)/shard_map/ppermute | solution.py:726
  79.2 5.6 %all-to-all-done.2.refs_4_ = f32[32,8,128]{2,1,0:T(8,128)} async-done(((f32[32,8,128]{2,1,0:T(8,128)}), f32[32,8,128]{2,1,0:T(8,128)}, u32[]{:S(2)}, u32[]{:S(2)}) %all-to-all-start.2) | async-done | bytes 131104 | tf_op jit(solution)/shard_map/all_to_all | solution.py:752
  84.8 6.7 %shard_map.347 = (bf16[256,512]{1,0:T(8,128)(2,1)}, f32[8,128]{1,0:T(8,128)}, bf16[4,4,2,32,128]{4,3,2,1,0:T(8,128)(2,1)}, bf16[256,128]{1,0:T(8,128)(2,1)}, bf1...) custom-call(s32[2]{0:T(128)} %pad_add_fusion.refs_0_, ...), custom_call_target="tpu_custom_call" | custom-call | flops 1207959552 | bytes 7671816 | tf_op jit(solution)/shard_map/pallas_call | solution.py:117
  91.5 3.5 %all-to-all-start.3 = ((bf16[32,32,128]{2,1,0:T(8,128)(2,1)}), bf16[32,32,128]{2,1,0:T(8,128)(2,1)}, u32[]{:S(2)}, u32[]{:S(2)}) async-start(bf16[32,32,128]{2,1,0:T(8,128)(2,1)} %bitcast.47), calls=%async_computation.3 | async-start | bytes 524288 | tf_op jit(solution)/shard_map/all_to_all | solution.py:752
  99.5 2.2 shard_map.348.refs_0_
  101.7 4.4 %shard_map.349 = (bf16[256,128]{1,0:T(8,128)(2,1)}, bf16[256,128]{1,0:T(8,128)(2,1)}, bf16[256,128]{1,0:T(8,128)(2,1)}, bf16[256,128]{1,0:T(8,128)(2,1)}) custom-call(s32[2]{0:T(128)} %pad_add_fusion.refs_0_, f32[8,512]{1,0:T(8,128)} %get-tuple-element.143.refs_4_.refs_7_.refs_1_.refs_2_, bf16[1024,128]{1,0:T(8,128)(2,1)} %get-tuple-element.162.refs_3_.refs_2_, ...), custom_call_target="tpu_custom_call" | custom-call | bytes 2113544 | tf_op jit(solution)/shard_map/pallas_call | solution.py:117
  106.2 6.8 %shard_map.350 = (bf16[2304,128]{1,0:T(8,128)(2,1)}, bf16[2304,128]{1,0:T(8,128)(2,1)}, f32[8,128]{1,0:T(8,128)}, f32[72,128]{1,0:T(8,128)}) custom-call(s32[2]{0:T(128)} %pad_add_fusion.refs_0_, bf16[32,32,128]{2,1,0:T(8,128)(2,1)} %all-to-all-done.3.refs_1_, f32[8,512]{1,0:T(8,128)} %get-tuple-element.143.refs_4_.refs_7_.refs_1_.refs_2_, ...), custom_call_target="tpu_custom_call" | custom-call | flops 1207959552 | bytes 4659288 | tf_op jit(solution)/shard_map/pallas_call | solution.py:117
  113.1 2.2 collective-permute-done.18.refs_2_
  121.5 4.1 %collective-permute-done.19.refs_2_ = bf16[1152,128]{1,0:T(8,128)(2,1)S(1)} collective-permute-done((bf16[1152,128]{1,0:T(8,128)(2,1)S(1)}, bf16[1152,128]{1,0:T(8,128)(2,1)S(1)}, u32[]{:S(2)}, u32[]{:S(2)}) %collective-permute-start.19) | collective-permute-done | bytes 294944 | tf_op jit(solution)/shard_map/ppermute | solution.py:726
  125.7 2.5 %collective-permute-start.23 = (bf16[576,128]{1,0:T(8,128)(2,1)S(1)}, bf16[576,128]{1,0:T(8,128)(2,1)S(1)}, u32[]{:S(2)}, u32[]{:S(2)}) collective-permute-start(bf16[576,128]{1,0:T(8,128)(2,1)S(1)} %get-tuple-element.178), channel_id=1, source_target_pairs={{0,16},{8,24},{16,0},{24,8},{1,17},{9,25},{17,1},{25,9},{2,18},{10... | collective-permute-start | bytes 442376 | tf_op jit(solution)/shard_map/ppermute | solution.py:726
  128.2 4.7 %collective-permute-done.21.refs_2_ = bf16[512,256]{1,0:T(8,128)(2,1)S(1)} collective-permute-done((bf16[512,256]{1,0:T(8,128)(2,1)S(1)}, bf16[512,256]{1,0:T(8,128)(2,1)S(1)}, u32[]{:S(2)}, u32[]{:S(2)}) %collective-permute-start.21) | collective-permute-done | bytes 262176 | tf_op jit(solution)/shard_map/ppermute | solution.py:726
  132.9 2.0 collective-permute-done.23
  135.5 2.4 %shard_map.353.refs_1_ = bf16[4608,128]{1,0:T(8,128)(2,1)S(1)} custom-call(bf16[512,256]{1,0:T(8,128)(2,1)S(1)} %copy-done.17, bf16[512,256]{1,0:T(8,128)(2,1)S(1)} %collective-permute-done.20.refs_1_, bf16[512,256]{1,0:T(8,128)(2,1)S(1)} %collective-permute-done.21.refs_2_, bf16[512,256]{1,0:T(8,128)(2,1)S(1)} %collective-permute-done.22.refs_3_, ...), custom_call_target="tpu_custom_call" | custom-call | flops 1207959552 | bytes 2490368 | tf_op jit(solution)/shard_map/pallas_call | solution.py:117
  138.1 5.8 %collective-permute-done.27.refs_2_ = bf16[576,128]{1,0:T(8,128)(2,1)S(1)} collective-permute-done((bf16[576,128]{1,0:T(8,128)(2,1)S(1)}, bf16[576,128]{1,0:T(8,128)(2,1)S(1)}, u32[]{:S(2)}, u32[]{:S(2)}) %collective-permute-start.27) | collective-permute-done | bytes 147488 | tf_op jit(solution)/shard_map/ppermute | solution.py:726
  144.1 6.7 %collective-permute-done.28.refs_2_ = bf16[1152,128]{1,0:T(8,128)(2,1)S(1)} collective-permute-done((bf16[1152,128]{1,0:T(8,128)(2,1)S(1)}, bf16[1152,128]{1,0:T(8,128)(2,1)S(1)}, u32[]{:S(2)}, u32[]{:S(2)}) %collective-permute-start.28) | collective-permute-done | bytes 294944 | tf_op jit(solution)/shard_map/ppermute | solution.py:726
  152.0 8.6 %collective-permute-done.25.refs_2_ = bf16[1152,128]{1,0:T(8,128)(2,1)S(1)} collective-permute-done((bf16[1152,128]{1,0:T(8,128)(2,1)S(1)}, bf16[1152,128]{1,0:T(8,128)(2,1)S(1)}, u32[]{:S(2)}, u32[]{:S(2)}) %collective-permute-start.25) | collective-permute-done | bytes 294944 | tf_op jit(solution)/shard_map/ppermute | solution.py:726
  160.7 2.5 %collective-permute-start.26 = (bf16[576,128]{1,0:T(8,128)(2,1)S(1)}, bf16[576,128]{1,0:T(8,128)(2,1)S(1)}, u32[]{:S(2)}, u32[]{:S(2)}) collective-permute-start(bf16[576,128]{1,0:T(8,128)(2,1)S(1)} %get-tuple-element.185), channel_id=1, source_target_pairs={{0,16},{8,24},{16,0},{24,8},{1,17},{9,25},{17,1},{25,9},{2,18},{10... | collective-permute-start | bytes 442376 | tf_op jit(solution)/shard_map/ppermute | solution.py:726
  163.3 2.9 %shard_map.360 = (f32[4608,128]{1,0:T(8,128)}, bf16[2304,128]{1,0:T(8,128)(2,1)S(1)}) custom-call(s32[2]{0:T(128)S(1)} %copy-done.19, bf16[4608,128]{1,0:T(8,128)(2,1)S(1)} %shard_map.359.refs_1_, f32[4608,128]{1,0:T(8,128)S(1)} %bitcast.43), custom_call_target="tpu_custom_call" | custom-call | bytes 6488072 | tf_op jit(solution)/shard_map/pallas_call | solution.py:117
  166.2 4.0 %collective-permute-done.26.refs_1_ = bf16[576,128]{1,0:T(8,128)(2,1)S(1)} collective-permute-done((bf16[576,128]{1,0:T(8,128)(2,1)S(1)}, bf16[576,128]{1,0:T(8,128)(2,1)S(1)}, u32[]{:S(2)}, u32[]{:S(2)}) %collective-permute-start.26) | collective-permute-done | bytes 147488 | tf_op jit(solution)/shard_map/ppermute | solution.py:726
  175.5 3.9 %collective-permute-done.34.refs_2_ = bf16[576,128]{1,0:T(8,128)(2,1)S(1)} collective-permute-done((bf16[576,128]{1,0:T(8,128)(2,1)S(1)}, bf16[576,128]{1,0:T(8,128)(2,1)S(1)}, u32[]{:S(2)}, u32[]{:S(2)}) %collective-permute-start.34) | collective-permute-done | bytes 147488 | tf_op jit(solution)/shard_map/ppermute | solution.py:726
  180.9 1.8 collective-permute-start.32
  184.9 7.4 %collective-permute-done.38.refs_2_ = bf16[576,128]{1,0:T(8,128)(2,1)S(1)} collective-permute-done((bf16[576,128]{1,0:T(8,128)(2,1)S(1)}, bf16[576,128]{1,0:T(8,128)(2,1)S(1)}, u32[]{:S(2)}, u32[]{:S(2)}) %collective-permute-start.38) | collective-permute-done | bytes 147488 | tf_op jit(solution)/shard_map/ppermute | solution.py:726
  192.4 2.0 collective-permute-start.41
  195.2 7.1 %collective-permute-done.39.refs_2_ = bf16[1152,128]{1,0:T(8,128)(2,1)S(1)} collective-permute-done((bf16[1152,128]{1,0:T(8,128)(2,1)S(1)}, bf16[1152,128]{1,0:T(8,128)(2,1)S(1)}, u32[]{:S(2)}, u32[]{:S(2)}) %collective-permute-start.39) | collective-permute-done | bytes 294944 | tf_op jit(solution)/shard_map/ppermute | solution.py:726
  202.5 3.1 %collective-permute-done.31.refs_3_ = bf16[2304,128]{1,0:T(8,128)(2,1)S(1)} collective-permute-done((bf16[2304,128]{1,0:T(8,128)(2,1)S(1)}, bf16[2304,128]{1,0:T(8,128)(2,1)S(1)}, u32[]{:S(2)}, u32[]{:S(2)}) %collective-permute-start.31) | collective-permute-done | bytes 589856 | tf_op jit(solution)/shard_map/ppermute | solution.py:726
  208.7 3.0 %shard_map.372 = (bf16[9,512,128]{2,1,0:T(8,128)(2,1)S(1)}, bf16[9,128,512]{2,1,0:T(8,128)(2,1)S(1)}, f32[8,128]{1,0:T(8,128)S(1)}, f32[72,128]{1,0:T(8,128)S(1)}) custom-call(s32[2]{0:T(128)S(1)} %copy-done.19, bf16[512,512]{1,0:T(8,128)(2,1)S(1)} %copy-done.12, bf16[4608,128]{1,0:T(8,128)(2,1)S(1)} %shard_map.365.refs_2_, bf16[512,512]{1,0:T(8,128)(2,1)S(1)} %copy-done.10, ...), custom_call_target="tpu_custom_call" | custom-call | flops 1207959552 | bytes 5853192 | tf_op jit(solution)/shard_map/pallas_call | solution.py:117
  211.8 3.3 %collective-permute-start.43 = (f32[8,128]{1,0:T(8,128)S(1)}, f32[8,128]{1,0:T(8,128)S(1)}, u32[]{:S(2)}, u32[]{:S(2)}) collective-permute-start(f32[8,128]{1,0:T(8,128)S(1)} %get-tuple-element.204.refs_0_), channel_id=1, source_target_pairs={{0,2},{2,0},{4,6},{6,4},{1,3},{3,1},{5,7},{7,5},{8,10},{10,8},{12,... | collective-permute-start | bytes 12296 | tf_op jit(solution)/shard_map/ppermute | solution.py:726
  215.1 1.7 collective-permute-start.44
  216.9 2.2 shard_map.376
  219.1 2.2 collective-permute-done.45.refs_3_
  221.3 7.8 %shard_map.375 = (f32[9,512,128]{2,1,0:T(8,128)}, f32[9,128,512]{2,1,0:T(8,128)}, f32[9,512,128]{2,1,0:T(8,128)}, f32[9,128,512]{2,1,0:T(8,128)}, f32[9,512,128]...) custom-call(f32[8,128]{1,0:T(8,128)S(1)} %get-tuple-element.204.refs, ...), custom_call_target="tpu_custom_call" | custom-call | tf_op jit(solution)/shard_map/pallas_call | solution.py:1188
  (166 shorter events, 45.9 us)
Async XLA Ops:
  2.8 21.3 %collective-permute-start = (bf16[9,128,256]{2,1,0:T(8,128)(2,1)}, bf16[9,128,256]{2,1,0:T(8,128)(2,1)}, u32[]{:S(2)}, u32[]{:S(2)}) collective-permute-start(bf16[9,128,256]{2,1,0:T(8,128)(2,1)} %dynamic-slice_convert_fusion.refs_4_.refs_10_), channel_id=1, source_target_pairs={{0,2},{2,0},{4,6},{6,4},{1,3},{3,1},{5,7},{7,5},{8,10},{10,8},{12,... | collective-permute-start | bytes 1769480 | tf_op jit(solution)/shard_map/ppermute | solution.py:726
  5.8 18.4 %collective-permute-start.1 = (bf16[9,128,256]{2,1,0:T(8,128)(2,1)}, bf16[9,128,256]{2,1,0:T(8,128)(2,1)}, u32[]{:S(2)}, u32[]{:S(2)}) collective-permute-start(bf16[9,128,256]{2,1,0:T(8,128)(2,1)} %dynamic-slice_convert_fusion.refs_4_.refs_10_), channel_id=1, source_target_pairs={{0,4},{2,6},{4,0},{6,2},{1,5},{3,7},{5,1},{7,3},{8,12},{10,14},{12... | collective-permute-start | bytes 1769480 | tf_op jit(solution)/shard_map/ppermute | solution.py:726
  13.4 10.8 %all-to-all-start = ((f32[8,8,128]{2,1,0:T(8,128)}), f32[8,8,128]{2,1,0:T(8,128)S(1)}, u32[]{:S(2)}, u32[]{:S(2)}) async-start(f32[8,8,128]{2,1,0:T(8,128)} %get-tuple-element.122), calls=%async_computation | async-start | bytes 65536 | tf_op jit(solution)/shard_map/all_to_all | solution.py:884
  18.3 25.7 %collective-permute-start.6 = (bf16[9,128,256]{2,1,0:T(8,128)(2,1)}, bf16[9,128,256]{2,1,0:T(8,128)(2,1)}, u32[]{:S(2)}, u32[]{:S(2)}) collective-permute-start(bf16[9,128,256]{2,1,0:T(8,128)(2,1)} %dynamic-slice_convert_fusion.refs_4_.refs_10_), channel_id=1, source_target_pairs={{0,6},{2,4},{4,2},{6,0},{1,7},{3,5},{5,3},{7,1},{8,14},{10,12},{12... | collective-permute-start | bytes 1769480 | tf_op jit(solution)/shard_map/ppermute | solution.py:726
  28.5 9.2 %collective-permute-start.2 = (bf16[528,128]{1,0:T(8,128)(2,1)}, bf16[528,128]{1,0:T(8,128)(2,1)}, u32[]{:S(2)}, u32[]{:S(2)}) collective-permute-start(bf16[528,128]{1,0:T(8,128)(2,1)} %get-tuple-element.130), channel_id=1, source_target_pairs={{0,2},{2,0},{4,6},{6,4},{1,3},{3,1},{5,7},{7,5},{8,10},{10,8},{12,... | collective-permute-start | bytes 405512 | tf_op jit(solution)/shard_map/ppermute | solution.py:726
  30.1 8.4 %collective-permute-start.3 = (bf16[528,128]{1,0:T(8,128)(2,1)}, bf16[528,128]{1,0:T(8,128)(2,1)}, u32[]{:S(2)}, u32[]{:S(2)}) collective-permute-start(bf16[528,128]{1,0:T(8,128)(2,1)} %get-tuple-element.131), channel_id=1, source_target_pairs={{0,4},{2,6},{4,0},{6,2},{1,5},{3,7},{5,1},{7,3},{8,12},{10,14},{12... | collective-permute-start | bytes 405512 | tf_op jit(solution)/shard_map/ppermute | solution.py:726
  31.6 9.5 %collective-permute-start.4 = (bf16[528,128]{1,0:T(8,128)(2,1)}, bf16[528,128]{1,0:T(8,128)(2,1)}, u32[]{:S(2)}, u32[]{:S(2)}) collective-permute-start(bf16[528,128]{1,0:T(8,128)(2,1)} %get-tuple-element.132), channel_id=1, source_target_pairs={{0,6},{2,4},{4,2},{6,0},{1,7},{3,5},{5,3},{7,1},{8,14},{10,12},{12... | collective-permute-start | bytes 405512 | tf_op jit(solution)/shard_map/ppermute | solution.py:726
  51.5 13.2 %collective-permute-start.11 = (bf16[9,128,256]{2,1,0:T(8,128)(2,1)}, bf16[9,128,256]{2,1,0:T(8,128)(2,1)}, u32[]{:S(2)}, u32[]{:S(2)}) collective-permute-start(bf16[9,128,256]{2,1,0:T(8,128)(2,1)} %collective-permute-done.6.refs_7_.refs_13_), channel_id=1, source_target_pairs={{0,1},{1,0},{2,3},{3,2},{4,5},{5,4},{6,7},{7,6},{8,9},{9,8},{10,11... | collective-permute-start | bytes 1769480 | tf_op jit(solution)/shard_map/ppermute | solution.py:726
  51.7 13.5 %collective-permute-start.10 = (bf16[9,128,256]{2,1,0:T(8,128)(2,1)}, bf16[9,128,256]{2,1,0:T(8,128)(2,1)}, u32[]{:S(2)}, u32[]{:S(2)}) collective-permute-start(bf16[9,128,256]{2,1,0:T(8,128)(2,1)} %collective-permute-done.1.refs_6_.refs_12_), channel_id=1, source_target_pairs={{0,1},{1,0},{2,3},{3,2},{4,5},{5,4},{6,7},{7,6},{8,9},{9,8},{10,11... | collective-permute-start | bytes 1769480 | tf_op jit(solution)/shard_map/ppermute | solution.py:726
  52.1 14.1 %collective-permute-start.9 = (bf16[9,128,256]{2,1,0:T(8,128)(2,1)}, bf16[9,128,256]{2,1,0:T(8,128)(2,1)}, u32[]{:S(2)}, u32[]{:S(2)}) collective-permute-start(bf16[9,128,256]{2,1,0:T(8,128)(2,1)} %collective-permute-done.refs_5_.refs_11_), channel_id=1, source_target_pairs={{0,1},{1,0},{2,3},{3,2},{4,5},{5,4},{6,7},{7,6},{8,9},{9,8},{10,11... | collective-permute-start | bytes 1769480 | tf_op jit(solution)/shard_map/ppermute | solution.py:726
  52.2 16.8 %collective-permute-start.8 = (bf16[9,128,256]{2,1,0:T(8,128)(2,1)}, bf16[9,128,256]{2,1,0:T(8,128)(2,1)}, u32[]{:S(2)}, u32[]{:S(2)}) collective-permute-start(bf16[9,128,256]{2,1,0:T(8,128)(2,1)} %dynamic-slice_convert_fusion.refs_4_.refs_10_), channel_id=1, source_target_pairs={{0,1},{1,0},{2,3},{3,2},{4,5},{5,4},{6,7},{7,6},{8,9},{9,8},{10,11... | collective-permute-start | bytes 1769480 | tf_op jit(solution)/shard_map/ppermute | solution.py:726
  52.6 12.1 %all-to-all-start.1 = ((f32[32,8,128]{2,1,0:T(8,128)}), f32[32,8,128]{2,1,0:T(8,128)}, u32[]{:S(2)}, u32[]{:S(2)}) async-start(f32[32,8,128]{2,1,0:T(8,128)} %get-tuple-element.141), calls=%async_computation.1 | async-start | bytes 262144 | tf_op jit(solution)/shard_map/all_to_all | solution.py:752
  56.5 12.5 %collective-permute-start.7 = (f32[256,256]{1,0:T(8,128)}, f32[256,256]{1,0:T(8,128)}, u32[]{:S(2)}, u32[]{:S(2)}) collective-permute-start(f32[256,256]{1,0:T(8,128)} %get-tuple-element.140), channel_id=1, source_target_pairs={{0,1},{1,0},{2,3},{3,2},{4,5},{5,4},{6,7},{7,6},{8,9},{9,8},{10,11... | collective-permute-start | bytes 786440 | tf_op jit(solution)/shard_map/ppermute | solution.py:726
  64.7 11.8 %collective-permute-start.12 = (bf16[256,512]{1,0:T(8,128)(2,1)}, bf16[256,512]{1,0:T(8,128)(2,1)}, u32[]{:S(2)}, u32[]{:S(2)}) collective-permute-start(bf16[256,512]{1,0:T(8,128)(2,1)} %get-tuple-element.155.refs_6_.refs_4_.refs_19_), channel_id=1, source_target_pairs={{0,2},{2,0},{4,6},{6,4},{1,3},{3,1},{5,7},{7,5},{8,10},{10,8},{12,... | collective-permute-start | bytes 786440 | tf_op jit(solution)/shard_map/ppermute | solution.py:726
  65.2 14.0 %collective-permute-start.13 = (bf16[256,512]{1,0:T(8,128)(2,1)}, bf16[256,512]{1,0:T(8,128)(2,1)}, u32[]{:S(2)}, u32[]{:S(2)}) collective-permute-start(bf16[256,512]{1,0:T(8,128)(2,1)} %get-tuple-element.155.refs_6_.refs_4_.refs_19_), channel_id=1, source_target_pairs={{0,4},{2,6},{4,0},{6,2},{1,5},{3,7},{5,1},{7,3},{8,12},{10,14},{12... | collective-permute-start | bytes 786440 | tf_op jit(solution)/shard_map/ppermute | solution.py:726
  66.2 13.0 %collective-permute-start.14 = (bf16[256,512]{1,0:T(8,128)(2,1)}, bf16[256,512]{1,0:T(8,128)(2,1)}, u32[]{:S(2)}, u32[]{:S(2)}) collective-permute-start(bf16[256,512]{1,0:T(8,128)(2,1)} %get-tuple-element.155.refs_6_.refs_4_.refs_19_), channel_id=1, source_target_pairs={{0,6},{2,4},{4,2},{6,0},{1,7},{3,5},{5,3},{7,1},{8,14},{10,12},{12... | collective-permute-start | bytes 786440 | tf_op jit(solution)/shard_map/ppermute | solution.py:726
  73.2 11.5 %all-to-all-start.2 = ((f32[32,8,128]{2,1,0:T(8,128)}), f32[32,8,128]{2,1,0:T(8,128)}, u32[]{:S(2)}, u32[]{:S(2)}) async-start(f32[32,8,128]{2,1,0:T(8,128)} %get-tuple-element.153), calls=%async_computation.2 | async-start | bytes 262144 | tf_op jit(solution)/shard_map/all_to_all | solution.py:752
  91.5 14.7 %all-to-all-start.3 = ((bf16[32,32,128]{2,1,0:T(8,128)(2,1)}), bf16[32,32,128]{2,1,0:T(8,128)(2,1)}, u32[]{:S(2)}, u32[]{:S(2)}) async-start(bf16[32,32,128]{2,1,0:T(8,128)(2,1)} %bitcast.47), calls=%async_computation.3 | async-start | bytes 524288 | tf_op jit(solution)/shard_map/all_to_all | solution.py:752
  95.0 11.2 %collective-permute-start.15 = (bf16[256,128]{1,0:T(8,128)(2,1)}, bf16[256,128]{1,0:T(8,128)(2,1)}, u32[]{:S(2)}, u32[]{:S(2)}) collective-permute-start(bf16[256,128]{1,0:T(8,128)(2,1)} %get-tuple-element.169), channel_id=1, source_target_pairs={{0,2},{2,0},{4,6},{6,4},{1,3},{3,1},{5,7},{7,5},{8,10},{10,8},{12,... | collective-permute-start | bytes 196616 | tf_op jit(solution)/shard_map/ppermute | solution.py:726
  96.4 9.7 %collective-permute-start.16 = (bf16[256,128]{1,0:T(8,128)(2,1)}, bf16[256,128]{1,0:T(8,128)(2,1)}, u32[]{:S(2)}, u32[]{:S(2)}) collective-permute-start(bf16[256,128]{1,0:T(8,128)(2,1)} %get-tuple-element.170), channel_id=1, source_target_pairs={{0,4},{2,6},{4,0},{6,2},{1,5},{3,7},{5,1},{7,3},{8,12},{10,14},{12... | collective-permute-start | bytes 196616 | tf_op jit(solution)/shard_map/ppermute | solution.py:726
  97.9 8.2 %collective-permute-start.17 = (bf16[256,128]{1,0:T(8,128)(2,1)}, bf16[256,128]{1,0:T(8,128)(2,1)}, u32[]{:S(2)}, u32[]{:S(2)}) collective-permute-start(bf16[256,128]{1,0:T(8,128)(2,1)} %get-tuple-element.171), channel_id=1, source_target_pairs={{0,6},{2,4},{4,2},{6,0},{1,7},{3,5},{5,3},{7,1},{8,14},{10,12},{12... | collective-permute-start | bytes 196616 | tf_op jit(solution)/shard_map/ppermute | solution.py:726
  113.0 2.3 collective-permute-start.18
  116.5 9.1 %collective-permute-start.19 = (bf16[1152,128]{1,0:T(8,128)(2,1)S(1)}, bf16[1152,128]{1,0:T(8,128)(2,1)S(1)}, u32[]{:S(2)}, u32[]{:S(2)}) collective-permute-start(bf16[1152,128]{1,0:T(8,128)(2,1)S(1)} %get-tuple-element.175), channel_id=1, source_target_pairs={{0,8},{8,0},{16,24},{24,16},{1,9},{9,1},{17,25},{25,17},{2,10},{10... | collective-permute-start | bytes 884744 | tf_op jit(solution)/shard_map/ppermute | solution.py:726
  118.0 10.2 %collective-permute-start.20 = (bf16[512,256]{1,0:T(8,128)(2,1)S(1)}, bf16[512,256]{1,0:T(8,128)(2,1)S(1)}, u32[]{:S(2)}, u32[]{:S(2)}) collective-permute-start(bf16[512,256]{1,0:T(8,128)(2,1)S(1)} %copy-done.17), channel_id=1, source_target_pairs={{0,2},{2,0},{4,6},{6,4},{1,3},{3,1},{5,7},{7,5},{8,10},{10,8},{12,... | collective-permute-start | bytes 786440 | tf_op jit(solution)/shard_map/ppermute | solution.py:726
  119.5 13.4 %collective-permute-start.21 = (bf16[512,256]{1,0:T(8,128)(2,1)S(1)}, bf16[512,256]{1,0:T(8,128)(2,1)S(1)}, u32[]{:S(2)}, u32[]{:S(2)}) collective-permute-start(bf16[512,256]{1,0:T(8,128)(2,1)S(1)} %copy-done.17), channel_id=1, source_target_pairs={{0,4},{2,6},{4,0},{6,2},{1,5},{3,7},{5,1},{7,3},{8,12},{10,14},{12... | collective-permute-start | bytes 786440 | tf_op jit(solution)/shard_map/ppermute | solution.py:726
  121.0 11.9 %collective-permute-start.22 = (bf16[512,256]{1,0:T(8,128)(2,1)S(1)}, bf16[512,256]{1,0:T(8,128)(2,1)S(1)}, u32[]{:S(2)}, u32[]{:S(2)}) collective-permute-start(bf16[512,256]{1,0:T(8,128)(2,1)S(1)} %copy-done.17), channel_id=1, source_target_pairs={{0,6},{2,4},{4,2},{6,0},{1,7},{3,5},{5,3},{7,1},{8,14},{10,12},{12... | collective-permute-start | bytes 786440 | tf_op jit(solution)/shard_map/ppermute | solution.py:726
  125.7 9.2 %collective-permute-start.23 = (bf16[576,128]{1,0:T(8,128)(2,1)S(1)}, bf16[576,128]{1,0:T(8,128)(2,1)S(1)}, u32[]{:S(2)}, u32[]{:S(2)}) collective-permute-start(bf16[576,128]{1,0:T(8,128)(2,1)S(1)} %get-tuple-element.178), channel_id=1, source_target_pairs={{0,16},{8,24},{16,0},{24,8},{1,17},{9,25},{17,1},{25,9},{2,18},{10... | collective-permute-start | bytes 442376 | tf_op jit(solution)/shard_map/ppermute | solution.py:726
  134.9 9.0 %collective-permute-start.27 = (bf16[576,128]{1,0:T(8,128)(2,1)S(1)}, bf16[576,128]{1,0:T(8,128)(2,1)S(1)}, u32[]{:S(2)}, u32[]{:S(2)}) collective-permute-start(bf16[576,128]{1,0:T(8,128)(2,1)S(1)} %add_convert_fusion.refs_1_), channel_id=1, source_target_pairs={{0,16},{8,24},{16,0},{24,8},{1,17},{9,25},{17,1},{25,9},{2,18},{10... | collective-permute-start | bytes 442376 | tf_op jit(solution)/shard_map/ppermute | solution.py:726
  138.1 12.9 %collective-permute-start.24 = (bf16[2304,128]{1,0:T(8,128)(2,1)S(1)}, bf16[2304,128]{1,0:T(8,128)(2,1)S(1)}, u32[]{:S(2)}, u32[]{:S(2)}) collective-permute-start(bf16[2304,128]{1,0:T(8,128)(2,1)S(1)} %get-tuple-element.181), channel_id=1, source_target_pairs={{0,1},{1,0},{2,3},{3,2},{4,5},{5,4},{6,7},{7,6},{8,9},{9,8},{10,11... | collective-permute-start | bytes 1769480 | tf_op jit(solution)/shard_map/ppermute | solution.py:726
  144.0 6.8 %collective-permute-start.28 = (bf16[1152,128]{1,0:T(8,128)(2,1)S(1)}, bf16[1152,128]{1,0:T(8,128)(2,1)S(1)}, u32[]{:S(2)}, u32[]{:S(2)}) collective-permute-start(bf16[1152,128]{1,0:T(8,128)(2,1)S(1)} %shard_map.357.refs_1_), channel_id=1, source_target_pairs={{0,8},{8,0},{16,24},{24,16},{1,9},{9,1},{17,25},{25,17},{2,10},{10... | collective-permute-start | bytes 884744 | tf_op jit(solution)/shard_map/ppermute | solution.py:726
  150.9 12.3 %collective-permute-start.29 = (bf16[2304,128]{1,0:T(8,128)(2,1)S(1)}, bf16[2304,128]{1,0:T(8,128)(2,1)S(1)}, u32[]{:S(2)}, u32[]{:S(2)}) collective-permute-start(bf16[2304,128]{1,0:T(8,128)(2,1)S(1)} %shard_map.358.refs_1_), channel_id=1, source_target_pairs={{0,1},{1,0},{2,3},{3,2},{4,5},{5,4},{6,7},{7,6},{8,9},{9,8},{10,11... | collective-permute-start | bytes 1769480 | tf_op jit(solution)/shard_map/ppermute | solution.py:726
  151.1 9.5 %collective-permute-start.25 = (bf16[1152,128]{1,0:T(8,128)(2,1)S(1)}, bf16[1152,128]{1,0:T(8,128)(2,1)S(1)}, u32[]{:S(2)}, u32[]{:S(2)}) collective-permute-start(bf16[1152,128]{1,0:T(8,128)(2,1)S(1)} %get-tuple-element.183), channel_id=1, source_target_pairs={{0,8},{8,0},{16,24},{24,16},{1,9},{9,1},{17,25},{25,17},{2,10},{10... | collective-permute-start | bytes 884744 | tf_op jit(solution)/shard_map/ppermute | solution.py:726
  160.7 9.6 %collective-permute-start.26 = (bf16[576,128]{1,0:T(8,128)(2,1)S(1)}, bf16[576,128]{1,0:T(8,128)(2,1)S(1)}, u32[]{:S(2)}, u32[]{:S(2)}) collective-permute-start(bf16[576,128]{1,0:T(8,128)(2,1)S(1)} %get-tuple-element.185), channel_id=1, source_target_pairs={{0,16},{8,24},{16,0},{24,8},{1,17},{9,25},{17,1},{25,9},{2,18},{10... | collective-permute-start | bytes 442376 | tf_op jit(solution)/shard_map/ppermute | solution.py:726
  170.4 9.0 %collective-permute-start.34 = (bf16[576,128]{1,0:T(8,128)(2,1)S(1)}, bf16[576,128]{1,0:T(8,128)(2,1)S(1)}, u32[]{:S(2)}, u32[]{:S(2)}) collective-permute-start(bf16[576,128]{1,0:T(8,128)(2,1)S(1)} %get-tuple-element.188.refs_1_), channel_id=1, source_target_pairs={{0,16},{8,24},{16,0},{24,8},{1,17},{9,25},{17,1},{25,9},{2,18},{10... | collective-permute-start | bytes 442376 | tf_op jit(solution)/shard_map/ppermute | solution.py:726
  170.5 10.5 %collective-permute-start.35 = (bf16[576,128]{1,0:T(8,128)(2,1)S(1)}, bf16[576,128]{1,0:T(8,128)(2,1)S(1)}, u32[]{:S(2)}, u32[]{:S(2)}) collective-permute-start(bf16[576,128]{1,0:T(8,128)(2,1)S(1)} %get-tuple-element.196.refs_1_), channel_id=1, source_target_pairs={{0,2},{2,0},{4,6},{6,4},{1,3},{3,1},{5,7},{7,5},{8,10},{10,8},{12,... | collective-permute-start | bytes 442376 | tf_op jit(solution)/shard_map/ppermute | solution.py:726
  172.0 10.7 %collective-permute-start.36 = (bf16[576,128]{1,0:T(8,128)(2,1)S(1)}, bf16[576,128]{1,0:T(8,128)(2,1)S(1)}, u32[]{:S(2)}, u32[]{:S(2)}) collective-permute-start(bf16[576,128]{1,0:T(8,128)(2,1)S(1)} %get-tuple-element.196.refs_1_), channel_id=1, source_target_pairs={{0,4},{2,6},{4,0},{6,2},{1,5},{3,7},{5,1},{7,3},{8,12},{10,14},{12... | collective-permute-start | bytes 442376 | tf_op jit(solution)/shard_map/ppermute | solution.py:726
  173.5 9.3 %collective-permute-start.37 = (bf16[576,128]{1,0:T(8,128)(2,1)S(1)}, bf16[576,128]{1,0:T(8,128)(2,1)S(1)}, u32[]{:S(2)}, u32[]{:S(2)}) collective-permute-start(bf16[576,128]{1,0:T(8,128)(2,1)S(1)} %get-tuple-element.196.refs_1_), channel_id=1, source_target_pairs={{0,6},{2,4},{4,2},{6,0},{1,7},{3,5},{5,3},{7,1},{8,14},{10,12},{12... | collective-permute-start | bytes 442376 | tf_op jit(solution)/shard_map/ppermute | solution.py:726
  174.0 28.5 %collective-permute-start.30 = (bf16[2304,128]{1,0:T(8,128)(2,1)S(1)}, bf16[2304,128]{1,0:T(8,128)(2,1)S(1)}, u32[]{:S(2)}, u32[]{:S(2)}) collective-permute-start(bf16[2304,128]{1,0:T(8,128)(2,1)S(1)} %get-tuple-element.186.refs_1_), channel_id=1, source_target_pairs={{0,2},{2,0},{4,6},{6,4},{1,3},{3,1},{5,7},{7,5},{8,10},{10,8},{12,... | collective-permute-start | bytes 1769480 | tf_op jit(solution)/shard_map/ppermute | solution.py:726
  179.4 26.2 %collective-permute-start.31 = (bf16[2304,128]{1,0:T(8,128)(2,1)S(1)}, bf16[2304,128]{1,0:T(8,128)(2,1)S(1)}, u32[]{:S(2)}, u32[]{:S(2)}) collective-permute-start(bf16[2304,128]{1,0:T(8,128)(2,1)S(1)} %get-tuple-element.186.refs_1_), channel_id=1, source_target_pairs={{0,4},{2,6},{4,0},{6,2},{1,5},{3,7},{5,1},{7,3},{8,12},{10,14},{12... | collective-permute-start | bytes 1769480 | tf_op jit(solution)/shard_map/ppermute | solution.py:726
  180.9 24.7 %collective-permute-start.32 = (bf16[2304,128]{1,0:T(8,128)(2,1)S(1)}, bf16[2304,128]{1,0:T(8,128)(2,1)S(1)}, u32[]{:S(2)}, u32[]{:S(2)}) collective-permute-start(bf16[2304,128]{1,0:T(8,128)(2,1)S(1)} %get-tuple-element.186.refs_1_), channel_id=1, source_target_pairs={{0,6},{2,4},{4,2},{6,0},{1,7},{3,5},{5,3},{7,1},{8,14},{10,12},{12... | collective-permute-start | bytes 1769480 | tf_op jit(solution)/shard_map/ppermute | solution.py:726
  183.2 9.1 %collective-permute-start.38 = (bf16[576,128]{1,0:T(8,128)(2,1)S(1)}, bf16[576,128]{1,0:T(8,128)(2,1)S(1)}, u32[]{:S(2)}, u32[]{:S(2)}) collective-permute-start(bf16[576,128]{1,0:T(8,128)(2,1)S(1)} %shard_map.367.refs_1_), channel_id=1, source_target_pairs={{0,16},{8,24},{16,0},{24,8},{1,17},{9,25},{17,1},{25,9},{2,18},{10... | collective-permute-start | bytes 442376 | tf_op jit(solution)/shard_map/ppermute | solution.py:726
  192.4 10.0 %collective-permute-start.39 = (bf16[1152,128]{1,0:T(8,128)(2,1)S(1)}, bf16[1152,128]{1,0:T(8,128)(2,1)S(1)}, u32[]{:S(2)}, u32[]{:S(2)}) collective-permute-start(bf16[1152,128]{1,0:T(8,128)(2,1)S(1)} %shard_map.368.refs_1_), channel_id=1, source_target_pairs={{0,8},{8,0},{16,24},{24,16},{1,9},{9,1},{17,25},{25,17},{2,10},{10... | collective-permute-start | bytes 884744 | tf_op jit(solution)/shard_map/ppermute | solution.py:726
  192.4 15.0 %collective-permute-start.41 = (bf16[1152,128]{1,0:T(8,128)(2,1)S(1)}, bf16[1152,128]{1,0:T(8,128)(2,1)S(1)}, u32[]{:S(2)}, u32[]{:S(2)}) collective-permute-start(bf16[1152,128]{1,0:T(8,128)(2,1)S(1)} %shard_map.366.refs_1_), channel_id=1, source_target_pairs={{0,8},{8,0},{16,24},{24,16},{1,9},{9,1},{17,25},{25,17},{2,10},{10... | collective-permute-start | bytes 884744 | tf_op jit(solution)/shard_map/ppermute | solution.py:726
  202.4 5.3 %collective-permute-start.40 = (bf16[2304,128]{1,0:T(8,128)(2,1)S(1)}, bf16[2304,128]{1,0:T(8,128)(2,1)S(1)}, u32[]{:S(2)}, u32[]{:S(2)}) collective-permute-start(bf16[2304,128]{1,0:T(8,128)(2,1)S(1)} %shard_map.370.refs_1_), channel_id=1, source_target_pairs={{0,1},{1,0},{2,3},{3,2},{4,5},{5,4},{6,7},{7,6},{8,9},{9,8},{10,11... | collective-permute-start | bytes 1769480 | tf_op jit(solution)/shard_map/ppermute | solution.py:726
  207.6 9.2 %collective-permute-start.42 = (bf16[2304,128]{1,0:T(8,128)(2,1)S(1)}, bf16[2304,128]{1,0:T(8,128)(2,1)S(1)}, u32[]{:S(2)}, u32[]{:S(2)}) collective-permute-start(bf16[2304,128]{1,0:T(8,128)(2,1)S(1)} %shard_map.373.refs_1_), channel_id=1, source_target_pairs={{0,1},{1,0},{2,3},{3,2},{4,5},{5,4},{6,7},{7,6},{8,9},{9,8},{10,11... | collective-permute-start | bytes 1769480 | tf_op jit(solution)/shard_map/ppermute | solution.py:726
  211.8 7.3 %collective-permute-start.43 = (f32[8,128]{1,0:T(8,128)S(1)}, f32[8,128]{1,0:T(8,128)S(1)}, u32[]{:S(2)}, u32[]{:S(2)}) collective-permute-start(f32[8,128]{1,0:T(8,128)S(1)} %get-tuple-element.204.refs_0_), channel_id=1, source_target_pairs={{0,2},{2,0},{4,6},{6,4},{1,3},{3,1},{5,7},{7,5},{8,10},{10,8},{12,... | collective-permute-start | bytes 12296 | tf_op jit(solution)/shard_map/ppermute | solution.py:726
  215.1 4.0 %collective-permute-start.44 = (f32[8,128]{1,0:T(8,128)S(1)}, f32[8,128]{1,0:T(8,128)S(1)}, u32[]{:S(2)}, u32[]{:S(2)}) collective-permute-start(f32[8,128]{1,0:T(8,128)S(1)} %get-tuple-element.204.refs_0_), channel_id=1, source_target_pairs={{0,4},{2,6},{4,0},{6,2},{1,5},{3,7},{5,1},{7,3},{8,12},{10,14},{12... | collective-permute-start | bytes 12296 | tf_op jit(solution)/shard_map/ppermute | solution.py:726
  216.8 4.5 %collective-permute-start.45 = (f32[8,128]{1,0:T(8,128)S(1)}, f32[8,128]{1,0:T(8,128)S(1)}, u32[]{:S(2)}, u32[]{:S(2)}) collective-permute-start(f32[8,128]{1,0:T(8,128)S(1)} %get-tuple-element.204.refs_0_), channel_id=1, source_target_pairs={{0,6},{2,4},{4,2},{6,0},{1,7},{3,5},{5,3},{7,1},{8,14},{10,12},{12... | collective-permute-start | bytes 12296 | tf_op jit(solution)/shard_map/ppermute | solution.py:726
  (34 other events, 396.8 us)

commit v8 on v7

--- a/solution.py
+++ b/solution.py
@@ -355,7 +355,11 @@
     logits = jnp.where(class_index < CLASSES, logits, -1e30)
     logits = logits - jnp.max(logits, axis=1, keepdims=True)
     log_probs = logits - jnp.log(jnp.sum(jnp.exp(logits), axis=1, keepdims=True))
-    wanted = jnp.where(class_index == labels_ref[...], 1.0 - SMOOTH, 0.0) + SMOOTH / CLASSES
+    same = lax.broadcasted_iota(jnp.int32, (part, part), 0) == lax.broadcasted_iota(
+        jnp.int32, (part, part), 1
+    )
+    label = jnp.sum(jnp.where(same, labels_ref[...].astype(F32), 0.0), axis=1, keepdims=True)
+    wanted = jnp.where(class_index.astype(F32) == label, 1.0 - SMOOTH, 0.0) + SMOOTH / CLASSES
     wanted = jnp.where(class_index < CLASSES, wanted, 0.0)
     loss = -jnp.sum(jnp.sum(wanted * log_probs, axis=1, keepdims=True), axis=0, keepdims=True)
     logit_grad = jnp.exp(log_probs) - wanted
@@ -856,7 +860,7 @@
     bases_all = (basis_in_first, basis_out_first, basis_in_second, basis_out_second)
 
     piece = lax.dynamic_slice_in_dim(w_second, side * half, half, 2).astype(BF)
-    own_labels = lax.dynamic_slice_in_dim(labels, me * part, part, 0)[:, None]
+    own_labels = lax.dynamic_slice_in_dim(labels, me * part, part, 0)[None]
     bias_row = jnp.pad(head_b, (0, LANES - CLASSES))[None]
 
     flat_images = images.reshape(PIX * count, channels)
@@ -1072,12 +1076,12 @@
     left_parts = [left_turned[step] for step in range(groups)]
     *products_first, sums_first, smalls = call(
         lambda *refs: first_products_kernel(
-            *refs[:5], refs[5:11], *[refs[11 + at * groups : 11 + (at + 1) * groups] for at in range(3)],
+            *refs[:5], refs[5:11], *[refs[11 + at * groups : 11 + (at + 1) * groups] for at in (2, 0, 1)],
             *refs[11 + 3 * groups :]
         ),
         [shape((TAPS * channels // 2, width), BF)] * 2 + [shape((8, LANES), F32), shape((72, LANES), F32)],
         [
-            place, after(got, right_turned, *left_slots), norm_first, all_mask, basis_out_first, *small_old, *left_parts, *right_parts, *scaled_slots,
+            place, after(got, right_turned, *left_slots), norm_first, all_mask, basis_out_first, *small_old, *right_parts, *scaled_slots, *left_parts,
         ],
         [
             pltpu.VMEM((channels, groups * rows), BF),

time: 230 us -> 230 us (level)
  no operation moved by 1% of the time
where the time goes in v8:
time: 230 us; the launch traced here: 229 us
  waiting for transfers between devices  81.6 us (35%)
  Pallas kernels  67.2 us (29%)
  starting transfers between devices  61.4 us (27%)
  local copies, waits for them, and re-layouts  15.6 us (7%)
    ppermute x46, waiting for transfers between devices, swap(): lax.ppermute(values, axis, [(here, here ^ step) for here in range(count)])  71.3 us
    pallas_call x35, Pallas kernels, call(): pl.pallas_call(body, out_shape=list(outs), in_specs=specs, out_specs=[pl....  57.2 us
    ppermute x46, starting transfers between devices, swap(): lax.ppermute(values, axis, [(here, here ^ step) for here in range(count)])  45.8 us
    all_to_all x3, starting transfers between devices, every_device(): return lax.all_to_all(tiles, EVERY, 0, 0, tiled=True)  10.7 us
    all_to_all x3, waiting for transfers between devices, every_device(): return lax.all_to_all(tiles, EVERY, 0, 0, tiled=True)  10.3 us
    pallas_call x1, Pallas kernels, local(): pl.pallas_call(update, grid=(TAPS // 3,), scratch_shapes=[pltpu.VMEM((8,...  7.8 us
    unnamed x64, local copies, waits for them, and re-layouts  5.08 us
    all_to_all x1, starting transfers between devices, local(): got = lax.all_to_all(stats, ('dp', 'cin'), 0, 0, tiled=True)  4.89 us
  transfers between devices with their start and end apart: 50, of which 21 were waited for; matrix products, arithmetic and copies ran while one was open for 4% of the time, Pallas kernels for 18%

profile of v8, /device:TPU:0, one launch (start us, length us, event | category | flops | bytes accessed | tf_op | source)
XLA Modules:
  0.0 228.9 jit_solution(9443326261036446975)
XLA Ops:
  0.7 2.2 dynamic-slice_convert_fusion.refs_4_.refs_10_
  2.8 2.9 %collective-permute-start = (bf16[9,128,256]{2,1,0:T(8,128)(2,1)}, bf16[9,128,256]{2,1,0:T(8,128)(2,1)}, u32[]{:S(2)}, u32[]{:S(2)}) collective-permute-start(bf16[9,128,256]{2,1,0:T(8,128)(2,1)} %dynamic-slice_convert_fusion.refs_4_.refs_10_), channel_id=1, source_target_pairs={{0,2},{2,0},{4,6},{6,4},{1,3},{3,1},{5,7},{7,5},{8,10},{10,8},{12,... | collective-permute-start | bytes 1769480 | tf_op jit(solution)/shard_map/ppermute | solution.py:730
  7.9 5.4 %shard_map.340 = (f32[1024,128]{1,0:T(8,128)}, bf16[1024,128]{1,0:T(8,128)(2,1)}, f32[8,8,128]{2,1,0:T(8,128)}, f32[256,128]{1,0:T(8,128)}) custom-call(s32[2]{0:T(128)} %pad_add_fusion.refs_0_, bf16[1024,512]{1,0:T(8,128)(2,1)} %bitcast.44, s32[16,64]{1,0:T(8,128)} %refs_2_.3, f32[9,512,128]{2,1,0:T(8,128)} %refs_0_), custom_call_target="tpu_custom_call" | custom-call | flops 1207959552 | bytes 4362248 | tf_op jit(solution)/shard_map/pallas_call | solution.py:117
  13.4 4.9 %all-to-all-start = ((f32[8,8,128]{2,1,0:T(8,128)}), f32[8,8,128]{2,1,0:T(8,128)S(1)}, u32[]{:S(2)}, u32[]{:S(2)}) async-start(f32[8,8,128]{2,1,0:T(8,128)} %get-tuple-element.122), calls=%async_computation | async-start | bytes 65536 | tf_op jit(solution)/shard_map/all_to_all | solution.py:888
  24.8 3.7 %shard_map.342 = (bf16[528,128]{1,0:T(8,128)(2,1)}, bf16[528,128]{1,0:T(8,128)(2,1)}, bf16[528,128]{1,0:T(8,128)(2,1)}, bf16[528,128]{1,0:T(8,128)(2,1)}, f32[8,128]{1,0:T(8,128)}) custom-call(s32[2]{0:T(128)} %pad_add_fusion.refs_0_, f32[8,8,128]{2,1,0:T(8,128)} %copy-done.29, f32[1024,128]{1,0:T(8,128)} %get-tuple-element.123.refs_2_, ...), custom_call_target="tpu_custom_call" | custom-call | bytes 1371144 | tf_op jit(solution)/shard_map/pallas_call | solution.py:117
  34.1 1.9 copy.39
  36.0 1.7 constant_dynamic-slice_fusion.refs_2_
  38.4 2.6 %collective-permute-done.4.refs_4_ = bf16[528,128]{1,0:T(8,128)(2,1)} collective-permute-done((bf16[528,128]{1,0:T(8,128)(2,1)}, bf16[528,128]{1,0:T(8,128)(2,1)}, u32[]{:S(2)}, u32[]{:S(2)}) %collective-permute-start.4) | collective-permute-done | bytes 135200 | tf_op jit(solution)/shard_map/ppermute | solution.py:730
  41.0 2.8 %shard_map.343.refs_1_ = bf16[256,640]{1,0:T(8,128)(2,1)} custom-call(s32[2]{0:T(128)} %pad_add_fusion.refs_0_, bf16[528,128]{1,0:T(8,128)(2,1)} %get-tuple-element.129.refs_1_, bf16[528,128]{1,0:T(8,128)(2,1)} %collective-permute-done.2.refs_2_, bf16[528,128]{1,0:T(8,128)(2,1)} %collective-permute-done.3.refs_3_, ...), custom_call_target="tpu_custom_call" | custom-call | bytes 999432 | tf_op jit(solution)/shard_map/pallas_call | solution.py:117
  43.9 1.8 collective-permute-done.5.refs_2_
  46.5 5.0 %shard_map.344 = (f32[256,256]{1,0:T(8,128)}, f32[256,256]{1,0:T(8,128)}, f32[32,8,128]{2,1,0:T(8,128)}) custom-call(s32[2]{0:T(128)} %pad_add_fusion.refs_0_, bf16[256,640]{1,0:T(8,128)(2,1)} %shard_map.343.refs_1_, bf16[256,640]{1,0:T(8,128)(2,1)} %copy-done.30, f32[4,128]{1,0:T(4,128)} %refs_3_.3, ...), custom_call_target="tpu_custom_call" | custom-call | flops 1207959552 | bytes 3672072 | tf_op jit(solution)/shard_map/pallas_call | solution.py:117
  52.6 3.9 %all-to-all-start.1 = ((f32[32,8,128]{2,1,0:T(8,128)}), f32[32,8,128]{2,1,0:T(8,128)}, u32[]{:S(2)}, u32[]{:S(2)}) async-start(f32[32,8,128]{2,1,0:T(8,128)} %get-tuple-element.141), calls=%async_computation.1 | async-start | bytes 262144 | tf_op jit(solution)/shard_map/all_to_all | solution.py:756
  57.3 2.6 %shard_map.345 = (bf16[256,512]{1,0:T(8,128)(2,1)}, f32[8,512]{1,0:T(8,128)}, bf16[16,512]{1,0:T(8,128)(2,1)}) custom-call(s32[2]{0:T(128)} %pad_add_fusion.refs_0_, bf16[528,128]{1,0:T(8,128)(2,1)} %get-tuple-element.129.refs_1_, bf16[528,128]{1,0:T(8,128)(2,1)} %collective-permute-done.2.refs_2_, bf16[528,128]{1,0:T(8,128)(2,1)} %collective-permute-done.3.refs_3_, ...), custom_call_target="tpu_custom_call" | custom-call | bytes 839688 | tf_op jit(solution)/shard_map/pallas_call | solution.py:117
  59.8 4.9 %all-to-all-done.1.refs_3_ = f32[32,8,128]{2,1,0:T(8,128)} async-done(((f32[32,8,128]{2,1,0:T(8,128)}), f32[32,8,128]{2,1,0:T(8,128)}, u32[]{:S(2)}, u32[]{:S(2)}) %all-to-all-start.1) | async-done | bytes 131104 | tf_op jit(solution)/shard_map/all_to_all | solution.py:756
  66.2 2.1 collective-permute-start.14
  68.8 4.3 %shard_map.346 = (f32[256,512]{1,0:T(8,128)}, f32[8,512]{1,0:T(8,128)}, f32[256,512]{1,0:T(8,128)}, f32[32,8,128]{2,1,0:T(8,128)}, f32[4,16,128]{2,1,0:T(8,128)}) custom-call(s32[2]{0:T(128)} %pad_add_fusion.refs_0_, f32[256,256]{1,0:T(8,128)} %get-tuple-element.139.refs_1_, f32[256,256]{1,0:T(8,128)} %collective-permute-done.7.refs_2_, ...), custom_call_target="tpu_custom_call" | custom-call | bytes 2048584 | tf_op jit(solution)/shard_map/pallas_call | solution.py:117
  73.1 3.3 %all-to-all-start.2 = ((f32[32,8,128]{2,1,0:T(8,128)}), f32[32,8,128]{2,1,0:T(8,128)}, u32[]{:S(2)}, u32[]{:S(2)}) async-start(f32[32,8,128]{2,1,0:T(8,128)} %get-tuple-element.153), calls=%async_computation.2 | async-start | bytes 262144 | tf_op jit(solution)/shard_map/all_to_all | solution.py:756
  76.4 2.8 %collective-permute-done.13.refs_6_.refs_17_ = bf16[256,512]{1,0:T(8,128)(2,1)} collective-permute-done((bf16[256,512]{1,0:T(8,128)(2,1)}, bf16[256,512]{1,0:T(8,128)(2,1)}, u32[]{:S(2)}, u32[]{:S(2)}) %collective-permute-start.13) | collective-permute-done | bytes 262176 | tf_op jit(solution)/shard_map/ppermute | solution.py:730
  79.2 5.4 %all-to-all-done.2.refs_4_ = f32[32,8,128]{2,1,0:T(8,128)} async-done(((f32[32,8,128]{2,1,0:T(8,128)}), f32[32,8,128]{2,1,0:T(8,128)}, u32[]{:S(2)}, u32[]{:S(2)}) %all-to-all-start.2) | async-done | bytes 131104 | tf_op jit(solution)/shard_map/all_to_all | solution.py:756
  84.6 6.7 %shard_map.347 = (bf16[256,512]{1,0:T(8,128)(2,1)}, f32[8,128]{1,0:T(8,128)}, bf16[4,4,2,32,128]{4,3,2,1,0:T(8,128)(2,1)}, bf16[256,128]{1,0:T(8,128)(2,1)}, bf1...) custom-call(s32[2]{0:T(128)} %pad_add_fusion.refs_0_, ...), custom_call_target="tpu_custom_call" | custom-call | flops 1207959552 | bytes 7671816 | tf_op jit(solution)/shard_map/pallas_call | solution.py:117
  91.3 3.5 %all-to-all-start.3 = ((bf16[32,32,128]{2,1,0:T(8,128)(2,1)}), bf16[32,32,128]{2,1,0:T(8,128)(2,1)}, u32[]{:S(2)}, u32[]{:S(2)}) async-start(bf16[32,32,128]{2,1,0:T(8,128)(2,1)} %bitcast.47), calls=%async_computation.3 | async-start | bytes 524288 | tf_op jit(solution)/shard_map/all_to_all | solution.py:756
  99.3 2.2 shard_map.348.refs_0_
  101.6 4.4 %shard_map.349 = (bf16[256,128]{1,0:T(8,128)(2,1)}, bf16[256,128]{1,0:T(8,128)(2,1)}, bf16[256,128]{1,0:T(8,128)(2,1)}, bf16[256,128]{1,0:T(8,128)(2,1)}) custom-call(s32[2]{0:T(128)} %pad_add_fusion.refs_0_, f32[8,512]{1,0:T(8,128)} %get-tuple-element.143.refs_4_.refs_7_.refs_1_.refs_2_, bf16[1024,128]{1,0:T(8,128)(2,1)} %get-tuple-element.162.refs_3_.refs_2_, ...), custom_call_target="tpu_custom_call" | custom-call | bytes 2113544 | tf_op jit(solution)/shard_map/pallas_call | solution.py:117
  106.0 6.5 %shard_map.350 = (bf16[2304,128]{1,0:T(8,128)(2,1)}, bf16[2304,128]{1,0:T(8,128)(2,1)}, f32[8,128]{1,0:T(8,128)}, f32[72,128]{1,0:T(8,128)}) custom-call(s32[2]{0:T(128)} %pad_add_fusion.refs_0_, bf16[32,32,128]{2,1,0:T(8,128)(2,1)} %all-to-all-done.3.refs_1_, f32[8,512]{1,0:T(8,128)} %get-tuple-element.143.refs_4_.refs_7_.refs_1_.refs_2_, ...), custom_call_target="tpu_custom_call" | custom-call | flops 1207959552 | bytes 4659288 | tf_op jit(solution)/shard_map/pallas_call | solution.py:117
  112.6 2.2 collective-permute-done.18.refs_2_
  121.1 4.1 %collective-permute-done.19.refs_2_ = bf16[1152,128]{1,0:T(8,128)(2,1)S(1)} collective-permute-done((bf16[1152,128]{1,0:T(8,128)(2,1)S(1)}, bf16[1152,128]{1,0:T(8,128)(2,1)S(1)}, u32[]{:S(2)}, u32[]{:S(2)}) %collective-permute-start.19) | collective-permute-done | bytes 294944 | tf_op jit(solution)/shard_map/ppermute | solution.py:730
  125.3 2.5 %collective-permute-start.23 = (bf16[576,128]{1,0:T(8,128)(2,1)S(1)}, bf16[576,128]{1,0:T(8,128)(2,1)S(1)}, u32[]{:S(2)}, u32[]{:S(2)}) collective-permute-start(bf16[576,128]{1,0:T(8,128)(2,1)S(1)} %get-tuple-element.178), channel_id=1, source_target_pairs={{0,16},{8,24},{16,0},{24,8},{1,17},{9,25},{17,1},{25,9},{2,18},{10... | collective-permute-start | bytes 442376 | tf_op jit(solution)/shard_map/ppermute | solution.py:730
  127.7 4.7 %collective-permute-done.21.refs_2_ = bf16[512,256]{1,0:T(8,128)(2,1)S(1)} collective-permute-done((bf16[512,256]{1,0:T(8,128)(2,1)S(1)}, bf16[512,256]{1,0:T(8,128)(2,1)S(1)}, u32[]{:S(2)}, u32[]{:S(2)}) %collective-permute-start.21) | collective-permute-done | bytes 262176 | tf_op jit(solution)/shard_map/ppermute | solution.py:730
  132.5 2.0 collective-permute-done.23
  135.1 2.4 %shard_map.353.refs_1_ = bf16[4608,128]{1,0:T(8,128)(2,1)S(1)} custom-call(bf16[512,256]{1,0:T(8,128)(2,1)S(1)} %copy-done.17, bf16[512,256]{1,0:T(8,128)(2,1)S(1)} %collective-permute-done.20.refs_1_, bf16[512,256]{1,0:T(8,128)(2,1)S(1)} %collective-permute-done.21.refs_2_, bf16[512,256]{1,0:T(8,128)(2,1)S(1)} %collective-permute-done.22.refs_3_, ...), custom_call_target="tpu_custom_call" | custom-call | flops 1207959552 | bytes 2490368 | tf_op jit(solution)/shard_map/pallas_call | solution.py:117
  137.7 5.8 %collective-permute-done.27.refs_2_ = bf16[576,128]{1,0:T(8,128)(2,1)S(1)} collective-permute-done((bf16[576,128]{1,0:T(8,128)(2,1)S(1)}, bf16[576,128]{1,0:T(8,128)(2,1)S(1)}, u32[]{:S(2)}, u32[]{:S(2)}) %collective-permute-start.27) | collective-permute-done | bytes 147488 | tf_op jit(solution)/shard_map/ppermute | solution.py:730
  143.6 6.7 %collective-permute-done.28.refs_2_ = bf16[1152,128]{1,0:T(8,128)(2,1)S(1)} collective-permute-done((bf16[1152,128]{1,0:T(8,128)(2,1)S(1)}, bf16[1152,128]{1,0:T(8,128)(2,1)S(1)}, u32[]{:S(2)}, u32[]{:S(2)}) %collective-permute-start.28) | collective-permute-done | bytes 294944 | tf_op jit(solution)/shard_map/ppermute | solution.py:730
  151.6 8.6 %collective-permute-done.25.refs_2_ = bf16[1152,128]{1,0:T(8,128)(2,1)S(1)} collective-permute-done((bf16[1152,128]{1,0:T(8,128)(2,1)S(1)}, bf16[1152,128]{1,0:T(8,128)(2,1)S(1)}, u32[]{:S(2)}, u32[]{:S(2)}) %collective-permute-start.25) | collective-permute-done | bytes 294944 | tf_op jit(solution)/shard_map/ppermute | solution.py:730
  160.2 2.5 %collective-permute-start.26 = (bf16[576,128]{1,0:T(8,128)(2,1)S(1)}, bf16[576,128]{1,0:T(8,128)(2,1)S(1)}, u32[]{:S(2)}, u32[]{:S(2)}) collective-permute-start(bf16[576,128]{1,0:T(8,128)(2,1)S(1)} %get-tuple-element.185), channel_id=1, source_target_pairs={{0,16},{8,24},{16,0},{24,8},{1,17},{9,25},{17,1},{25,9},{2,18},{10... | collective-permute-start | bytes 442376 | tf_op jit(solution)/shard_map/ppermute | solution.py:730
  162.9 2.9 %shard_map.360 = (f32[4608,128]{1,0:T(8,128)}, bf16[2304,128]{1,0:T(8,128)(2,1)S(1)}) custom-call(s32[2]{0:T(128)S(1)} %copy-done.19, bf16[4608,128]{1,0:T(8,128)(2,1)S(1)} %shard_map.359.refs_1_, f32[4608,128]{1,0:T(8,128)S(1)} %bitcast.43), custom_call_target="tpu_custom_call" | custom-call | bytes 6488072 | tf_op jit(solution)/shard_map/pallas_call | solution.py:117
  165.8 4.0 %collective-permute-done.26.refs_1_ = bf16[576,128]{1,0:T(8,128)(2,1)S(1)} collective-permute-done((bf16[576,128]{1,0:T(8,128)(2,1)S(1)}, bf16[576,128]{1,0:T(8,128)(2,1)S(1)}, u32[]{:S(2)}, u32[]{:S(2)}) %collective-permute-start.26) | collective-permute-done | bytes 147488 | tf_op jit(solution)/shard_map/ppermute | solution.py:730
  175.1 3.9 %collective-permute-done.34.refs_2_ = bf16[576,128]{1,0:T(8,128)(2,1)S(1)} collective-permute-done((bf16[576,128]{1,0:T(8,128)(2,1)S(1)}, bf16[576,128]{1,0:T(8,128)(2,1)S(1)}, u32[]{:S(2)}, u32[]{:S(2)}) %collective-permute-start.34) | collective-permute-done | bytes 147488 | tf_op jit(solution)/shard_map/ppermute | solution.py:730
  180.5 1.8 collective-permute-start.32
  184.5 7.4 %collective-permute-done.38.refs_2_ = bf16[576,128]{1,0:T(8,128)(2,1)S(1)} collective-permute-done((bf16[576,128]{1,0:T(8,128)(2,1)S(1)}, bf16[576,128]{1,0:T(8,128)(2,1)S(1)}, u32[]{:S(2)}, u32[]{:S(2)}) %collective-permute-start.38) | collective-permute-done | bytes 147488 | tf_op jit(solution)/shard_map/ppermute | solution.py:730
  192.0 2.0 collective-permute-start.41
  194.8 7.1 %collective-permute-done.39.refs_2_ = bf16[1152,128]{1,0:T(8,128)(2,1)S(1)} collective-permute-done((bf16[1152,128]{1,0:T(8,128)(2,1)S(1)}, bf16[1152,128]{1,0:T(8,128)(2,1)S(1)}, u32[]{:S(2)}, u32[]{:S(2)}) %collective-permute-start.39) | collective-permute-done | bytes 294944 | tf_op jit(solution)/shard_map/ppermute | solution.py:730
  202.0 3.1 %collective-permute-done.31.refs_3_ = bf16[2304,128]{1,0:T(8,128)(2,1)S(1)} collective-permute-done((bf16[2304,128]{1,0:T(8,128)(2,1)S(1)}, bf16[2304,128]{1,0:T(8,128)(2,1)S(1)}, u32[]{:S(2)}, u32[]{:S(2)}) %collective-permute-start.31) | collective-permute-done | bytes 589856 | tf_op jit(solution)/shard_map/ppermute | solution.py:730
  208.3 3.0 %shard_map.372 = (bf16[9,512,128]{2,1,0:T(8,128)(2,1)S(1)}, bf16[9,128,512]{2,1,0:T(8,128)(2,1)S(1)}, f32[8,128]{1,0:T(8,128)S(1)}, f32[72,128]{1,0:T(8,128)S(1)}) custom-call(s32[2]{0:T(128)S(1)} %copy-done.19, bf16[512,512]{1,0:T(8,128)(2,1)S(1)} %copy-done.12, bf16[4608,128]{1,0:T(8,128)(2,1)S(1)} %shard_map.365.refs_2_, bf16[512,512]{1,0:T(8,128)(2,1)S(1)} %copy-done.10, ...), custom_call_target="tpu_custom_call" | custom-call | flops 1207959552 | bytes 5853192 | tf_op jit(solution)/shard_map/pallas_call | solution.py:117
  211.3 3.3 %collective-permute-start.43 = (f32[8,128]{1,0:T(8,128)S(1)}, f32[8,128]{1,0:T(8,128)S(1)}, u32[]{:S(2)}, u32[]{:S(2)}) collective-permute-start(f32[8,128]{1,0:T(8,128)S(1)} %get-tuple-element.204.refs_0_), channel_id=1, source_target_pairs={{0,2},{2,0},{4,6},{6,4},{1,3},{3,1},{5,7},{7,5},{8,10},{10,8},{12,... | collective-permute-start | bytes 12296 | tf_op jit(solution)/shard_map/ppermute | solution.py:730
  214.6 1.7 collective-permute-start.44
  216.5 2.2 shard_map.376
  218.7 2.2 collective-permute-done.45.refs_3_
  220.9 7.8 %shard_map.375 = (f32[9,512,128]{2,1,0:T(8,128)}, f32[9,128,512]{2,1,0:T(8,128)}, f32[9,512,128]{2,1,0:T(8,128)}, f32[9,128,512]{2,1,0:T(8,128)}, f32[9,512,128]...) custom-call(f32[8,128]{1,0:T(8,128)S(1)} %get-tuple-element.204.refs, ...), custom_call_target="tpu_custom_call" | custom-call | tf_op jit(solution)/shard_map/pallas_call | solution.py:1192
  (165 shorter events, 45.7 us)
Async XLA Ops:
  2.8 21.3 %collective-permute-start = (bf16[9,128,256]{2,1,0:T(8,128)(2,1)}, bf16[9,128,256]{2,1,0:T(8,128)(2,1)}, u32[]{:S(2)}, u32[]{:S(2)}) collective-permute-start(bf16[9,128,256]{2,1,0:T(8,128)(2,1)} %dynamic-slice_convert_fusion.refs_4_.refs_10_), channel_id=1, source_target_pairs={{0,2},{2,0},{4,6},{6,4},{1,3},{3,1},{5,7},{7,5},{8,10},{10,8},{12,... | collective-permute-start | bytes 1769480 | tf_op jit(solution)/shard_map/ppermute | solution.py:730
  5.8 18.4 %collective-permute-start.1 = (bf16[9,128,256]{2,1,0:T(8,128)(2,1)}, bf16[9,128,256]{2,1,0:T(8,128)(2,1)}, u32[]{:S(2)}, u32[]{:S(2)}) collective-permute-start(bf16[9,128,256]{2,1,0:T(8,128)(2,1)} %dynamic-slice_convert_fusion.refs_4_.refs_10_), channel_id=1, source_target_pairs={{0,4},{2,6},{4,0},{6,2},{1,5},{3,7},{5,1},{7,3},{8,12},{10,14},{12... | collective-permute-start | bytes 1769480 | tf_op jit(solution)/shard_map/ppermute | solution.py:730
  13.4 10.8 %all-to-all-start = ((f32[8,8,128]{2,1,0:T(8,128)}), f32[8,8,128]{2,1,0:T(8,128)S(1)}, u32[]{:S(2)}, u32[]{:S(2)}) async-start(f32[8,8,128]{2,1,0:T(8,128)} %get-tuple-element.122), calls=%async_computation | async-start | bytes 65536 | tf_op jit(solution)/shard_map/all_to_all | solution.py:888
  18.3 25.7 %collective-permute-start.6 = (bf16[9,128,256]{2,1,0:T(8,128)(2,1)}, bf16[9,128,256]{2,1,0:T(8,128)(2,1)}, u32[]{:S(2)}, u32[]{:S(2)}) collective-permute-start(bf16[9,128,256]{2,1,0:T(8,128)(2,1)} %dynamic-slice_convert_fusion.refs_4_.refs_10_), channel_id=1, source_target_pairs={{0,6},{2,4},{4,2},{6,0},{1,7},{3,5},{5,3},{7,1},{8,14},{10,12},{12... | collective-permute-start | bytes 1769480 | tf_op jit(solution)/shard_map/ppermute | solution.py:730
  28.5 9.2 %collective-permute-start.2 = (bf16[528,128]{1,0:T(8,128)(2,1)}, bf16[528,128]{1,0:T(8,128)(2,1)}, u32[]{:S(2)}, u32[]{:S(2)}) collective-permute-start(bf16[528,128]{1,0:T(8,128)(2,1)} %get-tuple-element.130), channel_id=1, source_target_pairs={{0,2},{2,0},{4,6},{6,4},{1,3},{3,1},{5,7},{7,5},{8,10},{10,8},{12,... | collective-permute-start | bytes 405512 | tf_op jit(solution)/shard_map/ppermute | solution.py:730
  30.1 8.4 %collective-permute-start.3 = (bf16[528,128]{1,0:T(8,128)(2,1)}, bf16[528,128]{1,0:T(8,128)(2,1)}, u32[]{:S(2)}, u32[]{:S(2)}) collective-permute-start(bf16[528,128]{1,0:T(8,128)(2,1)} %get-tuple-element.131), channel_id=1, source_target_pairs={{0,4},{2,6},{4,0},{6,2},{1,5},{3,7},{5,1},{7,3},{8,12},{10,14},{12... | collective-permute-start | bytes 405512 | tf_op jit(solution)/shard_map/ppermute | solution.py:730
  31.6 9.5 %collective-permute-start.4 = (bf16[528,128]{1,0:T(8,128)(2,1)}, bf16[528,128]{1,0:T(8,128)(2,1)}, u32[]{:S(2)}, u32[]{:S(2)}) collective-permute-start(bf16[528,128]{1,0:T(8,128)(2,1)} %get-tuple-element.132), channel_id=1, source_target_pairs={{0,6},{2,4},{4,2},{6,0},{1,7},{3,5},{5,3},{7,1},{8,14},{10,12},{12... | collective-permute-start | bytes 405512 | tf_op jit(solution)/shard_map/ppermute | solution.py:730
  51.5 13.2 %collective-permute-start.11 = (bf16[9,128,256]{2,1,0:T(8,128)(2,1)}, bf16[9,128,256]{2,1,0:T(8,128)(2,1)}, u32[]{:S(2)}, u32[]{:S(2)}) collective-permute-start(bf16[9,128,256]{2,1,0:T(8,128)(2,1)} %collective-permute-done.6.refs_7_.refs_13_), channel_id=1, source_target_pairs={{0,1},{1,0},{2,3},{3,2},{4,5},{5,4},{6,7},{7,6},{8,9},{9,8},{10,11... | collective-permute-start | bytes 1769480 | tf_op jit(solution)/shard_map/ppermute | solution.py:730
  51.7 13.5 %collective-permute-start.10 = (bf16[9,128,256]{2,1,0:T(8,128)(2,1)}, bf16[9,128,256]{2,1,0:T(8,128)(2,1)}, u32[]{:S(2)}, u32[]{:S(2)}) collective-permute-start(bf16[9,128,256]{2,1,0:T(8,128)(2,1)} %collective-permute-done.1.refs_6_.refs_12_), channel_id=1, source_target_pairs={{0,1},{1,0},{2,3},{3,2},{4,5},{5,4},{6,7},{7,6},{8,9},{9,8},{10,11... | collective-permute-start | bytes 1769480 | tf_op jit(solution)/shard_map/ppermute | solution.py:730
  52.1 14.1 %collective-permute-start.9 = (bf16[9,128,256]{2,1,0:T(8,128)(2,1)}, bf16[9,128,256]{2,1,0:T(8,128)(2,1)}, u32[]{:S(2)}, u32[]{:S(2)}) collective-permute-start(bf16[9,128,256]{2,1,0:T(8,128)(2,1)} %collective-permute-done.refs_5_.refs_11_), channel_id=1, source_target_pairs={{0,1},{1,0},{2,3},{3,2},{4,5},{5,4},{6,7},{7,6},{8,9},{9,8},{10,11... | collective-permute-start | bytes 1769480 | tf_op jit(solution)/shard_map/ppermute | solution.py:730
  52.2 16.6 %collective-permute-start.8 = (bf16[9,128,256]{2,1,0:T(8,128)(2,1)}, bf16[9,128,256]{2,1,0:T(8,128)(2,1)}, u32[]{:S(2)}, u32[]{:S(2)}) collective-permute-start(bf16[9,128,256]{2,1,0:T(8,128)(2,1)} %dynamic-slice_convert_fusion.refs_4_.refs_10_), channel_id=1, source_target_pairs={{0,1},{1,0},{2,3},{3,2},{4,5},{5,4},{6,7},{7,6},{8,9},{9,8},{10,11... | collective-permute-start | bytes 1769480 | tf_op jit(solution)/shard_map/ppermute | solution.py:730
  52.6 12.1 %all-to-all-start.1 = ((f32[32,8,128]{2,1,0:T(8,128)}), f32[32,8,128]{2,1,0:T(8,128)}, u32[]{:S(2)}, u32[]{:S(2)}) async-start(f32[32,8,128]{2,1,0:T(8,128)} %get-tuple-element.141), calls=%async_computation.1 | async-start | bytes 262144 | tf_op jit(solution)/shard_map/all_to_all | solution.py:756
  56.5 12.3 %collective-permute-start.7 = (f32[256,256]{1,0:T(8,128)}, f32[256,256]{1,0:T(8,128)}, u32[]{:S(2)}, u32[]{:S(2)}) collective-permute-start(f32[256,256]{1,0:T(8,128)} %get-tuple-element.140), channel_id=1, source_target_pairs={{0,1},{1,0},{2,3},{3,2},{4,5},{5,4},{6,7},{7,6},{8,9},{9,8},{10,11... | collective-permute-start | bytes 786440 | tf_op jit(solution)/shard_map/ppermute | solution.py:730
  64.7 11.7 %collective-permute-start.12 = (bf16[256,512]{1,0:T(8,128)(2,1)}, bf16[256,512]{1,0:T(8,128)(2,1)}, u32[]{:S(2)}, u32[]{:S(2)}) collective-permute-start(bf16[256,512]{1,0:T(8,128)(2,1)} %get-tuple-element.155.refs_6_.refs_4_.refs_15_), channel_id=1, source_target_pairs={{0,2},{2,0},{4,6},{6,4},{1,3},{3,1},{5,7},{7,5},{8,10},{10,8},{12,... | collective-permute-start | bytes 786440 | tf_op jit(solution)/shard_map/ppermute | solution.py:730
  65.2 14.0 %collective-permute-start.13 = (bf16[256,512]{1,0:T(8,128)(2,1)}, bf16[256,512]{1,0:T(8,128)(2,1)}, u32[]{:S(2)}, u32[]{:S(2)}) collective-permute-start(bf16[256,512]{1,0:T(8,128)(2,1)} %get-tuple-element.155.refs_6_.refs_4_.refs_15_), channel_id=1, source_target_pairs={{0,4},{2,6},{4,0},{6,2},{1,5},{3,7},{5,1},{7,3},{8,12},{10,14},{12... | collective-permute-start | bytes 786440 | tf_op jit(solution)/shard_map/ppermute | solution.py:730
  66.2 13.0 %collective-permute-start.14 = (bf16[256,512]{1,0:T(8,128)(2,1)}, bf16[256,512]{1,0:T(8,128)(2,1)}, u32[]{:S(2)}, u32[]{:S(2)}) collective-permute-start(bf16[256,512]{1,0:T(8,128)(2,1)} %get-tuple-element.155.refs_6_.refs_4_.refs_15_), channel_id=1, source_target_pairs={{0,6},{2,4},{4,2},{6,0},{1,7},{3,5},{5,3},{7,1},{8,14},{10,12},{12... | collective-permute-start | bytes 786440 | tf_op jit(solution)/shard_map/ppermute | solution.py:730
  73.1 11.5 %all-to-all-start.2 = ((f32[32,8,128]{2,1,0:T(8,128)}), f32[32,8,128]{2,1,0:T(8,128)}, u32[]{:S(2)}, u32[]{:S(2)}) async-start(f32[32,8,128]{2,1,0:T(8,128)} %get-tuple-element.153), calls=%async_computation.2 | async-start | bytes 262144 | tf_op jit(solution)/shard_map/all_to_all | solution.py:756
  91.3 14.7 %all-to-all-start.3 = ((bf16[32,32,128]{2,1,0:T(8,128)(2,1)}), bf16[32,32,128]{2,1,0:T(8,128)(2,1)}, u32[]{:S(2)}, u32[]{:S(2)}) async-start(bf16[32,32,128]{2,1,0:T(8,128)(2,1)} %bitcast.47), calls=%async_computation.3 | async-start | bytes 524288 | tf_op jit(solution)/shard_map/all_to_all | solution.py:756
  94.8 11.2 %collective-permute-start.15 = (bf16[256,128]{1,0:T(8,128)(2,1)}, bf16[256,128]{1,0:T(8,128)(2,1)}, u32[]{:S(2)}, u32[]{:S(2)}) collective-permute-start(bf16[256,128]{1,0:T(8,128)(2,1)} %get-tuple-element.169), channel_id=1, source_target_pairs={{0,2},{2,0},{4,6},{6,4},{1,3},{3,1},{5,7},{7,5},{8,10},{10,8},{12,... | collective-permute-start | bytes 196616 | tf_op jit(solution)/shard_map/ppermute | solution.py:730
  96.3 9.7 %collective-permute-start.16 = (bf16[256,128]{1,0:T(8,128)(2,1)}, bf16[256,128]{1,0:T(8,128)(2,1)}, u32[]{:S(2)}, u32[]{:S(2)}) collective-permute-start(bf16[256,128]{1,0:T(8,128)(2,1)} %get-tuple-element.170), channel_id=1, source_target_pairs={{0,4},{2,6},{4,0},{6,2},{1,5},{3,7},{5,1},{7,3},{8,12},{10,14},{12... | collective-permute-start | bytes 196616 | tf_op jit(solution)/shard_map/ppermute | solution.py:730
  97.8 8.2 %collective-permute-start.17 = (bf16[256,128]{1,0:T(8,128)(2,1)}, bf16[256,128]{1,0:T(8,128)(2,1)}, u32[]{:S(2)}, u32[]{:S(2)}) collective-permute-start(bf16[256,128]{1,0:T(8,128)(2,1)} %get-tuple-element.171), channel_id=1, source_target_pairs={{0,6},{2,4},{4,2},{6,0},{1,7},{3,5},{5,3},{7,1},{8,14},{10,12},{12... | collective-permute-start | bytes 196616 | tf_op jit(solution)/shard_map/ppermute | solution.py:730
  112.6 2.3 collective-permute-start.18
  116.1 9.1 %collective-permute-start.19 = (bf16[1152,128]{1,0:T(8,128)(2,1)S(1)}, bf16[1152,128]{1,0:T(8,128)(2,1)S(1)}, u32[]{:S(2)}, u32[]{:S(2)}) collective-permute-start(bf16[1152,128]{1,0:T(8,128)(2,1)S(1)} %get-tuple-element.175), channel_id=1, source_target_pairs={{0,8},{8,0},{16,24},{24,16},{1,9},{9,1},{17,25},{25,17},{2,10},{10... | collective-permute-start | bytes 884744 | tf_op jit(solution)/shard_map/ppermute | solution.py:730
  117.6 10.2 %collective-permute-start.20 = (bf16[512,256]{1,0:T(8,128)(2,1)S(1)}, bf16[512,256]{1,0:T(8,128)(2,1)S(1)}, u32[]{:S(2)}, u32[]{:S(2)}) collective-permute-start(bf16[512,256]{1,0:T(8,128)(2,1)S(1)} %copy-done.17), channel_id=1, source_target_pairs={{0,2},{2,0},{4,6},{6,4},{1,3},{3,1},{5,7},{7,5},{8,10},{10,8},{12,... | collective-permute-start | bytes 786440 | tf_op jit(solution)/shard_map/ppermute | solution.py:730
  119.1 13.4 %collective-permute-start.21 = (bf16[512,256]{1,0:T(8,128)(2,1)S(1)}, bf16[512,256]{1,0:T(8,128)(2,1)S(1)}, u32[]{:S(2)}, u32[]{:S(2)}) collective-permute-start(bf16[512,256]{1,0:T(8,128)(2,1)S(1)} %copy-done.17), channel_id=1, source_target_pairs={{0,4},{2,6},{4,0},{6,2},{1,5},{3,7},{5,1},{7,3},{8,12},{10,14},{12... | collective-permute-start | bytes 786440 | tf_op jit(solution)/shard_map/ppermute | solution.py:730
  120.6 11.9 %collective-permute-start.22 = (bf16[512,256]{1,0:T(8,128)(2,1)S(1)}, bf16[512,256]{1,0:T(8,128)(2,1)S(1)}, u32[]{:S(2)}, u32[]{:S(2)}) collective-permute-start(bf16[512,256]{1,0:T(8,128)(2,1)S(1)} %copy-done.17), channel_id=1, source_target_pairs={{0,6},{2,4},{4,2},{6,0},{1,7},{3,5},{5,3},{7,1},{8,14},{10,12},{12... | collective-permute-start | bytes 786440 | tf_op jit(solution)/shard_map/ppermute | solution.py:730
  125.3 9.2 %collective-permute-start.23 = (bf16[576,128]{1,0:T(8,128)(2,1)S(1)}, bf16[576,128]{1,0:T(8,128)(2,1)S(1)}, u32[]{:S(2)}, u32[]{:S(2)}) collective-permute-start(bf16[576,128]{1,0:T(8,128)(2,1)S(1)} %get-tuple-element.178), channel_id=1, source_target_pairs={{0,16},{8,24},{16,0},{24,8},{1,17},{9,25},{17,1},{25,9},{2,18},{10... | collective-permute-start | bytes 442376 | tf_op jit(solution)/shard_map/ppermute | solution.py:730
  134.5 9.0 %collective-permute-start.27 = (bf16[576,128]{1,0:T(8,128)(2,1)S(1)}, bf16[576,128]{1,0:T(8,128)(2,1)S(1)}, u32[]{:S(2)}, u32[]{:S(2)}) collective-permute-start(bf16[576,128]{1,0:T(8,128)(2,1)S(1)} %add_convert_fusion.refs_1_), channel_id=1, source_target_pairs={{0,16},{8,24},{16,0},{24,8},{1,17},{9,25},{17,1},{25,9},{2,18},{10... | collective-permute-start | bytes 442376 | tf_op jit(solution)/shard_map/ppermute | solution.py:730
  137.6 12.9 %collective-permute-start.24 = (bf16[2304,128]{1,0:T(8,128)(2,1)S(1)}, bf16[2304,128]{1,0:T(8,128)(2,1)S(1)}, u32[]{:S(2)}, u32[]{:S(2)}) collective-permute-start(bf16[2304,128]{1,0:T(8,128)(2,1)S(1)} %get-tuple-element.181), channel_id=1, source_target_pairs={{0,1},{1,0},{2,3},{3,2},{4,5},{5,4},{6,7},{7,6},{8,9},{9,8},{10,11... | collective-permute-start | bytes 1769480 | tf_op jit(solution)/shard_map/ppermute | solution.py:730
  143.6 6.8 %collective-permute-start.28 = (bf16[1152,128]{1,0:T(8,128)(2,1)S(1)}, bf16[1152,128]{1,0:T(8,128)(2,1)S(1)}, u32[]{:S(2)}, u32[]{:S(2)}) collective-permute-start(bf16[1152,128]{1,0:T(8,128)(2,1)S(1)} %shard_map.357.refs_1_), channel_id=1, source_target_pairs={{0,8},{8,0},{16,24},{24,16},{1,9},{9,1},{17,25},{25,17},{2,10},{10... | collective-permute-start | bytes 884744 | tf_op jit(solution)/shard_map/ppermute | solution.py:730
  150.4 12.3 %collective-permute-start.29 = (bf16[2304,128]{1,0:T(8,128)(2,1)S(1)}, bf16[2304,128]{1,0:T(8,128)(2,1)S(1)}, u32[]{:S(2)}, u32[]{:S(2)}) collective-permute-start(bf16[2304,128]{1,0:T(8,128)(2,1)S(1)} %shard_map.358.refs_1_), channel_id=1, source_target_pairs={{0,1},{1,0},{2,3},{3,2},{4,5},{5,4},{6,7},{7,6},{8,9},{9,8},{10,11... | collective-permute-start | bytes 1769480 | tf_op jit(solution)/shard_map/ppermute | solution.py:730
  150.7 9.5 %collective-permute-start.25 = (bf16[1152,128]{1,0:T(8,128)(2,1)S(1)}, bf16[1152,128]{1,0:T(8,128)(2,1)S(1)}, u32[]{:S(2)}, u32[]{:S(2)}) collective-permute-start(bf16[1152,128]{1,0:T(8,128)(2,1)S(1)} %get-tuple-element.183), channel_id=1, source_target_pairs={{0,8},{8,0},{16,24},{24,16},{1,9},{9,1},{17,25},{25,17},{2,10},{10... | collective-permute-start | bytes 884744 | tf_op jit(solution)/shard_map/ppermute | solution.py:730
  160.2 9.6 %collective-permute-start.26 = (bf16[576,128]{1,0:T(8,128)(2,1)S(1)}, bf16[576,128]{1,0:T(8,128)(2,1)S(1)}, u32[]{:S(2)}, u32[]{:S(2)}) collective-permute-start(bf16[576,128]{1,0:T(8,128)(2,1)S(1)} %get-tuple-element.185), channel_id=1, source_target_pairs={{0,16},{8,24},{16,0},{24,8},{1,17},{9,25},{17,1},{25,9},{2,18},{10... | collective-permute-start | bytes 442376 | tf_op jit(solution)/shard_map/ppermute | solution.py:730
  170.0 9.0 %collective-permute-start.34 = (bf16[576,128]{1,0:T(8,128)(2,1)S(1)}, bf16[576,128]{1,0:T(8,128)(2,1)S(1)}, u32[]{:S(2)}, u32[]{:S(2)}) collective-permute-start(bf16[576,128]{1,0:T(8,128)(2,1)S(1)} %get-tuple-element.188.refs_1_), channel_id=1, source_target_pairs={{0,16},{8,24},{16,0},{24,8},{1,17},{9,25},{17,1},{25,9},{2,18},{10... | collective-permute-start | bytes 442376 | tf_op jit(solution)/shard_map/ppermute | solution.py:730
  170.0 10.5 %collective-permute-start.35 = (bf16[576,128]{1,0:T(8,128)(2,1)S(1)}, bf16[576,128]{1,0:T(8,128)(2,1)S(1)}, u32[]{:S(2)}, u32[]{:S(2)}) collective-permute-start(bf16[576,128]{1,0:T(8,128)(2,1)S(1)} %get-tuple-element.196.refs_1_), channel_id=1, source_target_pairs={{0,2},{2,0},{4,6},{6,4},{1,3},{3,1},{5,7},{7,5},{8,10},{10,8},{12,... | collective-permute-start | bytes 442376 | tf_op jit(solution)/shard_map/ppermute | solution.py:730
  171.6 10.7 %collective-permute-start.36 = (bf16[576,128]{1,0:T(8,128)(2,1)S(1)}, bf16[576,128]{1,0:T(8,128)(2,1)S(1)}, u32[]{:S(2)}, u32[]{:S(2)}) collective-permute-start(bf16[576,128]{1,0:T(8,128)(2,1)S(1)} %get-tuple-element.196.refs_1_), channel_id=1, source_target_pairs={{0,4},{2,6},{4,0},{6,2},{1,5},{3,7},{5,1},{7,3},{8,12},{10,14},{12... | collective-permute-start | bytes 442376 | tf_op jit(solution)/shard_map/ppermute | solution.py:730
  173.1 9.2 %collective-permute-start.37 = (bf16[576,128]{1,0:T(8,128)(2,1)S(1)}, bf16[576,128]{1,0:T(8,128)(2,1)S(1)}, u32[]{:S(2)}, u32[]{:S(2)}) collective-permute-start(bf16[576,128]{1,0:T(8,128)(2,1)S(1)} %get-tuple-element.196.refs_1_), channel_id=1, source_target_pairs={{0,6},{2,4},{4,2},{6,0},{1,7},{3,5},{5,3},{7,1},{8,14},{10,12},{12... | collective-permute-start | bytes 442376 | tf_op jit(solution)/shard_map/ppermute | solution.py:730
  173.6 28.5 %collective-permute-start.30 = (bf16[2304,128]{1,0:T(8,128)(2,1)S(1)}, bf16[2304,128]{1,0:T(8,128)(2,1)S(1)}, u32[]{:S(2)}, u32[]{:S(2)}) collective-permute-start(bf16[2304,128]{1,0:T(8,128)(2,1)S(1)} %get-tuple-element.186.refs_1_), channel_id=1, source_target_pairs={{0,2},{2,0},{4,6},{6,4},{1,3},{3,1},{5,7},{7,5},{8,10},{10,8},{12,... | collective-permute-start | bytes 1769480 | tf_op jit(solution)/shard_map/ppermute | solution.py:730
  179.0 26.2 %collective-permute-start.31 = (bf16[2304,128]{1,0:T(8,128)(2,1)S(1)}, bf16[2304,128]{1,0:T(8,128)(2,1)S(1)}, u32[]{:S(2)}, u32[]{:S(2)}) collective-permute-start(bf16[2304,128]{1,0:T(8,128)(2,1)S(1)} %get-tuple-element.186.refs_1_), channel_id=1, source_target_pairs={{0,4},{2,6},{4,0},{6,2},{1,5},{3,7},{5,1},{7,3},{8,12},{10,14},{12... | collective-permute-start | bytes 1769480 | tf_op jit(solution)/shard_map/ppermute | solution.py:730
  180.5 24.7 %collective-permute-start.32 = (bf16[2304,128]{1,0:T(8,128)(2,1)S(1)}, bf16[2304,128]{1,0:T(8,128)(2,1)S(1)}, u32[]{:S(2)}, u32[]{:S(2)}) collective-permute-start(bf16[2304,128]{1,0:T(8,128)(2,1)S(1)} %get-tuple-element.186.refs_1_), channel_id=1, source_target_pairs={{0,6},{2,4},{4,2},{6,0},{1,7},{3,5},{5,3},{7,1},{8,14},{10,12},{12... | collective-permute-start | bytes 1769480 | tf_op jit(solution)/shard_map/ppermute | solution.py:730
  182.7 9.1 %collective-permute-start.38 = (bf16[576,128]{1,0:T(8,128)(2,1)S(1)}, bf16[576,128]{1,0:T(8,128)(2,1)S(1)}, u32[]{:S(2)}, u32[]{:S(2)}) collective-permute-start(bf16[576,128]{1,0:T(8,128)(2,1)S(1)} %shard_map.367.refs_1_), channel_id=1, source_target_pairs={{0,16},{8,24},{16,0},{24,8},{1,17},{9,25},{17,1},{25,9},{2,18},{10... | collective-permute-start | bytes 442376 | tf_op jit(solution)/shard_map/ppermute | solution.py:730
  191.9 10.0 %collective-permute-start.39 = (bf16[1152,128]{1,0:T(8,128)(2,1)S(1)}, bf16[1152,128]{1,0:T(8,128)(2,1)S(1)}, u32[]{:S(2)}, u32[]{:S(2)}) collective-permute-start(bf16[1152,128]{1,0:T(8,128)(2,1)S(1)} %shard_map.368.refs_1_), channel_id=1, source_target_pairs={{0,8},{8,0},{16,24},{24,16},{1,9},{9,1},{17,25},{25,17},{2,10},{10... | collective-permute-start | bytes 884744 | tf_op jit(solution)/shard_map/ppermute | solution.py:730
  192.0 15.0 %collective-permute-start.41 = (bf16[1152,128]{1,0:T(8,128)(2,1)S(1)}, bf16[1152,128]{1,0:T(8,128)(2,1)S(1)}, u32[]{:S(2)}, u32[]{:S(2)}) collective-permute-start(bf16[1152,128]{1,0:T(8,128)(2,1)S(1)} %shard_map.366.refs_1_), channel_id=1, source_target_pairs={{0,8},{8,0},{16,24},{24,16},{1,9},{9,1},{17,25},{25,17},{2,10},{10... | collective-permute-start | bytes 884744 | tf_op jit(solution)/shard_map/ppermute | solution.py:730
  202.0 5.3 %collective-permute-start.40 = (bf16[2304,128]{1,0:T(8,128)(2,1)S(1)}, bf16[2304,128]{1,0:T(8,128)(2,1)S(1)}, u32[]{:S(2)}, u32[]{:S(2)}) collective-permute-start(bf16[2304,128]{1,0:T(8,128)(2,1)S(1)} %shard_map.370.refs_1_), channel_id=1, source_target_pairs={{0,1},{1,0},{2,3},{3,2},{4,5},{5,4},{6,7},{7,6},{8,9},{9,8},{10,11... | collective-permute-start | bytes 1769480 | tf_op jit(solution)/shard_map/ppermute | solution.py:730
  207.2 9.2 %collective-permute-start.42 = (bf16[2304,128]{1,0:T(8,128)(2,1)S(1)}, bf16[2304,128]{1,0:T(8,128)(2,1)S(1)}, u32[]{:S(2)}, u32[]{:S(2)}) collective-permute-start(bf16[2304,128]{1,0:T(8,128)(2,1)S(1)} %shard_map.373.refs_1_), channel_id=1, source_target_pairs={{0,1},{1,0},{2,3},{3,2},{4,5},{5,4},{6,7},{7,6},{8,9},{9,8},{10,11... | collective-permute-start | bytes 1769480 | tf_op jit(solution)/shard_map/ppermute | solution.py:730
  211.3 7.3 %collective-permute-start.43 = (f32[8,128]{1,0:T(8,128)S(1)}, f32[8,128]{1,0:T(8,128)S(1)}, u32[]{:S(2)}, u32[]{:S(2)}) collective-permute-start(f32[8,128]{1,0:T(8,128)S(1)} %get-tuple-element.204.refs_0_), channel_id=1, source_target_pairs={{0,2},{2,0},{4,6},{6,4},{1,3},{3,1},{5,7},{7,5},{8,10},{10,8},{12,... | collective-permute-start | bytes 12296 | tf_op jit(solution)/shard_map/ppermute | solution.py:730
  214.6 4.0 %collective-permute-start.44 = (f32[8,128]{1,0:T(8,128)S(1)}, f32[8,128]{1,0:T(8,128)S(1)}, u32[]{:S(2)}, u32[]{:S(2)}) collective-permute-start(f32[8,128]{1,0:T(8,128)S(1)} %get-tuple-element.204.refs_0_), channel_id=1, source_target_pairs={{0,4},{2,6},{4,0},{6,2},{1,5},{3,7},{5,1},{7,3},{8,12},{10,14},{12... | collective-permute-start | bytes 12296 | tf_op jit(solution)/shard_map/ppermute | solution.py:730
  216.4 4.5 %collective-permute-start.45 = (f32[8,128]{1,0:T(8,128)S(1)}, f32[8,128]{1,0:T(8,128)S(1)}, u32[]{:S(2)}, u32[]{:S(2)}) collective-permute-start(f32[8,128]{1,0:T(8,128)S(1)} %get-tuple-element.204.refs_0_), channel_id=1, source_target_pairs={{0,6},{2,4},{4,2},{6,0},{1,7},{3,5},{5,3},{7,1},{8,14},{10,12},{12... | collective-permute-start | bytes 12296 | tf_op jit(solution)/shard_map/ppermute | solution.py:730
  (34 other events, 395.5 us)
